TPU v7x, 32 devices: a whole 2x2x4 slice. The times are simulated.
32 devices in a mesh: region: 4 (over z), dev: 8 (over y, x, core).
Axes of the slice: x: 2, y: 2, z: 4, core: 2. Of those that a mesh axis runs over, the one named last changes fastest.
Arguments:
- basis_values: bfloat16 [384, 4, 256, 128], P(('region', 'dev')), may hold values from -6 to 6
- density_rows: bfloat16 [96, 4, 128, 128], P(('region', 'dev')), may hold values from -0.013671875 to 0.013671875
- block_mask: int32 [96, 4], P(('region', 'dev')), may hold values 0 or 1
- window_start: int32 [32], P(('region', 'dev')), may hold values from 0 to 23
- batch_offsets: int32 [32, 12], P(('region', 'dev')), may hold values from 0 to 4, as said below
- batch_sizes: int32 [32, 12], P(('region', 'dev')), may hold values from 1 to 256, 1920 in all within a row
- atom_near: int32 [384, 6], P(('region', 'dev')), may hold values from 0 to 383
- harmonics: bfloat16 [384, 6, 25, 256], P(('region', 'dev')), may hold values from -6 to 6
- partition: float32 [384, 6, 256], P(('region', 'dev')), may hold values from 0.002 to 0.05
- radius: float32 [384, 6, 256], P(('region', 'dev')), may hold values from 0 to 15
- radial_table: float32 [25, 16], replicated, may hold values from -1.5 to 1.5
Outputs:
- density: float32 [384, 256], P(('region', 'dev'))
- moments: float32 [25, 512], P(None, ('region', 'dev'))
- potential: float32 [384, 256], P(('region', 'dev'))
Inputs may be any that keep to these rules, and one draw needn't show every extreme that they name: The blocks of a batch are positions batch_offsets to batch_offsets + 3 of its device's window of 8 consecutive blocks.
All inputs are finite; a program needn't handle non-finite values. No bound on the sum of `block_mask` on one device may be relied on, other than what follows from the above.
Results may differ from a plain program's by a relative error of at most 0.0029.
Values may be sent and summed in bfloat16 or wider, within the bound.
No kernel may reach another device: no remote copies, remote signals or barrier semaphores. Data moves between devices by JAX's collectives and lax.ppermute only.
A program may use at most 64 MiB of HBM per device.

v0:
```python
import jax
import jax.numpy as jnp
from jax import lax
from jax.sharding import PartitionSpec as P

ATOM_DEV = 16


def padded_2(cells, sides, width):
    for axis, dim in sides:
        count = lax.axis_size(axis)
        head = lax.slice_in_dim(cells, 0, width, axis=dim)
        tail = lax.slice_in_dim(cells, cells.shape[dim] - width, cells.shape[dim], axis=dim)
        cells = jnp.concatenate(
            [
                lax.ppermute(tail, axis, [(i, (i + 1) % count) for i in range(count)]),
                cells,
                lax.ppermute(head, axis, [((i + 1) % count, i) for i in range(count)]),
            ],
            axis=dim,
        )
    return cells


def spline_basis(radii_row, knot_count):
    knot_points = jnp.arange(knot_count).astype(jnp.float32)
    distance = jnp.abs(radii_row[..., None, :] - knot_points[:, None])
    inner_part = 2.0 / 3.0 - distance * distance + 0.5 * distance * distance * distance
    remote = 2.0 - distance
    outer_part = remote * remote * remote / 6.0
    return jnp.where(distance < 1.0, inner_part, jnp.where(distance < 2.0, outer_part, 0.0))


def batch_density(values, row_blocks):
    block_total = values.shape[0]
    band_width = row_blocks.shape[1]
    leading = jnp.zeros((1,) + values.shape[1:], values.dtype)
    trailing = jnp.zeros((band_width - 2,) + values.shape[1:], values.dtype)
    padded = jnp.concatenate([leading, values, trailing], axis=0)
    stacked = jnp.stack(
        [padded[column : column + block_total] for column in range(band_width)], axis=2
    )
    mixed_rows = jnp.einsum(
        "jpkf,jkgf->jpg", stacked, row_blocks, preferred_element_type=jnp.float32
    )
    return jnp.sum(values.astype(jnp.float32) * mixed_rows, axis=(0, 2))


def per_device(
    basis_values,
    density_rows,
    block_mask,
    window_start,
    batch_offsets,
    batch_sizes,
    atom_near,
    harmonics,
    partition,
    radius,
    radial_table,
):
    dev_count = lax.axis_size("dev")
    blocks_dev = density_rows.shape[0]
    block_count = blocks_dev * dev_count
    masked = density_rows * block_mask.astype(jnp.bfloat16)[:, :, None, None]
    first_block = window_start[0]
    positions = jnp.arange(dev_count, dtype=jnp.int32)
    spatial = (first_block + positions) % block_count
    owner_index = spatial % dev_count
    peer_index = jnp.arange(dev_count, dtype=jnp.int32)
    ahead_count = (peer_index - first_block) % dev_count
    wanted = (first_block + ahead_count) % block_count // dev_count
    requested = lax.all_to_all(wanted[:, None], "dev", split_axis=0, concat_axis=0, tiled=True)[
        :, 0
    ]
    served = jnp.take(masked, jnp.clip(requested, 0, blocks_dev - 1), axis=0)
    replies = lax.all_to_all(served, "dev", split_axis=0, concat_axis=0, tiled=True)
    window = jnp.take(replies, owner_index, axis=0)

    def one_density(batch_item):
        values, offset = batch_item
        row_blocks = lax.dynamic_slice_in_dim(window, offset, values.shape[0], 0)
        return batch_density(values, row_blocks)

    point_total = basis_values.shape[2]
    alive_mask = (
        jnp.arange(point_total, dtype=jnp.int32)[None, :] < batch_sizes[0][:, None]
    ).astype(jnp.float32)
    density = lax.map(one_density, (basis_values, batch_offsets[0])) * alive_mask
    moment_terms = jnp.einsum(
        "bip,bilp->bil",
        partition * density[:, None, :],
        harmonics.astype(jnp.float32),
        precision=lax.Precision.HIGHEST,
    )
    comp_total = moment_terms.shape[2]
    atom_region = ATOM_DEV * dev_count
    flattened = atom_near.reshape(-1)
    onehot = (flattened[:, None] == jnp.arange(3 * atom_region, dtype=jnp.int32)[None, :]).astype(
        jnp.float32
    )
    partial_value = jnp.dot(
        moment_terms.reshape(-1, comp_total).T, onehot, precision=lax.Precision.HIGHEST
    )
    partial_value = partial_value.reshape(comp_total, 3, atom_region).transpose(1, 0, 2)
    owner_sums = lax.psum_scatter(partial_value, "dev", scatter_dimension=2, tiled=True)
    side_parts = jnp.stack([owner_sums[0], owner_sums[2]])[None]
    rim_parts = padded_2(side_parts, (("region", 0),), 1)
    moments = owner_sums[1] + rim_parts[0, 1] + rim_parts[2, 0]
    own_table = (moments[:, None, :] * radial_table[:, :, None]).astype(jnp.bfloat16)
    rim_table = padded_2(own_table[None], (("region", 0),), 1)
    spline_table = lax.all_gather(rim_table, "dev", axis=3, tiled=True)
    knot_total = radial_table.shape[1]
    batch_total = atom_near.shape[0]
    near_total = atom_near.shape[1]
    table_flat = spline_table.transpose(1, 2, 0, 3).reshape(comp_total, knot_total, 3 * atom_region)
    selected = jnp.take(table_flat, flattened, axis=2).reshape(
        comp_total, knot_total, batch_total, near_total
    )
    spline = spline_basis(radius, knot_total)
    radial = jnp.einsum(
        "lrbi,birp->bilp", selected.astype(jnp.float32), spline, precision=lax.Precision.HIGHEST
    )
    potential = jnp.sum(harmonics.astype(jnp.float32) * radial, axis=(1, 2)) * alive_mask
    return (density, moments, potential)


def solution(mesh):
    placed = (
        P(("region", "dev"), None, None, None),
        P(("region", "dev"), None, None, None),
        P(("region", "dev"), None),
        P(("region", "dev")),
        P(("region", "dev"), None),
        P(("region", "dev"), None),
        P(("region", "dev"), None),
        P(("region", "dev"), None, None, None),
        P(("region", "dev"), None, None),
        P(("region", "dev"), None, None),
        P(),
    )
    return jax.shard_map(
        per_device,
        mesh=mesh,
        in_specs=placed,
        out_specs=(
            P(("region", "dev"), None),
            P(None, ("region", "dev")),
            P(("region", "dev"), None),
        ),
        check_vma=False,
    )
```

profile of v0, /device:TPU:0, one launch (start us, length us, event | category | flops | bytes accessed | tf_op | source)
XLA Modules:
  0.0 143.9 jit_solution(17455729678010167332)
XLA Ops:
  1.3 0.6 and_select_fusion
  1.9 5.2 %all-to-all-start = ((s32[8,1,1]{2,1,0:T(1,128)}), s32[8,1,1]{2,1,0:T(1,128)S(1)}, u32[]{:S(2)}, u32[]{:S(2)}) async-start(s32[8,1,1]{2,1,0:T(1,128)} %and_select_fusion), calls=%async_computation | async-start | bytes 8192 | tf_op jit(solution)/shard_map/all_to_all | solution.py:73
  7.1 0.7 convert_element_type.30
  7.8 1.1 broadcast_multiply_fusion
  8.9 2.8 %all-to-all-done = s32[8,1,1]{2,1,0:T(1,128)S(1)} async-done(((s32[8,1,1]{2,1,0:T(1,128)}), s32[8,1,1]{2,1,0:T(1,128)S(1)}, u32[]{:S(2)}, u32[]{:S(2)}) %all-to-all-start) | async-done | bytes 64 | tf_op jit(solution)/shard_map/all_to_all | solution.py:73
  11.7 0.2 clamp_reduce_fusion
  12.0 0.7 gather_fusion
  12.7 1.1 broadcast_select_fusion
  13.9 3.7 %all-to-all-start.1 = ((bf16[8,4,128,128]{3,2,1,0:T(8,128)(2,1)}), bf16[8,4,128,128]{3,2,1,0:T(8,128)(2,1)S(1)}, u32[]{:S(2)}, u32[]{:S(2)}) async-start(bf16[8,4,128,128]{3,2,1,0:T(8,128)(2,1)} %broadcast_select_fusion), calls=%async_computation.1 | async-start | bytes 2097152 | tf_op jit(solution)/shard_map/all_to_all | solution.py:77
  17.9 0.6 dynamic-slice
  19.2 13.7 %all-to-all-done.1 = bf16[8,4,128,128]{3,2,1,0:T(8,128)(2,1)S(1)} async-done(((bf16[8,4,128,128]{3,2,1,0:T(8,128)(2,1)}), bf16[8,4,128,128]{3,2,1,0:T(8,128)(2,1)S(1)}, u32[]{:S(2)}, u32[]{:S(2)}) %all-to-all-start.1) | async-done | bytes 1048608 | tf_op jit(solution)/shard_map/all_to_all | solution.py:77
  32.9 0.7 gather_fusion.1
  33.8 0.5 copy-done.8
  34.3 51.1 %while.11 = (s32[]{:T(128)}, f32[12,256]{1,0:T(8,128)S(1)}, bf16[12,4,256,128]{3,2,1,0:T(8,128)(2,1)}, s32[12]{0:T(128)S(1)}, bf16[8,4,128,128]{3,2,1,0:T(8,128)(2,1)S(1)}) while((s32[]{:T(128)}, f32[12,256]{1,0:T(8,128)S(1)}, bf16[12,4,256,128]{3,2,1,0:T(8,128)(2,1)}, s32[12]{0:T(128)S(1)}, ...), condition=%wide.region_2.3_spmd.clone, body=%wide.region_0.2_spmd.sunk.clone | while | flops 136183552 | bytes 3673215 | solution.py:89
  34.3 0.6 dynamic_slice.23
  36.8 1.0 dynamic-slice_bitcast_fusion.4
  38.0 0.5 fusion.75
  38.6 0.6 dynamic_slice.23
  41.1 1.0 dynamic-slice_bitcast_fusion.4
  42.2 0.5 fusion.75
  42.8 0.6 dynamic_slice.23
  45.4 1.0 dynamic-slice_bitcast_fusion.4
  46.5 0.5 fusion.75
  47.1 0.6 dynamic_slice.23
  49.6 1.0 dynamic-slice_bitcast_fusion.4
  50.7 0.5 fusion.75
  51.3 0.6 dynamic_slice.23
  53.9 1.0 dynamic-slice_bitcast_fusion.4
  55.0 0.5 fusion.75
  55.6 0.6 dynamic_slice.23
  58.1 1.0 dynamic-slice_bitcast_fusion.4
  59.3 0.5 fusion.75
  59.8 0.6 dynamic_slice.23
  62.4 1.0 dynamic-slice_bitcast_fusion.4
  63.5 0.5 fusion.75
  64.1 0.6 dynamic_slice.23
  66.6 1.0 dynamic-slice_bitcast_fusion.4
  67.8 0.5 fusion.75
  68.4 0.6 dynamic_slice.23
  70.9 1.0 dynamic-slice_bitcast_fusion.4
  72.0 0.5 fusion.75
  72.6 0.6 dynamic_slice.23
  75.2 1.0 dynamic-slice_bitcast_fusion.4
  76.3 0.5 fusion.75
  76.9 0.6 dynamic_slice.23
  79.4 1.0 dynamic-slice_bitcast_fusion.4
  80.5 0.5 fusion.75
  81.1 0.6 dynamic_slice.23
  83.7 1.0 dynamic-slice_bitcast_fusion.4
  84.8 0.5 fusion.75
  85.5 1.0 fusion.39
  86.6 0.2 convolution_bitcast_fusion.1
  87.0 25.3 %all-reduce.2 = f32[3,25,128]{1,0,2:T(4,128)S(1)} all-reduce(f32[3,25,128]{1,0,2:T(4,128)S(1)} %copy.50), channel_id=2, replica_groups=mesh['region'=4,'dev'=8] {'dev'}, use_global_device_ids=true, to_apply=%region_3.4.clone | all-reduce | flops 9600 | bytes 76800
  112.4 3.7 %collective-permute-start.1 = (f32[1,2,25,16]{2,1,3,0:T(2,128)S(1)}, f32[1,2,25,16]{2,1,3,0:T(2,128)S(1)}, u32[]{:S(2)}, u32[]{:S(2)}) collective-permute-start(f32[1,2,25,16]{2,1,3,0:T(2,128)S(1)} %maximum_bitcast_fusion), channel_id=1, source_target_pairs={{8,0},{16,8},{24,16},{0,24},{9,1},{17,9},{25,17},{1,25},{10,2},{18... | collective-permute-start | bytes 9608 | tf_op jit(solution)/shard_map/ppermute | solution.py:18
  116.1 1.4 collective-permute-done.1
  117.5 4.1 %collective-permute-done = f32[1,2,25,16]{2,3,1,0:T(8,128)S(1)} collective-permute-done((f32[1,2,25,16]{2,3,1,0:T(8,128)S(1)}, f32[1,2,25,16]{2,3,1,0:T(8,128)S(1)}, u32[]{:S(2)}, u32[]{:S(2)}) %collective-permute-start) | collective-permute-done | bytes 3232 | tf_op jit(solution)/shard_map/ppermute | solution.py:16
  121.7 2.0 %collective-permute-start.2 = (bf16[1,25,16,16]{1,3,2,0:T(8,128)(2,1)S(1)}, bf16[1,25,16,16]{1,3,2,0:T(8,128)(2,1)S(1)}, u32[]{:S(2)}, u32[]{:S(2)}) collective-permute-start(bf16[1,25,16,16]{1,3,2,0:T(8,128)(2,1)S(1)} %multiply_convert_fusion), channel_id=1, source_target_pairs={{0,8},{8,16},{16,24},{24,0},{1,9},{9,17},{17,25},{25,1},{2,10},{10... | collective-permute-start | bytes 38408 | tf_op jit(solution)/shard_map/ppermute | solution.py:16
  123.8 2.1 %collective-permute-done.3 = bf16[1,25,16,16]{1,3,2,0:T(8,128)(2,1)S(1)} collective-permute-done((bf16[1,25,16,16]{1,3,2,0:T(8,128)(2,1)S(1)}, bf16[1,25,16,16]{1,3,2,0:T(8,128)(2,1)S(1)}, u32[]{:S(2)}, u32[]{:S(2)}) %collective-permute-start.3) | collective-permute-done | bytes 12832 | tf_op jit(solution)/shard_map/ppermute | solution.py:18
  126.0 1.9 %collective-permute-done.2 = bf16[1,25,16,16]{1,3,2,0:T(8,128)(2,1)S(1)} collective-permute-done((bf16[1,25,16,16]{1,3,2,0:T(8,128)(2,1)S(1)}, bf16[1,25,16,16]{1,3,2,0:T(8,128)(2,1)S(1)}, u32[]{:S(2)}, u32[]{:S(2)}) %collective-permute-start.2) | collective-permute-done | bytes 12832 | tf_op jit(solution)/shard_map/ppermute | solution.py:16
  127.9 12.2 %all_gather.3 = bf16[3,25,16,128]{1,2,0,3:T(8,128)(2,1)S(1)} all-gather(bf16[3,25,16,16]{1,2,0,3:T(8,128)(2,1)S(1)} %copy.54), channel_id=1, replica_groups=mesh['region'=4,'dev'=8] {'dev'}, dimensions={3}, use_global_device_ids=true | all-gather | bytes 345600 | tf_op jit(solution)/shard_map/all_gather | solution.py:112
  140.1 0.3 copy.64
  140.4 0.6 gather_fusion.2
  141.0 2.2 %multiply_reduce_fusion = f32[12,256]{1,0:T(8,128)S(1)} fusion(bf16[12,6,25,256]{3,2,1,0:T(8,128)(2,1)S(1)} %copy-done.6, f32[16]{0:T(128)S(1)} %iota_convert_fusion, f32[12,6,256]{2,1,0:T(8,128)S(1)} %copy-done.7, bf16[25,16,12,6]{0,1,3,2:T(8,128)(2,1)S(1)} %bitcast.83, pred[12,6]{1,0:T(8,128)(4,1)S(1)} %copy.53), kind=kOutput, calls=%fused_computation.24 | convolution fusion | flops 94600320 | bytes 1065352 | tf_op jit(solution)/shard_map/lrbi,birp->bilp/dot_general | solution.py:121
  143.3 0.7 fusion.44
  (75 shorter events, 2.9 us)
Async XLA Ops:
  1.9 9.8 %all-to-all-start = ((s32[8,1,1]{2,1,0:T(1,128)}), s32[8,1,1]{2,1,0:T(1,128)S(1)}, u32[]{:S(2)}, u32[]{:S(2)}) async-start(s32[8,1,1]{2,1,0:T(1,128)} %and_select_fusion), calls=%async_computation | async-start | bytes 8192 | tf_op jit(solution)/shard_map/all_to_all | solution.py:73
  13.8 3.7 %copy-start.3 = (s32[12,6]{0,1:T(8,128)S(1)}, s32[12,6]{0,1:T(8,128)}, u32[]{:S(2)}) copy-start(s32[12,6]{0,1:T(8,128)} %param.19) | copy-start | bytes 868
  13.9 4.0 %copy-start.9 = (u32[32]{0:T(128)S(1)}, u32[32]{0:T(128)}, u32[]{:S(2)}) copy-start(u32[32]{0:T(128)} %constant.139) | copy-start | bytes 388
  13.9 19.0 %all-to-all-start.1 = ((bf16[8,4,128,128]{3,2,1,0:T(8,128)(2,1)}), bf16[8,4,128,128]{3,2,1,0:T(8,128)(2,1)S(1)}, u32[]{:S(2)}, u32[]{:S(2)}) async-start(bf16[8,4,128,128]{3,2,1,0:T(8,128)(2,1)} %broadcast_select_fusion), calls=%async_computation.1 | async-start | bytes 2097152 | tf_op jit(solution)/shard_map/all_to_all | solution.py:77
  33.6 0.7 copy-start.8
  34.3 51.1 %copy-start.5 = (s32[1,12]{1,0:T(1,128)S(1)}, s32[1,12]{1,0:T(1,128)}, u32[]{:S(2)}) copy-start(s32[1,12]{1,0:T(1,128)} %param.18) | copy-start | bytes 148
  34.3 51.2 %copy-start = (f32[12,6,256]{2,1,0:T(8,128)S(1)}, f32[12,6,256]{2,1,0:T(8,128)}, u32[]{:S(2)}) copy-start(f32[12,6,256]{2,1,0:T(8,128)} %param.21) | copy-start | bytes 221188
  34.3 51.2 %copy-start.6 = (bf16[12,6,25,256]{3,2,1,0:T(8,128)(2,1)S(1)}, bf16[12,6,25,256]{3,2,1,0:T(8,128)(2,1)}, u32[]{:S(2)}) copy-start(bf16[12,6,25,256]{3,2,1,0:T(8,128)(2,1)} %param.20) | copy-start | bytes 2764804
  85.5 26.8 %copy-start.1 = (f32[12,256]{1,0:T(8,128)}, f32[12,256]{1,0:T(8,128)S(1)}, u32[]{:S(2)}) copy-start(f32[12,256]{1,0:T(8,128)S(1)} %fusion.45) | copy-start | bytes 36868
  85.5 36.1 %copy-start.4 = (f32[25,16]{0,1:T(8,128)S(1)}, f32[25,16]{0,1:T(8,128)}, u32[]{:S(2)}) copy-start(f32[25,16]{0,1:T(8,128)} %param.23) | copy-start | bytes 4804
  112.4 5.1 %collective-permute-start.1 = (f32[1,2,25,16]{2,1,3,0:T(2,128)S(1)}, f32[1,2,25,16]{2,1,3,0:T(2,128)S(1)}, u32[]{:S(2)}, u32[]{:S(2)}) collective-permute-start(f32[1,2,25,16]{2,1,3,0:T(2,128)S(1)} %maximum_bitcast_fusion), channel_id=1, source_target_pairs={{8,0},{16,8},{24,16},{0,24},{9,1},{17,9},{25,17},{1,25},{10,2},{18... | collective-permute-start | bytes 9608 | tf_op jit(solution)/shard_map/ppermute | solution.py:18
  116.1 5.5 %collective-permute-start = (f32[1,2,25,16]{2,3,1,0:T(8,128)S(1)}, f32[1,2,25,16]{2,3,1,0:T(8,128)S(1)}, u32[]{:S(2)}, u32[]{:S(2)}) collective-permute-start(f32[1,2,25,16]{2,3,1,0:T(8,128)S(1)} %copy.52), channel_id=1, source_target_pairs={{0,8},{8,16},{16,24},{24,0},{1,9},{9,17},{17,25},{25,1},{2,10},{10... | collective-permute-start | bytes 9608 | tf_op jit(solution)/shard_map/ppermute | solution.py:16
  121.6 18.5 %copy-start.2 = (f32[25,16]{0,1:T(8,128)}, f32[25,16]{0,1:T(8,128)S(1)}, u32[]{:S(2)}) copy-start(f32[25,16]{0,1:T(8,128)S(1)} %fusion.47) | copy-start | bytes 4804
  121.6 4.3 %collective-permute-start.3 = (bf16[1,25,16,16]{1,3,2,0:T(8,128)(2,1)S(1)}, bf16[1,25,16,16]{1,3,2,0:T(8,128)(2,1)S(1)}, u32[]{:S(2)}, u32[]{:S(2)}) collective-permute-start(bf16[1,25,16,16]{1,3,2,0:T(8,128)(2,1)S(1)} %multiply_convert_fusion), channel_id=1, source_target_pairs={{8,0},{16,8},{24,16},{0,24},{9,1},{17,9},{25,17},{1,25},{10,2},{18... | collective-permute-start | bytes 38408 | tf_op jit(solution)/shard_map/ppermute | solution.py:18
  121.7 6.1 %collective-permute-start.2 = (bf16[1,25,16,16]{1,3,2,0:T(8,128)(2,1)S(1)}, bf16[1,25,16,16]{1,3,2,0:T(8,128)(2,1)S(1)}, u32[]{:S(2)}, u32[]{:S(2)}) collective-permute-start(bf16[1,25,16,16]{1,3,2,0:T(8,128)(2,1)S(1)} %multiply_convert_fusion), channel_id=1, source_target_pairs={{0,8},{8,16},{16,24},{24,0},{1,9},{9,17},{17,25},{25,1},{2,10},{10... | collective-permute-start | bytes 38408 | tf_op jit(solution)/shard_map/ppermute | solution.py:16
  140.1 0.9 copy-start.7
where the time goes:
time: 145 us; the launch traced here: 144 us
  blocking collectives  37.5 us (26%)
  waiting for transfers between devices  26 us (18%)
  local copies, waits for them, and re-layouts  25.2 us (17%)
  loops' own time  23.7 us (16%)
  starting transfers between devices  14.6 us (10%)
  matrix products  9.84 us (7%)
  other arithmetic  4.92 us (3%)
  between operations  2.23 us (2%)
    unnamed x1, blocking collectives  25.3 us
    another operation x1, loops' own time, per_device(): lax.map(one_density, (basis_values, batch_offsets[0])) * alive_mask  23.7 us
    all_to_all x1, waiting for transfers between devices, per_device(): lax.all_to_all(served, 'dev', split_axis=0, concat_axis=0, tiled=True)  13.7 us
    another operation x24, local copies, waits for them, and re-layouts, batch_density(): jnp.stack([padded[column:column + block_total] for column in range(band_w...  13.5 us
    all_gather x1, blocking collectives, per_device(): spline_table = lax.all_gather(rim_table, 'dev', axis=3, tiled=True)  12.2 us
    dynamic_slice x12, local copies, waits for them, and re-layouts, per_device(): lax.map(one_density, (basis_values, batch_offsets[0])) * alive_mask  7.03 us
    dot_general x12, matrix products, batch_density(): jnp.einsum('jpkf,jkgf->jpg', stacked, row_blocks, preferred_element_type=...  6.34 us
    ppermute x2, waiting for transfers between devices, padded_2(): lax.ppermute(tail, axis, [(i, (i + 1) % count) for i in range(count)])  5.95 us
  transfers between devices with their start and end apart: 6, of which 6 were waited for; matrix products, arithmetic and copies ran while one was open for 2% of the time, Pallas kernels for 0%

commit v1 on v0

v1 whole, which is shorter than its diff:
```python
import functools
import jax
import jax.numpy as jnp
from jax import lax
from jax.experimental import pallas as pl
from jax.experimental.pallas import tpu as pltpu
from jax.sharding import PartitionSpec as P

LANES = 128
ROWS = 32
SLOT = 8
NT = (((1,), (1,)), ((), ()))
NN = (((1,), (0,)), ((), ()))
VMEM = pl.BlockSpec(memory_space=pltpu.VMEM)
SMEM = pl.BlockSpec(memory_space=pltpu.SMEM)
PARAMS = pltpu.CompilerParams(vmem_limit_bytes=40 * 1024 * 1024)


def dot(a, b, dims=NN):
    return lax.dot_general(a, b, dims, preferred_element_type=jnp.float32)


def split2(x):
    hi = x.astype(jnp.bfloat16)
    lo = (x - hi.astype(jnp.float32)).astype(jnp.bfloat16)
    return hi, lo


def split3(x):
    hi, mid = split2(x)
    rest = x - hi.astype(jnp.float32) - mid.astype(jnp.float32)
    return hi, mid, rest.astype(jnp.bfloat16)


def cubic(distance):
    inner = 2.0 / 3.0 - distance * distance + 0.5 * distance * distance * distance
    remote = 2.0 - distance
    outer = remote * remote * remote * (1.0 / 6.0)
    return jnp.where(distance < 1.0, inner, jnp.where(distance < 2.0, outer, 0.0))


def pre_kernel(harm_ref, radius_ref, table_ref, g_ref, hpad_ref):
    batches, near, comps, points = harm_ref.shape
    knots = table_ref.shape[1]
    hpad_ref[...] = jnp.zeros(hpad_ref.shape, hpad_ref.dtype)
    r_hi, r_lo = split2(table_ref[...])
    coeffs = jnp.concatenate([r_hi, r_hi, r_lo], axis=1)
    knot = lax.broadcasted_iota(jnp.int32, (knots, points), 0).astype(jnp.float32)

    def body(b, carry):
        rows = radius_ref[b]
        for i in range(near):
            spline = cubic(jnp.abs(rows[i : i + 1, :] - knot))
            s_hi, s_lo = split2(spline)
            radial = dot(coeffs, jnp.concatenate([s_hi, s_lo, s_hi], axis=0))
            h = harm_ref[b, i]
            g_ref[b * near + i] = radial * h.astype(jnp.float32)
            hpad_ref[b * near + i, 0:comps, :] = h
        return carry

    lax.fori_loop(0, batches, body, 0)


def density_kernel(
    start_ref, offset_ref, size_ref, basis_ref, blocks_ref, part_ref, hpad_ref, atom_ref,
    dens_ref, terms_ref, w_ref,
):
    batches, near_blocks, points, width = basis_ref.shape
    owners = blocks_ref.shape[0]
    near = part_ref.shape[1]
    w_ref[...] = jnp.zeros(w_ref.shape, w_ref.dtype)
    lane = lax.broadcasted_iota(jnp.int32, (1, points), 1)
    ones = jnp.ones((8, 3 * width), jnp.bfloat16)
    zero = jnp.zeros((width, width), jnp.bfloat16)

    def body(b, carry):
        first = start_ref[0] + offset_ref[0, b]
        spot = [lax.rem(first + j, owners) for j in range(near_blocks)]
        phi = [basis_ref[b, j] for j in range(near_blocks)]

        def block(j, q):
            k = q - j + 1
            return blocks_ref[spot[j], k] if 0 <= k < 4 else zero

        total = jnp.zeros((points, width), jnp.float32)
        for q0, js in ((0, (0, 1, 2)), (2, (0, 1, 2, 3))):
            left = jnp.concatenate([phi[j] for j in js], axis=1)
            right = jnp.concatenate(
                [jnp.concatenate([block(j, q0), block(j, q0 + 1)], axis=1) for j in js], axis=0
            )
            mixed = dot(left, right)
            total = total + mixed[:, :width] * phi[q0].astype(jnp.float32)
            total = total + mixed[:, width:] * phi[q0 + 1].astype(jnp.float32)
        summed = dot(ones, jnp.concatenate(split3(total), axis=1), NT)[0:1]
        alive = lane < size_ref[0, b]
        row = jnp.where(alive, summed, 0.0)
        dens_ref[pl.ds(b, 1), :] = row
        w_ref[b, 0:near, :] = part_ref[b] * row
        return carry

    lax.fori_loop(0, batches, body, 0)
    weights = w_ref[...].reshape(LANES, points)
    columns = jnp.concatenate(split2(weights), axis=0)
    slot = lax.broadcasted_iota(jnp.int32, (1, 2 * LANES), 1) % LANES
    terms = jnp.zeros((ROWS, 2 * LANES), jnp.float32)
    for b in range(batches):
        rows = hpad_ref[b * near : (b + 1) * near].reshape(near * ROWS, points)
        cross = dot(rows, columns, NT)
        for i in range(near):
            terms = terms + jnp.where(
                slot == b * SLOT + i, cross[i * ROWS : (i + 1) * ROWS], 0.0
            )
    result = terms[:, :LANES] + terms[:, LANES:]
    row_id = lax.broadcasted_iota(jnp.int32, (ROWS, LANES), 0)
    comps = ROWS - 7
    terms_ref[...] = jnp.where(row_id == comps, atom_ref[...].astype(jnp.float32), result)


def scatter_kernel(comps, atoms, *refs):
    outs = refs[-5:]
    pieces = refs[:-5]
    row_id = lax.broadcasted_iota(jnp.int32, (3 * atoms, LANES), 0)
    total = jnp.zeros((3 * ROWS, 3 * atoms), jnp.float32)
    for m in range(0, len(pieces), 2):
        left, right = [], []
        for piece in pieces[m : m + 2]:
            values = piece[...]
            chosen = values[comps : comps + 1, :].astype(jnp.int32)
            right.append((row_id == chosen).astype(jnp.float32).astype(jnp.bfloat16))
            left.append(jnp.concatenate(split3(values), axis=0))
        total = total + dot(jnp.concatenate(left, axis=1), jnp.concatenate(right, axis=1), NT)
    sums = total[:ROWS] + total[ROWS : 2 * ROWS] + total[2 * ROWS :]
    own, ahead1, back1, ahead2, back2 = outs
    own[...] = sums
    ahead1[...] = sums[:, atoms:]
    back1[...] = sums[:, : 2 * atoms]
    ahead2[...] = sums[:, 2 * atoms :]
    back2[...] = sums[:, :atoms]


def potential_kernel(
    comps, atoms, size_ref, own_ref, a1_ref, b1_ref, a2_ref, b2_ref, atom_ref, g_ref,
    mom_ref, pot_ref,
):
    batches, points = pot_ref.shape
    near = g_ref.shape[0] // batches
    own = own_ref[...]
    before = a2_ref[...] + a1_ref[:, :atoms] + own[:, :atoms]
    here = a1_ref[:, atoms:] + own[:, atoms : 2 * atoms] + b1_ref[:, :atoms]
    after = own[:, 2 * atoms :] + b1_ref[:, atoms:] + b2_ref[...]
    mom_ref[...] = here[:comps]
    moments = jnp.concatenate([before, here, after], axis=1)
    row_id = lax.broadcasted_iota(jnp.int32, (3 * atoms, LANES), 0)
    pick = (row_id == atom_ref[...]).astype(jnp.float32).astype(jnp.bfloat16)
    got = dot(jnp.concatenate(split3(moments), axis=0), pick)
    chosen = got[:ROWS] + got[ROWS : 2 * ROWS] + got[2 * ROWS :]
    chosen = chosen[:comps]
    lane = lax.broadcasted_iota(jnp.int32, (1, points), 1)
    for b in range(batches):
        total = jnp.zeros((comps, points), jnp.float32)
        for i in range(near):
            column = chosen[:, b * SLOT + i : b * SLOT + i + 1]
            total = total + column * g_ref[b * near + i]
        row = jnp.sum(total, axis=0, keepdims=True)
        pot_ref[b : b + 1, :] = jnp.where(lane < size_ref[0, b], row, 0.0)


def shifted(value, axis, step):
    count = lax.axis_size(axis)
    return lax.ppermute(value, axis, [(i, (i + step) % count) for i in range(count)])


def per_device(
    basis_values,
    density_rows,
    block_mask,
    window_start,
    batch_offsets,
    batch_sizes,
    atom_near,
    harmonics,
    partition,
    radius,
    radial_table,
):
    dev_count = lax.axis_size("dev")
    blocks_dev = density_rows.shape[0]
    block_count = blocks_dev * dev_count
    batches, near, comps, points = harmonics.shape
    atoms = 16 * dev_count

    first_block = window_start[0]
    peer_index = jnp.arange(dev_count, dtype=jnp.int32)
    ahead_count = (peer_index - first_block) % dev_count
    wanted = (first_block + ahead_count) % block_count // dev_count
    requested = lax.all_to_all(wanted[:, None], "dev", split_axis=0, concat_axis=0, tiled=True)[:, 0]
    masked = density_rows * block_mask.astype(jnp.bfloat16)[:, :, None, None]
    served = jnp.take(masked, requested, axis=0, mode="clip")
    replies = lax.all_to_all(served, "dev", split_axis=0, concat_axis=0, tiled=True)

    f32, bf16 = jnp.float32, jnp.bfloat16
    g, hpad = pl.pallas_call(
        pre_kernel,
        out_shape=(
            jax.ShapeDtypeStruct((batches * near, comps, points), f32),
            jax.ShapeDtypeStruct((batches * near, ROWS, points), bf16),
        ),
        in_specs=[VMEM] * 3,
        out_specs=(VMEM, VMEM),
        compiler_params=PARAMS,
        cost_estimate=pl.CostEstimate(flops=400_000_000, bytes_accessed=6_000_000, transcendentals=0),
        name="pre",
    )(harmonics, radius, radial_table)

    atom_rows = jnp.pad(atom_near, ((0, LANES // SLOT - batches), (0, SLOT - near)), constant_values=-1)
    atom_rows = atom_rows.reshape(1, LANES)

    density, terms = pl.pallas_call(
        density_kernel,
        out_shape=(
            jax.ShapeDtypeStruct((batches, points), f32),
            jax.ShapeDtypeStruct((ROWS, LANES), f32),
        ),
        in_specs=[SMEM] * 3 + [VMEM] * 5,
        out_specs=(VMEM, VMEM),
        scratch_shapes=[pltpu.VMEM((LANES // SLOT, SLOT, points), f32)],
        compiler_params=PARAMS,
        cost_estimate=pl.CostEstimate(flops=2_000_000_000, bytes_accessed=6_000_000, transcendentals=0),
        name="density",
    )(window_start, batch_offsets, batch_sizes, basis_values, replies, partition, hpad, atom_rows)

    pieces = [terms] + [
        lax.ppermute(terms, "dev", [(i, i ^ m) for i in range(dev_count)]) for m in range(1, dev_count)
    ]
    own, ahead1, back1, ahead2, back2 = pl.pallas_call(
        functools.partial(scatter_kernel, comps, atoms),
        out_shape=tuple(
            jax.ShapeDtypeStruct((ROWS, n * atoms), f32) for n in (3, 2, 2, 1, 1)
        ),
        in_specs=[VMEM] * len(pieces),
        out_specs=(VMEM,) * 5,
        compiler_params=PARAMS,
        name="scatter",
    )(*pieces)
    ahead2 = shifted(ahead2, "region", 2)
    back2 = shifted(back2, "region", -2)
    ahead1 = shifted(ahead1, "region", 1)
    back1 = shifted(back1, "region", -1)

    region_moments, potential = pl.pallas_call(
        functools.partial(potential_kernel, comps, atoms),
        out_shape=(
            jax.ShapeDtypeStruct((comps, atoms), f32),
            jax.ShapeDtypeStruct((batches, points), f32),
        ),
        in_specs=[SMEM] + [VMEM] * 7,
        out_specs=(VMEM, VMEM),
        compiler_params=PARAMS,
        name="potential",
    )(batch_sizes, own, ahead1, back1, ahead2, back2, atom_rows, g)
    moments = lax.dynamic_slice_in_dim(region_moments, lax.axis_index("dev") * 16, 16, 1)
    return (density, moments, potential)


def solution(mesh):
    both = ("region", "dev")
    placed = (
        P(both, None, None, None),
        P(both, None, None, None),
        P(both, None),
        P(both),
        P(both, None),
        P(both, None),
        P(both, None),
        P(both, None, None, None),
        P(both, None, None),
        P(both, None, None),
        P(),
    )
    return jax.shard_map(
        per_device,
        mesh=mesh,
        in_specs=placed,
        out_specs=(P(both, None), P(None, both), P(both, None)),
        check_vma=False,
    )
```

time: 145 us -> 64.6 us (0.45)
  blocking collectives: 37.5 us -> 0 us
  loops' own time: 23.7 us -> 0 us
  local copies, waits for them, and re-layouts: 25.2 us -> 9.06 us
  Pallas kernels: 0 us -> 11.7 us
  matrix products: 9.84 us -> 0 us
  waiting for transfers between devices: 26 us -> 17.5 us
  starting transfers between devices: 14.6 us -> 21.8 us
  other arithmetic: 4.92 us -> 2.7 us
    unnamed x1 -> x0, blocking collectives: 25.3 us -> none
    another operation x1 -> x0, loops' own time: 23.7 us -> none  [per_device(): lax.map(one_density, (basis_values, batch_offsets[0])) * alive_mask]
    another operation x24 -> x0, local copies, waits for them, and re-layouts: 13.5 us -> none  [batch_density(): jnp.stack([padded[column:column + block_total] for column in range(band_w...]
    all_gather x1 -> x0, blocking collectives: 12.2 us -> none  [per_device(): spline_table = lax.all_gather(rim_table, 'dev', axis=3, tiled=True)]
    pallas_call x0 -> x4, Pallas kernels: none -> 11.7 us  [the longest x1 7.03 us: per_device(): pl.pallas_call(density_kernel, out_shape=(jax.ShapeDtypeStruct((batches,...]
    dot_general x15 -> x0, matrix products: 9.84 us -> none  [the longest x12 6.34 us: batch_density(): jnp.einsum('jpkf,jkgf->jpg', stacked, row_blocks, preferred_element_type=...]
    ppermute x4 -> x11, starting transfers between devices: 5.74 us -> 13.1 us  [the longest x4 6.8 us: shifted(): lax.ppermute(value, axis, [(i, (i + step) % count) for i in range(count)])]
    dynamic_slice x12 -> x1, local copies, waits for them, and re-layouts: 7.03 us -> 0.07 us  [per_device(): lax.dynamic_slice_in_dim(region_moments, lax.axis_index('dev') * 16, 16, 1)]
  transfers between devices with their start and end apart: 6 -> 13, of which waited for: 6 -> 5; matrix products, arithmetic and copies ran while one was open for 2% -> 3% of each run, Pallas kernels for 0% -> 4%
where the time goes in v1:
time: 64.6 us; the launch traced here: 64.2 us
  starting transfers between devices  21.8 us (34%)
  waiting for transfers between devices  17.5 us (27%)
  Pallas kernels  11.7 us (18%)
  local copies, waits for them, and re-layouts  9.06 us (14%)
  other arithmetic  2.7 us (4%)
  between operations  1.39 us (2%)
    all_to_all x1, waiting for transfers between devices, per_device(): lax.all_to_all(served, 'dev', split_axis=0, concat_axis=0, tiled=True)  10.2 us
    unnamed x23, local copies, waits for them, and re-layouts  7.25 us
    pallas_call x1, Pallas kernels, per_device(): pl.pallas_call(density_kernel, out_shape=(jax.ShapeDtypeStruct((batches,...  7.03 us
    ppermute x4, starting transfers between devices, shifted(): lax.ppermute(value, axis, [(i, (i + step) % count) for i in range(count)])  6.8 us
    ppermute x7, starting transfers between devices, per_device(): lax.ppermute(terms, 'dev', [(i, i ^ m) for i in range(dev_count)])  6.25 us
    all_to_all x1, starting transfers between devices, per_device(): lax.all_to_all(wanted[:, None], 'dev', split_axis=0, concat_axis=0, tiled...  5.17 us
    all_to_all x1, starting transfers between devices, per_device(): lax.all_to_all(served, 'dev', split_axis=0, concat_axis=0, tiled=True)  3.56 us
    all_to_all x1, waiting for transfers between devices, per_device(): lax.all_to_all(wanted[:, None], 'dev', split_axis=0, concat_axis=0, tiled...  2.76 us
  transfers between devices with their start and end apart: 13, of which 5 were waited for; matrix products, arithmetic and copies ran while one was open for 3% of the time, Pallas kernels for 4%

profile of v1, /device:TPU:0, one launch (start us, length us, event | category | flops | bytes accessed | tf_op | source)
XLA Modules:
  0.0 64.2 jit_solution(6112873502480224914)
XLA Ops:
  1.3 0.6 %and_select_fusion = s32[8,1,1]{2,1,0:T(1,128)} fusion(s32[]{:T(128)} %bitcast.1), kind=kLoop, calls=%fused_computation.4 | loop fusion | flops 272 | bytes 36 | tf_op jit(solution)/shard_map/jit(floor_divide)/jit(_where)/select_n | solution.py:195
  1.9 5.2 %all-to-all-start = ((s32[8,1,1]{2,1,0:T(1,128)}), s32[8,1,1]{2,1,0:T(1,128)S(1)}, u32[]{:S(2)}, u32[]{:S(2)}) async-start(s32[8,1,1]{2,1,0:T(1,128)} %and_select_fusion), calls=%async_computation | async-start | bytes 8192 | tf_op jit(solution)/shard_map/all_to_all | solution.py:196
  7.1 0.7 %convert_element_type.3 = bf16[3,4]{1,0:T(4,128)(2,1)S(1)} convert(s32[3,4]{1,0:T(4,128)} %param.13) | non-fusion elementwise | flops 12 | bytes 72 | tf_op jit(solution)/shard_map/convert_element_type | solution.py:197
  7.8 0.0 copy-start.8
  7.8 0.0 copy-start.9
  7.8 0.0 copy-start.3
  7.8 1.1 %broadcast_multiply_fusion = bf16[3,4,128,128]{3,2,1,0:T(8,128)(2,1)S(1)} fusion(bf16[3,4,128,128]{3,2,1,0:T(8,128)(2,1)} %param.12, bf16[3,4]{1,0:T(4,128)(2,1)S(1)} %convert_element_type.3), kind=kLoop, calls=%fused_computation.1 | loop fusion | flops 196608 | bytes 786456 | tf_op jit(solution)/shard_map/mul | solution.py:197
  8.9 2.8 %all-to-all-done = s32[8,1,1]{2,1,0:T(1,128)S(1)} async-done(((s32[8,1,1]{2,1,0:T(1,128)}), s32[8,1,1]{2,1,0:T(1,128)S(1)}, u32[]{:S(2)}, u32[]{:S(2)}) %all-to-all-start) | async-done | bytes 64 | tf_op jit(solution)/shard_map/all_to_all | solution.py:196
  11.7 0.2 reduce
  11.9 0.0 copy-start
  11.9 0.0 copy-start.5
  12.0 1.6 %gather_fusion = bf16[8,4,128,128]{3,2,1,0:T(8,128)(2,1)} fusion(bf16[3,4,128,128]{3,2,1,0:T(8,128)(2,1)S(1)} %broadcast_multiply_fusion, s32[1024]{0:T(1024)S(1)} %pad_clamp_fusion), kind=kCustom, calls=%fused_computation | custom fusion | bytes 2097184 | tf_op jit(solution)/shard_map/jit(_take)/gather | solution.py:198
  13.6 3.6 %all-to-all-start.1 = ((bf16[8,4,128,128]{3,2,1,0:T(8,128)(2,1)}), bf16[8,4,128,128]{3,2,1,0:T(8,128)(2,1)S(1)}, u32[]{:S(2)}, u32[]{:S(2)}) async-start(bf16[8,4,128,128]{3,2,1,0:T(8,128)(2,1)} %gather_fusion), calls=%async_computation.1 | async-start | bytes 2097152 | tf_op jit(solution)/shard_map/all_to_all | solution.py:199
  17.2 0.0 copy-done.8
  17.2 0.1 copy.23.table_ref
  17.3 0.0 copy-done.9
  17.3 0.1 copy.26
  17.4 0.1 reshape.119.atom_ref
  17.5 0.0 copy-done.3
  17.5 0.0 copy-start.2
  17.5 1.3 %copy-done.2 = bf16[12,6,25,256]{3,2,1,0:T(8,128)(2,1)S(1)} copy-done((bf16[12,6,25,256]{3,2,1,0:T(8,128)(2,1)S(1)}, bf16[12,6,25,256]{3,2,1,0:T(8,128)(2,1)}, u32[]{:S(2)}) %copy-start.2) | copy-done | bytes 921624
  18.7 2.5 %pre.1 = (f32[72,25,256]{2,1,0:T(8,128)S(1)}, bf16[72,32,256]{2,1,0:T(8,128)(2,1)S(1)}) custom-call(bf16[12,6,25,256]{3,2,1,0:T(8,128)(2,1)S(1)} %copy-done.2, f32[12,6,256]{2,1,0:T(8,128)S(1)} %copy-done.3, f32[25,16]{1,0:T(8,128)S(1)} %copy.23.table_ref), custom_call_target="tpu_custom_call" | custom-call | flops 400000000 | bytes 6000000 | tf_op jit(solution)/shard_map/pre/pallas_call | solution.py:202
  21.3 0.0 copy-start.6
  21.3 1.0 %copy-done.6 = bf16[72,32,256]{2,1,0:T(8,128)(2,1)} copy-done((bf16[72,32,256]{2,1,0:T(8,128)(2,1)}, bf16[72,32,256]{2,1,0:T(8,128)(2,1)S(1)}, u32[]{:S(2)}) %copy-start.6) | copy-done | bytes 1179672
  22.3 10.2 %all-to-all-done.1.blocks_ref = bf16[8,4,128,128]{3,2,1,0:T(8,128)(2,1)S(1)} async-done(((bf16[8,4,128,128]{3,2,1,0:T(8,128)(2,1)}), bf16[8,4,128,128]{3,2,1,0:T(8,128)(2,1)S(1)}, u32[]{:S(2)}, u32[]{:S(2)}) %all-to-all-start.1) | async-done | bytes 1048608 | tf_op jit(solution)/shard_map/all_to_all | solution.py:199
  32.5 0.0 copy-done
  32.5 0.0 copy-done.5
  32.5 0.0 copy-start.1
  32.5 1.9 %copy-done.1 = bf16[12,4,256,128]{3,2,1,0:T(8,128)(2,1)S(1)} copy-done((bf16[12,4,256,128]{3,2,1,0:T(8,128)(2,1)S(1)}, bf16[12,4,256,128]{3,2,1,0:T(8,128)(2,1)}, u32[]{:S(2)}) %copy-start.1) | copy-done | bytes 3145752
  34.4 0.0 copy-start.4
  34.4 0.9 %copy-done.4 = f32[12,6,256]{2,1,0:T(8,128)S(1)} copy-done((f32[12,6,256]{2,1,0:T(8,128)S(1)}, f32[12,6,256]{2,1,0:T(8,128)}, u32[]{:S(2)}) %copy-start.4) | copy-done | bytes 73752
  35.3 0.0 copy-start.7
  35.3 1.3 %copy-done.7 = bf16[72,32,256]{2,1,0:T(8,128)(2,1)S(1)} copy-done((bf16[72,32,256]{2,1,0:T(8,128)(2,1)S(1)}, bf16[72,32,256]{2,1,0:T(8,128)(2,1)}, u32[]{:S(2)}) %copy-start.7) | copy-done | bytes 1179672
  36.6 7.0 %density.1 = (f32[12,256]{1,0:T(8,128)}, f32[32,128]{1,0:T(8,128)S(1)}) custom-call(s32[1]{0:T(128)} %copy.27.start_ref, s32[1,12]{1,0:T(1,128)S(1)} %copy-done.5, s32[1,12]{1,0:T(1,128)S(1)} %copy-done, bf16[12,4,256,128]{3,2,1,0:T(8,128)(2,1)S(1)} %copy-done.1, bf16[8,4,128,128]{3,2,1,0:T(8,128)(2,1)S(1)} %all-to-all-done.1.blocks_ref, ...), custom_call_target="tpu_custom_call" | custom-call | flops 2000000000 | bytes 6000000 | tf_op jit(solution)/shard_map/density/pallas_call | solution.py:218
  43.6 0.0 collective-permute-start
  43.6 0.6 collective-permute-start.1
  44.2 1.3 %collective-permute-start.2 = (f32[32,128]{1,0:T(8,128)S(1)}, f32[32,128]{1,0:T(8,128)S(1)}, u32[]{:S(2)}, u32[]{:S(2)}) collective-permute-start(f32[32,128]{1,0:T(8,128)S(1)} %get-tuple-element.16.refs_0_), channel_id=1, source_target_pairs={{0,3},{1,2},{2,1},{3,0},{4,7},{5,6},{6,5},{7,4},{8,11},{9,10},{10,... | collective-permute-start | bytes 49160 | tf_op jit(solution)/shard_map/ppermute | solution.py:233
  45.5 0.5 collective-permute-start.3
  46.0 1.1 %collective-permute-start.4 = (f32[32,128]{1,0:T(8,128)S(1)}, f32[32,128]{1,0:T(8,128)S(1)}, u32[]{:S(2)}, u32[]{:S(2)}) collective-permute-start(f32[32,128]{1,0:T(8,128)S(1)} %get-tuple-element.16.refs_0_), channel_id=1, source_target_pairs={{0,5},{1,4},{2,7},{3,6},{4,1},{5,0},{6,3},{7,2},{8,13},{9,12},{10,... | collective-permute-start | bytes 49160 | tf_op jit(solution)/shard_map/ppermute | solution.py:233
  47.1 0.0 collective-permute-done.refs_1_
  47.1 0.6 collective-permute-start.5
  47.7 0.0 collective-permute-done.1.refs_2_
  47.7 2.2 %collective-permute-start.6 = (f32[32,128]{1,0:T(8,128)S(1)}, f32[32,128]{1,0:T(8,128)S(1)}, u32[]{:S(2)}, u32[]{:S(2)}) collective-permute-start(f32[32,128]{1,0:T(8,128)S(1)} %get-tuple-element.16.refs_0_), channel_id=1, source_target_pairs={{0,7},{1,6},{2,5},{3,4},{4,3},{5,2},{6,1},{7,0},{8,15},{9,14},{10,... | collective-permute-start | bytes 49160 | tf_op jit(solution)/shard_map/ppermute | solution.py:233
  49.9 0.0 collective-permute-done.2.refs_3_
  49.9 0.0 collective-permute-done.3.refs_4_
  49.9 0.0 collective-permute-done.4.refs_5_
  49.9 2.0 %collective-permute-done.5.refs_6_ = f32[32,128]{1,0:T(8,128)S(1)} collective-permute-done((f32[32,128]{1,0:T(8,128)S(1)}, f32[32,128]{1,0:T(8,128)S(1)}, u32[]{:S(2)}, u32[]{:S(2)}) %collective-permute-start.5) | collective-permute-done | bytes 16416 | tf_op jit(solution)/shard_map/ppermute | solution.py:233
  51.9 0.0 collective-permute-done.6.refs_7_
  51.9 0.4 scatter.1
  52.3 1.6 %collective-permute-start.7 = (f32[32,256]{1,0:T(8,128)S(1)}, f32[32,256]{1,0:T(8,128)S(1)}, u32[]{:S(2)}, u32[]{:S(2)}) collective-permute-start(f32[32,256]{1,0:T(8,128)S(1)} %get-tuple-element.18), channel_id=1, source_target_pairs={{0,8},{8,16},{16,24},{24,0},{1,9},{9,17},{17,25},{25,1},{2,10},{10... | collective-permute-start | bytes 98312 | tf_op jit(solution)/shard_map/ppermute | solution.py:170
  53.9 2.2 %collective-permute-start.8 = (f32[32,256]{1,0:T(8,128)S(1)}, f32[32,256]{1,0:T(8,128)S(1)}, u32[]{:S(2)}, u32[]{:S(2)}) collective-permute-start(f32[32,256]{1,0:T(8,128)S(1)} %get-tuple-element.19), channel_id=1, source_target_pairs={{0,24},{8,0},{16,8},{24,16},{1,25},{9,1},{17,9},{25,17},{2,26},{10... | collective-permute-start | bytes 98312 | tf_op jit(solution)/shard_map/ppermute | solution.py:170
  56.2 0.8 %collective-permute-start.9 = (f32[32,128]{1,0:T(8,128)S(1)}, f32[32,128]{1,0:T(8,128)S(1)}, u32[]{:S(2)}, u32[]{:S(2)}) collective-permute-start(f32[32,128]{1,0:T(8,128)S(1)} %get-tuple-element.20), channel_id=1, source_target_pairs={{0,16},{8,24},{16,0},{24,8},{1,17},{9,25},{17,1},{25,9},{2,18},{10... | collective-permute-start | bytes 49160 | tf_op jit(solution)/shard_map/ppermute | solution.py:170
  56.9 2.1 %collective-permute-start.10 = (f32[32,128]{1,0:T(8,128)S(1)}, f32[32,128]{1,0:T(8,128)S(1)}, u32[]{:S(2)}, u32[]{:S(2)}) collective-permute-start(f32[32,128]{1,0:T(8,128)S(1)} %get-tuple-element.21), channel_id=1, source_target_pairs={{0,16},{8,24},{16,0},{24,8},{1,17},{9,25},{17,1},{25,9},{2,18},{10... | collective-permute-start | bytes 49160 | tf_op jit(solution)/shard_map/ppermute | solution.py:170
  59.1 1.7 %collective-permute-done.9.a2_ref = f32[32,128]{1,0:T(8,128)S(1)} collective-permute-done((f32[32,128]{1,0:T(8,128)S(1)}, f32[32,128]{1,0:T(8,128)S(1)}, u32[]{:S(2)}, u32[]{:S(2)}) %collective-permute-start.9) | collective-permute-done | bytes 16416 | tf_op jit(solution)/shard_map/ppermute | solution.py:170
  60.8 0.8 %collective-permute-done.10.b2_ref = f32[32,128]{1,0:T(8,128)S(1)} collective-permute-done((f32[32,128]{1,0:T(8,128)S(1)}, f32[32,128]{1,0:T(8,128)S(1)}, u32[]{:S(2)}, u32[]{:S(2)}) %collective-permute-start.10) | collective-permute-done | bytes 16416 | tf_op jit(solution)/shard_map/ppermute | solution.py:170
  61.6 0.0 collective-permute-done.7.a1_ref
  61.6 0.0 collective-permute-done.8.b1_ref
  61.6 1.8 %potential.1 = (f32[25,128]{1,0:T(8,128)S(1)}, f32[12,256]{1,0:T(8,128)}) custom-call(s32[1,12]{1,0:T(1,128)S(1)} %copy-done, f32[32,384]{1,0:T(8,128)S(1)} %get-tuple-element.17.own_ref, f32[32,256]{1,0:T(8,128)S(1)} %collective-permute-done.7.a1_ref, f32[32,256]{1,0:T(8,128)S(1)} %collective-permute-done.8.b1_ref, ...), custom_call_target="tpu_custom_call" | custom-call | tf_op jit(solution)/shard_map/potential/pallas_call | solution.py:250
  63.4 0.1 constant_dynamic-slice_fusion
  63.5 0.7 %copy.25 = f32[25,16]{0,1:T(8,128)} copy(f32[25,16]{1,0:T(8,128)S(1)} %constant_dynamic-slice_fusion) | data formatting | bytes 3200
  (2 shorter events, 0.0 us)
Async XLA Ops:
  1.9 9.8 %all-to-all-start = ((s32[8,1,1]{2,1,0:T(1,128)}), s32[8,1,1]{2,1,0:T(1,128)S(1)}, u32[]{:S(2)}, u32[]{:S(2)}) async-start(s32[8,1,1]{2,1,0:T(1,128)} %and_select_fusion), calls=%async_computation | async-start | bytes 8192 | tf_op jit(solution)/shard_map/all_to_all | solution.py:196
  7.8 9.4 %copy-start.8 = (f32[25,16]{0,1:T(8,128)S(1)}, f32[25,16]{0,1:T(8,128)}, u32[]{:S(2)}) copy-start(f32[25,16]{0,1:T(8,128)} %param.21) | copy-start | bytes 4804
  7.8 9.5 %copy-start.9 = (s32[12,6]{0,1:T(8,128)S(1)}, s32[12,6]{0,1:T(8,128)}, u32[]{:S(2)}) copy-start(s32[12,6]{0,1:T(8,128)} %param.17) | copy-start | bytes 868
  7.8 9.7 %copy-start.3 = (f32[12,6,256]{2,1,0:T(8,128)S(1)}, f32[12,6,256]{2,1,0:T(8,128)}, u32[]{:S(2)}) copy-start(f32[12,6,256]{2,1,0:T(8,128)} %radius_ref.1) | copy-start | bytes 221188
  11.9 20.6 %copy-start = (s32[1,12]{1,0:T(1,128)S(1)}, s32[1,12]{1,0:T(1,128)}, u32[]{:S(2)}) copy-start(s32[1,12]{1,0:T(1,128)} %size_ref.3) | copy-start | bytes 148
  11.9 20.6 %copy-start.5 = (s32[1,12]{1,0:T(1,128)S(1)}, s32[1,12]{1,0:T(1,128)}, u32[]{:S(2)}) copy-start(s32[1,12]{1,0:T(1,128)} %offset_ref.1) | copy-start | bytes 148
  13.6 18.9 %all-to-all-start.1 = ((bf16[8,4,128,128]{3,2,1,0:T(8,128)(2,1)}), bf16[8,4,128,128]{3,2,1,0:T(8,128)(2,1)S(1)}, u32[]{:S(2)}, u32[]{:S(2)}) async-start(bf16[8,4,128,128]{3,2,1,0:T(8,128)(2,1)} %gather_fusion), calls=%async_computation.1 | async-start | bytes 2097152 | tf_op jit(solution)/shard_map/all_to_all | solution.py:199
  17.5 1.3 %copy-start.2 = (bf16[12,6,25,256]{3,2,1,0:T(8,128)(2,1)S(1)}, bf16[12,6,25,256]{3,2,1,0:T(8,128)(2,1)}, u32[]{:S(2)}) copy-start(bf16[12,6,25,256]{3,2,1,0:T(8,128)(2,1)} %harm_ref.1) | copy-start | bytes 2764804
  21.3 1.1 %copy-start.6 = (bf16[72,32,256]{2,1,0:T(8,128)(2,1)}, bf16[72,32,256]{2,1,0:T(8,128)(2,1)S(1)}, u32[]{:S(2)}) copy-start(bf16[72,32,256]{2,1,0:T(8,128)(2,1)S(1)} %get-tuple-element.14.hpad_ref) | copy-start | bytes 3538948
  32.5 1.9 %copy-start.1 = (bf16[12,4,256,128]{3,2,1,0:T(8,128)(2,1)S(1)}, bf16[12,4,256,128]{3,2,1,0:T(8,128)(2,1)}, u32[]{:S(2)}) copy-start(bf16[12,4,256,128]{3,2,1,0:T(8,128)(2,1)} %basis_ref.1) | copy-start | bytes 9437188
  34.4 0.9 %copy-start.4 = (f32[12,6,256]{2,1,0:T(8,128)S(1)}, f32[12,6,256]{2,1,0:T(8,128)}, u32[]{:S(2)}) copy-start(f32[12,6,256]{2,1,0:T(8,128)} %part_ref.1) | copy-start | bytes 221188
  35.3 1.3 %copy-start.7 = (bf16[72,32,256]{2,1,0:T(8,128)(2,1)S(1)}, bf16[72,32,256]{2,1,0:T(8,128)(2,1)}, u32[]{:S(2)}) copy-start(bf16[72,32,256]{2,1,0:T(8,128)(2,1)} %copy-done.6) | copy-start | bytes 3538948
  43.6 3.5 %collective-permute-start = (f32[32,128]{1,0:T(8,128)S(1)}, f32[32,128]{1,0:T(8,128)S(1)}, u32[]{:S(2)}, u32[]{:S(2)}) collective-permute-start(f32[32,128]{1,0:T(8,128)S(1)} %get-tuple-element.16.refs_0_), channel_id=1, source_target_pairs={{0,1},{1,0},{2,3},{3,2},{4,5},{5,4},{6,7},{7,6},{8,9},{9,8},{10,11... | collective-permute-start | bytes 49160 | tf_op jit(solution)/shard_map/ppermute | solution.py:233
  43.6 4.1 %collective-permute-start.1 = (f32[32,128]{1,0:T(8,128)S(1)}, f32[32,128]{1,0:T(8,128)S(1)}, u32[]{:S(2)}, u32[]{:S(2)}) collective-permute-start(f32[32,128]{1,0:T(8,128)S(1)} %get-tuple-element.16.refs_0_), channel_id=1, source_target_pairs={{0,2},{1,3},{2,0},{3,1},{4,6},{5,7},{6,4},{7,5},{8,10},{9,11},{10,... | collective-permute-start | bytes 49160 | tf_op jit(solution)/shard_map/ppermute | solution.py:233
  44.2 5.7 %collective-permute-start.2 = (f32[32,128]{1,0:T(8,128)S(1)}, f32[32,128]{1,0:T(8,128)S(1)}, u32[]{:S(2)}, u32[]{:S(2)}) collective-permute-start(f32[32,128]{1,0:T(8,128)S(1)} %get-tuple-element.16.refs_0_), channel_id=1, source_target_pairs={{0,3},{1,2},{2,1},{3,0},{4,7},{5,6},{6,5},{7,4},{8,11},{9,10},{10,... | collective-permute-start | bytes 49160 | tf_op jit(solution)/shard_map/ppermute | solution.py:233
  45.5 4.4 %collective-permute-start.3 = (f32[32,128]{1,0:T(8,128)S(1)}, f32[32,128]{1,0:T(8,128)S(1)}, u32[]{:S(2)}, u32[]{:S(2)}) collective-permute-start(f32[32,128]{1,0:T(8,128)S(1)} %get-tuple-element.16.refs_0_), channel_id=1, source_target_pairs={{0,4},{1,5},{2,6},{3,7},{4,0},{5,1},{6,2},{7,3},{8,12},{9,13},{10,... | collective-permute-start | bytes 49160 | tf_op jit(solution)/shard_map/ppermute | solution.py:233
  46.0 3.9 %collective-permute-start.4 = (f32[32,128]{1,0:T(8,128)S(1)}, f32[32,128]{1,0:T(8,128)S(1)}, u32[]{:S(2)}, u32[]{:S(2)}) collective-permute-start(f32[32,128]{1,0:T(8,128)S(1)} %get-tuple-element.16.refs_0_), channel_id=1, source_target_pairs={{0,5},{1,4},{2,7},{3,6},{4,1},{5,0},{6,3},{7,2},{8,13},{9,12},{10,... | collective-permute-start | bytes 49160 | tf_op jit(solution)/shard_map/ppermute | solution.py:233
  47.1 4.8 %collective-permute-start.5 = (f32[32,128]{1,0:T(8,128)S(1)}, f32[32,128]{1,0:T(8,128)S(1)}, u32[]{:S(2)}, u32[]{:S(2)}) collective-permute-start(f32[32,128]{1,0:T(8,128)S(1)} %get-tuple-element.16.refs_0_), channel_id=1, source_target_pairs={{0,6},{1,7},{2,4},{3,5},{4,2},{5,3},{6,0},{7,1},{8,14},{9,15},{10,... | collective-permute-start | bytes 49160 | tf_op jit(solution)/shard_map/ppermute | solution.py:233
  47.7 4.2 %collective-permute-start.6 = (f32[32,128]{1,0:T(8,128)S(1)}, f32[32,128]{1,0:T(8,128)S(1)}, u32[]{:S(2)}, u32[]{:S(2)}) collective-permute-start(f32[32,128]{1,0:T(8,128)S(1)} %get-tuple-element.16.refs_0_), channel_id=1, source_target_pairs={{0,7},{1,6},{2,5},{3,4},{4,3},{5,2},{6,1},{7,0},{8,15},{9,14},{10,... | collective-permute-start | bytes 49160 | tf_op jit(solution)/shard_map/ppermute | solution.py:233
  52.3 9.3 %collective-permute-start.7 = (f32[32,256]{1,0:T(8,128)S(1)}, f32[32,256]{1,0:T(8,128)S(1)}, u32[]{:S(2)}, u32[]{:S(2)}) collective-permute-start(f32[32,256]{1,0:T(8,128)S(1)} %get-tuple-element.18), channel_id=1, source_target_pairs={{0,8},{8,16},{16,24},{24,0},{1,9},{9,17},{17,25},{25,1},{2,10},{10... | collective-permute-start | bytes 98312 | tf_op jit(solution)/shard_map/ppermute | solution.py:170
  53.9 7.7 %collective-permute-start.8 = (f32[32,256]{1,0:T(8,128)S(1)}, f32[32,256]{1,0:T(8,128)S(1)}, u32[]{:S(2)}, u32[]{:S(2)}) collective-permute-start(f32[32,256]{1,0:T(8,128)S(1)} %get-tuple-element.19), channel_id=1, source_target_pairs={{0,24},{8,0},{16,8},{24,16},{1,25},{9,1},{17,9},{25,17},{2,26},{10... | collective-permute-start | bytes 98312 | tf_op jit(solution)/shard_map/ppermute | solution.py:170
  56.2 4.6 %collective-permute-start.9 = (f32[32,128]{1,0:T(8,128)S(1)}, f32[32,128]{1,0:T(8,128)S(1)}, u32[]{:S(2)}, u32[]{:S(2)}) collective-permute-start(f32[32,128]{1,0:T(8,128)S(1)} %get-tuple-element.20), channel_id=1, source_target_pairs={{0,16},{8,24},{16,0},{24,8},{1,17},{9,25},{17,1},{25,9},{2,18},{10... | collective-permute-start | bytes 49160 | tf_op jit(solution)/shard_map/ppermute | solution.py:170
  56.9 4.6 %collective-permute-start.10 = (f32[32,128]{1,0:T(8,128)S(1)}, f32[32,128]{1,0:T(8,128)S(1)}, u32[]{:S(2)}, u32[]{:S(2)}) collective-permute-start(f32[32,128]{1,0:T(8,128)S(1)} %get-tuple-element.21), channel_id=1, source_target_pairs={{0,16},{8,24},{16,0},{24,8},{1,17},{9,25},{17,1},{25,9},{2,18},{10... | collective-permute-start | bytes 49160 | tf_op jit(solution)/shard_map/ppermute | solution.py:170

commit v2 on v1

--- a/solution.py
+++ b/solution.py
@@ -13,7 +13,7 @@
 NN = (((1,), (0,)), ((), ()))
 VMEM = pl.BlockSpec(memory_space=pltpu.VMEM)
 SMEM = pl.BlockSpec(memory_space=pltpu.SMEM)
-PARAMS = pltpu.CompilerParams(vmem_limit_bytes=40 * 1024 * 1024)
+PARAMS = pltpu.CompilerParams(vmem_limit_bytes=16 * 1024 * 1024)
 
 
 def dot(a, b, dims=NN):
@@ -62,11 +62,12 @@
 
 
 def density_kernel(
-    start_ref, offset_ref, size_ref, basis_ref, blocks_ref, part_ref, hpad_ref, atom_ref,
+    rows_dev, start_ref, offset_ref, size_ref, basis_ref, blocks_ref, part_ref, hpad_ref, atom_ref,
     dens_ref, terms_ref, w_ref,
 ):
     batches, near_blocks, points, width = basis_ref.shape
-    owners = blocks_ref.shape[0]
+    stored = blocks_ref.shape[0]
+    owners = stored // rows_dev
     near = part_ref.shape[1]
     w_ref[...] = jnp.zeros(w_ref.shape, w_ref.dtype)
     lane = lax.broadcasted_iota(jnp.int32, (1, points), 1)
@@ -75,7 +76,10 @@
 
     def body(b, carry):
         first = start_ref[0] + offset_ref[0, b]
-        spot = [lax.rem(first + j, owners) for j in range(near_blocks)]
+        spot = []
+        for j in range(near_blocks):
+            index = lax.rem(first + j, stored)
+            spot.append(lax.rem(index, owners) * rows_dev + index // owners)
         phi = [basis_ref[b, j] for j in range(near_blocks)]
 
         def block(j, q):
@@ -185,18 +189,11 @@
 ):
     dev_count = lax.axis_size("dev")
     blocks_dev = density_rows.shape[0]
-    block_count = blocks_dev * dev_count
     batches, near, comps, points = harmonics.shape
     atoms = 16 * dev_count
 
-    first_block = window_start[0]
-    peer_index = jnp.arange(dev_count, dtype=jnp.int32)
-    ahead_count = (peer_index - first_block) % dev_count
-    wanted = (first_block + ahead_count) % block_count // dev_count
-    requested = lax.all_to_all(wanted[:, None], "dev", split_axis=0, concat_axis=0, tiled=True)[:, 0]
     masked = density_rows * block_mask.astype(jnp.bfloat16)[:, :, None, None]
-    served = jnp.take(masked, requested, axis=0, mode="clip")
-    replies = lax.all_to_all(served, "dev", split_axis=0, concat_axis=0, tiled=True)
+    gathered = lax.all_gather(masked, "dev", axis=0, tiled=True)
 
     f32, bf16 = jnp.float32, jnp.bfloat16
     g, hpad = pl.pallas_call(
@@ -216,7 +213,7 @@
     atom_rows = atom_rows.reshape(1, LANES)
 
     density, terms = pl.pallas_call(
-        density_kernel,
+        functools.partial(density_kernel, blocks_dev),
         out_shape=(
             jax.ShapeDtypeStruct((batches, points), f32),
             jax.ShapeDtypeStruct((ROWS, LANES), f32),
@@ -227,7 +224,7 @@
         compiler_params=PARAMS,
         cost_estimate=pl.CostEstimate(flops=2_000_000_000, bytes_accessed=6_000_000, transcendentals=0),
         name="density",
-    )(window_start, batch_offsets, batch_sizes, basis_values, replies, partition, hpad, atom_rows)
+    )(window_start, batch_offsets, batch_sizes, basis_values, gathered, partition, hpad, atom_rows)
 
     pieces = [terms] + [
         lax.ppermute(terms, "dev", [(i, i ^ m) for i in range(dev_count)]) for m in range(1, dev_count)

time: 64.6 us -> 87.3 us (1.35)
  waiting for transfers between devices: 17.5 us -> 33.1 us
  between operations: 1.39 us -> 14.7 us
  starting transfers between devices: 21.8 us -> 13.1 us
  local copies, waits for them, and re-layouts: 9.06 us -> 11.7 us
    all_gather x0 -> x1, waiting for transfers between devices: none -> 27.7 us  [per_device(): gathered = lax.all_gather(masked, 'dev', axis=0, tiled=True)]
    all_to_all x2 -> x0, waiting for transfers between devices: 13 us -> none  [the longest x1 10.2 us: per_device(): lax.all_to_all(served, 'dev', split_axis=0, concat_axis=0, tiled=True)]
    all_to_all x2 -> x0, starting transfers between devices: 8.73 us -> none  [the longest x1 5.17 us: per_device(): lax.all_to_all(wanted[:, None], 'dev', split_axis=0, concat_axis=0, tiled...]
    unnamed x23, local copies, waits for them, and re-layouts: 7.25 us -> 11 us
    gather x1 -> x0, local copies, waits for them, and re-layouts: 1.65 us -> none  [per_device(): served = jnp.take(masked, requested, axis=0, mode='clip')]
    ppermute x7, waiting for transfers between devices: 2.05 us -> 3.04 us  [per_device(): lax.ppermute(terms, 'dev', [(i, i ^ m) for i in range(dev_count)])]
  transfers between devices with their start and end apart: 13 -> 12, of which waited for: 5 -> 6; matrix products, arithmetic and copies ran while one was open for 3% -> 2% of each run, Pallas kernels for 4% -> 3%
where the time goes in v2:
time: 87.3 us; the launch traced here: 86.9 us
  waiting for transfers between devices  33.1 us (38%)
  between operations  14.7 us (17%)
  starting transfers between devices  13.1 us (15%)
  local copies, waits for them, and re-layouts  11.7 us (13%)
  Pallas kernels  11.7 us (13%)
  other arithmetic  2.52 us (3%)
    all_gather x1, waiting for transfers between devices, per_device(): gathered = lax.all_gather(masked, 'dev', axis=0, tiled=True)  27.7 us
    unnamed x23, local copies, waits for them, and re-layouts  11 us
    pallas_call x1, Pallas kernels, per_device(): pl.pallas_call(functools.partial(density_kernel, blocks_dev), out_shape=(...  7.02 us
    ppermute x4, starting transfers between devices, shifted(): lax.ppermute(value, axis, [(i, (i + step) % count) for i in range(count)])  6.8 us
    ppermute x7, starting transfers between devices, per_device(): lax.ppermute(terms, 'dev', [(i, i ^ m) for i in range(dev_count)])  6.25 us
    ppermute x7, waiting for transfers between devices, per_device(): lax.ppermute(terms, 'dev', [(i, i ^ m) for i in range(dev_count)])  3.04 us
    pallas_call x1, Pallas kernels, per_device(): pl.pallas_call(pre_kernel, out_shape=(jax.ShapeDtypeStruct((batches * nea...  2.5 us
    ppermute x4, waiting for transfers between devices, shifted(): lax.ppermute(value, axis, [(i, (i + step) % count) for i in range(count)])  2.33 us
  transfers between devices with their start and end apart: 12, of which 6 were waited for; matrix products, arithmetic and copies ran while one was open for 2% of the time, Pallas kernels for 3%

profile of v2, /device:TPU:0, one launch (start us, length us, event | category | flops | bytes accessed | tf_op | source)
XLA Modules:
  0.0 86.9 jit_solution(2888784719316005865)
XLA Ops:
  7.2 0.0 all-gather.2.cloned.1.call-start
  7.2 0.7 convert_element_type.3
  7.9 1.8 %broadcast_multiply_fusion = bf16[3,4,128,128]{3,2,1,0:T(8,128)(2,1)} fusion(bf16[3,4,128,128]{3,2,1,0:T(8,128)(2,1)} %param.12, bf16[3,4]{1,0:T(4,128)(2,1)S(1)} %convert_element_type.3), kind=kLoop, calls=%fused_computation | loop fusion | flops 196608 | bytes 786456 | tf_op jit(solution)/shard_map/mul | solution.py:195
  9.7 0.0 all-gather.2.cloned.1.call-update
  10.4 0.8 copy.20.table_ref
  11.2 0.8 copy.23
  12.0 0.6 reshape.10.atom_ref
  12.6 0.0 copy-start.8
  12.6 1.3 %copy-done.8 = bf16[12,6,25,256]{3,2,1,0:T(8,128)(2,1)S(1)} copy-done((bf16[12,6,25,256]{3,2,1,0:T(8,128)(2,1)S(1)}, bf16[12,6,25,256]{3,2,1,0:T(8,128)(2,1)}, u32[]{:S(2)}) %copy-start.8) | copy-done | bytes 921624
  13.8 0.0 copy-start.9
  13.8 0.9 %copy-done.9 = f32[12,6,256]{2,1,0:T(8,128)S(1)} copy-done((f32[12,6,256]{2,1,0:T(8,128)S(1)}, f32[12,6,256]{2,1,0:T(8,128)}, u32[]{:S(2)}) %copy-start.9) | copy-done | bytes 73752
  14.7 2.5 %pre.1 = (f32[72,25,256]{2,1,0:T(8,128)S(1)}, bf16[72,32,256]{2,1,0:T(8,128)(2,1)S(1)}) custom-call(bf16[12,6,25,256]{3,2,1,0:T(8,128)(2,1)S(1)} %copy-done.8, f32[12,6,256]{2,1,0:T(8,128)S(1)} %copy-done.9, f32[25,16]{1,0:T(8,128)S(1)} %copy.20.table_ref), custom_call_target="tpu_custom_call" | custom-call | flops 400000000 | bytes 6000000 | tf_op jit(solution)/shard_map/pre/pallas_call | solution.py:199
  17.2 27.7 %all-gather.2.cloned.1.call-done.blocks_ref = bf16[24,4,128,128]{3,2,1,0:T(8,128)(2,1)} async-done(((bf16[3,4,128,128]{3,2,1,0:T(8,128)(2,1)}), bf16[24,4,128,128]{3,2,1,0:T(8,128)(2,1)}) %all-gather.2.cloned.1.call-update) | async-done | bytes 3145744 | tf_op jit(solution)/shard_map/all_gather | solution.py:196
  44.9 0.0 copy-start
  44.9 1.9 %copy-done = bf16[12,4,256,128]{3,2,1,0:T(8,128)(2,1)S(1)} copy-done((bf16[12,4,256,128]{3,2,1,0:T(8,128)(2,1)S(1)}, bf16[12,4,256,128]{3,2,1,0:T(8,128)(2,1)}, u32[]{:S(2)}) %copy-start) | copy-done | bytes 3145752
  46.8 0.0 copy-start.1
  46.8 1.9 %copy-done.1 = bf16[24,4,128,128]{3,2,1,0:T(8,128)(2,1)S(1)} copy-done((bf16[24,4,128,128]{3,2,1,0:T(8,128)(2,1)S(1)}, bf16[24,4,128,128]{3,2,1,0:T(8,128)(2,1)}, u32[]{:S(2)}) %copy-start.1) | copy-done | bytes 3145752
  48.7 0.0 copy-start.2
  48.7 0.9 %copy-done.2 = f32[12,6,256]{2,1,0:T(8,128)S(1)} copy-done((f32[12,6,256]{2,1,0:T(8,128)S(1)}, f32[12,6,256]{2,1,0:T(8,128)}, u32[]{:S(2)}) %copy-start.2) | copy-done | bytes 73752
  49.6 0.0 copy-start.3
  49.6 0.7 copy-done.3
  50.3 0.0 copy-start.5
  50.3 0.7 copy-done.5
  50.9 0.0 copy-start.7
  50.9 0.7 copy-done.7
  51.6 0.0 copy-start.4
  51.6 0.0 copy-start.6
  51.6 7.0 %density.1 = (f32[12,256]{1,0:T(8,128)}, f32[32,128]{1,0:T(8,128)S(1)}) custom-call(s32[1]{0:T(128)S(6)} %copy.24.start_ref, s32[1,12]{1,0:T(1,128)S(1)} %copy-done.7, s32[1,12]{1,0:T(1,128)S(1)} %copy-done.5, bf16[12,4,256,128]{3,2,1,0:T(8,128)(2,1)S(1)} %copy-done, bf16[24,4,128,128]{3,2,1,0:T(8,128)(2,1)S(1)} %copy-done.1, f32[12,6,256]{2,1,0:T(8,128)S(1)} %copy-done.2, ...), custom_call_target="tpu_custom_call" | custom-call | flops 2000000000 | bytes 6000000 | tf_op jit(solution)/shard_map/density/pallas_call | solution.py:215
  58.6 0.3 collective-permute-start
  58.9 1.5 %collective-permute-start.1 = (f32[32,128]{1,0:T(8,128)S(1)}, f32[32,128]{1,0:T(8,128)S(1)}, u32[]{:S(2)}, u32[]{:S(2)}) collective-permute-start(f32[32,128]{1,0:T(8,128)S(1)} %get-tuple-element.16.refs_0_), channel_id=1, source_target_pairs={{0,2},{1,3},{2,0},{3,1},{4,6},{5,7},{6,4},{7,5},{8,10},{9,11},{10,... | collective-permute-start | bytes 49160 | tf_op jit(solution)/shard_map/ppermute | solution.py:230
  60.3 0.1 collective-permute-start.2
  60.5 1.4 %collective-permute-start.3 = (f32[32,128]{1,0:T(8,128)S(1)}, f32[32,128]{1,0:T(8,128)S(1)}, u32[]{:S(2)}, u32[]{:S(2)}) collective-permute-start(f32[32,128]{1,0:T(8,128)S(1)} %get-tuple-element.16.refs_0_), channel_id=1, source_target_pairs={{0,4},{1,5},{2,6},{3,7},{4,0},{5,1},{6,2},{7,3},{8,12},{9,13},{10,... | collective-permute-start | bytes 49160 | tf_op jit(solution)/shard_map/ppermute | solution.py:230
  61.8 0.5 collective-permute-start.4
  62.4 0.0 collective-permute-done.refs_1_
  62.4 1.5 %collective-permute-start.5 = (f32[32,128]{1,0:T(8,128)S(1)}, f32[32,128]{1,0:T(8,128)S(1)}, u32[]{:S(2)}, u32[]{:S(2)}) collective-permute-start(f32[32,128]{1,0:T(8,128)S(1)} %get-tuple-element.16.refs_0_), channel_id=1, source_target_pairs={{0,6},{1,7},{2,4},{3,5},{4,2},{5,3},{6,0},{7,1},{8,14},{9,15},{10,... | collective-permute-start | bytes 49160 | tf_op jit(solution)/shard_map/ppermute | solution.py:230
  63.8 0.0 collective-permute-done.1.refs_2_
  63.8 1.0 %collective-permute-start.6 = (f32[32,128]{1,0:T(8,128)S(1)}, f32[32,128]{1,0:T(8,128)S(1)}, u32[]{:S(2)}, u32[]{:S(2)}) collective-permute-start(f32[32,128]{1,0:T(8,128)S(1)} %get-tuple-element.16.refs_0_), channel_id=1, source_target_pairs={{0,7},{1,6},{2,5},{3,4},{4,3},{5,2},{6,1},{7,0},{8,15},{9,14},{10,... | collective-permute-start | bytes 49160 | tf_op jit(solution)/shard_map/ppermute | solution.py:230
  64.9 0.0 collective-permute-done.2.refs_3_
  64.9 0.0 collective-permute-done.3.refs_4_
  64.9 0.1 collective-permute-done.4.refs_5_
  65.0 2.0 %collective-permute-done.5.refs_6_ = f32[32,128]{1,0:T(8,128)S(1)} collective-permute-done((f32[32,128]{1,0:T(8,128)S(1)}, f32[32,128]{1,0:T(8,128)S(1)}, u32[]{:S(2)}, u32[]{:S(2)}) %collective-permute-start.5) | collective-permute-done | bytes 16416 | tf_op jit(solution)/shard_map/ppermute | solution.py:230
  67.0 0.9 %collective-permute-done.6.refs_7_ = f32[32,128]{1,0:T(8,128)S(1)} collective-permute-done((f32[32,128]{1,0:T(8,128)S(1)}, f32[32,128]{1,0:T(8,128)S(1)}, u32[]{:S(2)}, u32[]{:S(2)}) %collective-permute-start.6) | collective-permute-done | bytes 16416 | tf_op jit(solution)/shard_map/ppermute | solution.py:230
  67.9 0.4 scatter.1
  68.3 1.5 %collective-permute-start.7 = (f32[32,256]{1,0:T(8,128)S(1)}, f32[32,256]{1,0:T(8,128)S(1)}, u32[]{:S(2)}, u32[]{:S(2)}) collective-permute-start(f32[32,256]{1,0:T(8,128)S(1)} %get-tuple-element.18), channel_id=1, source_target_pairs={{0,8},{8,16},{16,24},{24,0},{1,9},{9,17},{17,25},{25,1},{2,10},{10... | collective-permute-start | bytes 98312 | tf_op jit(solution)/shard_map/ppermute | solution.py:174
  69.8 2.3 %collective-permute-start.8 = (f32[32,256]{1,0:T(8,128)S(1)}, f32[32,256]{1,0:T(8,128)S(1)}, u32[]{:S(2)}, u32[]{:S(2)}) collective-permute-start(f32[32,256]{1,0:T(8,128)S(1)} %get-tuple-element.19), channel_id=1, source_target_pairs={{0,24},{8,0},{16,8},{24,16},{1,25},{9,1},{17,9},{25,17},{2,26},{10... | collective-permute-start | bytes 98312 | tf_op jit(solution)/shard_map/ppermute | solution.py:174
  72.2 0.6 collective-permute-start.9
  72.8 2.3 %collective-permute-start.10 = (f32[32,128]{1,0:T(8,128)S(1)}, f32[32,128]{1,0:T(8,128)S(1)}, u32[]{:S(2)}, u32[]{:S(2)}) collective-permute-start(f32[32,128]{1,0:T(8,128)S(1)} %get-tuple-element.21), channel_id=1, source_target_pairs={{0,16},{8,24},{16,0},{24,8},{1,17},{9,25},{17,1},{25,9},{2,18},{10... | collective-permute-start | bytes 49160 | tf_op jit(solution)/shard_map/ppermute | solution.py:174
  75.1 1.7 %collective-permute-done.9.a2_ref = f32[32,128]{1,0:T(8,128)S(1)} collective-permute-done((f32[32,128]{1,0:T(8,128)S(1)}, f32[32,128]{1,0:T(8,128)S(1)}, u32[]{:S(2)}, u32[]{:S(2)}) %collective-permute-start.9) | collective-permute-done | bytes 16416 | tf_op jit(solution)/shard_map/ppermute | solution.py:174
  76.8 0.6 collective-permute-done.10.b2_ref
  77.4 0.0 collective-permute-done.7.a1_ref
  77.4 0.0 collective-permute-done.8.b1_ref
  77.4 0.0 copy-done.4
  77.4 0.0 copy-done.6
  77.4 1.8 %potential.1 = (f32[25,128]{1,0:T(8,128)S(1)}, f32[12,256]{1,0:T(8,128)}) custom-call(s32[1,12]{1,0:T(1,128)S(1)} %copy-done.6, f32[32,384]{1,0:T(8,128)S(1)} %get-tuple-element.17.own_ref, f32[32,256]{1,0:T(8,128)S(1)} %collective-permute-done.7.a1_ref, f32[32,256]{1,0:T(8,128)S(1)} %collective-permute-done.8.b1_ref, ...), custom_call_target="tpu_custom_call" | custom-call | tf_op jit(solution)/shard_map/potential/pallas_call | solution.py:247
  79.3 0.1 constant_dynamic-slice_fusion
  79.3 0.7 copy.22
  (1 shorter events, 0.0 us)
Async XLA Ops:
  7.2 37.8 %all-gather.2.cloned.1.call-start = ((), (), s32[]{:S(2)}) async-start(), calls=%async_computation | async-start | bytes 3538944 | tf_op jit(solution)/shard_map/all_gather | solution.py:196
  12.6 1.3 %copy-start.8 = (bf16[12,6,25,256]{3,2,1,0:T(8,128)(2,1)S(1)}, bf16[12,6,25,256]{3,2,1,0:T(8,128)(2,1)}, u32[]{:S(2)}) copy-start(bf16[12,6,25,256]{3,2,1,0:T(8,128)(2,1)} %harm_ref.1) | copy-start | bytes 2764804
  13.8 0.9 %copy-start.9 = (f32[12,6,256]{2,1,0:T(8,128)S(1)}, f32[12,6,256]{2,1,0:T(8,128)}, u32[]{:S(2)}) copy-start(f32[12,6,256]{2,1,0:T(8,128)} %radius_ref.1) | copy-start | bytes 221188
  44.9 1.9 %copy-start = (bf16[12,4,256,128]{3,2,1,0:T(8,128)(2,1)S(1)}, bf16[12,4,256,128]{3,2,1,0:T(8,128)(2,1)}, u32[]{:S(2)}) copy-start(bf16[12,4,256,128]{3,2,1,0:T(8,128)(2,1)} %basis_ref.1) | copy-start | bytes 9437188
  46.8 1.9 %copy-start.1 = (bf16[24,4,128,128]{3,2,1,0:T(8,128)(2,1)S(1)}, bf16[24,4,128,128]{3,2,1,0:T(8,128)(2,1)}, u32[]{:S(2)}) copy-start(bf16[24,4,128,128]{3,2,1,0:T(8,128)(2,1)} %all-gather.2.cloned.1.call-done.blocks_ref) | copy-start | bytes 9437188
  48.7 0.9 %copy-start.2 = (f32[12,6,256]{2,1,0:T(8,128)S(1)}, f32[12,6,256]{2,1,0:T(8,128)}, u32[]{:S(2)}) copy-start(f32[12,6,256]{2,1,0:T(8,128)} %part_ref.1) | copy-start | bytes 221188
  49.6 0.7 copy-start.3
  50.3 0.7 copy-start.5
  50.9 0.7 copy-start.7
  51.6 25.8 %copy-start.4 = (s32[1,128]{1,0:T(1,128)S(1)}, s32[1,128]{1,0:T(1,128)}, u32[]{:S(2)}) copy-start(s32[1,128]{1,0:T(1,128)} %reshape.10.atom_ref) | copy-start | bytes 1540
  51.6 25.8 %copy-start.6 = (s32[1,12]{1,0:T(1,128)S(1)}, s32[1,12]{1,0:T(1,128)}, u32[]{:S(2)}) copy-start(s32[1,12]{1,0:T(1,128)} %size_ref.3) | copy-start | bytes 148
  58.6 3.8 %collective-permute-start = (f32[32,128]{1,0:T(8,128)S(1)}, f32[32,128]{1,0:T(8,128)S(1)}, u32[]{:S(2)}, u32[]{:S(2)}) collective-permute-start(f32[32,128]{1,0:T(8,128)S(1)} %get-tuple-element.16.refs_0_), channel_id=1, source_target_pairs={{0,1},{1,0},{2,3},{3,2},{4,5},{5,4},{6,7},{7,6},{8,9},{9,8},{10,11... | collective-permute-start | bytes 49160 | tf_op jit(solution)/shard_map/ppermute | solution.py:230
  58.9 5.0 %collective-permute-start.1 = (f32[32,128]{1,0:T(8,128)S(1)}, f32[32,128]{1,0:T(8,128)S(1)}, u32[]{:S(2)}, u32[]{:S(2)}) collective-permute-start(f32[32,128]{1,0:T(8,128)S(1)} %get-tuple-element.16.refs_0_), channel_id=1, source_target_pairs={{0,2},{1,3},{2,0},{3,1},{4,6},{5,7},{6,4},{7,5},{8,10},{9,11},{10,... | collective-permute-start | bytes 49160 | tf_op jit(solution)/shard_map/ppermute | solution.py:230
  60.3 4.5 %collective-permute-start.2 = (f32[32,128]{1,0:T(8,128)S(1)}, f32[32,128]{1,0:T(8,128)S(1)}, u32[]{:S(2)}, u32[]{:S(2)}) collective-permute-start(f32[32,128]{1,0:T(8,128)S(1)} %get-tuple-element.16.refs_0_), channel_id=1, source_target_pairs={{0,3},{1,2},{2,1},{3,0},{4,7},{5,6},{6,5},{7,4},{8,11},{9,10},{10,... | collective-permute-start | bytes 49160 | tf_op jit(solution)/shard_map/ppermute | solution.py:230
  60.5 4.4 %collective-permute-start.3 = (f32[32,128]{1,0:T(8,128)S(1)}, f32[32,128]{1,0:T(8,128)S(1)}, u32[]{:S(2)}, u32[]{:S(2)}) collective-permute-start(f32[32,128]{1,0:T(8,128)S(1)} %get-tuple-element.16.refs_0_), channel_id=1, source_target_pairs={{0,4},{1,5},{2,6},{3,7},{4,0},{5,1},{6,2},{7,3},{8,12},{9,13},{10,... | collective-permute-start | bytes 49160 | tf_op jit(solution)/shard_map/ppermute | solution.py:230
  61.8 3.2 %collective-permute-start.4 = (f32[32,128]{1,0:T(8,128)S(1)}, f32[32,128]{1,0:T(8,128)S(1)}, u32[]{:S(2)}, u32[]{:S(2)}) collective-permute-start(f32[32,128]{1,0:T(8,128)S(1)} %get-tuple-element.16.refs_0_), channel_id=1, source_target_pairs={{0,5},{1,4},{2,7},{3,6},{4,1},{5,0},{6,3},{7,2},{8,13},{9,12},{10,... | collective-permute-start | bytes 49160 | tf_op jit(solution)/shard_map/ppermute | solution.py:230
  62.4 4.6 %collective-permute-start.5 = (f32[32,128]{1,0:T(8,128)S(1)}, f32[32,128]{1,0:T(8,128)S(1)}, u32[]{:S(2)}, u32[]{:S(2)}) collective-permute-start(f32[32,128]{1,0:T(8,128)S(1)} %get-tuple-element.16.refs_0_), channel_id=1, source_target_pairs={{0,6},{1,7},{2,4},{3,5},{4,2},{5,3},{6,0},{7,1},{8,14},{9,15},{10,... | collective-permute-start | bytes 49160 | tf_op jit(solution)/shard_map/ppermute | solution.py:230
  63.8 4.1 %collective-permute-start.6 = (f32[32,128]{1,0:T(8,128)S(1)}, f32[32,128]{1,0:T(8,128)S(1)}, u32[]{:S(2)}, u32[]{:S(2)}) collective-permute-start(f32[32,128]{1,0:T(8,128)S(1)} %get-tuple-element.16.refs_0_), channel_id=1, source_target_pairs={{0,7},{1,6},{2,5},{3,4},{4,3},{5,2},{6,1},{7,0},{8,15},{9,14},{10,... | collective-permute-start | bytes 49160 | tf_op jit(solution)/shard_map/ppermute | solution.py:230
  68.3 9.1 %collective-permute-start.7 = (f32[32,256]{1,0:T(8,128)S(1)}, f32[32,256]{1,0:T(8,128)S(1)}, u32[]{:S(2)}, u32[]{:S(2)}) collective-permute-start(f32[32,256]{1,0:T(8,128)S(1)} %get-tuple-element.18), channel_id=1, source_target_pairs={{0,8},{8,16},{16,24},{24,0},{1,9},{9,17},{17,25},{25,1},{2,10},{10... | collective-permute-start | bytes 98312 | tf_op jit(solution)/shard_map/ppermute | solution.py:174
  69.8 7.6 %collective-permute-start.8 = (f32[32,256]{1,0:T(8,128)S(1)}, f32[32,256]{1,0:T(8,128)S(1)}, u32[]{:S(2)}, u32[]{:S(2)}) collective-permute-start(f32[32,256]{1,0:T(8,128)S(1)} %get-tuple-element.19), channel_id=1, source_target_pairs={{0,24},{8,0},{16,8},{24,16},{1,25},{9,1},{17,9},{25,17},{2,26},{10... | collective-permute-start | bytes 98312 | tf_op jit(solution)/shard_map/ppermute | solution.py:174
  72.2 4.6 %collective-permute-start.9 = (f32[32,128]{1,0:T(8,128)S(1)}, f32[32,128]{1,0:T(8,128)S(1)}, u32[]{:S(2)}, u32[]{:S(2)}) collective-permute-start(f32[32,128]{1,0:T(8,128)S(1)} %get-tuple-element.20), channel_id=1, source_target_pairs={{0,16},{8,24},{16,0},{24,8},{1,17},{9,25},{17,1},{25,9},{2,18},{10... | collective-permute-start | bytes 49160 | tf_op jit(solution)/shard_map/ppermute | solution.py:174
  72.8 4.6 %collective-permute-start.10 = (f32[32,128]{1,0:T(8,128)S(1)}, f32[32,128]{1,0:T(8,128)S(1)}, u32[]{:S(2)}, u32[]{:S(2)}) collective-permute-start(f32[32,128]{1,0:T(8,128)S(1)} %get-tuple-element.21), channel_id=1, source_target_pairs={{0,16},{8,24},{16,0},{24,8},{1,17},{9,25},{17,1},{25,9},{2,18},{10... | collective-permute-start | bytes 49160 | tf_op jit(solution)/shard_map/ppermute | solution.py:174
Sparse Core Ops, SparseCore 0:
  9.9 35.0 all-gather.1

commit v3 on v2

v3 whole, which is shorter than its diff:
```python
import functools
import jax
import jax.numpy as jnp
from jax import lax
from jax.experimental import pallas as pl
from jax.experimental.pallas import tpu as pltpu
from jax.sharding import PartitionSpec as P

LANES = 128
ROWS = 32
SLOT = 8
NT = (((1,), (1,)), ((), ()))
NN = (((1,), (0,)), ((), ()))
VMEM = pl.BlockSpec(memory_space=pltpu.VMEM)
SMEM = pl.BlockSpec(memory_space=pltpu.SMEM)
ANY = pl.BlockSpec(memory_space=pl.ANY)
PARAMS = pltpu.CompilerParams(vmem_limit_bytes=16 * 1024 * 1024)


def dot(a, b, dims=NN):
    return lax.dot_general(a, b, dims, preferred_element_type=jnp.float32)


def split2(x):
    hi = x.astype(jnp.bfloat16)
    lo = (x - hi.astype(jnp.float32)).astype(jnp.bfloat16)
    return hi, lo


def split3(x):
    hi, mid = split2(x)
    rest = x - hi.astype(jnp.float32) - mid.astype(jnp.float32)
    return hi, mid, rest.astype(jnp.bfloat16)


def cubic(distance):
    inner = 2.0 / 3.0 - distance * distance + 0.5 * distance * distance * distance
    remote = 2.0 - distance
    outer = remote * remote * remote * (1.0 / 6.0)
    return jnp.where(distance < 1.0, inner, jnp.where(distance < 2.0, outer, 0.0))


def select_kernel(dev_count, starts_ref, mask_ref, rows_ref, *outs):
    me = lax.axis_index("dev")
    stored, band = rows_ref.shape[0], rows_ref.shape[1]
    for m, out in enumerate(outs):
        start = starts_ref[m]
        ahead = lax.rem(me - start + stored * dev_count, dev_count)
        held = lax.rem(start + ahead, stored * dev_count) // dev_count
        for k in range(band):
            factor = mask_ref[held, k].astype(jnp.float32)
            out[k] = (rows_ref[held, k].astype(jnp.float32) * factor).astype(jnp.bfloat16)


def pre_kernel(basis_ref, harm_ref, radius_ref, table_ref, g_ref, hpad_ref, phit_ref, basis, sem):
    batches, near, comps, points = harm_ref.shape
    near_blocks = basis.shape[1]
    knots = table_ref.shape[1]
    copy = pltpu.make_async_copy(basis_ref, basis, sem)
    copy.start()
    hpad_ref[...] = jnp.zeros(hpad_ref.shape, hpad_ref.dtype)
    r_hi, r_lo = split2(table_ref[...])
    coeffs = jnp.concatenate([r_hi, r_hi, r_lo], axis=1)
    knot = lax.broadcasted_iota(jnp.int32, (knots, points), 0).astype(jnp.float32)

    def body(b, carry):
        rows = radius_ref[b]
        for i in range(near):
            spline = cubic(jnp.abs(rows[i : i + 1, :] - knot))
            s_hi, s_lo = split2(spline)
            radial = dot(coeffs, jnp.concatenate([s_hi, s_lo, s_hi], axis=0))
            h = harm_ref[b, i]
            g_ref[b * near + i] = radial * h.astype(jnp.float32)
            hpad_ref[b * near + i, 0:comps, :] = h
        return carry

    lax.fori_loop(0, batches, body, 0)
    copy.wait()

    def turn(b, carry):
        for j in range(near_blocks):
            phit_ref[b, j] = basis[b, j].T
        return carry

    lax.fori_loop(0, batches, turn, 0)


def density_kernel(start_ref, offset_ref, size_ref, atom_ref, phit_ref, part_ref, hpad_ref, *refs):
    dens_ref, terms_ref, window_ref, w_ref = refs[-4:]
    pieces = refs[:-4]
    owners = len(pieces)
    batches, near_blocks, width, points = phit_ref.shape
    near = part_ref.shape[1]
    me = lax.axis_index("dev")
    for m, piece in enumerate(pieces):
        spot = lax.rem(lax.bitwise_xor(me, m) - start_ref[0] + 3 * owners, owners)
        window_ref[spot] = piece[...]
    w_ref[...] = jnp.zeros(w_ref.shape, w_ref.dtype)
    lane = lax.broadcasted_iota(jnp.int32, (1, points), 1)
    zero = jnp.zeros((width, width), jnp.bfloat16)

    def body(b, carry):
        first = offset_ref[0, b]
        total = jnp.zeros((width, points), jnp.float32)
        for q, js in ((0, (0, 1, 2)), (2, (0, 1, 2, 3))):
            left = []
            for j in js:
                pair = [
                    window_ref[first + j, f - j + 1] if 0 <= f - j + 1 < 4 else zero
                    for f in (q, q + 1)
                ]
                left.append(jnp.concatenate(pair, axis=1))
            right = jnp.concatenate([phit_ref[b, q], phit_ref[b, q + 1]], axis=0)
            mixed = dot(jnp.concatenate(left, axis=0), right)
            for at, j in enumerate(js):
                part = mixed[at * width : (at + 1) * width]
                total = total + part * phit_ref[b, j].astype(jnp.float32)
        summed = jnp.sum(total, axis=0, keepdims=True)
        alive = lane < size_ref[0, b]
        row = jnp.where(alive, summed, 0.0)
        dens_ref[pl.ds(b, 1), :] = row
        w_ref[b, 0:near, :] = part_ref[b] * row
        return carry

    lax.fori_loop(0, batches, body, 0, unroll=2)
    weights = w_ref[...].reshape(LANES, points)
    columns = jnp.concatenate(split2(weights), axis=0)
    slot = lax.broadcasted_iota(jnp.int32, (1, 2 * LANES), 1) % LANES
    cross = dot(hpad_ref[...].reshape(batches * near * ROWS, points), columns, NT)
    terms = jnp.zeros((ROWS, 2 * LANES), jnp.float32)
    for b in range(batches):
        for i in range(near):
            at = (b * near + i) * ROWS
            terms = terms + jnp.where(slot == b * SLOT + i, cross[at : at + ROWS], 0.0)
    result = terms[:, :LANES] + terms[:, LANES:]
    row_id = lax.broadcasted_iota(jnp.int32, (ROWS, LANES), 0)
    comps = ROWS - 7
    terms_ref[...] = jnp.where(row_id == comps, atom_ref[...].astype(jnp.float32), result)


def scatter_kernel(comps, atoms, flip, *refs):
    outs = refs[-4:]
    pieces = refs[:-4]
    row_id = lax.broadcasted_iota(jnp.int32, (3 * atoms, LANES), 0)
    total = jnp.zeros((3 * ROWS, 3 * atoms), jnp.float32)
    for piece in pieces:
        left, right = [], []
        for part in range(piece.shape[0]):
            values = piece[part]
            chosen = values[comps : comps + 1, :].astype(jnp.int32)
            right.append((row_id == chosen).astype(jnp.float32).astype(jnp.bfloat16))
            left.append(jnp.concatenate(split3(values), axis=0))
        total = total + dot(jnp.concatenate(left, axis=1), jnp.concatenate(right, axis=1), NT)
    sums = total[:ROWS] + total[ROWS : 2 * ROWS] + total[2 * ROWS :]
    own, near_a, near_b, far = outs
    own[...] = sums
    ahead, back = sums[:, atoms:], sums[:, : 2 * atoms]
    if flip:
        odd = lax.rem(lax.axis_index("region"), 2) == 1
        near_a[...] = jnp.where(odd, back, ahead)
        near_b[...] = jnp.where(odd, ahead, back)
    else:
        near_a[...] = ahead
        near_b[...] = back
    far[:, :atoms] = sums[:, :atoms]
    far[:, atoms:] = sums[:, 2 * atoms :]


def potential_kernel(
    comps, atoms, flip, size_ref, own_ref, near_a_ref, near_b_ref, fa_ref, fb_ref, atom_ref, g_ref,
    mom_ref, pot_ref,
):
    batches, points = pot_ref.shape
    near = g_ref.shape[0] // batches
    own = own_ref[...]
    near_a, near_b = near_a_ref[...], near_b_ref[...]
    if flip:
        odd = lax.rem(lax.axis_index("region"), 2) == 1
        low = jnp.where(odd, near_a, near_b)
        high = jnp.where(odd, near_b, near_a)
    else:
        low, high = near_a, near_b
    before = fa_ref[:, atoms:] + low[:, :atoms] + own[:, :atoms]
    here = low[:, atoms:] + own[:, atoms : 2 * atoms] + high[:, :atoms]
    after = own[:, 2 * atoms :] + high[:, atoms:] + fb_ref[:, :atoms]

    mine = mom_ref.shape[0]
    want = lax.broadcasted_iota(jnp.int32, (mine, atoms), 0) + lax.axis_index("dev") * mine
    keep = want == lax.broadcasted_iota(jnp.int32, (mine, atoms), 1)
    keep = keep.astype(jnp.float32).astype(jnp.bfloat16)
    taken = dot(keep, jnp.concatenate(split3(here), axis=0), NT)
    taken = taken[:, :ROWS] + taken[:, ROWS : 2 * ROWS] + taken[:, 2 * ROWS :]
    mom_ref[...] = taken[:, :comps]

    moments = jnp.concatenate([before, here, after], axis=1)
    row_id = lax.broadcasted_iota(jnp.int32, (3 * atoms, LANES), 0)
    pick = (row_id == atom_ref[...]).astype(jnp.float32).astype(jnp.bfloat16)
    got = dot(jnp.concatenate(split3(moments), axis=0), pick)
    chosen = got[:ROWS] + got[ROWS : 2 * ROWS] + got[2 * ROWS :]
    chosen = chosen[:comps]
    lane = lax.broadcasted_iota(jnp.int32, (1, points), 1)
    for b in range(batches):
        total = jnp.zeros((comps, points), jnp.float32)
        for i in range(near):
            column = chosen[:, b * SLOT + i : b * SLOT + i + 1]
            total = total + column * g_ref[b * near + i]
        row = jnp.sum(total, axis=0, keepdims=True)
        pot_ref[b : b + 1, :] = jnp.where(lane < size_ref[0, b], row, 0.0)


def crossed(value, axis, m):
    return lax.ppermute(value, axis, [(i, i ^ m) for i in range(lax.axis_size(axis))])


def shifted(value, axis, step):
    count = lax.axis_size(axis)
    return lax.ppermute(value, axis, [(i, (i + step) % count) for i in range(count)])


def per_device(
    basis_values,
    density_rows,
    block_mask,
    window_start,
    batch_offsets,
    batch_sizes,
    atom_near,
    harmonics,
    partition,
    radius,
    radial_table,
):
    dev_count = lax.axis_size("dev")
    region_count = lax.axis_size("region")
    blocks_dev, band, width = density_rows.shape[:3]
    batches, near, comps, points = harmonics.shape
    near_blocks = basis_values.shape[1]
    mine = 16
    atoms = mine * dev_count
    f32, bf16 = jnp.float32, jnp.bfloat16

    pair = jnp.concatenate([window_start, crossed(window_start, "dev", 1)])
    starts = jnp.concatenate([pair] + [crossed(pair, "dev", m) for m in range(2, dev_count, 2)])
    served = pl.pallas_call(
        functools.partial(select_kernel, dev_count),
        out_shape=tuple(
            jax.ShapeDtypeStruct((band, width, width), bf16) for _ in range(dev_count)
        ),
        in_specs=[SMEM, SMEM, VMEM],
        out_specs=(VMEM,) * dev_count,
        compiler_params=PARAMS,
        name="select",
    )(starts, block_mask, density_rows)
    order = sorted(range(1, dev_count), key=lambda m: -bin(m).count("1"))
    pieces = {m: crossed(served[m], "dev", m) for m in order}
    pieces[0] = served[0]

    g, hpad, phit = pl.pallas_call(
        pre_kernel,
        out_shape=(
            jax.ShapeDtypeStruct((batches * near, comps, points), f32),
            jax.ShapeDtypeStruct((batches * near, ROWS, points), bf16),
            jax.ShapeDtypeStruct((batches, near_blocks, width, points), bf16),
        ),
        in_specs=[ANY] + [VMEM] * 3,
        out_specs=(VMEM,) * 3,
        scratch_shapes=[pltpu.VMEM(basis_values.shape, bf16), pltpu.SemaphoreType.DMA],
        compiler_params=PARAMS,
        cost_estimate=pl.CostEstimate(flops=2_000_000_000, bytes_accessed=8_000_000, transcendentals=0),
        name="pre",
    )(basis_values, harmonics, radius, radial_table)

    atom_rows = jnp.pad(atom_near, ((0, LANES // SLOT - batches), (0, SLOT - near)), constant_values=-1)
    atom_rows = atom_rows.reshape(1, LANES)

    density, terms = pl.pallas_call(
        density_kernel,
        out_shape=(
            jax.ShapeDtypeStruct((batches, points), f32),
            jax.ShapeDtypeStruct((ROWS, LANES), f32),
        ),
        in_specs=[SMEM] * 3 + [VMEM] * (4 + dev_count),
        out_specs=(VMEM, VMEM),
        scratch_shapes=[
            pltpu.VMEM((dev_count, band, width, width), bf16),
            pltpu.VMEM((LANES // SLOT, SLOT, points), f32),
        ],
        compiler_params=PARAMS,
        cost_estimate=pl.CostEstimate(flops=2_000_000_000, bytes_accessed=6_000_000, transcendentals=0),
        name="density",
    )(
        window_start, batch_offsets, batch_sizes, atom_rows, phit, partition, hpad,
        *[pieces[m] for m in range(dev_count)],
    )

    both = jnp.stack([terms, crossed(terms, "dev", 1)])
    groups = [both] + [crossed(both, "dev", m) for m in range(2, dev_count, 2)]
    flip = region_count == 4
    own, near_a, near_b, far = pl.pallas_call(
        functools.partial(scatter_kernel, comps, atoms, flip),
        out_shape=tuple(jax.ShapeDtypeStruct((ROWS, n * atoms), f32) for n in (3, 2, 2, 2)),
        in_specs=[VMEM] * len(groups),
        out_specs=(VMEM,) * 4,
        compiler_params=PARAMS,
        name="scatter",
    )(*groups)
    if flip:
        far_a = far_b = crossed(far, "region", 2)
        near_a = crossed(near_a, "region", 1)
        near_b = crossed(near_b, "region", 3)
    else:
        far_a = shifted(far, "region", 2)
        far_b = shifted(far, "region", -2)
        near_a = shifted(near_a, "region", 1)
        near_b = shifted(near_b, "region", -1)

    moments, potential = pl.pallas_call(
        functools.partial(potential_kernel, comps, atoms, flip),
        out_shape=(
            jax.ShapeDtypeStruct((mine, comps), f32),
            jax.ShapeDtypeStruct((batches, points), f32),
        ),
        in_specs=[SMEM] + [VMEM] * 7,
        out_specs=(VMEM, VMEM),
        compiler_params=PARAMS,
        name="potential",
    )(batch_sizes, own, near_a, near_b, far_a, far_b, atom_rows, g)
    return (density, moments.T, potential)


def solution(mesh):
    both = ("region", "dev")
    placed = (
        P(both, None, None, None),
        P(both, None, None, None),
        P(both, None),
        P(both),
        P(both, None),
        P(both, None),
        P(both, None),
        P(both, None, None, None),
        P(both, None, None),
        P(both, None, None),
        P(),
    )
    return jax.shard_map(
        per_device,
        mesh=mesh,
        in_specs=placed,
        out_specs=(P(both, None), P(None, both), P(both, None)),
        check_vma=False,
    )
```

time: 87.3 us -> 54.4 us (0.62)
  waiting for transfers between devices: 33.1 us -> 12.7 us
  between operations: 14.7 us -> 1.38 us
  starting transfers between devices: 13.1 us -> 19.5 us
  local copies, waits for them, and re-layouts: 11.7 us -> 8.09 us
  other arithmetic: 2.52 us -> 0.69 us
    all_gather x1 -> x0, waiting for transfers between devices: 27.7 us -> none  [per_device(): gathered = lax.all_gather(masked, 'dev', axis=0, tiled=True)]
    ppermute x11 -> x18, waiting for transfers between devices: 5.37 us -> 12.7 us  [crossed(): lax.ppermute(value, axis, [(i, i ^ m) for i in range(lax.axis_size(axis))])]
    ppermute x11 -> x18, starting transfers between devices: 13.1 us -> 19.5 us  [crossed(): lax.ppermute(value, axis, [(i, i ^ m) for i in range(lax.axis_size(axis))])]
    unnamed x23 -> x18, local copies, waits for them, and re-layouts: 11 us -> 7.31 us
    mul x1 -> x0, other arithmetic: 1.83 us -> none  [per_device(): masked = density_rows * block_mask.astype(jnp.bfloat16)[:, :, None, None]]
    pallas_call x3 -> x4, Pallas kernels: 9.22 us -> 7.4 us  [the longest x1 4.41 us: per_device(): pl.pallas_call(density_kernel, out_shape=(jax.ShapeDtypeStruct((batches,...]
    pallas_call x1, Pallas kernels: 2.5 us -> 4.21 us  [per_device(): pl.pallas_call(pre_kernel, out_shape=(jax.ShapeDtypeStruct((batches * nea...]
  transfers between devices with their start and end apart: 12 -> 18, of which waited for: 6 -> 11; matrix products, arithmetic and copies ran while one was open for 2% -> 3% of each run, Pallas kernels for 3% -> 8%
where the time goes in v3:
time: 54.4 us; the launch traced here: 54 us
  starting transfers between devices  19.5 us (36%)
  waiting for transfers between devices  12.7 us (23%)
  Pallas kernels  11.6 us (21%)
  local copies, waits for them, and re-layouts  8.09 us (15%)
  between operations  1.38 us (3%)
  other arithmetic  0.69 us (1%)
    ppermute x18, starting transfers between devices, crossed(): lax.ppermute(value, axis, [(i, i ^ m) for i in range(lax.axis_size(axis))])  19.5 us
    ppermute x18, waiting for transfers between devices, crossed(): lax.ppermute(value, axis, [(i, i ^ m) for i in range(lax.axis_size(axis))])  12.7 us
    unnamed x18, local copies, waits for them, and re-layouts  7.31 us
    pallas_call x1, Pallas kernels, per_device(): pl.pallas_call(density_kernel, out_shape=(jax.ShapeDtypeStruct((batches,...  4.41 us
    pallas_call x1, Pallas kernels, per_device(): pl.pallas_call(pre_kernel, out_shape=(jax.ShapeDtypeStruct((batches * nea...  4.21 us
    pallas_call x1, Pallas kernels, per_device(): pl.pallas_call(functools.partial(potential_kernel, comps, atoms, flip), o...  1.86 us
  transfers between devices with their start and end apart: 18, of which 11 were waited for; matrix products, arithmetic and copies ran while one was open for 3% of the time, Pallas kernels for 8%

profile of v3, /device:TPU:0, one launch (start us, length us, event | category | flops | bytes accessed | tf_op | source)
XLA Modules:
  0.0 54.0 jit_solution(11582183019607616054)
XLA Ops:
  0.6 0.5 collective-permute-start
  1.8 0.3 collective-permute-done
  2.1 0.7 %pad_add_fusion = s32[2]{0:T(128)S(1)} fusion(s32[1]{0:T(128)} %collective-permute-done, s32[1]{0:T(128)S(6)} %copy.19.start_ref), kind=kLoop, calls=%fused_computation.1 | loop fusion | flops 2 | bytes 16 | tf_op jit(solution)/shard_map/concatenate | solution.py:242
  2.8 3.7 %collective-permute-start.3 = (s32[2]{0:T(128)S(1)}, s32[2]{0:T(128)S(1)}, u32[]{:S(2)}, u32[]{:S(2)}) collective-permute-start(s32[2]{0:T(128)S(1)} %pad_add_fusion), channel_id=1, source_target_pairs={{0,6},{1,7},{2,4},{3,5},{4,2},{5,3},{6,0},{7,1},{8,14},{9,15},{10,... | collective-permute-start | bytes 32 | tf_op jit(solution)/shard_map/ppermute | solution.py:212
  6.5 0.5 collective-permute-start.2
  7.0 0.1 collective-permute-start.1
  7.2 0.9 %collective-permute-done.3 = s32[2]{0:T(128)S(1)} collective-permute-done((s32[2]{0:T(128)S(1)}, s32[2]{0:T(128)S(1)}, u32[]{:S(2)}, u32[]{:S(2)}) %collective-permute-start.3) | collective-permute-done | bytes 40 | tf_op jit(solution)/shard_map/ppermute | solution.py:212
  8.0 2.0 %collective-permute-done.2 = s32[2]{0:T(128)S(1)} collective-permute-done((s32[2]{0:T(128)S(1)}, s32[2]{0:T(128)S(1)}, u32[]{:S(2)}, u32[]{:S(2)}) %collective-permute-start.2) | collective-permute-done | bytes 40 | tf_op jit(solution)/shard_map/ppermute | solution.py:212
  10.1 0.5 collective-permute-done.1
  10.6 0.7 %concatenate.8.starts_ref = s32[8]{0:T(128)S(1)} concatenate(s32[1]{0:T(128)S(6)} %copy.19.start_ref, s32[1]{0:T(128)} %collective-permute-done, s32[2]{0:T(128)S(1)} %collective-permute-done.1, s32[2]{0:T(128)S(1)} %collective-permute-done.2, s32[2]{0:T(128)S(1)} %collective-permute-done.3), dimensions={0} | concatenate | bytes 64 | tf_op jit(solution)/shard_map/concatenate | solution.py:243
  11.2 0.0 copy-start
  11.2 1.0 %copy-done = bf16[3,4,128,128]{3,2,1,0:T(8,128)(2,1)S(1)} copy-done((bf16[3,4,128,128]{3,2,1,0:T(8,128)(2,1)S(1)}, bf16[3,4,128,128]{3,2,1,0:T(8,128)(2,1)}, u32[]{:S(2)}) %copy-start) | copy-done | bytes 393240
  12.3 0.0 copy-start.1
  12.3 0.7 %copy-done.1 = s32[3,4]{1,0:T(4,128)S(1)} copy-done((s32[3,4]{1,0:T(4,128)S(1)}, s32[3,4]{1,0:T(4,128)}, u32[]{:S(2)}) %copy-start.1) | copy-done | bytes 72
  12.9 0.8 %select.2 = (bf16[4,128,128]{2,1,0:T(8,128)(2,1)S(1)}, bf16[4,128,128]{2,1,0:T(8,128)(2,1)S(1)}, bf16[4,128,128]{2,1,0:T(8,128)(2,1)S(1)}, bf16[4,128,128]{2,1,0...) custom-call(s32[8]{0:T(128)S(1)} %concatenate.8.starts_ref, ...), custom_call_target="tpu_custom_call" | custom-call | tf_op jit(solution)/shard_map/select/pallas_call | solution.py:244
  13.7 0.1 collective-permute-start.4
  13.8 0.2 collective-permute-start.5
  14.0 0.8 %copy.18 = s32[12,6]{1,0:T(8,128)S(1)} copy(s32[12,6]{0,1:T(8,128)} %param.17) | data formatting | bytes 576
  14.8 0.1 reshape.9.atom_ref
  14.9 0.8 %copy.17.table_ref = f32[25,16]{1,0:T(8,128)S(1)} copy(f32[25,16]{0,1:T(8,128)} %param.21) | data formatting | bytes 3200 | tf_op args[10]
  15.6 1.7 %collective-permute-start.6 = (bf16[4,128,128]{2,1,0:T(8,128)(2,1)S(1)}, bf16[4,128,128]{2,1,0:T(8,128)(2,1)S(1)}, u32[]{:S(2)}, u32[]{:S(2)}) collective-permute-start(bf16[4,128,128]{2,1,0:T(8,128)(2,1)S(1)} %get-tuple-element.27), channel_id=1, source_target_pairs={{0,3},{1,2},{2,1},{3,0},{4,7},{5,6},{6,5},{7,4},{8,11},{9,10},{10,... | collective-permute-start | bytes 393224 | tf_op jit(solution)/shard_map/ppermute | solution.py:212
  17.3 1.5 %collective-permute-start.7 = (bf16[4,128,128]{2,1,0:T(8,128)(2,1)S(1)}, bf16[4,128,128]{2,1,0:T(8,128)(2,1)S(1)}, u32[]{:S(2)}, u32[]{:S(2)}) collective-permute-start(bf16[4,128,128]{2,1,0:T(8,128)(2,1)S(1)} %get-tuple-element.28), channel_id=1, source_target_pairs={{0,4},{1,5},{2,6},{3,7},{4,0},{5,1},{6,2},{7,3},{8,12},{9,13},{10,... | collective-permute-start | bytes 393224 | tf_op jit(solution)/shard_map/ppermute | solution.py:212
  18.8 0.2 collective-permute-start.8
  19.0 0.0 collective-permute-done.4.refs_1_
  19.0 1.5 %collective-permute-start.9 = (bf16[4,128,128]{2,1,0:T(8,128)(2,1)S(1)}, bf16[4,128,128]{2,1,0:T(8,128)(2,1)S(1)}, u32[]{:S(2)}, u32[]{:S(2)}) collective-permute-start(bf16[4,128,128]{2,1,0:T(8,128)(2,1)S(1)} %get-tuple-element.30), channel_id=1, source_target_pairs={{0,6},{1,7},{2,4},{3,5},{4,2},{5,3},{6,0},{7,1},{8,14},{9,15},{10,... | collective-permute-start | bytes 393224 | tf_op jit(solution)/shard_map/ppermute | solution.py:212
  20.5 0.0 collective-permute-done.5.refs_2_
  20.5 0.0 copy-start.2
  20.5 1.2 %collective-permute-start.10 = (bf16[4,128,128]{2,1,0:T(8,128)(2,1)S(1)}, bf16[4,128,128]{2,1,0:T(8,128)(2,1)S(1)}, u32[]{:S(2)}, u32[]{:S(2)}) collective-permute-start(bf16[4,128,128]{2,1,0:T(8,128)(2,1)S(1)} %get-tuple-element.31), channel_id=1, source_target_pairs={{0,7},{1,6},{2,5},{3,4},{4,3},{5,2},{6,1},{7,0},{8,15},{9,14},{10,... | collective-permute-start | bytes 393224 | tf_op jit(solution)/shard_map/ppermute | solution.py:212
  21.7 0.0 copy-start.3
  21.7 1.9 %copy-done.3 = bf16[12,4,256,128]{3,2,1,0:T(8,128)(2,1)S(1)} copy-done((bf16[12,4,256,128]{3,2,1,0:T(8,128)(2,1)S(1)}, bf16[12,4,256,128]{3,2,1,0:T(8,128)(2,1)}, u32[]{:S(2)}) %copy-start.3) | copy-done | bytes 3145752
  23.6 0.0 copy-start.4
  23.6 1.3 %copy-done.4 = bf16[12,6,25,256]{3,2,1,0:T(8,128)(2,1)S(1)} copy-done((bf16[12,6,25,256]{3,2,1,0:T(8,128)(2,1)S(1)}, bf16[12,6,25,256]{3,2,1,0:T(8,128)(2,1)}, u32[]{:S(2)}) %copy-start.4) | copy-done | bytes 921624
  24.9 0.0 copy-start.5
  24.9 0.9 %copy-done.5 = f32[12,6,256]{2,1,0:T(8,128)S(1)} copy-done((f32[12,6,256]{2,1,0:T(8,128)S(1)}, f32[12,6,256]{2,1,0:T(8,128)}, u32[]{:S(2)}) %copy-start.5) | copy-done | bytes 73752
  25.8 0.0 copy-start.6
  25.8 0.0 copy-start.7
  25.8 4.2 %pre.1 = (f32[72,25,256]{2,1,0:T(8,128)S(1)}, bf16[72,32,256]{2,1,0:T(8,128)(2,1)S(1)}, bf16[12,4,128,256]{3,2,1,0:T(8,128)(2,1)S(1)}) custom-call(bf16[12,4,256,128]{3,2,1,0:T(8,128)(2,1)S(1)} %copy-done.3, bf16[12,6,25,256]{3,2,1,0:T(8,128)(2,1)S(1)} %copy-done.4, f32[12,6,256]{2,1,0:T(8,128)S(1)} %copy-done.5, f32[25,16]{1,0:T(8,128)S(1)} %copy.17.table_ref), custom_call_target="tpu_custom_call" | custom-call | flops 2000000000 | bytes 8000000 | tf_op jit(solution)/shard_map/pre/pallas_call | solution.py:258
  30.0 0.0 collective-permute-done.6.refs_3_
  30.0 0.0 collective-permute-done.7.refs_4_
  30.0 0.9 %collective-permute-done.8.refs_5_ = bf16[4,128,128]{2,1,0:T(8,128)(2,1)S(1)} collective-permute-done((bf16[4,128,128]{2,1,0:T(8,128)(2,1)S(1)}, bf16[4,128,128]{2,1,0:T(8,128)(2,1)S(1)}, u32[]{:S(2)}, u32[]{:S(2)}) %collective-permute-start.8) | collective-permute-done | bytes 131104 | tf_op jit(solution)/shard_map/ppermute | solution.py:212
  30.9 0.0 collective-permute-done.9.refs_6_
  30.9 0.0 collective-permute-done.10.refs_7_
  30.9 0.0 copy-done.2
  30.9 0.0 copy-done.6
  30.9 0.0 copy-done.7
  30.9 4.4 %density.1 = (f32[12,256]{1,0:T(8,128)}, f32[32,128]{1,0:T(8,128)S(1)}) custom-call(s32[1]{0:T(128)S(6)} %copy.19.start_ref, s32[1,12]{1,0:T(1,128)S(1)} %copy-done.7, s32[1,12]{1,0:T(1,128)S(1)} %copy-done.2, s32[1,128]{1,0:T(1,128)S(1)} %reshape.9.atom_ref, bf16[12,4,128,256]{3,2,1,0:T(8,128)(2,1)S(1)} %get-tuple-element.22.phit_ref, ...), custom_call_target="tpu_custom_call" | custom-call | flops 2000000000 | bytes 6000000 | tf_op jit(solution)/shard_map/density/pallas_call | solution.py:276
  35.4 0.4 collective-permute-start.11
  35.7 0.8 %collective-permute-done.11 = f32[32,128]{1,0:T(8,128)S(1)} collective-permute-done((f32[32,128]{1,0:T(8,128)S(1)}, f32[32,128]{1,0:T(8,128)S(1)}, u32[]{:S(2)}, u32[]{:S(2)}) %collective-permute-start.11) | collective-permute-done | bytes 16416 | tf_op jit(solution)/shard_map/ppermute | solution.py:212
  36.6 1.5 %collective-permute-start.14 = (f32[2,32,128]{2,1,0:T(8,128)S(1)}, f32[2,32,128]{2,1,0:T(8,128)S(1)}, u32[]{:S(2)}, u32[]{:S(2)}) collective-permute-start(f32[2,32,128]{2,1,0:T(8,128)S(1)} %pad_maximum_fusion.refs_0_), channel_id=1, source_target_pairs={{0,6},{1,7},{2,4},{3,5},{4,2},{5,3},{6,0},{7,1},{8,14},{9,15},{10,... | collective-permute-start | bytes 98312 | tf_op jit(solution)/shard_map/ppermute | solution.py:212
  38.1 0.3 collective-permute-start.13
  38.4 1.7 %collective-permute-start.12 = (f32[2,32,128]{2,1,0:T(8,128)S(1)}, f32[2,32,128]{2,1,0:T(8,128)S(1)}, u32[]{:S(2)}, u32[]{:S(2)}) collective-permute-start(f32[2,32,128]{2,1,0:T(8,128)S(1)} %pad_maximum_fusion.refs_0_), channel_id=1, source_target_pairs={{0,2},{1,3},{2,0},{3,1},{4,6},{5,7},{6,4},{7,5},{8,10},{9,11},{10,... | collective-permute-start | bytes 98312 | tf_op jit(solution)/shard_map/ppermute | solution.py:212
  40.1 1.4 %collective-permute-done.14.refs_3_ = f32[2,32,128]{2,1,0:T(8,128)S(1)} collective-permute-done((f32[2,32,128]{2,1,0:T(8,128)S(1)}, f32[2,32,128]{2,1,0:T(8,128)S(1)}, u32[]{:S(2)}, u32[]{:S(2)}) %collective-permute-start.14) | collective-permute-done | bytes 32800 | tf_op jit(solution)/shard_map/ppermute | solution.py:212
  41.4 0.6 %collective-permute-done.13.refs_2_ = f32[2,32,128]{2,1,0:T(8,128)S(1)} collective-permute-done((f32[2,32,128]{2,1,0:T(8,128)S(1)}, f32[2,32,128]{2,1,0:T(8,128)S(1)}, u32[]{:S(2)}, u32[]{:S(2)}) %collective-permute-start.13) | collective-permute-done | bytes 32800 | tf_op jit(solution)/shard_map/ppermute | solution.py:212
  42.0 0.3 collective-permute-done.12.refs_1_
  42.3 0.4 scatter.1
  42.6 1.9 %collective-permute-start.15 = (f32[32,256]{1,0:T(8,128)S(1)}, f32[32,256]{1,0:T(8,128)S(1)}, u32[]{:S(2)}, u32[]{:S(2)}) collective-permute-start(f32[32,256]{1,0:T(8,128)S(1)} %get-tuple-element.35), channel_id=1, source_target_pairs={{0,8},{8,0},{16,24},{24,16},{1,9},{9,1},{17,25},{25,17},{2,10},{10... | collective-permute-start | bytes 98312 | tf_op jit(solution)/shard_map/ppermute | solution.py:212
  44.5 2.5 %collective-permute-start.16 = (f32[32,256]{1,0:T(8,128)S(1)}, f32[32,256]{1,0:T(8,128)S(1)}, u32[]{:S(2)}, u32[]{:S(2)}) collective-permute-start(f32[32,256]{1,0:T(8,128)S(1)} %get-tuple-element.36), channel_id=1, source_target_pairs={{0,24},{8,16},{16,8},{24,0},{1,25},{9,17},{17,9},{25,1},{2,26},{10... | collective-permute-start | bytes 98312 | tf_op jit(solution)/shard_map/ppermute | solution.py:212
  47.0 0.1 collective-permute-start.17
  47.1 0.0 collective-permute-done.15.near_a_ref
  47.1 3.1 %collective-permute-done.16.near_b_ref = f32[32,256]{1,0:T(8,128)S(1)} collective-permute-done((f32[32,256]{1,0:T(8,128)S(1)}, f32[32,256]{1,0:T(8,128)S(1)}, u32[]{:S(2)}, u32[]{:S(2)}) %collective-permute-start.16) | collective-permute-done | bytes 32800 | tf_op jit(solution)/shard_map/ppermute | solution.py:212
  50.2 1.9 %collective-permute-done.17.fa_ref.fb_ref = f32[32,256]{1,0:T(8,128)S(1)} collective-permute-done((f32[32,256]{1,0:T(8,128)S(1)}, f32[32,256]{1,0:T(8,128)S(1)}, u32[]{:S(2)}, u32[]{:S(2)}) %collective-permute-start.17) | collective-permute-done | bytes 32800 | tf_op jit(solution)/shard_map/ppermute | solution.py:212
  52.2 1.9 %potential.1 = (f32[16,25]{1,0:T(8,128)}, f32[12,256]{1,0:T(8,128)}) custom-call(s32[1,12]{1,0:T(1,128)S(1)} %copy-done.2, f32[32,384]{1,0:T(8,128)S(1)} %get-tuple-element.34.own_ref, f32[32,256]{1,0:T(8,128)S(1)} %collective-permute-done.15.near_a_ref, f32[32,256]{1,0:T(8,128)S(1)} %collective-permute-done.16.near_b_ref, ...), custom_call_target="tpu_custom_call" | custom-call | tf_op jit(solution)/shard_map/potential/pallas_call | solution.py:317
  (2 shorter events, 0.0 us)
Async XLA Ops:
  0.6 1.5 %collective-permute-start = (s32[1]{0:T(128)}, s32[1]{0:T(128)}, u32[]{:S(2)}, u32[]{:S(2)}) collective-permute-start(s32[1]{0:T(128)} %param.14), channel_id=1, source_target_pairs={{0,1},{1,0},{2,3},{3,2},{4,5},{5,4},{6,7},{7,6},{8,9},{9,8},{10,11... | collective-permute-start | bytes 20 | tf_op jit(solution)/shard_map/ppermute | solution.py:212
  2.8 5.2 %collective-permute-start.3 = (s32[2]{0:T(128)S(1)}, s32[2]{0:T(128)S(1)}, u32[]{:S(2)}, u32[]{:S(2)}) collective-permute-start(s32[2]{0:T(128)S(1)} %pad_add_fusion), channel_id=1, source_target_pairs={{0,6},{1,7},{2,4},{3,5},{4,2},{5,3},{6,0},{7,1},{8,14},{9,15},{10,... | collective-permute-start | bytes 32 | tf_op jit(solution)/shard_map/ppermute | solution.py:212
  6.5 3.5 %collective-permute-start.2 = (s32[2]{0:T(128)S(1)}, s32[2]{0:T(128)S(1)}, u32[]{:S(2)}, u32[]{:S(2)}) collective-permute-start(s32[2]{0:T(128)S(1)} %pad_add_fusion), channel_id=1, source_target_pairs={{0,4},{1,5},{2,6},{3,7},{4,0},{5,1},{6,2},{7,3},{8,12},{9,13},{10,... | collective-permute-start | bytes 32 | tf_op jit(solution)/shard_map/ppermute | solution.py:212
  7.0 3.5 %collective-permute-start.1 = (s32[2]{0:T(128)S(1)}, s32[2]{0:T(128)S(1)}, u32[]{:S(2)}, u32[]{:S(2)}) collective-permute-start(s32[2]{0:T(128)S(1)} %pad_add_fusion), channel_id=1, source_target_pairs={{0,2},{1,3},{2,0},{3,1},{4,6},{5,7},{6,4},{7,5},{8,10},{9,11},{10,... | collective-permute-start | bytes 32 | tf_op jit(solution)/shard_map/ppermute | solution.py:212
  11.2 1.0 %copy-start = (bf16[3,4,128,128]{3,2,1,0:T(8,128)(2,1)S(1)}, bf16[3,4,128,128]{3,2,1,0:T(8,128)(2,1)}, u32[]{:S(2)}) copy-start(bf16[3,4,128,128]{3,2,1,0:T(8,128)(2,1)} %rows_ref.1) | copy-start | bytes 1179652
  12.3 0.7 %copy-start.1 = (s32[3,4]{1,0:T(4,128)S(1)}, s32[3,4]{1,0:T(4,128)}, u32[]{:S(2)}) copy-start(s32[3,4]{1,0:T(4,128)} %mask_ref.1) | copy-start | bytes 148
  13.7 5.3 %collective-permute-start.4 = (bf16[4,128,128]{2,1,0:T(8,128)(2,1)S(1)}, bf16[4,128,128]{2,1,0:T(8,128)(2,1)S(1)}, u32[]{:S(2)}, u32[]{:S(2)}) collective-permute-start(bf16[4,128,128]{2,1,0:T(8,128)(2,1)S(1)} %get-tuple-element.25), channel_id=1, source_target_pairs={{0,1},{1,0},{2,3},{3,2},{4,5},{5,4},{6,7},{7,6},{8,9},{9,8},{10,11... | collective-permute-start | bytes 393224 | tf_op jit(solution)/shard_map/ppermute | solution.py:212
  13.8 6.7 %collective-permute-start.5 = (bf16[4,128,128]{2,1,0:T(8,128)(2,1)S(1)}, bf16[4,128,128]{2,1,0:T(8,128)(2,1)S(1)}, u32[]{:S(2)}, u32[]{:S(2)}) collective-permute-start(bf16[4,128,128]{2,1,0:T(8,128)(2,1)S(1)} %get-tuple-element.26), channel_id=1, source_target_pairs={{0,2},{1,3},{2,0},{3,1},{4,6},{5,7},{6,4},{7,5},{8,10},{9,11},{10,... | collective-permute-start | bytes 393224 | tf_op jit(solution)/shard_map/ppermute | solution.py:212
  15.6 14.3 %collective-permute-start.6 = (bf16[4,128,128]{2,1,0:T(8,128)(2,1)S(1)}, bf16[4,128,128]{2,1,0:T(8,128)(2,1)S(1)}, u32[]{:S(2)}, u32[]{:S(2)}) collective-permute-start(bf16[4,128,128]{2,1,0:T(8,128)(2,1)S(1)} %get-tuple-element.27), channel_id=1, source_target_pairs={{0,3},{1,2},{2,1},{3,0},{4,7},{5,6},{6,5},{7,4},{8,11},{9,10},{10,... | collective-permute-start | bytes 393224 | tf_op jit(solution)/shard_map/ppermute | solution.py:212
  17.3 12.7 %collective-permute-start.7 = (bf16[4,128,128]{2,1,0:T(8,128)(2,1)S(1)}, bf16[4,128,128]{2,1,0:T(8,128)(2,1)S(1)}, u32[]{:S(2)}, u32[]{:S(2)}) collective-permute-start(bf16[4,128,128]{2,1,0:T(8,128)(2,1)S(1)} %get-tuple-element.28), channel_id=1, source_target_pairs={{0,4},{1,5},{2,6},{3,7},{4,0},{5,1},{6,2},{7,3},{8,12},{9,13},{10,... | collective-permute-start | bytes 393224 | tf_op jit(solution)/shard_map/ppermute | solution.py:212
  18.8 12.1 %collective-permute-start.8 = (bf16[4,128,128]{2,1,0:T(8,128)(2,1)S(1)}, bf16[4,128,128]{2,1,0:T(8,128)(2,1)S(1)}, u32[]{:S(2)}, u32[]{:S(2)}) collective-permute-start(bf16[4,128,128]{2,1,0:T(8,128)(2,1)S(1)} %get-tuple-element.29), channel_id=1, source_target_pairs={{0,5},{1,4},{2,7},{3,6},{4,1},{5,0},{6,3},{7,2},{8,13},{9,12},{10,... | collective-permute-start | bytes 393224 | tf_op jit(solution)/shard_map/ppermute | solution.py:212
  19.0 11.9 %collective-permute-start.9 = (bf16[4,128,128]{2,1,0:T(8,128)(2,1)S(1)}, bf16[4,128,128]{2,1,0:T(8,128)(2,1)S(1)}, u32[]{:S(2)}, u32[]{:S(2)}) collective-permute-start(bf16[4,128,128]{2,1,0:T(8,128)(2,1)S(1)} %get-tuple-element.30), channel_id=1, source_target_pairs={{0,6},{1,7},{2,4},{3,5},{4,2},{5,3},{6,0},{7,1},{8,14},{9,15},{10,... | collective-permute-start | bytes 393224 | tf_op jit(solution)/shard_map/ppermute | solution.py:212
  20.5 10.4 %copy-start.2 = (s32[1,12]{1,0:T(1,128)S(1)}, s32[1,12]{1,0:T(1,128)}, u32[]{:S(2)}) copy-start(s32[1,12]{1,0:T(1,128)} %size_ref.3) | copy-start | bytes 148
  20.5 10.4 %collective-permute-start.10 = (bf16[4,128,128]{2,1,0:T(8,128)(2,1)S(1)}, bf16[4,128,128]{2,1,0:T(8,128)(2,1)S(1)}, u32[]{:S(2)}, u32[]{:S(2)}) collective-permute-start(bf16[4,128,128]{2,1,0:T(8,128)(2,1)S(1)} %get-tuple-element.31), channel_id=1, source_target_pairs={{0,7},{1,6},{2,5},{3,4},{4,3},{5,2},{6,1},{7,0},{8,15},{9,14},{10,... | collective-permute-start | bytes 393224 | tf_op jit(solution)/shard_map/ppermute | solution.py:212
  21.7 1.9 %copy-start.3 = (bf16[12,4,256,128]{3,2,1,0:T(8,128)(2,1)S(1)}, bf16[12,4,256,128]{3,2,1,0:T(8,128)(2,1)}, u32[]{:S(2)}) copy-start(bf16[12,4,256,128]{3,2,1,0:T(8,128)(2,1)} %basis_ref.1) | copy-start | bytes 9437188
  23.6 1.3 %copy-start.4 = (bf16[12,6,25,256]{3,2,1,0:T(8,128)(2,1)S(1)}, bf16[12,6,25,256]{3,2,1,0:T(8,128)(2,1)}, u32[]{:S(2)}) copy-start(bf16[12,6,25,256]{3,2,1,0:T(8,128)(2,1)} %harm_ref.1) | copy-start | bytes 2764804
  24.9 0.9 %copy-start.5 = (f32[12,6,256]{2,1,0:T(8,128)S(1)}, f32[12,6,256]{2,1,0:T(8,128)}, u32[]{:S(2)}) copy-start(f32[12,6,256]{2,1,0:T(8,128)} %radius_ref.1) | copy-start | bytes 221188
  25.8 5.2 %copy-start.6 = (f32[12,6,256]{2,1,0:T(8,128)S(1)}, f32[12,6,256]{2,1,0:T(8,128)}, u32[]{:S(2)}) copy-start(f32[12,6,256]{2,1,0:T(8,128)} %part_ref.1) | copy-start | bytes 221188
  25.8 5.2 %copy-start.7 = (s32[1,12]{1,0:T(1,128)S(1)}, s32[1,12]{1,0:T(1,128)}, u32[]{:S(2)}) copy-start(s32[1,12]{1,0:T(1,128)} %offset_ref.1) | copy-start | bytes 148
  35.4 1.2 %collective-permute-start.11 = (f32[32,128]{1,0:T(8,128)S(1)}, f32[32,128]{1,0:T(8,128)S(1)}, u32[]{:S(2)}, u32[]{:S(2)}) collective-permute-start(f32[32,128]{1,0:T(8,128)S(1)} %get-tuple-element.33), channel_id=1, source_target_pairs={{0,1},{1,0},{2,3},{3,2},{4,5},{5,4},{6,7},{7,6},{8,9},{9,8},{10,11... | collective-permute-start | bytes 49160 | tf_op jit(solution)/shard_map/ppermute | solution.py:212
  36.6 4.9 %collective-permute-start.14 = (f32[2,32,128]{2,1,0:T(8,128)S(1)}, f32[2,32,128]{2,1,0:T(8,128)S(1)}, u32[]{:S(2)}, u32[]{:S(2)}) collective-permute-start(f32[2,32,128]{2,1,0:T(8,128)S(1)} %pad_maximum_fusion.refs_0_), channel_id=1, source_target_pairs={{0,6},{1,7},{2,4},{3,5},{4,2},{5,3},{6,0},{7,1},{8,14},{9,15},{10,... | collective-permute-start | bytes 98312 | tf_op jit(solution)/shard_map/ppermute | solution.py:212
  38.1 3.9 %collective-permute-start.13 = (f32[2,32,128]{2,1,0:T(8,128)S(1)}, f32[2,32,128]{2,1,0:T(8,128)S(1)}, u32[]{:S(2)}, u32[]{:S(2)}) collective-permute-start(f32[2,32,128]{2,1,0:T(8,128)S(1)} %pad_maximum_fusion.refs_0_), channel_id=1, source_target_pairs={{0,4},{1,5},{2,6},{3,7},{4,0},{5,1},{6,2},{7,3},{8,12},{9,13},{10,... | collective-permute-start | bytes 98312 | tf_op jit(solution)/shard_map/ppermute | solution.py:212
  38.4 3.9 %collective-permute-start.12 = (f32[2,32,128]{2,1,0:T(8,128)S(1)}, f32[2,32,128]{2,1,0:T(8,128)S(1)}, u32[]{:S(2)}, u32[]{:S(2)}) collective-permute-start(f32[2,32,128]{2,1,0:T(8,128)S(1)} %pad_maximum_fusion.refs_0_), channel_id=1, source_target_pairs={{0,2},{1,3},{2,0},{3,1},{4,6},{5,7},{6,4},{7,5},{8,10},{9,11},{10,... | collective-permute-start | bytes 98312 | tf_op jit(solution)/shard_map/ppermute | solution.py:212
  42.6 4.5 %collective-permute-start.15 = (f32[32,256]{1,0:T(8,128)S(1)}, f32[32,256]{1,0:T(8,128)S(1)}, u32[]{:S(2)}, u32[]{:S(2)}) collective-permute-start(f32[32,256]{1,0:T(8,128)S(1)} %get-tuple-element.35), channel_id=1, source_target_pairs={{0,8},{8,0},{16,24},{24,16},{1,9},{9,1},{17,25},{25,17},{2,10},{10... | collective-permute-start | bytes 98312 | tf_op jit(solution)/shard_map/ppermute | solution.py:212
  44.5 5.7 %collective-permute-start.16 = (f32[32,256]{1,0:T(8,128)S(1)}, f32[32,256]{1,0:T(8,128)S(1)}, u32[]{:S(2)}, u32[]{:S(2)}) collective-permute-start(f32[32,256]{1,0:T(8,128)S(1)} %get-tuple-element.36), channel_id=1, source_target_pairs={{0,24},{8,16},{16,8},{24,0},{1,25},{9,17},{17,9},{25,1},{2,26},{10... | collective-permute-start | bytes 98312 | tf_op jit(solution)/shard_map/ppermute | solution.py:212
  47.0 5.2 %collective-permute-start.17 = (f32[32,256]{1,0:T(8,128)S(1)}, f32[32,256]{1,0:T(8,128)S(1)}, u32[]{:S(2)}, u32[]{:S(2)}) collective-permute-start(f32[32,256]{1,0:T(8,128)S(1)} %get-tuple-element.37), channel_id=1, source_target_pairs={{0,16},{8,24},{16,0},{24,8},{1,17},{9,25},{17,1},{25,9},{2,18},{10... | collective-permute-start | bytes 98312 | tf_op jit(solution)/shard_map/ppermute | solution.py:212

commit v4 on v3

--- a/solution.py
+++ b/solution.py
@@ -6,6 +6,8 @@
 from jax.experimental.pallas import tpu as pltpu
 from jax.sharding import PartitionSpec as P
 
+EVEN_OWNERS = (0, 1, 4, 3, 2, 5, 6, 7)
+ODD_OWNERS = (0, 1, 2, 5, 4, 3, 6, 7)
 LANES = 128
 ROWS = 32
 SLOT = 8
@@ -13,7 +15,8 @@
 NN = (((1,), (0,)), ((), ()))
 VMEM = pl.BlockSpec(memory_space=pltpu.VMEM)
 SMEM = pl.BlockSpec(memory_space=pltpu.SMEM)
-ANY = pl.BlockSpec(memory_space=pl.ANY)
+HBM = pl.BlockSpec(memory_space=pltpu.HBM)
+WIDE = pltpu.CompilerParams(vmem_limit_bytes=50 * 1024 * 1024)
 PARAMS = pltpu.CompilerParams(vmem_limit_bytes=16 * 1024 * 1024)
 
 
@@ -40,28 +43,46 @@
     return jnp.where(distance < 1.0, inner, jnp.where(distance < 2.0, outer, 0.0))
 
 
-def select_kernel(dev_count, starts_ref, mask_ref, rows_ref, *outs):
-    me = lax.axis_index("dev")
-    stored, band = rows_ref.shape[0], rows_ref.shape[1]
-    for m, out in enumerate(outs):
-        start = starts_ref[m]
-        ahead = lax.rem(me - start + stored * dev_count, dev_count)
-        held = lax.rem(start + ahead, stored * dev_count) // dev_count
+def mask_kernel(mask_ref, rows_ref, out_ref, mask, rows, sems):
+    stored, band = rows_ref.shape[:2]
+    fetch = pltpu.make_async_copy(mask_ref, mask, sems.at[stored])
+    copies = [
+        pltpu.make_async_copy(rows_ref.at[t], rows.at[t], sems.at[t]) for t in range(stored)
+    ]
+    fetch.start()
+    for copy in copies:
+        copy.start()
+    fetch.wait()
+    factors = mask[...].astype(jnp.float32)
+    for t, copy in enumerate(copies):
+        copy.wait()
         for k in range(band):
-            factor = mask_ref[held, k].astype(jnp.float32)
-            out[k] = (rows_ref[held, k].astype(jnp.float32) * factor).astype(jnp.bfloat16)
-
-
-def pre_kernel(basis_ref, harm_ref, radius_ref, table_ref, g_ref, hpad_ref, phit_ref, basis, sem):
+            factor = factors[t : t + 1, k : k + 1]
+            out_ref[t, k] = (rows[t, k].astype(jnp.float32) * factor).astype(jnp.bfloat16)
+
+
+def field_kernel(
+    after_hbm, near_ref, table_hbm, radius_hbm, harm_hbm,
+    g_ref, hpad_ref, atom_ref, table_ref, radius_ref, harm_ref, sems,
+):
     batches, near, comps, points = harm_ref.shape
-    near_blocks = basis.shape[1]
-    knots = table_ref.shape[1]
-    copy = pltpu.make_async_copy(basis_ref, basis, sem)
-    copy.start()
+    knots = table_ref.shape[0]
+    moves = ((table_hbm, table_ref), (radius_hbm, radius_ref), (harm_hbm, harm_ref))
+    copies = [pltpu.make_async_copy(a, b, sems.at[n]) for n, (a, b) in enumerate(moves)]
+    for copy in copies:
+        copy.start()
+    lane = lax.broadcasted_iota(jnp.int32, atom_ref.shape, 1)
+    atom = jnp.full(atom_ref.shape, -1, jnp.int32)
+    for b in range(batches):
+        for i in range(near):
+            atom = jnp.where(lane == b * SLOT + i, near_ref[i, b], atom)
+    atom_ref[...] = atom
     hpad_ref[...] = jnp.zeros(hpad_ref.shape, hpad_ref.dtype)
-    r_hi, r_lo = split2(table_ref[...])
+    knot = lax.broadcasted_iota(jnp.int32, (knots, points), 0).astype(jnp.float32)
+    for copy in copies:
+        copy.wait()
+    r_hi, r_lo = split2(table_ref[...].T)
     coeffs = jnp.concatenate([r_hi, r_hi, r_lo], axis=1)
-    knot = lax.broadcasted_iota(jnp.int32, (knots, points), 0).astype(jnp.float32)
 
     def body(b, carry):
         rows = radius_ref[b]
@@ -75,26 +96,52 @@
         return carry
 
     lax.fori_loop(0, batches, body, 0)
-    copy.wait()
+
+
+def turn_kernel(after_hbm, basis_hbm, part_hbm, phit_ref, part_ref, basis, sems):
+    batches, near_blocks = basis.shape[:2]
+    halves = [pl.ds(0, batches // 2), pl.ds(batches // 2, batches - batches // 2)]
+    copies = [
+        pltpu.make_async_copy(basis_hbm.at[half], basis.at[half], sems.at[n])
+        for n, half in enumerate(halves)
+    ]
+    copies.append(pltpu.make_async_copy(part_hbm, part_ref, sems.at[2]))
+    for copy in copies:
+        copy.start()
 
     def turn(b, carry):
         for j in range(near_blocks):
             phit_ref[b, j] = basis[b, j].T
         return carry
 
-    lax.fori_loop(0, batches, turn, 0)
+    copies[0].wait()
+    lax.fori_loop(0, batches // 2, turn, 0)
+    copies[1].wait()
+    lax.fori_loop(batches // 2, batches, turn, 0)
+    copies[2].wait()
 
 
 def density_kernel(start_ref, offset_ref, size_ref, atom_ref, phit_ref, part_ref, hpad_ref, *refs):
     dens_ref, terms_ref, window_ref, w_ref = refs[-4:]
     pieces = refs[:-4]
-    owners = len(pieces)
+    owners = window_ref.shape[0]
     batches, near_blocks, width, points = phit_ref.shape
     near = part_ref.shape[1]
-    me = lax.axis_index("dev")
-    for m, piece in enumerate(pieces):
-        spot = lax.rem(lax.bitwise_xor(me, m) - start_ref[0] + 3 * owners, owners)
-        window_ref[spot] = piece[...]
+    if len(pieces) == owners:
+        me = lax.axis_index("dev")
+        odd = lax.rem(me, 2)
+        held = [
+            (piece, lax.bitwise_xor(me, jnp.where(odd == 1, b, a)))
+            for piece, a, b in zip(pieces, EVEN_OWNERS, ODD_OWNERS)
+        ]
+    else:
+        held = [(pieces[0].at[owner], owner) for owner in range(owners)]
+    stored = held[0][0].shape[0]
+    start = start_ref[0]
+    for piece, owner in held:
+        ahead = lax.rem(owner - start + stored * owners, owners)
+        row = lax.rem(start + ahead, stored * owners) // owners
+        window_ref[ahead] = piece[row]
     w_ref[...] = jnp.zeros(w_ref.shape, w_ref.dtype)
     lane = lax.broadcasted_iota(jnp.int32, (1, points), 1)
     zero = jnp.zeros((width, width), jnp.bfloat16)
@@ -212,6 +259,11 @@
     return lax.ppermute(value, axis, [(i, i ^ m) for i in range(lax.axis_size(axis))])
 
 
+def turned(value, even, odd):
+    count = lax.axis_size("dev")
+    return lax.ppermute(value, "dev", [(i, i ^ (odd if i % 2 else even)) for i in range(count)])
+
+
 def shifted(value, axis, step):
     count = lax.axis_size(axis)
     return lax.ppermute(value, axis, [(i, (i + step) % count) for i in range(count)])
@@ -239,39 +291,68 @@
     atoms = mine * dev_count
     f32, bf16 = jnp.float32, jnp.bfloat16
 
-    pair = jnp.concatenate([window_start, crossed(window_start, "dev", 1)])
-    starts = jnp.concatenate([pair] + [crossed(pair, "dev", m) for m in range(2, dev_count, 2)])
-    served = pl.pallas_call(
-        functools.partial(select_kernel, dev_count),
-        out_shape=tuple(
-            jax.ShapeDtypeStruct((band, width, width), bf16) for _ in range(dev_count)
-        ),
-        in_specs=[SMEM, SMEM, VMEM],
-        out_specs=(VMEM,) * dev_count,
-        compiler_params=PARAMS,
-        name="select",
-    )(starts, block_mask, density_rows)
-    order = sorted(range(1, dev_count), key=lambda m: -bin(m).count("1"))
-    pieces = {m: crossed(served[m], "dev", m) for m in order}
-    pieces[0] = served[0]
-
-    g, hpad, phit = pl.pallas_call(
-        pre_kernel,
+    masked = pl.pallas_call(
+        mask_kernel,
+        out_shape=jax.ShapeDtypeStruct(density_rows.shape, bf16),
+        in_specs=[HBM, HBM],
+        out_specs=VMEM,
+        scratch_shapes=[
+            pltpu.VMEM(block_mask.shape, jnp.int32),
+            pltpu.VMEM(density_rows.shape, bf16),
+            pltpu.SemaphoreType.DMA((blocks_dev + 1,)),
+        ],
+        compiler_params=pltpu.CompilerParams(vmem_limit_bytes=63 * 1024 * 1024),
+        name="mask",
+    )(block_mask, density_rows)
+    g, hpad, atom_rows = pl.pallas_call(
+        field_kernel,
         out_shape=(
             jax.ShapeDtypeStruct((batches * near, comps, points), f32),
             jax.ShapeDtypeStruct((batches * near, ROWS, points), bf16),
-            jax.ShapeDtypeStruct((batches, near_blocks, width, points), bf16),
+            jax.ShapeDtypeStruct((1, LANES), jnp.int32),
         ),
-        in_specs=[ANY] + [VMEM] * 3,
+        in_specs=[HBM, SMEM] + [HBM] * 3,
         out_specs=(VMEM,) * 3,
-        scratch_shapes=[pltpu.VMEM(basis_values.shape, bf16), pltpu.SemaphoreType.DMA],
-        compiler_params=PARAMS,
+        scratch_shapes=[
+            pltpu.VMEM(radial_table.shape[::-1], f32),
+            pltpu.VMEM(radius.shape, f32),
+            pltpu.VMEM(harmonics.shape, bf16),
+            pltpu.SemaphoreType.DMA((3,)),
+        ],
+        compiler_params=WIDE,
         cost_estimate=pl.CostEstimate(flops=2_000_000_000, bytes_accessed=8_000_000, transcendentals=0),
-        name="pre",
-    )(basis_values, harmonics, radius, radial_table)
-
-    atom_rows = jnp.pad(atom_near, ((0, LANES // SLOT - batches), (0, SLOT - near)), constant_values=-1)
-    atom_rows = atom_rows.reshape(1, LANES)
+        name="field",
+    )(masked, atom_near.T, radial_table.T, radius, harmonics)
+
+    def turned_basis(after):
+        return pl.pallas_call(
+            turn_kernel,
+            out_shape=(
+                jax.ShapeDtypeStruct((batches, near_blocks, width, points), bf16),
+                jax.ShapeDtypeStruct(partition.shape, f32),
+            ),
+            in_specs=[HBM] * 3,
+            out_specs=(VMEM,) * 2,
+            scratch_shapes=[pltpu.VMEM(basis_values.shape, bf16), pltpu.SemaphoreType.DMA((3,))],
+            compiler_params=WIDE,
+            cost_estimate=pl.CostEstimate(
+                flops=2_000_000_000, bytes_accessed=8_000_000, transcendentals=0
+            ),
+            name="turn",
+        )(after, basis_values, partition)
+
+    if dev_count == 8:
+        first = turned(masked, 4, 2)
+        second = turned(masked, 2, 4)
+        first, g = lax.optimization_barrier((first, g))
+        third = turned(first, 2, 4)
+        phit, weights = turned_basis(first)
+        second, phit = lax.optimization_barrier((second, phit))
+        sent = (masked, first, second, third)
+        pieces = [piece for value in sent for piece in (value, crossed(value, "dev", 1))]
+    else:
+        phit, weights = turned_basis(masked)
+        pieces = [lax.all_gather(masked, "dev", axis=0)]
 
     density, terms = pl.pallas_call(
         density_kernel,
@@ -279,7 +360,7 @@
             jax.ShapeDtypeStruct((batches, points), f32),
             jax.ShapeDtypeStruct((ROWS, LANES), f32),
         ),
-        in_specs=[SMEM] * 3 + [VMEM] * (4 + dev_count),
+        in_specs=[SMEM] * 3 + [VMEM] * (4 + len(pieces)),
         out_specs=(VMEM, VMEM),
         scratch_shapes=[
             pltpu.VMEM((dev_count, band, width, width), bf16),
@@ -289,8 +370,8 @@
         cost_estimate=pl.CostEstimate(flops=2_000_000_000, bytes_accessed=6_000_000, transcendentals=0),
         name="density",
     )(
-        window_start, batch_offsets, batch_sizes, atom_rows, phit, partition, hpad,
-        *[pieces[m] for m in range(dev_count)],
+        window_start, batch_offsets, batch_sizes, atom_rows, phit, weights, hpad,
+        *pieces,
     )
 
     both = jnp.stack([terms, crossed(terms, "dev", 1)])

time: 54.4 us -> 50 us (0.919)
  Pallas kernels: 11.6 us -> 17.3 us
  starting transfers between devices: 19.5 us -> 14.1 us
  local copies, waits for them, and re-layouts: 8.09 us -> 3.56 us
  other arithmetic: 0.69 us -> 0.01 us
  waiting for transfers between devices: 12.7 us -> 13.3 us
    ppermute x18 -> x11, starting transfers between devices: 19.5 us -> 8.6 us  [crossed(): lax.ppermute(value, axis, [(i, i ^ m) for i in range(lax.axis_size(axis))])]
    ppermute x0 -> x3, starting transfers between devices: none -> 5.46 us  [turned(): lax.ppermute(value, 'dev', [(i, i ^ (odd if i % 2 else even)) for i in ra...]
    pallas_call x2 -> x3, Pallas kernels: 4.97 us -> 10.1 us  [the longest x1 5.12 us: per_device(): pl.pallas_call(field_kernel, out_shape=(jax.ShapeDtypeStruct((batches * n...]
    unnamed x18 -> x16, local copies, waits for them, and re-layouts: 7.31 us -> 3.56 us
    ppermute x0 -> x3, waiting for transfers between devices: none -> 3.4 us  [turned(): lax.ppermute(value, 'dev', [(i, i ^ (odd if i % 2 else even)) for i in ra...]
    ppermute x18 -> x11, waiting for transfers between devices: 12.7 us -> 9.89 us  [crossed(): lax.ppermute(value, axis, [(i, i ^ m) for i in range(lax.axis_size(axis))])]
    concatenate x1 -> x0, other arithmetic: 0.68 us -> none  [per_device(): pair = jnp.concatenate([window_start, crossed(window_start, 'dev', 1)])]
    concatenate x1 -> x0, local copies, waits for them, and re-layouts: 0.68 us -> none  [per_device(): jnp.concatenate([pair] + [crossed(pair, 'dev', m) for m in range(2, dev_c...]
  transfers between devices with their start and end apart: 18 -> 14, of which waited for: 11 -> 8; matrix products, arithmetic and copies ran while one was open for 3% -> 0% of each run, Pallas kernels for 8% -> 16%
where the time goes in v4:
time: 50 us; the launch traced here: 49.7 us
  Pallas kernels  17.3 us (35%)
  starting transfers between devices  14.1 us (28%)
  waiting for transfers between devices  13.3 us (27%)
  local copies, waits for them, and re-layouts  3.56 us (7%)
  between operations  1.4 us (3%)
    ppermute x11, waiting for transfers between devices, crossed(): lax.ppermute(value, axis, [(i, i ^ m) for i in range(lax.axis_size(axis))])  9.89 us
    ppermute x11, starting transfers between devices, crossed(): lax.ppermute(value, axis, [(i, i ^ m) for i in range(lax.axis_size(axis))])  8.6 us
    ppermute x3, starting transfers between devices, turned(): lax.ppermute(value, 'dev', [(i, i ^ (odd if i % 2 else even)) for i in ra...  5.46 us
    pallas_call x1, Pallas kernels, per_device(): pl.pallas_call(field_kernel, out_shape=(jax.ShapeDtypeStruct((batches * n...  5.12 us
    pallas_call x1, Pallas kernels, per_device(): pl.pallas_call(density_kernel, out_shape=(jax.ShapeDtypeStruct((batches,...  5.01 us
    unnamed x16, local copies, waits for them, and re-layouts  3.56 us
    ppermute x3, waiting for transfers between devices, turned(): lax.ppermute(value, 'dev', [(i, i ^ (odd if i % 2 else even)) for i in ra...  3.4 us
    pallas_call x1, Pallas kernels, turned_basis(): pl.pallas_call(turn_kernel, out_shape=(jax.ShapeDtypeStruct((batches, nea...  2.9 us
  transfers between devices with their start and end apart: 14, of which 8 were waited for; matrix products, arithmetic and copies ran while one was open for 0% of the time, Pallas kernels for 16%

profile of v4, /device:TPU:0, one launch (start us, length us, event | category | flops | bytes accessed | tf_op | source)
XLA Modules:
  0.0 49.7 jit_solution(3645762548470054347)
XLA Ops:
  0.6 2.1 %mask.1.after_hbm.refs_0_ = bf16[3,4,128,128]{3,2,1,0:T(8,128)(2,1)} custom-call(s32[3,4]{1,0:T(4,128)} %mask_ref.1, bf16[3,4,128,128]{3,2,1,0:T(8,128)(2,1)} %rows_ref.1), custom_call_target="tpu_custom_call" | custom-call | tf_op jit(solution)/shard_map/mask/pallas_call | solution.py:294
  2.7 3.0 %collective-permute-start.1 = (bf16[3,4,128,128]{3,2,1,0:T(8,128)(2,1)}, bf16[3,4,128,128]{3,2,1,0:T(8,128)(2,1)S(1)}, u32[]{:S(2)}, u32[]{:S(2)}) collective-permute-start(bf16[3,4,128,128]{3,2,1,0:T(8,128)(2,1)} %mask.1.after_hbm.refs_0_), channel_id=1, source_target_pairs={{0,4},{1,3},{2,6},{3,1},{4,0},{5,7},{6,2},{7,5},{8,12},{9,11},{10,... | collective-permute-start | bytes 1179656 | tf_op jit(solution)/shard_map/ppermute | solution.py:264
  5.7 1.5 %collective-permute-start = (bf16[3,4,128,128]{3,2,1,0:T(8,128)(2,1)}, bf16[3,4,128,128]{3,2,1,0:T(8,128)(2,1)S(1)}, u32[]{:S(2)}, u32[]{:S(2)}) collective-permute-start(bf16[3,4,128,128]{3,2,1,0:T(8,128)(2,1)} %mask.1.after_hbm.refs_0_), channel_id=1, source_target_pairs={{0,2},{1,5},{2,0},{3,7},{4,6},{5,1},{6,4},{7,3},{8,10},{9,13},{10,... | collective-permute-start | bytes 1179656 | tf_op jit(solution)/shard_map/ppermute | solution.py:264
  7.2 0.0 copy-start.3
  7.2 1.3 %copy-done.3 = bf16[12,6,25,256]{3,2,1,0:T(8,128)(2,1)S(1)} copy-done((bf16[12,6,25,256]{3,2,1,0:T(8,128)(2,1)S(1)}, bf16[12,6,25,256]{3,2,1,0:T(8,128)(2,1)}, u32[]{:S(2)}) %copy-start.3) | copy-done | bytes 921624
  8.5 0.0 copy-start.4
  8.5 0.9 %copy-done.4 = f32[12,6,256]{2,1,0:T(8,128)S(1)} copy-done((f32[12,6,256]{2,1,0:T(8,128)S(1)}, f32[12,6,256]{2,1,0:T(8,128)}, u32[]{:S(2)}) %copy-start.4) | copy-done | bytes 73752
  9.4 0.0 copy-start.6
  9.4 0.7 %copy-done.6 = f32[25,16]{0,1:T(8,128)S(1)} copy-done((f32[25,16]{0,1:T(8,128)S(1)}, f32[25,16]{0,1:T(8,128)}, u32[]{:S(2)}) %copy-start.6) | copy-done | bytes 1624
  10.1 0.0 copy-start.7
  10.1 0.7 %copy-done.7 = s32[12,6]{0,1:T(8,128)S(1)} copy-done((s32[12,6]{0,1:T(8,128)S(1)}, s32[12,6]{0,1:T(8,128)}, u32[]{:S(2)}) %copy-start.7) | copy-done | bytes 312
  10.8 0.0 copy-start.5
  10.8 5.1 %field.1 = (f32[72,25,256]{2,1,0:T(8,128)}, bf16[72,32,256]{2,1,0:T(8,128)(2,1)S(1)}, s32[1,128]{1,0:T(1,128)S(1)}) custom-call(bf16[3,4,128,128]{3,2,1,0:T(8,128)(2,1)} %mask.1.after_hbm.refs_0_, s32[6,12]{1,0:T(8,128)S(1)} %bitcast.7, f32[16,25]{1,0:T(8,128)S(1)} %bitcast.6, f32[12,6,256]{2,1,0:T(8,128)S(1)} %copy-done.4, ...), custom_call_target="tpu_custom_call" | custom-call | flops 2000000000 | bytes 8000000 | tf_op jit(solution)/shard_map/field/pallas_call | solution.py:307
  15.9 0.0 collective-permute-done.1.after_hbm.refs_2_
  15.9 0.0 copy-start.1
  15.9 0.0 copy-start.2
  15.9 0.9 %collective-permute-start.5 = (bf16[3,4,128,128]{3,2,1,0:T(8,128)(2,1)S(1)}, bf16[3,4,128,128]{3,2,1,0:T(8,128)(2,1)S(1)}, u32[]{:S(2)}, u32[]{:S(2)}) collective-permute-start(bf16[3,4,128,128]{3,2,1,0:T(8,128)(2,1)S(1)} %collective-permute-done.1.after_hbm.refs_2_), channel_id=1, source_target_pairs={{0,2},{1,5},{2,0},{3,7},{4,6},{5,1},{6,4},{7,3},{8,10},{9,13},{10,... | collective-permute-start | bytes 1179656 | tf_op jit(solution)/shard_map/ppermute | solution.py:264
  16.9 0.0 collective-permute-start.2
  16.9 0.5 %collective-permute-start.3 = (bf16[3,4,128,128]{3,2,1,0:T(8,128)(2,1)S(1)}, bf16[3,4,128,128]{3,2,1,0:T(8,128)(2,1)S(1)}, u32[]{:S(2)}, u32[]{:S(2)}) collective-permute-start(bf16[3,4,128,128]{3,2,1,0:T(8,128)(2,1)S(1)} %collective-permute-done.1.after_hbm.refs_2_), channel_id=1, source_target_pairs={{0,1},{1,0},{2,3},{3,2},{4,5},{5,4},{6,7},{7,6},{8,9},{9,8},{10,11... | collective-permute-start | bytes 1179656 | tf_op jit(solution)/shard_map/ppermute | solution.py:259
  17.4 0.0 copy-done.5
  17.4 2.9 %turn.1 = (bf16[12,4,128,256]{3,2,1,0:T(8,128)(2,1)S(1)}, f32[12,6,256]{2,1,0:T(8,128)S(1)}) custom-call(bf16[3,4,128,128]{3,2,1,0:T(8,128)(2,1)S(1)} %collective-permute-done.1.after_hbm.refs_2_, bf16[12,4,256,128]{3,2,1,0:T(8,128)(2,1)} %basis_hbm.1, f32[12,6,256]{2,1,0:T(8,128)S(1)} %copy-done.5), custom_call_target="tpu_custom_call" | custom-call | flops 2000000000 | bytes 8000000 | tf_op jit(solution)/shard_map/turn/pallas_call | solution.py:328
  20.3 0.0 collective-permute-done.refs_4_
  20.3 0.1 collective-permute-start.4
  20.4 3.4 %collective-permute-done.5.refs_6_ = bf16[3,4,128,128]{3,2,1,0:T(8,128)(2,1)S(1)} collective-permute-done((bf16[3,4,128,128]{3,2,1,0:T(8,128)(2,1)S(1)}, bf16[3,4,128,128]{3,2,1,0:T(8,128)(2,1)S(1)}, u32[]{:S(2)}, u32[]{:S(2)}) %collective-permute-start.5) | collective-permute-done | bytes 393248 | tf_op jit(solution)/shard_map/ppermute | solution.py:264
  23.8 0.0 collective-permute-start.6
  24.4 0.0 collective-permute-done.2.refs_1_
  24.4 0.0 collective-permute-done.3.refs_3_
  24.5 0.0 collective-permute-done.4.refs_5_
  24.5 1.0 %collective-permute-done.6.refs_7_ = bf16[3,4,128,128]{3,2,1,0:T(8,128)(2,1)S(1)} collective-permute-done((bf16[3,4,128,128]{3,2,1,0:T(8,128)(2,1)S(1)}, bf16[3,4,128,128]{3,2,1,0:T(8,128)(2,1)S(1)}, u32[]{:S(2)}, u32[]{:S(2)}) %collective-permute-start.6) | collective-permute-done | bytes 393248 | tf_op jit(solution)/shard_map/ppermute | solution.py:259
  25.5 0.0 copy-done.1
  25.5 0.0 copy-done.2
  25.5 0.0 copy-start
  25.5 5.0 %density.1 = (f32[12,256]{1,0:T(8,128)}, f32[32,128]{1,0:T(8,128)S(1)}) custom-call(s32[1]{0:T(128)S(6)} %copy.14.start_ref, s32[1,12]{1,0:T(1,128)S(1)} %copy-done.2, s32[1,12]{1,0:T(1,128)S(1)} %copy-done.1, s32[1,128]{1,0:T(1,128)S(1)} %get-tuple-element.20.atom_ref, bf16[12,4,128,256]{3,2,1,0:T(8,128)(2,1)S(1)} %get-tuple-element.24.phit_ref, ...), custom_call_target="tpu_custom_call" | custom-call | flops 2000000000 | bytes 6000000 | tf_op jit(solution)/shard_map/density/pallas_call | solution.py:357
  30.5 0.1 collective-permute-start.7
  30.6 1.1 %collective-permute-done.7 = f32[32,128]{1,0:T(8,128)S(1)} collective-permute-done((f32[32,128]{1,0:T(8,128)S(1)}, f32[32,128]{1,0:T(8,128)S(1)}, u32[]{:S(2)}, u32[]{:S(2)}) %collective-permute-start.7) | collective-permute-done | bytes 16416 | tf_op jit(solution)/shard_map/ppermute | solution.py:259
  31.7 2.0 %collective-permute-start.10 = (f32[2,32,128]{2,1,0:T(8,128)S(1)}, f32[2,32,128]{2,1,0:T(8,128)S(1)}, u32[]{:S(2)}, u32[]{:S(2)}) collective-permute-start(f32[2,32,128]{2,1,0:T(8,128)S(1)} %pad_maximum_fusion.refs_0_), channel_id=1, source_target_pairs={{0,6},{1,7},{2,4},{3,5},{4,2},{5,3},{6,0},{7,1},{8,14},{9,15},{10,... | collective-permute-start | bytes 98312 | tf_op jit(solution)/shard_map/ppermute | solution.py:259
  33.7 0.4 collective-permute-start.9
  34.0 1.2 %collective-permute-start.8 = (f32[2,32,128]{2,1,0:T(8,128)S(1)}, f32[2,32,128]{2,1,0:T(8,128)S(1)}, u32[]{:S(2)}, u32[]{:S(2)}) collective-permute-start(f32[2,32,128]{2,1,0:T(8,128)S(1)} %pad_maximum_fusion.refs_0_), channel_id=1, source_target_pairs={{0,2},{1,3},{2,0},{3,1},{4,6},{5,7},{6,4},{7,5},{8,10},{9,11},{10,... | collective-permute-start | bytes 98312 | tf_op jit(solution)/shard_map/ppermute | solution.py:259
  35.2 1.4 %collective-permute-done.10.refs_3_ = f32[2,32,128]{2,1,0:T(8,128)S(1)} collective-permute-done((f32[2,32,128]{2,1,0:T(8,128)S(1)}, f32[2,32,128]{2,1,0:T(8,128)S(1)}, u32[]{:S(2)}, u32[]{:S(2)}) %collective-permute-start.10) | collective-permute-done | bytes 32800 | tf_op jit(solution)/shard_map/ppermute | solution.py:259
  36.6 1.0 %collective-permute-done.9.refs_2_ = f32[2,32,128]{2,1,0:T(8,128)S(1)} collective-permute-done((f32[2,32,128]{2,1,0:T(8,128)S(1)}, f32[2,32,128]{2,1,0:T(8,128)S(1)}, u32[]{:S(2)}, u32[]{:S(2)}) %collective-permute-start.9) | collective-permute-done | bytes 32800 | tf_op jit(solution)/shard_map/ppermute | solution.py:259
  37.6 0.4 collective-permute-done.8.refs_1_
  38.0 0.4 scatter.1
  38.3 1.8 %collective-permute-start.11 = (f32[32,256]{1,0:T(8,128)S(1)}, f32[32,256]{1,0:T(8,128)S(1)}, u32[]{:S(2)}, u32[]{:S(2)}) collective-permute-start(f32[32,256]{1,0:T(8,128)S(1)} %get-tuple-element.31), channel_id=1, source_target_pairs={{0,8},{8,0},{16,24},{24,16},{1,9},{9,1},{17,25},{25,17},{2,10},{10... | collective-permute-start | bytes 98312 | tf_op jit(solution)/shard_map/ppermute | solution.py:259
  40.1 2.5 %collective-permute-start.12 = (f32[32,256]{1,0:T(8,128)S(1)}, f32[32,256]{1,0:T(8,128)S(1)}, u32[]{:S(2)}, u32[]{:S(2)}) collective-permute-start(f32[32,256]{1,0:T(8,128)S(1)} %get-tuple-element.32), channel_id=1, source_target_pairs={{0,24},{8,16},{16,8},{24,0},{1,25},{9,17},{17,9},{25,1},{2,26},{10... | collective-permute-start | bytes 98312 | tf_op jit(solution)/shard_map/ppermute | solution.py:259
  42.6 0.1 collective-permute-start.13
  42.7 0.0 collective-permute-done.11.near_a_ref
  42.7 3.1 %collective-permute-done.12.near_b_ref = f32[32,256]{1,0:T(8,128)S(1)} collective-permute-done((f32[32,256]{1,0:T(8,128)S(1)}, f32[32,256]{1,0:T(8,128)S(1)}, u32[]{:S(2)}, u32[]{:S(2)}) %collective-permute-start.12) | collective-permute-done | bytes 32800 | tf_op jit(solution)/shard_map/ppermute | solution.py:259
  45.8 1.9 %collective-permute-done.13.fa_ref.fb_ref = f32[32,256]{1,0:T(8,128)S(1)} collective-permute-done((f32[32,256]{1,0:T(8,128)S(1)}, f32[32,256]{1,0:T(8,128)S(1)}, u32[]{:S(2)}, u32[]{:S(2)}) %collective-permute-start.13) | collective-permute-done | bytes 32800 | tf_op jit(solution)/shard_map/ppermute | solution.py:259
  47.8 0.0 copy-done
  47.8 1.9 %potential.1 = (f32[16,25]{1,0:T(8,128)}, f32[12,256]{1,0:T(8,128)}) custom-call(s32[1,12]{1,0:T(1,128)S(1)} %copy-done.1, f32[32,384]{1,0:T(8,128)S(1)} %get-tuple-element.30.own_ref, f32[32,256]{1,0:T(8,128)S(1)} %collective-permute-done.11.near_a_ref, f32[32,256]{1,0:T(8,128)S(1)} %collective-permute-done.12.near_b_ref, ...), custom_call_target="tpu_custom_call" | custom-call | tf_op jit(solution)/shard_map/potential/pallas_call | solution.py:398
  (1 shorter events, 0.0 us)
Async XLA Ops:
  2.7 13.2 %collective-permute-start.1 = (bf16[3,4,128,128]{3,2,1,0:T(8,128)(2,1)}, bf16[3,4,128,128]{3,2,1,0:T(8,128)(2,1)S(1)}, u32[]{:S(2)}, u32[]{:S(2)}) collective-permute-start(bf16[3,4,128,128]{3,2,1,0:T(8,128)(2,1)} %mask.1.after_hbm.refs_0_), channel_id=1, source_target_pairs={{0,4},{1,3},{2,6},{3,1},{4,0},{5,7},{6,2},{7,5},{8,12},{9,11},{10,... | collective-permute-start | bytes 1179656 | tf_op jit(solution)/shard_map/ppermute | solution.py:264
  5.7 14.6 %collective-permute-start = (bf16[3,4,128,128]{3,2,1,0:T(8,128)(2,1)}, bf16[3,4,128,128]{3,2,1,0:T(8,128)(2,1)S(1)}, u32[]{:S(2)}, u32[]{:S(2)}) collective-permute-start(bf16[3,4,128,128]{3,2,1,0:T(8,128)(2,1)} %mask.1.after_hbm.refs_0_), channel_id=1, source_target_pairs={{0,2},{1,5},{2,0},{3,7},{4,6},{5,1},{6,4},{7,3},{8,10},{9,13},{10,... | collective-permute-start | bytes 1179656 | tf_op jit(solution)/shard_map/ppermute | solution.py:264
  7.2 1.3 %copy-start.3 = (bf16[12,6,25,256]{3,2,1,0:T(8,128)(2,1)S(1)}, bf16[12,6,25,256]{3,2,1,0:T(8,128)(2,1)}, u32[]{:S(2)}) copy-start(bf16[12,6,25,256]{3,2,1,0:T(8,128)(2,1)} %harm_hbm.1) | copy-start | bytes 2764804
  8.5 0.9 %copy-start.4 = (f32[12,6,256]{2,1,0:T(8,128)S(1)}, f32[12,6,256]{2,1,0:T(8,128)}, u32[]{:S(2)}) copy-start(f32[12,6,256]{2,1,0:T(8,128)} %radius_hbm.1) | copy-start | bytes 221188
  9.4 0.7 %copy-start.6 = (f32[25,16]{0,1:T(8,128)S(1)}, f32[25,16]{0,1:T(8,128)}, u32[]{:S(2)}) copy-start(f32[25,16]{0,1:T(8,128)} %param.21) | copy-start | bytes 4804
  10.1 0.7 %copy-start.7 = (s32[12,6]{0,1:T(8,128)S(1)}, s32[12,6]{0,1:T(8,128)}, u32[]{:S(2)}) copy-start(s32[12,6]{0,1:T(8,128)} %param.17) | copy-start | bytes 868
  10.8 6.6 %copy-start.5 = (f32[12,6,256]{2,1,0:T(8,128)S(1)}, f32[12,6,256]{2,1,0:T(8,128)}, u32[]{:S(2)}) copy-start(f32[12,6,256]{2,1,0:T(8,128)} %part_hbm.1) | copy-start | bytes 221188
  15.9 9.6 %copy-start.1 = (s32[1,12]{1,0:T(1,128)S(1)}, s32[1,12]{1,0:T(1,128)}, u32[]{:S(2)}) copy-start(s32[1,12]{1,0:T(1,128)} %size_ref.3) | copy-start | bytes 148
  15.9 9.6 %copy-start.2 = (s32[1,12]{1,0:T(1,128)S(1)}, s32[1,12]{1,0:T(1,128)}, u32[]{:S(2)}) copy-start(s32[1,12]{1,0:T(1,128)} %offset_ref.1) | copy-start | bytes 148
  15.9 7.8 %collective-permute-start.5 = (bf16[3,4,128,128]{3,2,1,0:T(8,128)(2,1)S(1)}, bf16[3,4,128,128]{3,2,1,0:T(8,128)(2,1)S(1)}, u32[]{:S(2)}, u32[]{:S(2)}) collective-permute-start(bf16[3,4,128,128]{3,2,1,0:T(8,128)(2,1)S(1)} %collective-permute-done.1.after_hbm.refs_2_), channel_id=1, source_target_pairs={{0,2},{1,5},{2,0},{3,7},{4,6},{5,1},{6,4},{7,3},{8,10},{9,13},{10,... | collective-permute-start | bytes 1179656 | tf_op jit(solution)/shard_map/ppermute | solution.py:264
  16.9 7.6 %collective-permute-start.2 = (bf16[3,4,128,128]{3,2,1,0:T(8,128)(2,1)}, bf16[3,4,128,128]{3,2,1,0:T(8,128)(2,1)S(1)}, u32[]{:S(2)}, u32[]{:S(2)}) collective-permute-start(bf16[3,4,128,128]{3,2,1,0:T(8,128)(2,1)} %mask.1.after_hbm.refs_0_), channel_id=1, source_target_pairs={{0,1},{1,0},{2,3},{3,2},{4,5},{5,4},{6,7},{7,6},{8,9},{9,8},{10,11... | collective-permute-start | bytes 1179656 | tf_op jit(solution)/shard_map/ppermute | solution.py:259
  16.9 7.6 %collective-permute-start.3 = (bf16[3,4,128,128]{3,2,1,0:T(8,128)(2,1)S(1)}, bf16[3,4,128,128]{3,2,1,0:T(8,128)(2,1)S(1)}, u32[]{:S(2)}, u32[]{:S(2)}) collective-permute-start(bf16[3,4,128,128]{3,2,1,0:T(8,128)(2,1)S(1)} %collective-permute-done.1.after_hbm.refs_2_), channel_id=1, source_target_pairs={{0,1},{1,0},{2,3},{3,2},{4,5},{5,4},{6,7},{7,6},{8,9},{9,8},{10,11... | collective-permute-start | bytes 1179656 | tf_op jit(solution)/shard_map/ppermute | solution.py:259
  20.3 4.1 %collective-permute-start.4 = (bf16[3,4,128,128]{3,2,1,0:T(8,128)(2,1)S(1)}, bf16[3,4,128,128]{3,2,1,0:T(8,128)(2,1)S(1)}, u32[]{:S(2)}, u32[]{:S(2)}) collective-permute-start(bf16[3,4,128,128]{3,2,1,0:T(8,128)(2,1)S(1)} %collective-permute-done.refs_4_), channel_id=1, source_target_pairs={{0,1},{1,0},{2,3},{3,2},{4,5},{5,4},{6,7},{7,6},{8,9},{9,8},{10,11... | collective-permute-start | bytes 1179656 | tf_op jit(solution)/shard_map/ppermute | solution.py:259
  23.8 1.7 %collective-permute-start.6 = (bf16[3,4,128,128]{3,2,1,0:T(8,128)(2,1)S(1)}, bf16[3,4,128,128]{3,2,1,0:T(8,128)(2,1)S(1)}, u32[]{:S(2)}, u32[]{:S(2)}) collective-permute-start(bf16[3,4,128,128]{3,2,1,0:T(8,128)(2,1)S(1)} %collective-permute-done.5.refs_6_), channel_id=1, source_target_pairs={{0,1},{1,0},{2,3},{3,2},{4,5},{5,4},{6,7},{7,6},{8,9},{9,8},{10,11... | collective-permute-start | bytes 1179656 | tf_op jit(solution)/shard_map/ppermute | solution.py:259
  25.5 22.3 %copy-start = (f32[72,25,256]{2,1,0:T(8,128)S(1)}, f32[72,25,256]{2,1,0:T(8,128)}, u32[]{:S(2)}) copy-start(f32[72,25,256]{2,1,0:T(8,128)} %get-tuple-element.34.g_ref) | copy-start | bytes 5529604
  30.5 1.2 %collective-permute-start.7 = (f32[32,128]{1,0:T(8,128)S(1)}, f32[32,128]{1,0:T(8,128)S(1)}, u32[]{:S(2)}, u32[]{:S(2)}) collective-permute-start(f32[32,128]{1,0:T(8,128)S(1)} %get-tuple-element.29), channel_id=1, source_target_pairs={{0,1},{1,0},{2,3},{3,2},{4,5},{5,4},{6,7},{7,6},{8,9},{9,8},{10,11... | collective-permute-start | bytes 49160 | tf_op jit(solution)/shard_map/ppermute | solution.py:259
  31.7 4.9 %collective-permute-start.10 = (f32[2,32,128]{2,1,0:T(8,128)S(1)}, f32[2,32,128]{2,1,0:T(8,128)S(1)}, u32[]{:S(2)}, u32[]{:S(2)}) collective-permute-start(f32[2,32,128]{2,1,0:T(8,128)S(1)} %pad_maximum_fusion.refs_0_), channel_id=1, source_target_pairs={{0,6},{1,7},{2,4},{3,5},{4,2},{5,3},{6,0},{7,1},{8,14},{9,15},{10,... | collective-permute-start | bytes 98312 | tf_op jit(solution)/shard_map/ppermute | solution.py:259
  33.7 3.9 %collective-permute-start.9 = (f32[2,32,128]{2,1,0:T(8,128)S(1)}, f32[2,32,128]{2,1,0:T(8,128)S(1)}, u32[]{:S(2)}, u32[]{:S(2)}) collective-permute-start(f32[2,32,128]{2,1,0:T(8,128)S(1)} %pad_maximum_fusion.refs_0_), channel_id=1, source_target_pairs={{0,4},{1,5},{2,6},{3,7},{4,0},{5,1},{6,2},{7,3},{8,12},{9,13},{10,... | collective-permute-start | bytes 98312 | tf_op jit(solution)/shard_map/ppermute | solution.py:259
  34.0 3.9 %collective-permute-start.8 = (f32[2,32,128]{2,1,0:T(8,128)S(1)}, f32[2,32,128]{2,1,0:T(8,128)S(1)}, u32[]{:S(2)}, u32[]{:S(2)}) collective-permute-start(f32[2,32,128]{2,1,0:T(8,128)S(1)} %pad_maximum_fusion.refs_0_), channel_id=1, source_target_pairs={{0,2},{1,3},{2,0},{3,1},{4,6},{5,7},{6,4},{7,5},{8,10},{9,11},{10,... | collective-permute-start | bytes 98312 | tf_op jit(solution)/shard_map/ppermute | solution.py:259
  38.3 4.4 %collective-permute-start.11 = (f32[32,256]{1,0:T(8,128)S(1)}, f32[32,256]{1,0:T(8,128)S(1)}, u32[]{:S(2)}, u32[]{:S(2)}) collective-permute-start(f32[32,256]{1,0:T(8,128)S(1)} %get-tuple-element.31), channel_id=1, source_target_pairs={{0,8},{8,0},{16,24},{24,16},{1,9},{9,1},{17,25},{25,17},{2,10},{10... | collective-permute-start | bytes 98312 | tf_op jit(solution)/shard_map/ppermute | solution.py:259
  40.1 5.7 %collective-permute-start.12 = (f32[32,256]{1,0:T(8,128)S(1)}, f32[32,256]{1,0:T(8,128)S(1)}, u32[]{:S(2)}, u32[]{:S(2)}) collective-permute-start(f32[32,256]{1,0:T(8,128)S(1)} %get-tuple-element.32), channel_id=1, source_target_pairs={{0,24},{8,16},{16,8},{24,0},{1,25},{9,17},{17,9},{25,1},{2,26},{10... | collective-permute-start | bytes 98312 | tf_op jit(solution)/shard_map/ppermute | solution.py:259
  42.6 5.2 %collective-permute-start.13 = (f32[32,256]{1,0:T(8,128)S(1)}, f32[32,256]{1,0:T(8,128)S(1)}, u32[]{:S(2)}, u32[]{:S(2)}) collective-permute-start(f32[32,256]{1,0:T(8,128)S(1)} %get-tuple-element.33), channel_id=1, source_target_pairs={{0,16},{8,24},{16,0},{24,8},{1,17},{9,25},{17,1},{25,9},{2,18},{10... | collective-permute-start | bytes 98312 | tf_op jit(solution)/shard_map/ppermute | solution.py:259

commit v5 on v4

--- a/solution.py
+++ b/solution.py
@@ -8,6 +8,7 @@
 
 EVEN_OWNERS = (0, 1, 4, 3, 2, 5, 6, 7)
 ODD_OWNERS = (0, 1, 2, 5, 4, 3, 6, 7)
+DOUBLED = (0, 4, 2, 6, 1, 5, 3, 7)
 LANES = 128
 ROWS = 32
 SLOT = 8
@@ -16,7 +17,7 @@
 VMEM = pl.BlockSpec(memory_space=pltpu.VMEM)
 SMEM = pl.BlockSpec(memory_space=pltpu.SMEM)
 HBM = pl.BlockSpec(memory_space=pltpu.HBM)
-WIDE = pltpu.CompilerParams(vmem_limit_bytes=50 * 1024 * 1024)
+WIDE = pltpu.CompilerParams(vmem_limit_bytes=16 * 1024 * 1024)
 PARAMS = pltpu.CompilerParams(vmem_limit_bytes=16 * 1024 * 1024)
 
 
@@ -43,26 +44,8 @@
     return jnp.where(distance < 1.0, inner, jnp.where(distance < 2.0, outer, 0.0))
 
 
-def mask_kernel(mask_ref, rows_ref, out_ref, mask, rows, sems):
-    stored, band = rows_ref.shape[:2]
-    fetch = pltpu.make_async_copy(mask_ref, mask, sems.at[stored])
-    copies = [
-        pltpu.make_async_copy(rows_ref.at[t], rows.at[t], sems.at[t]) for t in range(stored)
-    ]
-    fetch.start()
-    for copy in copies:
-        copy.start()
-    fetch.wait()
-    factors = mask[...].astype(jnp.float32)
-    for t, copy in enumerate(copies):
-        copy.wait()
-        for k in range(band):
-            factor = factors[t : t + 1, k : k + 1]
-            out_ref[t, k] = (rows[t, k].astype(jnp.float32) * factor).astype(jnp.bfloat16)
-
-
 def field_kernel(
-    after_hbm, near_ref, table_hbm, radius_hbm, harm_hbm,
+    near_ref, table_hbm, radius_hbm, harm_hbm,
     g_ref, hpad_ref, atom_ref, table_ref, radius_ref, harm_ref, sems,
 ):
     batches, near, comps, points = harm_ref.shape
@@ -121,7 +104,7 @@
     copies[2].wait()
 
 
-def density_kernel(start_ref, offset_ref, size_ref, atom_ref, phit_ref, part_ref, hpad_ref, *refs):
+def density_kernel(start_ref, offset_ref, size_ref, mask_ref, atom_ref, phit_ref, part_ref, hpad_ref, *refs):
     dens_ref, terms_ref, window_ref, w_ref = refs[-4:]
     pieces = refs[:-4]
     owners = window_ref.shape[0]
@@ -129,19 +112,25 @@
     near = part_ref.shape[1]
     if len(pieces) == owners:
         me = lax.axis_index("dev")
-        odd = lax.rem(me, 2)
+        odd = lax.rem(me, 2) == 1
         held = [
-            (piece, lax.bitwise_xor(me, jnp.where(odd == 1, b, a)))
+            (
+                piece,
+                lax.bitwise_xor(me, jnp.where(odd, b, a)),
+                jnp.where(odd, DOUBLED.index(b), DOUBLED.index(a)),
+            )
             for piece, a, b in zip(pieces, EVEN_OWNERS, ODD_OWNERS)
         ]
     else:
-        held = [(pieces[0].at[owner], owner) for owner in range(owners)]
-    stored = held[0][0].shape[0]
+        held = [(pieces[0].at[owner], owner, owner) for owner in range(owners)]
+    stored, band = held[0][0].shape[:2]
     start = start_ref[0]
-    for piece, owner in held:
+    for piece, owner, at in held:
         ahead = lax.rem(owner - start + stored * owners, owners)
         row = lax.rem(start + ahead, stored * owners) // owners
-        window_ref[ahead] = piece[row]
+        for k in range(band):
+            factor = jnp.full((width, width), mask_ref[at * stored + row, k].astype(jnp.float32))
+            window_ref[ahead, k] = piece[row, k] * factor.astype(jnp.bfloat16)
     w_ref[...] = jnp.zeros(w_ref.shape, w_ref.dtype)
     lane = lax.broadcasted_iota(jnp.int32, (1, points), 1)
     zero = jnp.zeros((width, width), jnp.bfloat16)
@@ -169,7 +158,7 @@
         w_ref[b, 0:near, :] = part_ref[b] * row
         return carry
 
-    lax.fori_loop(0, batches, body, 0, unroll=2)
+    lax.fori_loop(0, batches, body, 0, unroll=4)
     weights = w_ref[...].reshape(LANES, points)
     columns = jnp.concatenate(split2(weights), axis=0)
     slot = lax.broadcasted_iota(jnp.int32, (1, 2 * LANES), 1) % LANES
@@ -185,21 +174,17 @@
     terms_ref[...] = jnp.where(row_id == comps, atom_ref[...].astype(jnp.float32), result)
 
 
-def scatter_kernel(comps, atoms, flip, *refs):
-    outs = refs[-4:]
-    pieces = refs[:-4]
+def scatter_kernel(comps, atoms, flip, pieces, own, near_a, near_b, far):
     row_id = lax.broadcasted_iota(jnp.int32, (3 * atoms, LANES), 0)
     total = jnp.zeros((3 * ROWS, 3 * atoms), jnp.float32)
-    for piece in pieces:
+    for m in range(0, pieces.shape[0], 2):
         left, right = [], []
-        for part in range(piece.shape[0]):
-            values = piece[part]
+        for values in (pieces[m], pieces[m + 1]):
             chosen = values[comps : comps + 1, :].astype(jnp.int32)
             right.append((row_id == chosen).astype(jnp.float32).astype(jnp.bfloat16))
             left.append(jnp.concatenate(split3(values), axis=0))
         total = total + dot(jnp.concatenate(left, axis=1), jnp.concatenate(right, axis=1), NT)
     sums = total[:ROWS] + total[ROWS : 2 * ROWS] + total[2 * ROWS :]
-    own, near_a, near_b, far = outs
     own[...] = sums
     ahead, back = sums[:, atoms:], sums[:, : 2 * atoms]
     if flip:
@@ -253,6 +238,10 @@
             total = total + column * g_ref[b * near + i]
         row = jnp.sum(total, axis=0, keepdims=True)
         pot_ref[b : b + 1, :] = jnp.where(lane < size_ref[0, b], row, 0.0)
+
+
+def held_in_hbm(*values):
+    return [pltpu.with_memory_space_constraint(value, pltpu.HBM) for value in values]
 
 
 def crossed(value, axis, m):
@@ -291,27 +280,14 @@
     atoms = mine * dev_count
     f32, bf16 = jnp.float32, jnp.bfloat16
 
-    masked = pl.pallas_call(
-        mask_kernel,
-        out_shape=jax.ShapeDtypeStruct(density_rows.shape, bf16),
-        in_specs=[HBM, HBM],
-        out_specs=VMEM,
-        scratch_shapes=[
-            pltpu.VMEM(block_mask.shape, jnp.int32),
-            pltpu.VMEM(density_rows.shape, bf16),
-            pltpu.SemaphoreType.DMA((blocks_dev + 1,)),
-        ],
-        compiler_params=pltpu.CompilerParams(vmem_limit_bytes=63 * 1024 * 1024),
-        name="mask",
-    )(block_mask, density_rows)
     g, hpad, atom_rows = pl.pallas_call(
         field_kernel,
         out_shape=(
-            jax.ShapeDtypeStruct((batches * near, comps, points), f32),
-            jax.ShapeDtypeStruct((batches * near, ROWS, points), bf16),
-            jax.ShapeDtypeStruct((1, LANES), jnp.int32),
+            pltpu.VMEM((batches * near, comps, points), f32),
+            pltpu.VMEM((batches * near, ROWS, points), bf16),
+            pltpu.VMEM((1, LANES), jnp.int32),
         ),
-        in_specs=[HBM, SMEM] + [HBM] * 3,
+        in_specs=[SMEM] + [HBM] * 3,
         out_specs=(VMEM,) * 3,
         scratch_shapes=[
             pltpu.VMEM(radial_table.shape[::-1], f32),
@@ -322,14 +298,14 @@
         compiler_params=WIDE,
         cost_estimate=pl.CostEstimate(flops=2_000_000_000, bytes_accessed=8_000_000, transcendentals=0),
         name="field",
-    )(masked, atom_near.T, radial_table.T, radius, harmonics)
+    )(atom_near.T, *held_in_hbm(radial_table.T, radius, harmonics))
 
     def turned_basis(after):
         return pl.pallas_call(
             turn_kernel,
             out_shape=(
-                jax.ShapeDtypeStruct((batches, near_blocks, width, points), bf16),
-                jax.ShapeDtypeStruct(partition.shape, f32),
+                pltpu.VMEM((batches, near_blocks, width, points), bf16),
+                pltpu.VMEM(partition.shape, f32),
             ),
             in_specs=[HBM] * 3,
             out_specs=(VMEM,) * 2,
@@ -339,20 +315,29 @@
                 flops=2_000_000_000, bytes_accessed=8_000_000, transcendentals=0
             ),
             name="turn",
-        )(after, basis_values, partition)
+        )(after, *held_in_hbm(basis_values, partition))
 
     if dev_count == 8:
-        first = turned(masked, 4, 2)
-        second = turned(masked, 2, 4)
-        first, g = lax.optimization_barrier((first, g))
+        masks = block_mask
+        other = crossed(masks, "dev", 4)
+        first = turned(density_rows, 4, 2)
+        rows, g = lax.optimization_barrier((density_rows, g))
+        first, other, g = lax.optimization_barrier((first, other, g))
+        second = turned(rows, 2, 4)
         third = turned(first, 2, 4)
+        masks = jnp.concatenate([masks, other])
+        other = crossed(masks, "dev", 2)
         phit, weights = turned_basis(first)
+        other, phit = lax.optimization_barrier((other, phit))
         second, phit = lax.optimization_barrier((second, phit))
-        sent = (masked, first, second, third)
+        masks = jnp.concatenate([masks, other])
+        masks = jnp.concatenate([masks, crossed(masks, "dev", 1)])
+        sent = (density_rows, first, second, third)
         pieces = [piece for value in sent for piece in (value, crossed(value, "dev", 1))]
     else:
-        phit, weights = turned_basis(masked)
-        pieces = [lax.all_gather(masked, "dev", axis=0)]
+        phit, weights = turned_basis(density_rows)
+        pieces = [lax.all_gather(density_rows, "dev", axis=0)]
+        masks = lax.all_gather(block_mask, "dev", axis=0, tiled=True)
 
     density, terms = pl.pallas_call(
         density_kernel,
@@ -360,7 +345,7 @@
             jax.ShapeDtypeStruct((batches, points), f32),
             jax.ShapeDtypeStruct((ROWS, LANES), f32),
         ),
-        in_specs=[SMEM] * 3 + [VMEM] * (4 + len(pieces)),
+        in_specs=[SMEM] * 4 + [VMEM] * (4 + len(pieces)),
         out_specs=(VMEM, VMEM),
         scratch_shapes=[
             pltpu.VMEM((dev_count, band, width, width), bf16),
@@ -370,21 +355,25 @@
         cost_estimate=pl.CostEstimate(flops=2_000_000_000, bytes_accessed=6_000_000, transcendentals=0),
         name="density",
     )(
-        window_start, batch_offsets, batch_sizes, atom_rows, phit, weights, hpad,
+        window_start, batch_offsets, batch_sizes, masks, atom_rows, phit, weights, hpad,
         *pieces,
     )
 
-    both = jnp.stack([terms, crossed(terms, "dev", 1)])
-    groups = [both] + [crossed(both, "dev", m) for m in range(2, dev_count, 2)]
+    if dev_count == 8:
+        groups = terms[None]
+        for m in (4, 2, 1):
+            groups = jnp.concatenate([groups, crossed(groups, "dev", m)])
+    else:
+        groups = lax.all_gather(terms, "dev", axis=0)
     flip = region_count == 4
     own, near_a, near_b, far = pl.pallas_call(
         functools.partial(scatter_kernel, comps, atoms, flip),
         out_shape=tuple(jax.ShapeDtypeStruct((ROWS, n * atoms), f32) for n in (3, 2, 2, 2)),
-        in_specs=[VMEM] * len(groups),
+        in_specs=[VMEM],
         out_specs=(VMEM,) * 4,
         compiler_params=PARAMS,
         name="scatter",
-    )(*groups)
+    )(groups)
     if flip:
         far_a = far_b = crossed(far, "region", 2)
         near_a = crossed(near_a, "region", 1)

time: 50 us -> 48.8 us (0.976)
  Pallas kernels: 17.3 us -> 13.8 us
  local copies, waits for them, and re-layouts: 3.56 us -> 0.71 us
  starting transfers between devices: 14.1 us -> 16.9 us
  waiting for transfers between devices: 13.3 us -> 15.7 us
    ppermute x11 -> x13, waiting for transfers between devices: 9.89 us -> 15.7 us  [crossed(): lax.ppermute(value, axis, [(i, i ^ m) for i in range(lax.axis_size(axis))])]
    ppermute x3, waiting for transfers between devices: 3.4 us -> 0.01 us  [turned(): lax.ppermute(value, 'dev', [(i, i ^ (odd if i % 2 else even)) for i in ra...]
    unnamed x16 -> x10, local copies, waits for them, and re-layouts: 3.56 us -> 0.71 us
    ppermute x11 -> x13, starting transfers between devices: 8.6 us -> 11.2 us  [crossed(): lax.ppermute(value, axis, [(i, i ^ m) for i in range(lax.axis_size(axis))])]
    pallas_call x3 -> x2, Pallas kernels: 10.1 us -> 7.47 us  [the longest x1 4.56 us: per_device(): pl.pallas_call(field_kernel, out_shape=(pltpu.VMEM((batches * near, comps...]
    pallas_call x1, Pallas kernels: 5.01 us -> 4.11 us  [per_device(): pl.pallas_call(density_kernel, out_shape=(jax.ShapeDtypeStruct((batches,...]
  transfers between devices with their start and end apart: 14 -> 16, of which waited for: 8 -> 7; matrix products, arithmetic and copies ran while one was open for 0% -> 0% of each run, Pallas kernels for 16% -> 15%
where the time goes in v5:
time: 48.8 us; the launch traced here: 48.6 us
  starting transfers between devices  16.9 us (35%)
  waiting for transfers between devices  15.7 us (32%)
  Pallas kernels  13.8 us (28%)
  between operations  1.42 us (3%)
  local copies, waits for them, and re-layouts  0.71 us (1%)
    ppermute x13, waiting for transfers between devices, crossed(): lax.ppermute(value, axis, [(i, i ^ m) for i in range(lax.axis_size(axis))])  15.7 us
    ppermute x13, starting transfers between devices, crossed(): lax.ppermute(value, axis, [(i, i ^ m) for i in range(lax.axis_size(axis))])  11.2 us
    ppermute x3, starting transfers between devices, turned(): lax.ppermute(value, 'dev', [(i, i ^ (odd if i % 2 else even)) for i in ra...  5.66 us
    pallas_call x1, Pallas kernels, per_device(): pl.pallas_call(field_kernel, out_shape=(pltpu.VMEM((batches * near, comps...  4.56 us
    pallas_call x1, Pallas kernels, per_device(): pl.pallas_call(density_kernel, out_shape=(jax.ShapeDtypeStruct((batches,...  4.11 us
    pallas_call x1, Pallas kernels, turned_basis(): pl.pallas_call(turn_kernel, out_shape=(pltpu.VMEM((batches, near_blocks,...  2.9 us
    pallas_call x1, Pallas kernels, per_device(): pl.pallas_call(functools.partial(potential_kernel, comps, atoms, flip), o...  1.88 us
  transfers between devices with their start and end apart: 16, of which 7 were waited for; matrix products, arithmetic and copies ran while one was open for 0% of the time, Pallas kernels for 15%

profile of v5, /device:TPU:0, one launch (start us, length us, event | category | flops | bytes accessed | tf_op | source)
XLA Modules:
  0.0 48.6 jit_solution(14005190549197188815)
XLA Ops:
  0.6 3.0 %collective-permute-start = (bf16[3,4,128,128]{3,2,1,0:T(8,128)(2,1)}, bf16[3,4,128,128]{3,2,1,0:T(8,128)(2,1)S(1)}, u32[]{:S(2)}, u32[]{:S(2)}) collective-permute-start(bf16[3,4,128,128]{3,2,1,0:T(8,128)(2,1)} %refs_0_.1), channel_id=1, source_target_pairs={{0,4},{1,3},{2,6},{3,1},{4,0},{5,7},{6,2},{7,5},{8,12},{9,11},{10,... | collective-permute-start | bytes 1179656 | tf_op jit(solution)/shard_map/ppermute | solution.py:253
  3.7 0.1 collective-permute-start.1
  3.7 0.0 copy-start.3
  3.7 0.7 %copy-done.3 = s32[12,6]{0,1:T(8,128)S(1)} copy-done((s32[12,6]{0,1:T(8,128)S(1)}, s32[12,6]{0,1:T(8,128)}, u32[]{:S(2)}) %copy-start.3) | copy-done | bytes 312
  4.4 0.0 copy-start
  4.4 0.0 copy-start.4
  4.4 4.6 %field.1 = (f32[72,25,256]{2,1,0:T(8,128)S(1)}, bf16[72,32,256]{2,1,0:T(8,128)(2,1)S(1)}, s32[1,128]{1,0:T(1,128)S(1)}) custom-call(s32[6,12]{1,0:T(8,128)S(1)} %bitcast.8, f32[16,25]{1,0:T(8,128)} %bitcast.9, f32[12,6,256]{2,1,0:T(8,128)} %radius_hbm.1, bf16[12,6,25,256]{3,2,1,0:T(8,128)(2,1)} %harm_hbm.1), custom_call_target="tpu_custom_call" | custom-call | flops 2000000000 | bytes 8000000 | tf_op jit(solution)/shard_map/field/pallas_call | solution.py:283
  9.0 0.0 copy-done
  9.0 2.0 %collective-permute-start.4 = (bf16[3,4,128,128]{3,2,1,0:T(8,128)(2,1)S(1)}, bf16[3,4,128,128]{3,2,1,0:T(8,128)(2,1)S(1)}, u32[]{:S(2)}, u32[]{:S(2)}) collective-permute-start(bf16[3,4,128,128]{3,2,1,0:T(8,128)(2,1)S(1)} %copy-done), channel_id=1, source_target_pairs={{0,2},{1,5},{2,0},{3,7},{4,6},{5,1},{6,4},{7,3},{8,10},{9,13},{10,... | collective-permute-start | bytes 1179656 | tf_op jit(solution)/shard_map/ppermute | solution.py:253
  11.0 0.0 collective-permute-done.1
  11.0 0.0 collective-permute-done.after_hbm.refs_2_
  11.0 0.6 %collective-permute-start.8 = (bf16[3,4,128,128]{3,2,1,0:T(8,128)(2,1)S(1)}, bf16[3,4,128,128]{3,2,1,0:T(8,128)(2,1)S(1)}, u32[]{:S(2)}, u32[]{:S(2)}) collective-permute-start(bf16[3,4,128,128]{3,2,1,0:T(8,128)(2,1)S(1)} %collective-permute-done.after_hbm.refs_2_), channel_id=1, source_target_pairs={{0,2},{1,5},{2,0},{3,7},{4,6},{5,1},{6,4},{7,3},{8,10},{9,13},{10,... | collective-permute-start | bytes 1179656 | tf_op jit(solution)/shard_map/ppermute | solution.py:253
  11.7 0.0 collective-permute-start.5
  11.7 0.5 %collective-permute-start.6 = (bf16[3,4,128,128]{3,2,1,0:T(8,128)(2,1)S(1)}, bf16[3,4,128,128]{3,2,1,0:T(8,128)(2,1)S(1)}, u32[]{:S(2)}, u32[]{:S(2)}) collective-permute-start(bf16[3,4,128,128]{3,2,1,0:T(8,128)(2,1)S(1)} %collective-permute-done.after_hbm.refs_2_), channel_id=1, source_target_pairs={{0,1},{1,0},{2,3},{3,2},{4,5},{5,4},{6,7},{7,6},{8,9},{9,8},{10,11... | collective-permute-start | bytes 1179656 | tf_op jit(solution)/shard_map/ppermute | solution.py:248
  12.2 0.0 copy-done.4
  12.2 0.0 copy-start.1
  12.2 0.0 copy-start.2
  12.2 1.5 %collective-permute-start.2 = (s32[6,4]{1,0:T(8,128)S(1)}, s32[6,4]{1,0:T(8,128)S(1)}, u32[]{:S(2)}, u32[]{:S(2)}) collective-permute-start(s32[6,4]{1,0:T(8,128)S(1)} %pad_add_fusion.2), channel_id=1, source_target_pairs={{0,2},{1,3},{2,0},{3,1},{4,6},{5,7},{6,4},{7,5},{8,10},{9,11},{10,... | collective-permute-start | bytes 296 | tf_op jit(solution)/shard_map/ppermute | solution.py:248
  13.7 2.9 %turn.1 = (bf16[12,4,128,256]{3,2,1,0:T(8,128)(2,1)S(1)}, f32[12,6,256]{2,1,0:T(8,128)S(1)}) custom-call(bf16[3,4,128,128]{3,2,1,0:T(8,128)(2,1)S(1)} %collective-permute-done.after_hbm.refs_2_, bf16[12,4,256,128]{3,2,1,0:T(8,128)(2,1)} %basis_hbm.1, f32[12,6,256]{2,1,0:T(8,128)} %part_hbm.1), custom_call_target="tpu_custom_call" | custom-call | flops 2000000000 | bytes 8000000 | tf_op jit(solution)/shard_map/turn/pallas_call | solution.py:304
  16.6 4.6 %collective-permute-done.2 = s32[6,4]{1,0:T(8,128)S(1)} collective-permute-done((s32[6,4]{1,0:T(8,128)S(1)}, s32[6,4]{1,0:T(8,128)S(1)}, u32[]{:S(2)}, u32[]{:S(2)}) %collective-permute-start.2) | collective-permute-done | bytes 128 | tf_op jit(solution)/shard_map/ppermute | solution.py:248
  21.2 0.0 collective-permute-done.4.refs_4_
  21.2 0.0 collective-permute-start.7
  21.2 0.0 collective-permute-done.8.refs_6_
  21.2 0.5 %collective-permute-start.9 = (bf16[3,4,128,128]{3,2,1,0:T(8,128)(2,1)S(1)}, bf16[3,4,128,128]{3,2,1,0:T(8,128)(2,1)S(1)}, u32[]{:S(2)}, u32[]{:S(2)}) collective-permute-start(bf16[3,4,128,128]{3,2,1,0:T(8,128)(2,1)S(1)} %collective-permute-done.8.refs_6_), channel_id=1, source_target_pairs={{0,1},{1,0},{2,3},{3,2},{4,5},{5,4},{6,7},{7,6},{8,9},{9,8},{10,11... | collective-permute-start | bytes 1179656 | tf_op jit(solution)/shard_map/ppermute | solution.py:248
  21.7 0.1 collective-permute-start.3
  22.5 1.0 %collective-permute-done.3 = s32[12,4]{1,0:T(8,128)S(1)} collective-permute-done((s32[12,4]{1,0:T(8,128)S(1)}, s32[12,4]{1,0:T(8,128)S(1)}, u32[]{:S(2)}, u32[]{:S(2)}) %collective-permute-start.3) | collective-permute-done | bytes 224 | tf_op jit(solution)/shard_map/ppermute | solution.py:248
  23.5 0.0 collective-permute-done.5.refs_1_
  23.5 0.0 collective-permute-done.6.refs_3_
  23.5 0.0 collective-permute-done.7.refs_5_
  23.5 0.0 collective-permute-done.9.refs_7_
  23.5 0.0 copy-done.1
  23.5 0.0 copy-done.2
  23.5 4.1 %density.1 = (f32[12,256]{1,0:T(8,128)}, f32[32,128]{1,0:T(8,128)S(1)}) custom-call(s32[1]{0:T(128)S(6)} %copy.23.start_ref, s32[1,12]{1,0:T(1,128)S(1)} %copy-done.2, s32[1,12]{1,0:T(1,128)S(1)} %copy-done.1, s32[24,4]{1,0:T(8,128)S(1)} %pad_add_fusion.mask_ref, s32[1,128]{1,0:T(1,128)S(1)} %get-tuple-element.31.atom_ref, ...), custom_call_target="tpu_custom_call" | custom-call | flops 2000000000 | bytes 6000000 | tf_op jit(solution)/shard_map/density/pallas_call | solution.py:342
  27.6 1.9 %collective-permute-start.10 = (f32[1,32,128]{2,1,0:T(8,128)S(1)}, f32[1,32,128]{2,1,0:T(8,128)S(1)}, u32[]{:S(2)}, u32[]{:S(2)}) collective-permute-start(f32[1,32,128]{2,1,0:T(8,128)S(1)} %bitcast.4), channel_id=1, source_target_pairs={{0,4},{1,5},{2,6},{3,7},{4,0},{5,1},{6,2},{7,3},{8,12},{9,13},{10,... | collective-permute-start | bytes 49160 | tf_op jit(solution)/shard_map/ppermute | solution.py:248
  29.6 1.8 %collective-permute-done.10 = f32[1,32,128]{2,1,0:T(8,128)S(1)} collective-permute-done((f32[1,32,128]{2,1,0:T(8,128)S(1)}, f32[1,32,128]{2,1,0:T(8,128)S(1)}, u32[]{:S(2)}, u32[]{:S(2)}) %collective-permute-start.10) | collective-permute-done | bytes 16416 | tf_op jit(solution)/shard_map/ppermute | solution.py:248
  31.4 1.9 %collective-permute-start.11 = (f32[2,32,128]{2,1,0:T(8,128)S(1)}, f32[2,32,128]{2,1,0:T(8,128)S(1)}, u32[]{:S(2)}, u32[]{:S(2)}) collective-permute-start(f32[2,32,128]{2,1,0:T(8,128)S(1)} %pad_maximum_fusion.2), channel_id=1, source_target_pairs={{0,2},{1,3},{2,0},{3,1},{4,6},{5,7},{6,4},{7,5},{8,10},{9,11},{10,... | collective-permute-start | bytes 98312 | tf_op jit(solution)/shard_map/ppermute | solution.py:248
  33.3 2.0 %collective-permute-done.11 = f32[2,32,128]{2,1,0:T(8,128)S(1)} collective-permute-done((f32[2,32,128]{2,1,0:T(8,128)S(1)}, f32[2,32,128]{2,1,0:T(8,128)S(1)}, u32[]{:S(2)}, u32[]{:S(2)}) %collective-permute-start.11) | collective-permute-done | bytes 32800 | tf_op jit(solution)/shard_map/ppermute | solution.py:248
  35.3 0.0 collective-permute-start.12
  35.3 1.2 %collective-permute-done.12 = f32[4,32,128]{2,1,0:T(8,128)S(1)} collective-permute-done((f32[4,32,128]{2,1,0:T(8,128)S(1)}, f32[4,32,128]{2,1,0:T(8,128)S(1)}, u32[]{:S(2)}, u32[]{:S(2)}) %collective-permute-start.12) | collective-permute-done | bytes 65568 | tf_op jit(solution)/shard_map/ppermute | solution.py:248
  36.6 0.4 scatter.1
  37.0 2.1 %collective-permute-start.13 = (f32[32,256]{1,0:T(8,128)S(1)}, f32[32,256]{1,0:T(8,128)S(1)}, u32[]{:S(2)}, u32[]{:S(2)}) collective-permute-start(f32[32,256]{1,0:T(8,128)S(1)} %get-tuple-element.41), channel_id=1, source_target_pairs={{0,8},{8,0},{16,24},{24,16},{1,9},{9,1},{17,25},{25,17},{2,10},{10... | collective-permute-start | bytes 98312 | tf_op jit(solution)/shard_map/ppermute | solution.py:248
  39.0 2.5 %collective-permute-start.14 = (f32[32,256]{1,0:T(8,128)S(1)}, f32[32,256]{1,0:T(8,128)S(1)}, u32[]{:S(2)}, u32[]{:S(2)}) collective-permute-start(f32[32,256]{1,0:T(8,128)S(1)} %get-tuple-element.42), channel_id=1, source_target_pairs={{0,24},{8,16},{16,8},{24,0},{1,25},{9,17},{17,9},{25,1},{2,26},{10... | collective-permute-start | bytes 98312 | tf_op jit(solution)/shard_map/ppermute | solution.py:248
  41.5 0.1 collective-permute-start.15
  41.6 0.0 collective-permute-done.13.near_a_ref
  41.6 3.2 %collective-permute-done.14.near_b_ref = f32[32,256]{1,0:T(8,128)S(1)} collective-permute-done((f32[32,256]{1,0:T(8,128)S(1)}, f32[32,256]{1,0:T(8,128)S(1)}, u32[]{:S(2)}, u32[]{:S(2)}) %collective-permute-start.14) | collective-permute-done | bytes 32800 | tf_op jit(solution)/shard_map/ppermute | solution.py:248
  44.8 1.9 %collective-permute-done.15.fa_ref.fb_ref = f32[32,256]{1,0:T(8,128)S(1)} collective-permute-done((f32[32,256]{1,0:T(8,128)S(1)}, f32[32,256]{1,0:T(8,128)S(1)}, u32[]{:S(2)}, u32[]{:S(2)}) %collective-permute-start.15) | collective-permute-done | bytes 32800 | tf_op jit(solution)/shard_map/ppermute | solution.py:248
  46.7 1.9 %potential.1 = (f32[16,25]{1,0:T(8,128)}, f32[12,256]{1,0:T(8,128)}) custom-call(s32[1,12]{1,0:T(1,128)S(1)} %copy-done.1, f32[32,384]{1,0:T(8,128)S(1)} %get-tuple-element.40.own_ref, f32[32,256]{1,0:T(8,128)S(1)} %collective-permute-done.13.near_a_ref, f32[32,256]{1,0:T(8,128)S(1)} %collective-permute-done.14.near_b_ref, ...), custom_call_target="tpu_custom_call" | custom-call | tf_op jit(solution)/shard_map/potential/pallas_call | solution.py:387
  (6 shorter events, 0.0 us)
Async XLA Ops:
  0.6 10.4 %collective-permute-start = (bf16[3,4,128,128]{3,2,1,0:T(8,128)(2,1)}, bf16[3,4,128,128]{3,2,1,0:T(8,128)(2,1)S(1)}, u32[]{:S(2)}, u32[]{:S(2)}) collective-permute-start(bf16[3,4,128,128]{3,2,1,0:T(8,128)(2,1)} %refs_0_.1), channel_id=1, source_target_pairs={{0,4},{1,3},{2,6},{3,1},{4,0},{5,7},{6,2},{7,5},{8,12},{9,11},{10,... | collective-permute-start | bytes 1179656 | tf_op jit(solution)/shard_map/ppermute | solution.py:253
  3.7 7.3 %collective-permute-start.1 = (s32[3,4]{1,0:T(4,128)}, s32[3,4]{1,0:T(4,128)S(1)}, u32[]{:S(2)}, u32[]{:S(2)}) collective-permute-start(s32[3,4]{1,0:T(4,128)} %param.13), channel_id=1, source_target_pairs={{0,4},{1,5},{2,6},{3,7},{4,0},{5,1},{6,2},{7,3},{8,12},{9,13},{10,... | collective-permute-start | bytes 152 | tf_op jit(solution)/shard_map/ppermute | solution.py:248
  3.7 0.7 %copy-start.3 = (s32[12,6]{0,1:T(8,128)S(1)}, s32[12,6]{0,1:T(8,128)}, u32[]{:S(2)}) copy-start(s32[12,6]{0,1:T(8,128)} %param.17) | copy-start | bytes 868
  4.4 4.6 %copy-start = (bf16[3,4,128,128]{3,2,1,0:T(8,128)(2,1)S(1)}, bf16[3,4,128,128]{3,2,1,0:T(8,128)(2,1)}, u32[]{:S(2)}) copy-start(bf16[3,4,128,128]{3,2,1,0:T(8,128)(2,1)} %refs_0_.1) | copy-start | bytes 1179652
  4.4 7.7 %copy-start.4 = (s32[3,4]{1,0:T(4,128)S(1)}, s32[3,4]{1,0:T(4,128)}, u32[]{:S(2)}) copy-start(s32[3,4]{1,0:T(4,128)} %param.13) | copy-start | bytes 148
  9.0 12.1 %collective-permute-start.4 = (bf16[3,4,128,128]{3,2,1,0:T(8,128)(2,1)S(1)}, bf16[3,4,128,128]{3,2,1,0:T(8,128)(2,1)S(1)}, u32[]{:S(2)}, u32[]{:S(2)}) collective-permute-start(bf16[3,4,128,128]{3,2,1,0:T(8,128)(2,1)S(1)} %copy-done), channel_id=1, source_target_pairs={{0,2},{1,5},{2,0},{3,7},{4,6},{5,1},{6,4},{7,3},{8,10},{9,13},{10,... | collective-permute-start | bytes 1179656 | tf_op jit(solution)/shard_map/ppermute | solution.py:253
  11.0 10.2 %collective-permute-start.8 = (bf16[3,4,128,128]{3,2,1,0:T(8,128)(2,1)S(1)}, bf16[3,4,128,128]{3,2,1,0:T(8,128)(2,1)S(1)}, u32[]{:S(2)}, u32[]{:S(2)}) collective-permute-start(bf16[3,4,128,128]{3,2,1,0:T(8,128)(2,1)S(1)} %collective-permute-done.after_hbm.refs_2_), channel_id=1, source_target_pairs={{0,2},{1,5},{2,0},{3,7},{4,6},{5,1},{6,4},{7,3},{8,10},{9,13},{10,... | collective-permute-start | bytes 1179656 | tf_op jit(solution)/shard_map/ppermute | solution.py:253
  11.7 11.8 %collective-permute-start.5 = (bf16[3,4,128,128]{3,2,1,0:T(8,128)(2,1)S(1)}, bf16[3,4,128,128]{3,2,1,0:T(8,128)(2,1)S(1)}, u32[]{:S(2)}, u32[]{:S(2)}) collective-permute-start(bf16[3,4,128,128]{3,2,1,0:T(8,128)(2,1)S(1)} %copy-done), channel_id=1, source_target_pairs={{0,1},{1,0},{2,3},{3,2},{4,5},{5,4},{6,7},{7,6},{8,9},{9,8},{10,11... | collective-permute-start | bytes 1179656 | tf_op jit(solution)/shard_map/ppermute | solution.py:248
  11.7 11.8 %collective-permute-start.6 = (bf16[3,4,128,128]{3,2,1,0:T(8,128)(2,1)S(1)}, bf16[3,4,128,128]{3,2,1,0:T(8,128)(2,1)S(1)}, u32[]{:S(2)}, u32[]{:S(2)}) collective-permute-start(bf16[3,4,128,128]{3,2,1,0:T(8,128)(2,1)S(1)} %collective-permute-done.after_hbm.refs_2_), channel_id=1, source_target_pairs={{0,1},{1,0},{2,3},{3,2},{4,5},{5,4},{6,7},{7,6},{8,9},{9,8},{10,11... | collective-permute-start | bytes 1179656 | tf_op jit(solution)/shard_map/ppermute | solution.py:248
  12.2 11.3 %copy-start.1 = (s32[1,12]{1,0:T(1,128)S(1)}, s32[1,12]{1,0:T(1,128)}, u32[]{:S(2)}) copy-start(s32[1,12]{1,0:T(1,128)} %size_ref.3) | copy-start | bytes 148
  12.2 11.3 %copy-start.2 = (s32[1,12]{1,0:T(1,128)S(1)}, s32[1,12]{1,0:T(1,128)}, u32[]{:S(2)}) copy-start(s32[1,12]{1,0:T(1,128)} %offset_ref.1) | copy-start | bytes 148
  12.2 9.0 %collective-permute-start.2 = (s32[6,4]{1,0:T(8,128)S(1)}, s32[6,4]{1,0:T(8,128)S(1)}, u32[]{:S(2)}, u32[]{:S(2)}) collective-permute-start(s32[6,4]{1,0:T(8,128)S(1)} %pad_add_fusion.2), channel_id=1, source_target_pairs={{0,2},{1,3},{2,0},{3,1},{4,6},{5,7},{6,4},{7,5},{8,10},{9,11},{10,... | collective-permute-start | bytes 296 | tf_op jit(solution)/shard_map/ppermute | solution.py:248
  21.2 2.3 %collective-permute-start.7 = (bf16[3,4,128,128]{3,2,1,0:T(8,128)(2,1)S(1)}, bf16[3,4,128,128]{3,2,1,0:T(8,128)(2,1)S(1)}, u32[]{:S(2)}, u32[]{:S(2)}) collective-permute-start(bf16[3,4,128,128]{3,2,1,0:T(8,128)(2,1)S(1)} %collective-permute-done.4.refs_4_), channel_id=1, source_target_pairs={{0,1},{1,0},{2,3},{3,2},{4,5},{5,4},{6,7},{7,6},{8,9},{9,8},{10,11... | collective-permute-start | bytes 1179656 | tf_op jit(solution)/shard_map/ppermute | solution.py:248
  21.2 2.3 %collective-permute-start.9 = (bf16[3,4,128,128]{3,2,1,0:T(8,128)(2,1)S(1)}, bf16[3,4,128,128]{3,2,1,0:T(8,128)(2,1)S(1)}, u32[]{:S(2)}, u32[]{:S(2)}) collective-permute-start(bf16[3,4,128,128]{3,2,1,0:T(8,128)(2,1)S(1)} %collective-permute-done.8.refs_6_), channel_id=1, source_target_pairs={{0,1},{1,0},{2,3},{3,2},{4,5},{5,4},{6,7},{7,6},{8,9},{9,8},{10,11... | collective-permute-start | bytes 1179656 | tf_op jit(solution)/shard_map/ppermute | solution.py:248
  21.7 1.8 %collective-permute-start.3 = (s32[12,4]{1,0:T(8,128)S(1)}, s32[12,4]{1,0:T(8,128)S(1)}, u32[]{:S(2)}, u32[]{:S(2)}) collective-permute-start(s32[12,4]{1,0:T(8,128)S(1)} %pad_add_fusion.1), channel_id=1, source_target_pairs={{0,1},{1,0},{2,3},{3,2},{4,5},{5,4},{6,7},{7,6},{8,9},{9,8},{10,11... | collective-permute-start | bytes 584 | tf_op jit(solution)/shard_map/ppermute | solution.py:248
  27.6 3.7 %collective-permute-start.10 = (f32[1,32,128]{2,1,0:T(8,128)S(1)}, f32[1,32,128]{2,1,0:T(8,128)S(1)}, u32[]{:S(2)}, u32[]{:S(2)}) collective-permute-start(f32[1,32,128]{2,1,0:T(8,128)S(1)} %bitcast.4), channel_id=1, source_target_pairs={{0,4},{1,5},{2,6},{3,7},{4,0},{5,1},{6,2},{7,3},{8,12},{9,13},{10,... | collective-permute-start | bytes 49160 | tf_op jit(solution)/shard_map/ppermute | solution.py:248
  31.4 3.9 %collective-permute-start.11 = (f32[2,32,128]{2,1,0:T(8,128)S(1)}, f32[2,32,128]{2,1,0:T(8,128)S(1)}, u32[]{:S(2)}, u32[]{:S(2)}) collective-permute-start(f32[2,32,128]{2,1,0:T(8,128)S(1)} %pad_maximum_fusion.2), channel_id=1, source_target_pairs={{0,2},{1,3},{2,0},{3,1},{4,6},{5,7},{6,4},{7,5},{8,10},{9,11},{10,... | collective-permute-start | bytes 98312 | tf_op jit(solution)/shard_map/ppermute | solution.py:248
  35.3 1.3 %collective-permute-start.12 = (f32[4,32,128]{2,1,0:T(8,128)S(1)}, f32[4,32,128]{2,1,0:T(8,128)S(1)}, u32[]{:S(2)}, u32[]{:S(2)}) collective-permute-start(f32[4,32,128]{2,1,0:T(8,128)S(1)} %pad_maximum_fusion.1), channel_id=1, source_target_pairs={{0,1},{1,0},{2,3},{3,2},{4,5},{5,4},{6,7},{7,6},{8,9},{9,8},{10,11... | collective-permute-start | bytes 196616 | tf_op jit(solution)/shard_map/ppermute | solution.py:248
  37.0 4.7 %collective-permute-start.13 = (f32[32,256]{1,0:T(8,128)S(1)}, f32[32,256]{1,0:T(8,128)S(1)}, u32[]{:S(2)}, u32[]{:S(2)}) collective-permute-start(f32[32,256]{1,0:T(8,128)S(1)} %get-tuple-element.41), channel_id=1, source_target_pairs={{0,8},{8,0},{16,24},{24,16},{1,9},{9,1},{17,25},{25,17},{2,10},{10... | collective-permute-start | bytes 98312 | tf_op jit(solution)/shard_map/ppermute | solution.py:248
  39.0 5.8 %collective-permute-start.14 = (f32[32,256]{1,0:T(8,128)S(1)}, f32[32,256]{1,0:T(8,128)S(1)}, u32[]{:S(2)}, u32[]{:S(2)}) collective-permute-start(f32[32,256]{1,0:T(8,128)S(1)} %get-tuple-element.42), channel_id=1, source_target_pairs={{0,24},{8,16},{16,8},{24,0},{1,25},{9,17},{17,9},{25,1},{2,26},{10... | collective-permute-start | bytes 98312 | tf_op jit(solution)/shard_map/ppermute | solution.py:248
  41.5 5.2 %collective-permute-start.15 = (f32[32,256]{1,0:T(8,128)S(1)}, f32[32,256]{1,0:T(8,128)S(1)}, u32[]{:S(2)}, u32[]{:S(2)}) collective-permute-start(f32[32,256]{1,0:T(8,128)S(1)} %get-tuple-element.43), channel_id=1, source_target_pairs={{0,16},{8,24},{16,0},{24,8},{1,17},{9,25},{17,1},{25,9},{2,18},{10... | collective-permute-start | bytes 98312 | tf_op jit(solution)/shard_map/ppermute | solution.py:248

commit v6 on v5

--- a/solution.py
+++ b/solution.py
@@ -174,12 +174,14 @@
     terms_ref[...] = jnp.where(row_id == comps, atom_ref[...].astype(jnp.float32), result)
 
 
-def scatter_kernel(comps, atoms, flip, pieces, own, near_a, near_b, far):
+def scatter_kernel(comps, atoms, flip, *refs):
+    own, near_a, near_b, far = refs[-4:]
+    pieces = [group.at[m] for group in refs[:-4] for m in range(group.shape[0])]
     row_id = lax.broadcasted_iota(jnp.int32, (3 * atoms, LANES), 0)
     total = jnp.zeros((3 * ROWS, 3 * atoms), jnp.float32)
-    for m in range(0, pieces.shape[0], 2):
+    for m in range(0, len(pieces), 2):
         left, right = [], []
-        for values in (pieces[m], pieces[m + 1]):
+        for values in (pieces[m][...], pieces[m + 1][...]):
             chosen = values[comps : comps + 1, :].astype(jnp.int32)
             right.append((row_id == chosen).astype(jnp.float32).astype(jnp.bfloat16))
             left.append(jnp.concatenate(split3(values), axis=0))
@@ -198,12 +200,7 @@
     far[:, atoms:] = sums[:, 2 * atoms :]
 
 
-def potential_kernel(
-    comps, atoms, flip, size_ref, own_ref, near_a_ref, near_b_ref, fa_ref, fb_ref, atom_ref, g_ref,
-    mom_ref, pot_ref,
-):
-    batches, points = pot_ref.shape
-    near = g_ref.shape[0] // batches
+def moments_kernel(atoms, flip, own_ref, near_a_ref, near_b_ref, fa_ref, fb_ref, out_ref):
     own = own_ref[...]
     near_a, near_b = near_a_ref[...], near_b_ref[...]
     if flip:
@@ -212,22 +209,31 @@
         high = jnp.where(odd, near_b, near_a)
     else:
         low, high = near_a, near_b
-    before = fa_ref[:, atoms:] + low[:, :atoms] + own[:, :atoms]
-    here = low[:, atoms:] + own[:, atoms : 2 * atoms] + high[:, :atoms]
-    after = own[:, 2 * atoms :] + high[:, atoms:] + fb_ref[:, :atoms]
+    out_ref[:, :atoms] = fa_ref[:, atoms:] + low[:, :atoms] + own[:, :atoms]
+    out_ref[:, atoms : 2 * atoms] = low[:, atoms:] + own[:, atoms : 2 * atoms] + high[:, :atoms]
+    out_ref[:, 2 * atoms :] = own[:, 2 * atoms :] + high[:, atoms:] + fb_ref[:, :atoms]
+
+
+def potential_kernel(
+    comps, atoms, size_ref, moments_ref, other_ref, atom_ref, g_ref, mom_ref, pot_ref
+):
+    batches, points = pot_ref.shape
+    near = g_ref.shape[0] // batches
+    odd = lax.rem(lax.axis_index("dev"), 2) == 1
+    moments = jnp.where(odd, moments_ref[...], other_ref[...])
+    parts = jnp.concatenate(split3(moments), axis=0)
 
     mine = mom_ref.shape[0]
     want = lax.broadcasted_iota(jnp.int32, (mine, atoms), 0) + lax.axis_index("dev") * mine
     keep = want == lax.broadcasted_iota(jnp.int32, (mine, atoms), 1)
     keep = keep.astype(jnp.float32).astype(jnp.bfloat16)
-    taken = dot(keep, jnp.concatenate(split3(here), axis=0), NT)
+    taken = dot(keep, parts[:, atoms : 2 * atoms], NT)
     taken = taken[:, :ROWS] + taken[:, ROWS : 2 * ROWS] + taken[:, 2 * ROWS :]
     mom_ref[...] = taken[:, :comps]
 
-    moments = jnp.concatenate([before, here, after], axis=1)
     row_id = lax.broadcasted_iota(jnp.int32, (3 * atoms, LANES), 0)
     pick = (row_id == atom_ref[...]).astype(jnp.float32).astype(jnp.bfloat16)
-    got = dot(jnp.concatenate(split3(moments), axis=0), pick)
+    got = dot(parts, pick)
     chosen = got[:ROWS] + got[ROWS : 2 * ROWS] + got[2 * ROWS :]
     chosen = chosen[:comps]
     lane = lax.broadcasted_iota(jnp.int32, (1, points), 1)
@@ -251,6 +257,22 @@
 def turned(value, even, odd):
     count = lax.axis_size("dev")
     return lax.ppermute(value, "dev", [(i, i ^ (odd if i % 2 else even)) for i in range(count)])
+
+
+def among_odd(value, m):
+    count = lax.axis_size("dev")
+    return lax.ppermute(value, "dev", [(i, i ^ m) for i in range(1, count, 2)])
+
+
+def regions_of_odd(value, m):
+    count, regions = lax.axis_size("dev"), lax.axis_size("region")
+    pairs = [(r * count + i, (r ^ m) * count + i) for r in range(regions) for i in range(1, count, 2)]
+    return lax.ppermute(value, ("region", "dev"), pairs)
+
+
+def from_core(value, parity):
+    count = lax.axis_size("dev")
+    return lax.ppermute(value, "dev", [(i, i ^ 1) for i in range(parity, count, 2)])
 
 
 def shifted(value, axis, step):
@@ -321,9 +343,8 @@
         masks = block_mask
         other = crossed(masks, "dev", 4)
         first = turned(density_rows, 4, 2)
-        rows, g = lax.optimization_barrier((density_rows, g))
         first, other, g = lax.optimization_barrier((first, other, g))
-        second = turned(rows, 2, 4)
+        second = turned(density_rows, 2, 4)
         third = turned(first, 2, 4)
         masks = jnp.concatenate([masks, other])
         other = crossed(masks, "dev", 2)
@@ -359,42 +380,50 @@
         *pieces,
     )
 
-    if dev_count == 8:
-        groups = terms[None]
-        for m in (4, 2, 1):
-            groups = jnp.concatenate([groups, crossed(groups, "dev", m)])
-    else:
-        groups = lax.all_gather(terms, "dev", axis=0)
-    flip = region_count == 4
+    small = dev_count == 8 and region_count == 4
+    if small:
+        both = jnp.stack([terms, from_core(terms, 0)])
+        groups = [both] + [among_odd(both, m) for m in (6, 2, 4)]
+    else:
+        groups = [lax.all_gather(terms, "dev", axis=0)]
     own, near_a, near_b, far = pl.pallas_call(
-        functools.partial(scatter_kernel, comps, atoms, flip),
+        functools.partial(scatter_kernel, comps, atoms, small),
         out_shape=tuple(jax.ShapeDtypeStruct((ROWS, n * atoms), f32) for n in (3, 2, 2, 2)),
-        in_specs=[VMEM],
+        in_specs=[VMEM] * len(groups),
         out_specs=(VMEM,) * 4,
         compiler_params=PARAMS,
         name="scatter",
-    )(groups)
-    if flip:
-        far_a = far_b = crossed(far, "region", 2)
-        near_a = crossed(near_a, "region", 1)
-        near_b = crossed(near_b, "region", 3)
+    )(*groups)
+    if small:
+        far_a = far_b = regions_of_odd(far, 2)
+        near_a = regions_of_odd(near_a, 1)
+        near_b = regions_of_odd(near_b, 3)
     else:
         far_a = shifted(far, "region", 2)
         far_b = shifted(far, "region", -2)
         near_a = shifted(near_a, "region", 1)
         near_b = shifted(near_b, "region", -1)
+    moments = pl.pallas_call(
+        functools.partial(moments_kernel, atoms, small),
+        out_shape=jax.ShapeDtypeStruct((ROWS, 3 * atoms), f32),
+        in_specs=[VMEM] * 5,
+        out_specs=VMEM,
+        compiler_params=PARAMS,
+        name="moments",
+    )(own, near_a, near_b, far_a, far_b)
+    other = from_core(moments, 1) if small else moments
 
     moments, potential = pl.pallas_call(
-        functools.partial(potential_kernel, comps, atoms, flip),
+        functools.partial(potential_kernel, comps, atoms),
         out_shape=(
             jax.ShapeDtypeStruct((mine, comps), f32),
             jax.ShapeDtypeStruct((batches, points), f32),
         ),
-        in_specs=[SMEM] + [VMEM] * 7,
+        in_specs=[SMEM] + [VMEM] * 4,
         out_specs=(VMEM, VMEM),
         compiler_params=PARAMS,
         name="potential",
-    )(batch_sizes, own, near_a, near_b, far_a, far_b, atom_rows, g)
+    )(batch_sizes, moments, other, atom_rows, g)
     return (density, moments.T, potential)
 
 

time: 48.8 us -> 60.8 us (1.25)
  waiting for transfers between devices: 15.7 us -> 28.8 us
  starting transfers between devices: 16.9 us -> 15.5 us
    ppermute x0 -> x8, waiting for transfers between devices: none -> 23 us  [the longest x2 22.9 us: from_core(): lax.ppermute(value, 'dev', [(i, i ^ 1) for i in range(parity, count, 2)])]
    ppermute x13 -> x7, waiting for transfers between devices: 15.7 us -> 5.79 us  [crossed(): lax.ppermute(value, axis, [(i, i ^ m) for i in range(lax.axis_size(axis))])]
    ppermute x13 -> x7, starting transfers between devices: 11.2 us -> 2.31 us  [crossed(): lax.ppermute(value, axis, [(i, i ^ m) for i in range(lax.axis_size(axis))])]
    ppermute x0 -> x8, starting transfers between devices: none -> 7.28 us  [the longest x2 3.31 us: from_core(): lax.ppermute(value, 'dev', [(i, i ^ 1) for i in range(parity, count, 2)])]
    pallas_call x2 -> x3, Pallas kernels: 2.25 us -> 2.27 us  [the longest x1 1.88 us: per_device(): pl.pallas_call(functools.partial(potential_kernel, comps, atoms), out_sha...]
  transfers between devices with their start and end apart: 16 -> 18, of which waited for: 7 -> 5; matrix products, arithmetic and copies ran while one was open for 0% -> 0% of each run, Pallas kernels for 15% -> 12%
where the time goes in v6:
time: 60.8 us; the launch traced here: 60.4 us
  waiting for transfers between devices  28.8 us (47%)
  starting transfers between devices  15.5 us (25%)
  Pallas kernels  13.9 us (23%)
  between operations  1.51 us (2%)
  local copies, waits for them, and re-layouts  0.71 us (1%)
    ppermute x2, waiting for transfers between devices, from_core(): lax.ppermute(value, 'dev', [(i, i ^ 1) for i in range(parity, count, 2)])  22.9 us
    ppermute x3, starting transfers between devices, turned(): lax.ppermute(value, 'dev', [(i, i ^ (odd if i % 2 else even)) for i in ra...  5.96 us
    ppermute x7, waiting for transfers between devices, crossed(): lax.ppermute(value, axis, [(i, i ^ m) for i in range(lax.axis_size(axis))])  5.79 us
    pallas_call x1, Pallas kernels, per_device(): pl.pallas_call(field_kernel, out_shape=(pltpu.VMEM((batches * near, comps...  4.56 us
    pallas_call x1, Pallas kernels, per_device(): pl.pallas_call(density_kernel, out_shape=(jax.ShapeDtypeStruct((batches,...  4.12 us
    ppermute x2, starting transfers between devices, from_core(): lax.ppermute(value, 'dev', [(i, i ^ 1) for i in range(parity, count, 2)])  3.31 us
    pallas_call x1, Pallas kernels, turned_basis(): pl.pallas_call(turn_kernel, out_shape=(pltpu.VMEM((batches, near_blocks,...  2.9 us
    ppermute x7, starting transfers between devices, crossed(): lax.ppermute(value, axis, [(i, i ^ m) for i in range(lax.axis_size(axis))])  2.31 us
  transfers between devices with their start and end apart: 18, of which 5 were waited for; matrix products, arithmetic and copies ran while one was open for 0% of the time, Pallas kernels for 12%

profile of v6, /device:TPU:0, one launch (start us, length us, event | category | flops | bytes accessed | tf_op | source)
XLA Modules:
  0.0 60.4 jit_solution(16353484607619718934)
XLA Ops:
  0.6 3.0 %collective-permute-start = (bf16[3,4,128,128]{3,2,1,0:T(8,128)(2,1)}, bf16[3,4,128,128]{3,2,1,0:T(8,128)(2,1)S(1)}, u32[]{:S(2)}, u32[]{:S(2)}) collective-permute-start(bf16[3,4,128,128]{3,2,1,0:T(8,128)(2,1)} %refs_0_.1), channel_id=1, source_target_pairs={{0,4},{1,3},{2,6},{3,1},{4,0},{5,7},{6,2},{7,5},{8,12},{9,11},{10,... | collective-permute-start | bytes 1179656 | tf_op jit(solution)/shard_map/ppermute | solution.py:259
  3.7 1.5 %collective-permute-start.4 = (bf16[3,4,128,128]{3,2,1,0:T(8,128)(2,1)}, bf16[3,4,128,128]{3,2,1,0:T(8,128)(2,1)S(1)}, u32[]{:S(2)}, u32[]{:S(2)}) collective-permute-start(bf16[3,4,128,128]{3,2,1,0:T(8,128)(2,1)} %refs_0_.1), channel_id=1, source_target_pairs={{0,2},{1,5},{2,0},{3,7},{4,6},{5,1},{6,4},{7,3},{8,10},{9,13},{10,... | collective-permute-start | bytes 1179656 | tf_op jit(solution)/shard_map/ppermute | solution.py:259
  5.2 0.5 collective-permute-start.1
  5.7 0.0 copy-start.3
  5.7 0.7 %copy-done.3 = s32[12,6]{0,1:T(8,128)S(1)} copy-done((s32[12,6]{0,1:T(8,128)S(1)}, s32[12,6]{0,1:T(8,128)}, u32[]{:S(2)}) %copy-start.3) | copy-done | bytes 312
  6.4 0.0 copy-start
  6.4 0.0 copy-start.4
  6.4 4.6 %field.1 = (f32[72,25,256]{2,1,0:T(8,128)S(1)}, bf16[72,32,256]{2,1,0:T(8,128)(2,1)S(1)}, s32[1,128]{1,0:T(1,128)S(1)}) custom-call(s32[6,12]{1,0:T(8,128)S(1)} %bitcast.6, f32[16,25]{1,0:T(8,128)} %bitcast.8, f32[12,6,256]{2,1,0:T(8,128)} %radius_hbm.1, bf16[12,6,25,256]{3,2,1,0:T(8,128)(2,1)} %harm_hbm.1), custom_call_target="tpu_custom_call" | custom-call | flops 2000000000 | bytes 8000000 | tf_op jit(solution)/shard_map/field/pallas_call | solution.py:305
  10.9 2.5 %collective-permute-done.1 = s32[3,4]{1,0:T(4,128)S(1)} collective-permute-done((s32[3,4]{1,0:T(4,128)}, s32[3,4]{1,0:T(4,128)S(1)}, u32[]{:S(2)}, u32[]{:S(2)}) %collective-permute-start.1) | collective-permute-done | bytes 80 | tf_op jit(solution)/shard_map/ppermute | solution.py:254
  13.4 0.0 collective-permute-done.after_hbm.refs_2_
  13.4 1.4 %collective-permute-start.8 = (bf16[3,4,128,128]{3,2,1,0:T(8,128)(2,1)S(1)}, bf16[3,4,128,128]{3,2,1,0:T(8,128)(2,1)S(1)}, u32[]{:S(2)}, u32[]{:S(2)}) collective-permute-start(bf16[3,4,128,128]{3,2,1,0:T(8,128)(2,1)S(1)} %collective-permute-done.after_hbm.refs_2_), channel_id=1, source_target_pairs={{0,2},{1,5},{2,0},{3,7},{4,6},{5,1},{6,4},{7,3},{8,10},{9,13},{10,... | collective-permute-start | bytes 1179656 | tf_op jit(solution)/shard_map/ppermute | solution.py:259
  14.9 0.0 copy-done
  14.9 0.8 %collective-permute-start.5 = (bf16[3,4,128,128]{3,2,1,0:T(8,128)(2,1)S(1)}, bf16[3,4,128,128]{3,2,1,0:T(8,128)(2,1)S(1)}, u32[]{:S(2)}, u32[]{:S(2)}) collective-permute-start(bf16[3,4,128,128]{3,2,1,0:T(8,128)(2,1)S(1)} %copy-done), channel_id=1, source_target_pairs={{0,1},{1,0},{2,3},{3,2},{4,5},{5,4},{6,7},{7,6},{8,9},{9,8},{10,11... | collective-permute-start | bytes 1179656 | tf_op jit(solution)/shard_map/ppermute | solution.py:254
  15.7 0.0 collective-permute-start.6
  15.7 0.0 copy-done.4
  15.7 0.0 copy-start.1
  15.7 0.0 copy-start.2
  15.7 0.3 collective-permute-start.2
  16.1 2.9 %turn.1 = (bf16[12,4,128,256]{3,2,1,0:T(8,128)(2,1)S(1)}, f32[12,6,256]{2,1,0:T(8,128)S(1)}) custom-call(bf16[3,4,128,128]{3,2,1,0:T(8,128)(2,1)S(1)} %collective-permute-done.after_hbm.refs_2_, bf16[12,4,256,128]{3,2,1,0:T(8,128)(2,1)} %basis_hbm.1, f32[12,6,256]{2,1,0:T(8,128)} %part_hbm.1), custom_call_target="tpu_custom_call" | custom-call | flops 2000000000 | bytes 8000000 | tf_op jit(solution)/shard_map/turn/pallas_call | solution.py:326
  19.0 2.3 %collective-permute-done.2 = s32[6,4]{1,0:T(8,128)S(1)} collective-permute-done((s32[6,4]{1,0:T(8,128)S(1)}, s32[6,4]{1,0:T(8,128)S(1)}, u32[]{:S(2)}, u32[]{:S(2)}) %collective-permute-start.2) | collective-permute-done | bytes 128 | tf_op jit(solution)/shard_map/ppermute | solution.py:254
  21.3 0.0 collective-permute-done.4.refs_4_
  21.3 0.0 collective-permute-start.7
  21.3 0.0 collective-permute-done.8.refs_6_
  21.3 0.5 collective-permute-start.9
  21.8 0.1 collective-permute-start.3
  22.6 1.0 %collective-permute-done.3 = s32[12,4]{1,0:T(8,128)S(1)} collective-permute-done((s32[12,4]{1,0:T(8,128)S(1)}, s32[12,4]{1,0:T(8,128)S(1)}, u32[]{:S(2)}, u32[]{:S(2)}) %collective-permute-start.3) | collective-permute-done | bytes 224 | tf_op jit(solution)/shard_map/ppermute | solution.py:254
  23.6 0.0 collective-permute-done.5.refs_1_
  23.6 0.0 collective-permute-done.6.refs_3_
  23.6 0.0 collective-permute-done.7.refs_5_
  23.6 0.0 collective-permute-done.9.refs_7_
  23.6 0.0 copy-done.1
  23.6 0.0 copy-done.2
  23.7 4.1 %density.1 = (f32[12,256]{1,0:T(8,128)}, f32[32,128]{1,0:T(8,128)S(1)}) custom-call(s32[1]{0:T(128)S(6)} %copy.23.start_ref, s32[1,12]{1,0:T(1,128)S(1)} %copy-done.2, s32[1,12]{1,0:T(1,128)S(1)} %copy-done.1, s32[24,4]{1,0:T(8,128)S(1)} %pad_add_fusion.mask_ref, s32[1,128]{1,0:T(1,128)S(1)} %get-tuple-element.28.atom_ref, ...), custom_call_target="tpu_custom_call" | custom-call | flops 2000000000 | bytes 6000000 | tf_op jit(solution)/shard_map/density/pallas_call | solution.py:363
  27.8 2.0 %collective-permute-start.10 = (f32[32,128]{1,0:T(8,128)S(1)}, f32[32,128]{1,0:T(8,128)S(1)}, u32[]{:S(2)}, u32[]{:S(2)}) collective-permute-start(f32[32,128]{1,0:T(8,128)S(1)} %get-tuple-element.35), channel_id=1, source_target_pairs={{0,1},{2,3},{4,5},{6,7},{8,9},{10,11},{12,13},{14,15},{16,17},{18,... | collective-permute-start | bytes 49160 | tf_op jit(solution)/shard_map/ppermute | solution.py:275
  29.8 0.8 %collective-permute-done.10 = f32[32,128]{1,0:T(8,128)S(1)} collective-permute-done((f32[32,128]{1,0:T(8,128)S(1)}, f32[32,128]{1,0:T(8,128)S(1)}, u32[]{:S(2)}, u32[]{:S(2)}) %collective-permute-start.10) | collective-permute-done | bytes 16416 | tf_op jit(solution)/shard_map/ppermute | solution.py:275
  30.6 0.7 %collective-permute-start.13 = (f32[2,32,128]{2,1,0:T(8,128)S(1)}, f32[2,32,128]{2,1,0:T(8,128)S(1)}, u32[]{:S(2)}, u32[]{:S(2)}) collective-permute-start(f32[2,32,128]{2,1,0:T(8,128)S(1)} %pad_maximum_fusion.refs_0_), channel_id=1, source_target_pairs={{1,5},{3,7},{5,1},{7,3},{9,13},{11,15},{13,9},{15,11},{17,21},{19,... | collective-permute-start | bytes 98312 | tf_op jit(solution)/shard_map/ppermute | solution.py:264
  31.3 0.7 %collective-permute-start.12 = (f32[2,32,128]{2,1,0:T(8,128)S(1)}, f32[2,32,128]{2,1,0:T(8,128)S(1)}, u32[]{:S(2)}, u32[]{:S(2)}) collective-permute-start(f32[2,32,128]{2,1,0:T(8,128)S(1)} %pad_maximum_fusion.refs_0_), channel_id=1, source_target_pairs={{1,3},{3,1},{5,7},{7,5},{9,11},{11,9},{13,15},{15,13},{17,19},{19,... | collective-permute-start | bytes 98312 | tf_op jit(solution)/shard_map/ppermute | solution.py:264
  32.0 0.7 %collective-permute-start.11 = (f32[2,32,128]{2,1,0:T(8,128)S(1)}, f32[2,32,128]{2,1,0:T(8,128)S(1)}, u32[]{:S(2)}, u32[]{:S(2)}) collective-permute-start(f32[2,32,128]{2,1,0:T(8,128)S(1)} %pad_maximum_fusion.refs_0_), channel_id=1, source_target_pairs={{1,7},{3,5},{5,3},{7,1},{9,15},{11,13},{13,11},{15,9},{17,23},{19,... | collective-permute-start | bytes 98312 | tf_op jit(solution)/shard_map/ppermute | solution.py:264
  32.6 0.0 collective-permute-done.13.refs_3_
  32.6 0.0 collective-permute-done.12.refs_2_
  32.6 0.0 collective-permute-done.11.refs_1_
  32.7 0.4 scatter.1
  33.0 0.7 %collective-permute-start.14 = (f32[32,256]{1,0:T(8,128)S(1)}, f32[32,256]{1,0:T(8,128)S(1)}, u32[]{:S(2)}, u32[]{:S(2)}) collective-permute-start(f32[32,256]{1,0:T(8,128)S(1)} %get-tuple-element.37), channel_id=1, source_target_pairs={{1,9},{3,11},{5,13},{7,15},{9,1},{11,3},{13,5},{15,7},{17,25},{19,... | collective-permute-start | bytes 98312 | tf_op jit(solution)/shard_map/ppermute | solution.py:270
  33.7 0.7 %collective-permute-start.15 = (f32[32,256]{1,0:T(8,128)S(1)}, f32[32,256]{1,0:T(8,128)S(1)}, u32[]{:S(2)}, u32[]{:S(2)}) collective-permute-start(f32[32,256]{1,0:T(8,128)S(1)} %get-tuple-element.38), channel_id=1, source_target_pairs={{1,25},{3,27},{5,29},{7,31},{9,17},{11,19},{13,21},{15,23},{17,9},... | collective-permute-start | bytes 98312 | tf_op jit(solution)/shard_map/ppermute | solution.py:270
  34.4 0.7 %collective-permute-start.16 = (f32[32,256]{1,0:T(8,128)S(1)}, f32[32,256]{1,0:T(8,128)S(1)}, u32[]{:S(2)}, u32[]{:S(2)}) collective-permute-start(f32[32,256]{1,0:T(8,128)S(1)} %get-tuple-element.39), channel_id=1, source_target_pairs={{1,17},{3,19},{5,21},{7,23},{9,25},{11,27},{13,29},{15,31},{17,1},... | collective-permute-start | bytes 98312 | tf_op jit(solution)/shard_map/ppermute | solution.py:270
  35.1 0.0 collective-permute-done.14.near_a_ref
  35.1 0.0 collective-permute-done.15.near_b_ref
  35.1 0.0 collective-permute-done.16.fa_ref.fb_ref
  35.1 1.3 %collective-permute-start.17 = (f32[32,384]{1,0:T(8,128)S(1)}, f32[32,384]{1,0:T(8,128)S(1)}, u32[]{:S(2)}, u32[]{:S(2)}) collective-permute-start(f32[32,384]{1,0:T(8,128)S(1)} %moments.1.moments_ref), channel_id=1, source_target_pairs={{1,0},{3,2},{5,4},{7,6},{9,8},{11,10},{13,12},{15,14},{17,16},{19,... | collective-permute-start | bytes 147464 | tf_op jit(solution)/shard_map/ppermute | solution.py:275
  36.4 22.1 %collective-permute-done.17.other_ref = f32[32,384]{1,0:T(8,128)S(1)} collective-permute-done((f32[32,384]{1,0:T(8,128)S(1)}, f32[32,384]{1,0:T(8,128)S(1)}, u32[]{:S(2)}, u32[]{:S(2)}) %collective-permute-start.17) | collective-permute-done | bytes 49184 | tf_op jit(solution)/shard_map/ppermute | solution.py:275
  58.5 1.9 %potential.1 = (f32[16,25]{1,0:T(8,128)}, f32[12,256]{1,0:T(8,128)}) custom-call(s32[1,12]{1,0:T(1,128)S(1)} %copy-done.1, f32[32,384]{1,0:T(8,128)S(1)} %moments.1.moments_ref, f32[32,384]{1,0:T(8,128)S(1)} %collective-permute-done.17.other_ref, s32[1,128]{1,0:T(1,128)S(1)} %get-tuple-element.28.atom_ref, f32[72,25,256]{2,1,0:T(8,128)S(1)} %get-tuple-element.40.g_ref), custom_call_target="tpu_custom_call" | custom-call | tf_op jit(solution)/shard_map/potential/pallas_call | solution.py:416
  (5 shorter events, 0.1 us)
Async XLA Ops:
  0.6 12.8 %collective-permute-start = (bf16[3,4,128,128]{3,2,1,0:T(8,128)(2,1)}, bf16[3,4,128,128]{3,2,1,0:T(8,128)(2,1)S(1)}, u32[]{:S(2)}, u32[]{:S(2)}) collective-permute-start(bf16[3,4,128,128]{3,2,1,0:T(8,128)(2,1)} %refs_0_.1), channel_id=1, source_target_pairs={{0,4},{1,3},{2,6},{3,1},{4,0},{5,7},{6,2},{7,5},{8,12},{9,11},{10,... | collective-permute-start | bytes 1179656 | tf_op jit(solution)/shard_map/ppermute | solution.py:259
  3.7 17.6 %collective-permute-start.4 = (bf16[3,4,128,128]{3,2,1,0:T(8,128)(2,1)}, bf16[3,4,128,128]{3,2,1,0:T(8,128)(2,1)S(1)}, u32[]{:S(2)}, u32[]{:S(2)}) collective-permute-start(bf16[3,4,128,128]{3,2,1,0:T(8,128)(2,1)} %refs_0_.1), channel_id=1, source_target_pairs={{0,2},{1,5},{2,0},{3,7},{4,6},{5,1},{6,4},{7,3},{8,10},{9,13},{10,... | collective-permute-start | bytes 1179656 | tf_op jit(solution)/shard_map/ppermute | solution.py:259
  5.2 8.3 %collective-permute-start.1 = (s32[3,4]{1,0:T(4,128)}, s32[3,4]{1,0:T(4,128)S(1)}, u32[]{:S(2)}, u32[]{:S(2)}) collective-permute-start(s32[3,4]{1,0:T(4,128)} %param.13), channel_id=1, source_target_pairs={{0,4},{1,5},{2,6},{3,7},{4,0},{5,1},{6,2},{7,3},{8,12},{9,13},{10,... | collective-permute-start | bytes 152 | tf_op jit(solution)/shard_map/ppermute | solution.py:254
  5.7 0.7 %copy-start.3 = (s32[12,6]{0,1:T(8,128)S(1)}, s32[12,6]{0,1:T(8,128)}, u32[]{:S(2)}) copy-start(s32[12,6]{0,1:T(8,128)} %param.17) | copy-start | bytes 868
  6.4 8.5 %copy-start = (bf16[3,4,128,128]{3,2,1,0:T(8,128)(2,1)S(1)}, bf16[3,4,128,128]{3,2,1,0:T(8,128)(2,1)}, u32[]{:S(2)}) copy-start(bf16[3,4,128,128]{3,2,1,0:T(8,128)(2,1)} %refs_0_.1) | copy-start | bytes 1179652
  6.4 9.3 %copy-start.4 = (s32[3,4]{1,0:T(4,128)S(1)}, s32[3,4]{1,0:T(4,128)}, u32[]{:S(2)}) copy-start(s32[3,4]{1,0:T(4,128)} %param.13) | copy-start | bytes 148
  13.4 7.9 %collective-permute-start.8 = (bf16[3,4,128,128]{3,2,1,0:T(8,128)(2,1)S(1)}, bf16[3,4,128,128]{3,2,1,0:T(8,128)(2,1)S(1)}, u32[]{:S(2)}, u32[]{:S(2)}) collective-permute-start(bf16[3,4,128,128]{3,2,1,0:T(8,128)(2,1)S(1)} %collective-permute-done.after_hbm.refs_2_), channel_id=1, source_target_pairs={{0,2},{1,5},{2,0},{3,7},{4,6},{5,1},{6,4},{7,3},{8,10},{9,13},{10,... | collective-permute-start | bytes 1179656 | tf_op jit(solution)/shard_map/ppermute | solution.py:259
  14.9 8.7 %collective-permute-start.5 = (bf16[3,4,128,128]{3,2,1,0:T(8,128)(2,1)S(1)}, bf16[3,4,128,128]{3,2,1,0:T(8,128)(2,1)S(1)}, u32[]{:S(2)}, u32[]{:S(2)}) collective-permute-start(bf16[3,4,128,128]{3,2,1,0:T(8,128)(2,1)S(1)} %copy-done), channel_id=1, source_target_pairs={{0,1},{1,0},{2,3},{3,2},{4,5},{5,4},{6,7},{7,6},{8,9},{9,8},{10,11... | collective-permute-start | bytes 1179656 | tf_op jit(solution)/shard_map/ppermute | solution.py:254
  15.7 7.9 %collective-permute-start.6 = (bf16[3,4,128,128]{3,2,1,0:T(8,128)(2,1)S(1)}, bf16[3,4,128,128]{3,2,1,0:T(8,128)(2,1)S(1)}, u32[]{:S(2)}, u32[]{:S(2)}) collective-permute-start(bf16[3,4,128,128]{3,2,1,0:T(8,128)(2,1)S(1)} %collective-permute-done.after_hbm.refs_2_), channel_id=1, source_target_pairs={{0,1},{1,0},{2,3},{3,2},{4,5},{5,4},{6,7},{7,6},{8,9},{9,8},{10,11... | collective-permute-start | bytes 1179656 | tf_op jit(solution)/shard_map/ppermute | solution.py:254
  15.7 7.9 %copy-start.1 = (s32[1,12]{1,0:T(1,128)S(1)}, s32[1,12]{1,0:T(1,128)}, u32[]{:S(2)}) copy-start(s32[1,12]{1,0:T(1,128)} %size_ref.3) | copy-start | bytes 148
  15.7 7.9 %copy-start.2 = (s32[1,12]{1,0:T(1,128)S(1)}, s32[1,12]{1,0:T(1,128)}, u32[]{:S(2)}) copy-start(s32[1,12]{1,0:T(1,128)} %offset_ref.1) | copy-start | bytes 148
  15.7 5.6 %collective-permute-start.2 = (s32[6,4]{1,0:T(8,128)S(1)}, s32[6,4]{1,0:T(8,128)S(1)}, u32[]{:S(2)}, u32[]{:S(2)}) collective-permute-start(s32[6,4]{1,0:T(8,128)S(1)} %pad_add_fusion.2), channel_id=1, source_target_pairs={{0,2},{1,3},{2,0},{3,1},{4,6},{5,7},{6,4},{7,5},{8,10},{9,11},{10,... | collective-permute-start | bytes 296 | tf_op jit(solution)/shard_map/ppermute | solution.py:254
  21.3 2.3 %collective-permute-start.7 = (bf16[3,4,128,128]{3,2,1,0:T(8,128)(2,1)S(1)}, bf16[3,4,128,128]{3,2,1,0:T(8,128)(2,1)S(1)}, u32[]{:S(2)}, u32[]{:S(2)}) collective-permute-start(bf16[3,4,128,128]{3,2,1,0:T(8,128)(2,1)S(1)} %collective-permute-done.4.refs_4_), channel_id=1, source_target_pairs={{0,1},{1,0},{2,3},{3,2},{4,5},{5,4},{6,7},{7,6},{8,9},{9,8},{10,11... | collective-permute-start | bytes 1179656 | tf_op jit(solution)/shard_map/ppermute | solution.py:254
  21.3 2.3 %collective-permute-start.9 = (bf16[3,4,128,128]{3,2,1,0:T(8,128)(2,1)S(1)}, bf16[3,4,128,128]{3,2,1,0:T(8,128)(2,1)S(1)}, u32[]{:S(2)}, u32[]{:S(2)}) collective-permute-start(bf16[3,4,128,128]{3,2,1,0:T(8,128)(2,1)S(1)} %collective-permute-done.8.refs_6_), channel_id=1, source_target_pairs={{0,1},{1,0},{2,3},{3,2},{4,5},{5,4},{6,7},{7,6},{8,9},{9,8},{10,11... | collective-permute-start | bytes 1179656 | tf_op jit(solution)/shard_map/ppermute | solution.py:254
  21.8 1.8 %collective-permute-start.3 = (s32[12,4]{1,0:T(8,128)S(1)}, s32[12,4]{1,0:T(8,128)S(1)}, u32[]{:S(2)}, u32[]{:S(2)}) collective-permute-start(s32[12,4]{1,0:T(8,128)S(1)} %pad_add_fusion.1), channel_id=1, source_target_pairs={{0,1},{1,0},{2,3},{3,2},{4,5},{5,4},{6,7},{7,6},{8,9},{9,8},{10,11... | collective-permute-start | bytes 584 | tf_op jit(solution)/shard_map/ppermute | solution.py:254
  27.8 2.8 %collective-permute-start.10 = (f32[32,128]{1,0:T(8,128)S(1)}, f32[32,128]{1,0:T(8,128)S(1)}, u32[]{:S(2)}, u32[]{:S(2)}) collective-permute-start(f32[32,128]{1,0:T(8,128)S(1)} %get-tuple-element.35), channel_id=1, source_target_pairs={{0,1},{2,3},{4,5},{6,7},{8,9},{10,11},{12,13},{14,15},{16,17},{18,... | collective-permute-start | bytes 49160 | tf_op jit(solution)/shard_map/ppermute | solution.py:275
  30.6 2.0 %collective-permute-start.13 = (f32[2,32,128]{2,1,0:T(8,128)S(1)}, f32[2,32,128]{2,1,0:T(8,128)S(1)}, u32[]{:S(2)}, u32[]{:S(2)}) collective-permute-start(f32[2,32,128]{2,1,0:T(8,128)S(1)} %pad_maximum_fusion.refs_0_), channel_id=1, source_target_pairs={{1,5},{3,7},{5,1},{7,3},{9,13},{11,15},{13,9},{15,11},{17,21},{19,... | collective-permute-start | bytes 98312 | tf_op jit(solution)/shard_map/ppermute | solution.py:264
  31.3 1.4 %collective-permute-start.12 = (f32[2,32,128]{2,1,0:T(8,128)S(1)}, f32[2,32,128]{2,1,0:T(8,128)S(1)}, u32[]{:S(2)}, u32[]{:S(2)}) collective-permute-start(f32[2,32,128]{2,1,0:T(8,128)S(1)} %pad_maximum_fusion.refs_0_), channel_id=1, source_target_pairs={{1,3},{3,1},{5,7},{7,5},{9,11},{11,9},{13,15},{15,13},{17,19},{19,... | collective-permute-start | bytes 98312 | tf_op jit(solution)/shard_map/ppermute | solution.py:264
  32.0 0.7 %collective-permute-start.11 = (f32[2,32,128]{2,1,0:T(8,128)S(1)}, f32[2,32,128]{2,1,0:T(8,128)S(1)}, u32[]{:S(2)}, u32[]{:S(2)}) collective-permute-start(f32[2,32,128]{2,1,0:T(8,128)S(1)} %pad_maximum_fusion.refs_0_), channel_id=1, source_target_pairs={{1,7},{3,5},{5,3},{7,1},{9,15},{11,13},{13,11},{15,9},{17,23},{19,... | collective-permute-start | bytes 98312 | tf_op jit(solution)/shard_map/ppermute | solution.py:264
  33.0 2.0 %collective-permute-start.14 = (f32[32,256]{1,0:T(8,128)S(1)}, f32[32,256]{1,0:T(8,128)S(1)}, u32[]{:S(2)}, u32[]{:S(2)}) collective-permute-start(f32[32,256]{1,0:T(8,128)S(1)} %get-tuple-element.37), channel_id=1, source_target_pairs={{1,9},{3,11},{5,13},{7,15},{9,1},{11,3},{13,5},{15,7},{17,25},{19,... | collective-permute-start | bytes 98312 | tf_op jit(solution)/shard_map/ppermute | solution.py:270
  33.7 1.4 %collective-permute-start.15 = (f32[32,256]{1,0:T(8,128)S(1)}, f32[32,256]{1,0:T(8,128)S(1)}, u32[]{:S(2)}, u32[]{:S(2)}) collective-permute-start(f32[32,256]{1,0:T(8,128)S(1)} %get-tuple-element.38), channel_id=1, source_target_pairs={{1,25},{3,27},{5,29},{7,31},{9,17},{11,19},{13,21},{15,23},{17,9},... | collective-permute-start | bytes 98312 | tf_op jit(solution)/shard_map/ppermute | solution.py:270
  34.4 0.7 %collective-permute-start.16 = (f32[32,256]{1,0:T(8,128)S(1)}, f32[32,256]{1,0:T(8,128)S(1)}, u32[]{:S(2)}, u32[]{:S(2)}) collective-permute-start(f32[32,256]{1,0:T(8,128)S(1)} %get-tuple-element.39), channel_id=1, source_target_pairs={{1,17},{3,19},{5,21},{7,23},{9,25},{11,27},{13,29},{15,31},{17,1},... | collective-permute-start | bytes 98312 | tf_op jit(solution)/shard_map/ppermute | solution.py:270
  35.1 23.4 %collective-permute-start.17 = (f32[32,384]{1,0:T(8,128)S(1)}, f32[32,384]{1,0:T(8,128)S(1)}, u32[]{:S(2)}, u32[]{:S(2)}) collective-permute-start(f32[32,384]{1,0:T(8,128)S(1)} %moments.1.moments_ref), channel_id=1, source_target_pairs={{1,0},{3,2},{5,4},{7,6},{9,8},{11,10},{13,12},{15,14},{17,16},{19,... | collective-permute-start | bytes 147464 | tf_op jit(solution)/shard_map/ppermute | solution.py:275

commit v7 on v6

--- a/solution.py
+++ b/solution.py
@@ -8,7 +8,6 @@
 
 EVEN_OWNERS = (0, 1, 4, 3, 2, 5, 6, 7)
 ODD_OWNERS = (0, 1, 2, 5, 4, 3, 6, 7)
-DOUBLED = (0, 4, 2, 6, 1, 5, 3, 7)
 LANES = 128
 ROWS = 32
 SLOT = 8
@@ -44,8 +43,26 @@
     return jnp.where(distance < 1.0, inner, jnp.where(distance < 2.0, outer, 0.0))
 
 
+def mask_kernel(mask_hbm, rows_hbm, out_ref, mask, rows, sems):
+    stored, band = rows.shape[:2]
+    fetch = pltpu.make_async_copy(mask_hbm, mask, sems.at[stored])
+    copies = [
+        pltpu.make_async_copy(rows_hbm.at[t], rows.at[t], sems.at[t]) for t in range(stored)
+    ]
+    fetch.start()
+    for copy in copies:
+        copy.start()
+    fetch.wait()
+    factors = mask[...].astype(jnp.float32)
+    for t, copy in enumerate(copies):
+        copy.wait()
+        for k in range(band):
+            factor = jnp.broadcast_to(factors[t : t + 1, k : k + 1], rows.shape[2:])
+            out_ref[t, k] = rows[t, k] * factor.astype(jnp.bfloat16)
+
+
 def field_kernel(
-    near_ref, table_hbm, radius_hbm, harm_hbm,
+    after_hbm, near_ref, table_hbm, radius_hbm, harm_hbm,
     g_ref, hpad_ref, atom_ref, table_ref, radius_ref, harm_ref, sems,
 ):
     batches, near, comps, points = harm_ref.shape
@@ -104,7 +121,7 @@
     copies[2].wait()
 
 
-def density_kernel(start_ref, offset_ref, size_ref, mask_ref, atom_ref, phit_ref, part_ref, hpad_ref, *refs):
+def density_kernel(start_ref, offset_ref, size_ref, atom_ref, phit_ref, part_ref, hpad_ref, *refs):
     dens_ref, terms_ref, window_ref, w_ref = refs[-4:]
     pieces = refs[:-4]
     owners = window_ref.shape[0]
@@ -114,23 +131,17 @@
         me = lax.axis_index("dev")
         odd = lax.rem(me, 2) == 1
         held = [
-            (
-                piece,
-                lax.bitwise_xor(me, jnp.where(odd, b, a)),
-                jnp.where(odd, DOUBLED.index(b), DOUBLED.index(a)),
-            )
+            (piece, lax.bitwise_xor(me, jnp.where(odd, b, a)))
             for piece, a, b in zip(pieces, EVEN_OWNERS, ODD_OWNERS)
         ]
     else:
-        held = [(pieces[0].at[owner], owner, owner) for owner in range(owners)]
-    stored, band = held[0][0].shape[:2]
+        held = [(pieces[0].at[owner], owner) for owner in range(owners)]
+    stored = held[0][0].shape[0]
     start = start_ref[0]
-    for piece, owner, at in held:
+    for piece, owner in held:
         ahead = lax.rem(owner - start + stored * owners, owners)
         row = lax.rem(start + ahead, stored * owners) // owners
-        for k in range(band):
-            factor = jnp.full((width, width), mask_ref[at * stored + row, k].astype(jnp.float32))
-            window_ref[ahead, k] = piece[row, k] * factor.astype(jnp.bfloat16)
+        window_ref[ahead] = piece[row]
     w_ref[...] = jnp.zeros(w_ref.shape, w_ref.dtype)
     lane = lax.broadcasted_iota(jnp.int32, (1, points), 1)
     zero = jnp.zeros((width, width), jnp.bfloat16)
@@ -261,18 +272,17 @@
 
 def among_odd(value, m):
     count = lax.axis_size("dev")
-    return lax.ppermute(value, "dev", [(i, i ^ m) for i in range(1, count, 2)])
+    return lax.ppermute(value, "dev", [(i, i ^ m if i % 2 else i) for i in range(count)])
 
 
 def regions_of_odd(value, m):
     count, regions = lax.axis_size("dev"), lax.axis_size("region")
-    pairs = [(r * count + i, (r ^ m) * count + i) for r in range(regions) for i in range(1, count, 2)]
+    pairs = [
+        (r * count + i, (r ^ m if i % 2 else r) * count + i)
+        for r in range(regions)
+        for i in range(count)
+    ]
     return lax.ppermute(value, ("region", "dev"), pairs)
-
-
-def from_core(value, parity):
-    count = lax.axis_size("dev")
-    return lax.ppermute(value, "dev", [(i, i ^ 1) for i in range(parity, count, 2)])
 
 
 def shifted(value, axis, step):
@@ -302,6 +312,20 @@
     atoms = mine * dev_count
     f32, bf16 = jnp.float32, jnp.bfloat16
 
+    masked = pl.pallas_call(
+        mask_kernel,
+        out_shape=pltpu.VMEM(density_rows.shape, bf16),
+        in_specs=[HBM, HBM],
+        out_specs=VMEM,
+        scratch_shapes=[
+            pltpu.VMEM(block_mask.shape, jnp.int32),
+            pltpu.VMEM(density_rows.shape, bf16),
+            pltpu.SemaphoreType.DMA((blocks_dev + 1,)),
+        ],
+        compiler_params=PARAMS,
+        name="mask",
+    )(*held_in_hbm(block_mask, density_rows))
+
     g, hpad, atom_rows = pl.pallas_call(
         field_kernel,
         out_shape=(
@@ -309,7 +333,7 @@
             pltpu.VMEM((batches * near, ROWS, points), bf16),
             pltpu.VMEM((1, LANES), jnp.int32),
         ),
-        in_specs=[SMEM] + [HBM] * 3,
+        in_specs=[HBM, SMEM] + [HBM] * 3,
         out_specs=(VMEM,) * 3,
         scratch_shapes=[
             pltpu.VMEM(radial_table.shape[::-1], f32),
@@ -320,7 +344,7 @@
         compiler_params=WIDE,
         cost_estimate=pl.CostEstimate(flops=2_000_000_000, bytes_accessed=8_000_000, transcendentals=0),
         name="field",
-    )(atom_near.T, *held_in_hbm(radial_table.T, radius, harmonics))
+    )(masked, atom_near.T, *held_in_hbm(radial_table.T, radius, harmonics))
 
     def turned_basis(after):
         return pl.pallas_call(
@@ -339,26 +363,16 @@
             name="turn",
         )(after, *held_in_hbm(basis_values, partition))
 
+    phit, weights = turned_basis(g)
     if dev_count == 8:
-        masks = block_mask
-        other = crossed(masks, "dev", 4)
-        first = turned(density_rows, 4, 2)
-        first, other, g = lax.optimization_barrier((first, other, g))
-        second = turned(density_rows, 2, 4)
+        first = turned(masked, 4, 2)
+        second = turned(masked, 2, 4)
+        first, phit = lax.optimization_barrier((first, phit))
         third = turned(first, 2, 4)
-        masks = jnp.concatenate([masks, other])
-        other = crossed(masks, "dev", 2)
-        phit, weights = turned_basis(first)
-        other, phit = lax.optimization_barrier((other, phit))
-        second, phit = lax.optimization_barrier((second, phit))
-        masks = jnp.concatenate([masks, other])
-        masks = jnp.concatenate([masks, crossed(masks, "dev", 1)])
-        sent = (density_rows, first, second, third)
+        sent = (masked, first, second, third)
         pieces = [piece for value in sent for piece in (value, crossed(value, "dev", 1))]
     else:
-        phit, weights = turned_basis(density_rows)
-        pieces = [lax.all_gather(density_rows, "dev", axis=0)]
-        masks = lax.all_gather(block_mask, "dev", axis=0, tiled=True)
+        pieces = [lax.all_gather(masked, "dev", axis=0)]
 
     density, terms = pl.pallas_call(
         density_kernel,
@@ -366,7 +380,7 @@
             jax.ShapeDtypeStruct((batches, points), f32),
             jax.ShapeDtypeStruct((ROWS, LANES), f32),
         ),
-        in_specs=[SMEM] * 4 + [VMEM] * (4 + len(pieces)),
+        in_specs=[SMEM] * 3 + [VMEM] * (4 + len(pieces)),
         out_specs=(VMEM, VMEM),
         scratch_shapes=[
             pltpu.VMEM((dev_count, band, width, width), bf16),
@@ -376,13 +390,13 @@
         cost_estimate=pl.CostEstimate(flops=2_000_000_000, bytes_accessed=6_000_000, transcendentals=0),
         name="density",
     )(
-        window_start, batch_offsets, batch_sizes, masks, atom_rows, phit, weights, hpad,
+        window_start, batch_offsets, batch_sizes, atom_rows, phit, weights, hpad,
         *pieces,
     )
 
     small = dev_count == 8 and region_count == 4
     if small:
-        both = jnp.stack([terms, from_core(terms, 0)])
+        both = jnp.stack([terms, crossed(terms, "dev", 1)])
         groups = [both] + [among_odd(both, m) for m in (6, 2, 4)]
     else:
         groups = [lax.all_gather(terms, "dev", axis=0)]
@@ -411,7 +425,7 @@
         compiler_params=PARAMS,
         name="moments",
     )(own, near_a, near_b, far_a, far_b)
-    other = from_core(moments, 1) if small else moments
+    other = crossed(moments, "dev", 1) if small else moments
 
     moments, potential = pl.pallas_call(
         functools.partial(potential_kernel, comps, atoms),

time: 60.8 us -> 57.8 us (0.951)
  waiting for transfers between devices: 28.8 us -> 9.11 us
  starting transfers between devices: 15.5 us -> 31.4 us
  Pallas kernels: 13.9 us -> 14.8 us
    ppermute x5 -> x3, waiting for transfers between devices: 23 us -> 0.01 us  [among_odd(): lax.ppermute(value, 'dev', [(i, i ^ m if i % 2 else i) for i in range(cou...]
    ppermute x7 -> x6, starting transfers between devices: 2.31 us -> 21.7 us  [crossed(): lax.ppermute(value, axis, [(i, i ^ m) for i in range(lax.axis_size(axis))])]
    ppermute x3, waiting for transfers between devices: 0.01 us -> 6.13 us  [turned(): lax.ppermute(value, 'dev', [(i, i ^ (odd if i % 2 else even)) for i in ra...]
    ppermute x5 -> x3, starting transfers between devices: 5.29 us -> 1.98 us  [among_odd(): lax.ppermute(value, 'dev', [(i, i ^ m if i % 2 else i) for i in range(cou...]
    ppermute x7 -> x6, waiting for transfers between devices: 5.79 us -> 2.97 us  [crossed(): lax.ppermute(value, axis, [(i, i ^ m) for i in range(lax.axis_size(axis))])]
    pallas_call x0 -> x1, Pallas kernels: none -> 1.31 us  [per_device(): pl.pallas_call(mask_kernel, out_shape=pltpu.VMEM(density_rows.shape, bf16...]
  transfers between devices with their start and end apart: 18 -> 15, of which waited for: 5 -> 4; matrix products, arithmetic and copies ran while one was open for 0% -> 0% of each run, Pallas kernels for 12% -> 13%
where the time goes in v7:
time: 57.8 us; the launch traced here: 57.4 us
  starting transfers between devices  31.4 us (54%)
  Pallas kernels  14.8 us (26%)
  waiting for transfers between devices  9.11 us (16%)
  between operations  1.47 us (3%)
  local copies, waits for them, and re-layouts  0.7 us (1%)
    ppermute x6, starting transfers between devices, crossed(): lax.ppermute(value, axis, [(i, i ^ m) for i in range(lax.axis_size(axis))])  21.7 us
    ppermute x3, waiting for transfers between devices, turned(): lax.ppermute(value, 'dev', [(i, i ^ (odd if i % 2 else even)) for i in ra...  6.13 us
    ppermute x3, starting transfers between devices, turned(): lax.ppermute(value, 'dev', [(i, i ^ (odd if i % 2 else even)) for i in ra...  5.72 us
    pallas_call x1, Pallas kernels, per_device(): pl.pallas_call(field_kernel, out_shape=(pltpu.VMEM((batches * near, comps...  4.56 us
    pallas_call x1, Pallas kernels, per_device(): pl.pallas_call(density_kernel, out_shape=(jax.ShapeDtypeStruct((batches,...  3.74 us
    ppermute x6, waiting for transfers between devices, crossed(): lax.ppermute(value, axis, [(i, i ^ m) for i in range(lax.axis_size(axis))])  2.97 us
    pallas_call x1, Pallas kernels, turned_basis(): pl.pallas_call(turn_kernel, out_shape=(pltpu.VMEM((batches, near_blocks,...  2.91 us
    ppermute x3, starting transfers between devices, regions_of_odd(): return lax.ppermute(value, ('region', 'dev'), pairs)  1.99 us
  transfers between devices with their start and end apart: 15, of which 4 were waited for; matrix products, arithmetic and copies ran while one was open for 0% of the time, Pallas kernels for 13%

profile of v7, /device:TPU:0, one launch (start us, length us, event | category | flops | bytes accessed | tf_op | source)
XLA Modules:
  0.0 57.4 jit_solution(241975308984745741)
XLA Ops:
  0.6 1.3 %mask.1.after_hbm.refs_0_ = bf16[3,4,128,128]{3,2,1,0:T(8,128)(2,1)S(1)} custom-call(s32[3,4]{1,0:T(4,128)} %mask_hbm.1, bf16[3,4,128,128]{3,2,1,0:T(8,128)(2,1)} %rows_hbm.1), custom_call_target="tpu_custom_call" | custom-call | tf_op jit(solution)/shard_map/mask/pallas_call | solution.py:315
  1.9 3.0 %collective-permute-start = (bf16[3,4,128,128]{3,2,1,0:T(8,128)(2,1)S(1)}, bf16[3,4,128,128]{3,2,1,0:T(8,128)(2,1)S(1)}, u32[]{:S(2)}, u32[]{:S(2)}) collective-permute-start(bf16[3,4,128,128]{3,2,1,0:T(8,128)(2,1)S(1)} %mask.1.after_hbm.refs_0_), channel_id=1, source_target_pairs={{0,4},{1,3},{2,6},{3,1},{4,0},{5,7},{6,2},{7,5},{8,12},{9,11},{10,... | collective-permute-start | bytes 1179656 | tf_op jit(solution)/shard_map/ppermute | solution.py:270
  5.0 1.5 %collective-permute-start.3 = (bf16[3,4,128,128]{3,2,1,0:T(8,128)(2,1)S(1)}, bf16[3,4,128,128]{3,2,1,0:T(8,128)(2,1)S(1)}, u32[]{:S(2)}, u32[]{:S(2)}) collective-permute-start(bf16[3,4,128,128]{3,2,1,0:T(8,128)(2,1)S(1)} %mask.1.after_hbm.refs_0_), channel_id=1, source_target_pairs={{0,2},{1,5},{2,0},{3,7},{4,6},{5,1},{6,4},{7,3},{8,10},{9,13},{10,... | collective-permute-start | bytes 1179656 | tf_op jit(solution)/shard_map/ppermute | solution.py:270
  6.5 0.0 copy-start.2
  6.5 0.7 %copy-done.2 = s32[12,6]{0,1:T(8,128)S(1)} copy-done((s32[12,6]{0,1:T(8,128)S(1)}, s32[12,6]{0,1:T(8,128)}, u32[]{:S(2)}) %copy-start.2) | copy-done | bytes 312
  7.2 4.6 %field.1 = (f32[72,25,256]{2,1,0:T(8,128)S(1)}, bf16[72,32,256]{2,1,0:T(8,128)(2,1)S(1)}, s32[1,128]{1,0:T(1,128)S(1)}) custom-call(bf16[3,4,128,128]{3,2,1,0:T(8,128)(2,1)S(1)} %mask.1.after_hbm.refs_0_, s32[6,12]{1,0:T(8,128)S(1)} %bitcast.6, f32[16,25]{1,0:T(8,128)} %bitcast.8, f32[12,6,256]{2,1,0:T(8,128)} %radius_hbm.1, bf16[12,6,25,256]{3,2,1,0:T(8,128)(2,1)} %harm_hbm.1), custom_call_target="tpu_custom_call" | custom-call | flops 2000000000 | bytes 8000000 | tf_op jit(solution)/shard_map/field/pallas_call | solution.py:329
  11.7 0.0 copy-start
  11.7 0.0 copy-start.1
  11.8 2.9 %turn.1 = (bf16[12,4,128,256]{3,2,1,0:T(8,128)(2,1)S(1)}, f32[12,6,256]{2,1,0:T(8,128)S(1)}) custom-call(f32[72,25,256]{2,1,0:T(8,128)S(1)} %get-tuple-element.19.after_hbm.g_ref, bf16[12,4,256,128]{3,2,1,0:T(8,128)(2,1)} %basis_hbm.1, f32[12,6,256]{2,1,0:T(8,128)} %part_hbm.1), custom_call_target="tpu_custom_call" | custom-call | flops 2000000000 | bytes 8000000 | tf_op jit(solution)/shard_map/turn/pallas_call | solution.py:350
  14.7 0.0 collective-permute-done.refs_2_
  14.7 1.2 %collective-permute-start.5 = (bf16[3,4,128,128]{3,2,1,0:T(8,128)(2,1)S(1)}, bf16[3,4,128,128]{3,2,1,0:T(8,128)(2,1)S(1)}, u32[]{:S(2)}, u32[]{:S(2)}) collective-permute-start(bf16[3,4,128,128]{3,2,1,0:T(8,128)(2,1)S(1)} %collective-permute-done.refs_2_), channel_id=1, source_target_pairs={{0,2},{1,5},{2,0},{3,7},{4,6},{5,1},{6,4},{7,3},{8,10},{9,13},{10,... | collective-permute-start | bytes 1179656 | tf_op jit(solution)/shard_map/ppermute | solution.py:270
  15.9 0.0 collective-permute-start.1
  15.9 0.5 collective-permute-start.2
  16.4 0.0 collective-permute-done.3.refs_4_
  16.4 0.0 collective-permute-start.4
  16.4 6.1 %collective-permute-done.5.refs_6_ = bf16[3,4,128,128]{3,2,1,0:T(8,128)(2,1)S(1)} collective-permute-done((bf16[3,4,128,128]{3,2,1,0:T(8,128)(2,1)S(1)}, bf16[3,4,128,128]{3,2,1,0:T(8,128)(2,1)S(1)}, u32[]{:S(2)}, u32[]{:S(2)}) %collective-permute-start.5) | collective-permute-done | bytes 393248 | tf_op jit(solution)/shard_map/ppermute | solution.py:270
  22.5 0.0 collective-permute-start.6
  23.2 0.0 collective-permute-done.1.refs_1_
  23.2 0.0 collective-permute-done.4.refs_5_
  23.2 0.0 collective-permute-done.2.refs_3_
  23.2 1.0 %collective-permute-done.6.refs_7_ = bf16[3,4,128,128]{3,2,1,0:T(8,128)(2,1)S(1)} collective-permute-done((bf16[3,4,128,128]{3,2,1,0:T(8,128)(2,1)S(1)}, bf16[3,4,128,128]{3,2,1,0:T(8,128)(2,1)S(1)}, u32[]{:S(2)}, u32[]{:S(2)}) %collective-permute-start.6) | collective-permute-done | bytes 393248 | tf_op jit(solution)/shard_map/ppermute | solution.py:265
  24.2 0.0 copy-done
  24.3 0.0 copy-done.1
  24.3 3.7 %density.1 = (f32[12,256]{1,0:T(8,128)}, f32[32,128]{1,0:T(8,128)S(1)}) custom-call(s32[1]{0:T(128)S(6)} %copy.14.start_ref, s32[1,12]{1,0:T(1,128)S(1)} %copy-done.1, s32[1,12]{1,0:T(1,128)S(1)} %copy-done, s32[1,128]{1,0:T(1,128)S(1)} %get-tuple-element.18.atom_ref, bf16[12,4,128,256]{3,2,1,0:T(8,128)(2,1)S(1)} %get-tuple-element.21.phit_ref, ...), custom_call_target="tpu_custom_call" | custom-call | flops 2000000000 | bytes 6000000 | tf_op jit(solution)/shard_map/density/pallas_call | solution.py:377
  28.0 0.1 collective-permute-start.7
  28.1 1.0 %collective-permute-done.7 = f32[32,128]{1,0:T(8,128)S(1)} collective-permute-done((f32[32,128]{1,0:T(8,128)S(1)}, f32[32,128]{1,0:T(8,128)S(1)}, u32[]{:S(2)}, u32[]{:S(2)}) %collective-permute-start.7) | collective-permute-done | bytes 16416 | tf_op jit(solution)/shard_map/ppermute | solution.py:265
  29.2 0.7 %collective-permute-start.10 = (f32[2,32,128]{2,1,0:T(8,128)S(1)}, f32[2,32,128]{2,1,0:T(8,128)S(1)}, u32[]{:S(2)}, u32[]{:S(2)}) collective-permute-start(f32[2,32,128]{2,1,0:T(8,128)S(1)} %pad_maximum_fusion.refs_0_), channel_id=1, source_target_pairs={{0,0},{1,5},{2,2},{3,7},{4,4},{5,1},{6,6},{7,3},{8,8},{9,13},{10,1... | collective-permute-start | bytes 98312 | tf_op jit(solution)/shard_map/ppermute | solution.py:275
  29.8 0.7 %collective-permute-start.9 = (f32[2,32,128]{2,1,0:T(8,128)S(1)}, f32[2,32,128]{2,1,0:T(8,128)S(1)}, u32[]{:S(2)}, u32[]{:S(2)}) collective-permute-start(f32[2,32,128]{2,1,0:T(8,128)S(1)} %pad_maximum_fusion.refs_0_), channel_id=1, source_target_pairs={{0,0},{1,3},{2,2},{3,1},{4,4},{5,7},{6,6},{7,5},{8,8},{9,11},{10,1... | collective-permute-start | bytes 98312 | tf_op jit(solution)/shard_map/ppermute | solution.py:275
  30.5 0.7 %collective-permute-start.8 = (f32[2,32,128]{2,1,0:T(8,128)S(1)}, f32[2,32,128]{2,1,0:T(8,128)S(1)}, u32[]{:S(2)}, u32[]{:S(2)}) collective-permute-start(f32[2,32,128]{2,1,0:T(8,128)S(1)} %pad_maximum_fusion.refs_0_), channel_id=1, source_target_pairs={{0,0},{1,7},{2,2},{3,5},{4,4},{5,3},{6,6},{7,1},{8,8},{9,15},{10,1... | collective-permute-start | bytes 98312 | tf_op jit(solution)/shard_map/ppermute | solution.py:275
  31.2 0.0 collective-permute-done.10.refs_3_
  31.2 0.0 collective-permute-done.9.refs_2_
  31.2 0.0 collective-permute-done.8.refs_1_
  31.2 0.4 scatter.1
  31.6 0.7 %collective-permute-start.11 = (f32[32,256]{1,0:T(8,128)S(1)}, f32[32,256]{1,0:T(8,128)S(1)}, u32[]{:S(2)}, u32[]{:S(2)}) collective-permute-start(f32[32,256]{1,0:T(8,128)S(1)} %get-tuple-element.28), channel_id=1, source_target_pairs={{0,0},{1,9},{2,2},{3,11},{4,4},{5,13},{6,6},{7,15},{8,8},{9,1},{10... | collective-permute-start | bytes 98312 | tf_op jit(solution)/shard_map/ppermute | solution.py:285
  32.3 0.7 %collective-permute-start.12 = (f32[32,256]{1,0:T(8,128)S(1)}, f32[32,256]{1,0:T(8,128)S(1)}, u32[]{:S(2)}, u32[]{:S(2)}) collective-permute-start(f32[32,256]{1,0:T(8,128)S(1)} %get-tuple-element.29), channel_id=1, source_target_pairs={{0,0},{1,25},{2,2},{3,27},{4,4},{5,29},{6,6},{7,31},{8,8},{9,17},{... | collective-permute-start | bytes 98312 | tf_op jit(solution)/shard_map/ppermute | solution.py:285
  32.9 0.7 %collective-permute-start.13 = (f32[32,256]{1,0:T(8,128)S(1)}, f32[32,256]{1,0:T(8,128)S(1)}, u32[]{:S(2)}, u32[]{:S(2)}) collective-permute-start(f32[32,256]{1,0:T(8,128)S(1)} %get-tuple-element.30), channel_id=1, source_target_pairs={{0,0},{1,17},{2,2},{3,19},{4,4},{5,21},{6,6},{7,23},{8,8},{9,25},{... | collective-permute-start | bytes 98312 | tf_op jit(solution)/shard_map/ppermute | solution.py:285
  33.6 0.0 collective-permute-done.11.near_a_ref
  33.6 0.0 collective-permute-done.12.near_b_ref
  33.6 0.0 collective-permute-done.13.fa_ref.fb_ref
  33.7 21.0 %collective-permute-start.14 = (f32[32,384]{1,0:T(8,128)S(1)}, f32[32,384]{1,0:T(8,128)S(1)}, u32[]{:S(2)}, u32[]{:S(2)}) collective-permute-start(f32[32,384]{1,0:T(8,128)S(1)} %moments.1.moments_ref), channel_id=1, source_target_pairs={{0,1},{1,0},{2,3},{3,2},{4,5},{5,4},{6,7},{7,6},{8,9},{9,8},{10,11... | collective-permute-start | bytes 147464 | tf_op jit(solution)/shard_map/ppermute | solution.py:265
  54.7 0.9 %collective-permute-done.14.other_ref = f32[32,384]{1,0:T(8,128)S(1)} collective-permute-done((f32[32,384]{1,0:T(8,128)S(1)}, f32[32,384]{1,0:T(8,128)S(1)}, u32[]{:S(2)}, u32[]{:S(2)}) %collective-permute-start.14) | collective-permute-done | bytes 49184 | tf_op jit(solution)/shard_map/ppermute | solution.py:265
  55.6 1.9 %potential.1 = (f32[16,25]{1,0:T(8,128)}, f32[12,256]{1,0:T(8,128)}) custom-call(s32[1,12]{1,0:T(1,128)S(1)} %copy-done, f32[32,384]{1,0:T(8,128)S(1)} %moments.1.moments_ref, f32[32,384]{1,0:T(8,128)S(1)} %collective-permute-done.14.other_ref, s32[1,128]{1,0:T(1,128)S(1)} %get-tuple-element.18.atom_ref, f32[72,25,256]{2,1,0:T(8,128)S(1)} %get-tuple-element.19.after_hbm.g_ref), custom_call_target="tpu_custom_call" | custom-call | tf_op jit(solution)/shard_map/potential/pallas_call | solution.py:430
  (2 shorter events, 0.0 us)
Async XLA Ops:
  1.9 12.7 %collective-permute-start = (bf16[3,4,128,128]{3,2,1,0:T(8,128)(2,1)S(1)}, bf16[3,4,128,128]{3,2,1,0:T(8,128)(2,1)S(1)}, u32[]{:S(2)}, u32[]{:S(2)}) collective-permute-start(bf16[3,4,128,128]{3,2,1,0:T(8,128)(2,1)S(1)} %mask.1.after_hbm.refs_0_), channel_id=1, source_target_pairs={{0,4},{1,3},{2,6},{3,1},{4,0},{5,7},{6,2},{7,5},{8,12},{9,11},{10,... | collective-permute-start | bytes 1179656 | tf_op jit(solution)/shard_map/ppermute | solution.py:270
  5.0 11.4 %collective-permute-start.3 = (bf16[3,4,128,128]{3,2,1,0:T(8,128)(2,1)S(1)}, bf16[3,4,128,128]{3,2,1,0:T(8,128)(2,1)S(1)}, u32[]{:S(2)}, u32[]{:S(2)}) collective-permute-start(bf16[3,4,128,128]{3,2,1,0:T(8,128)(2,1)S(1)} %mask.1.after_hbm.refs_0_), channel_id=1, source_target_pairs={{0,2},{1,5},{2,0},{3,7},{4,6},{5,1},{6,4},{7,3},{8,10},{9,13},{10,... | collective-permute-start | bytes 1179656 | tf_op jit(solution)/shard_map/ppermute | solution.py:270
  6.5 0.7 %copy-start.2 = (s32[12,6]{0,1:T(8,128)S(1)}, s32[12,6]{0,1:T(8,128)}, u32[]{:S(2)}) copy-start(s32[12,6]{0,1:T(8,128)} %param.17) | copy-start | bytes 868
  11.7 12.5 %copy-start = (s32[1,12]{1,0:T(1,128)S(1)}, s32[1,12]{1,0:T(1,128)}, u32[]{:S(2)}) copy-start(s32[1,12]{1,0:T(1,128)} %size_ref.3) | copy-start | bytes 148
  11.7 12.5 %copy-start.1 = (s32[1,12]{1,0:T(1,128)S(1)}, s32[1,12]{1,0:T(1,128)}, u32[]{:S(2)}) copy-start(s32[1,12]{1,0:T(1,128)} %offset_ref.1) | copy-start | bytes 148
  14.7 7.8 %collective-permute-start.5 = (bf16[3,4,128,128]{3,2,1,0:T(8,128)(2,1)S(1)}, bf16[3,4,128,128]{3,2,1,0:T(8,128)(2,1)S(1)}, u32[]{:S(2)}, u32[]{:S(2)}) collective-permute-start(bf16[3,4,128,128]{3,2,1,0:T(8,128)(2,1)S(1)} %collective-permute-done.refs_2_), channel_id=1, source_target_pairs={{0,2},{1,5},{2,0},{3,7},{4,6},{5,1},{6,4},{7,3},{8,10},{9,13},{10,... | collective-permute-start | bytes 1179656 | tf_op jit(solution)/shard_map/ppermute | solution.py:270
  15.9 7.3 %collective-permute-start.1 = (bf16[3,4,128,128]{3,2,1,0:T(8,128)(2,1)S(1)}, bf16[3,4,128,128]{3,2,1,0:T(8,128)(2,1)S(1)}, u32[]{:S(2)}, u32[]{:S(2)}) collective-permute-start(bf16[3,4,128,128]{3,2,1,0:T(8,128)(2,1)S(1)} %mask.1.after_hbm.refs_0_), channel_id=1, source_target_pairs={{0,1},{1,0},{2,3},{3,2},{4,5},{5,4},{6,7},{7,6},{8,9},{9,8},{10,11... | collective-permute-start | bytes 1179656 | tf_op jit(solution)/shard_map/ppermute | solution.py:265
  15.9 7.3 %collective-permute-start.2 = (bf16[3,4,128,128]{3,2,1,0:T(8,128)(2,1)S(1)}, bf16[3,4,128,128]{3,2,1,0:T(8,128)(2,1)S(1)}, u32[]{:S(2)}, u32[]{:S(2)}) collective-permute-start(bf16[3,4,128,128]{3,2,1,0:T(8,128)(2,1)S(1)} %collective-permute-done.refs_2_), channel_id=1, source_target_pairs={{0,1},{1,0},{2,3},{3,2},{4,5},{5,4},{6,7},{7,6},{8,9},{9,8},{10,11... | collective-permute-start | bytes 1179656 | tf_op jit(solution)/shard_map/ppermute | solution.py:265
  16.4 6.8 %collective-permute-start.4 = (bf16[3,4,128,128]{3,2,1,0:T(8,128)(2,1)S(1)}, bf16[3,4,128,128]{3,2,1,0:T(8,128)(2,1)S(1)}, u32[]{:S(2)}, u32[]{:S(2)}) collective-permute-start(bf16[3,4,128,128]{3,2,1,0:T(8,128)(2,1)S(1)} %collective-permute-done.3.refs_4_), channel_id=1, source_target_pairs={{0,1},{1,0},{2,3},{3,2},{4,5},{5,4},{6,7},{7,6},{8,9},{9,8},{10,11... | collective-permute-start | bytes 1179656 | tf_op jit(solution)/shard_map/ppermute | solution.py:265
  22.5 1.7 %collective-permute-start.6 = (bf16[3,4,128,128]{3,2,1,0:T(8,128)(2,1)S(1)}, bf16[3,4,128,128]{3,2,1,0:T(8,128)(2,1)S(1)}, u32[]{:S(2)}, u32[]{:S(2)}) collective-permute-start(bf16[3,4,128,128]{3,2,1,0:T(8,128)(2,1)S(1)} %collective-permute-done.5.refs_6_), channel_id=1, source_target_pairs={{0,1},{1,0},{2,3},{3,2},{4,5},{5,4},{6,7},{7,6},{8,9},{9,8},{10,11... | collective-permute-start | bytes 1179656 | tf_op jit(solution)/shard_map/ppermute | solution.py:265
  28.0 1.2 %collective-permute-start.7 = (f32[32,128]{1,0:T(8,128)S(1)}, f32[32,128]{1,0:T(8,128)S(1)}, u32[]{:S(2)}, u32[]{:S(2)}) collective-permute-start(f32[32,128]{1,0:T(8,128)S(1)} %get-tuple-element.26), channel_id=1, source_target_pairs={{0,1},{1,0},{2,3},{3,2},{4,5},{5,4},{6,7},{7,6},{8,9},{9,8},{10,11... | collective-permute-start | bytes 49160 | tf_op jit(solution)/shard_map/ppermute | solution.py:265
  29.2 2.0 %collective-permute-start.10 = (f32[2,32,128]{2,1,0:T(8,128)S(1)}, f32[2,32,128]{2,1,0:T(8,128)S(1)}, u32[]{:S(2)}, u32[]{:S(2)}) collective-permute-start(f32[2,32,128]{2,1,0:T(8,128)S(1)} %pad_maximum_fusion.refs_0_), channel_id=1, source_target_pairs={{0,0},{1,5},{2,2},{3,7},{4,4},{5,1},{6,6},{7,3},{8,8},{9,13},{10,1... | collective-permute-start | bytes 98312 | tf_op jit(solution)/shard_map/ppermute | solution.py:275
  29.8 1.4 %collective-permute-start.9 = (f32[2,32,128]{2,1,0:T(8,128)S(1)}, f32[2,32,128]{2,1,0:T(8,128)S(1)}, u32[]{:S(2)}, u32[]{:S(2)}) collective-permute-start(f32[2,32,128]{2,1,0:T(8,128)S(1)} %pad_maximum_fusion.refs_0_), channel_id=1, source_target_pairs={{0,0},{1,3},{2,2},{3,1},{4,4},{5,7},{6,6},{7,5},{8,8},{9,11},{10,1... | collective-permute-start | bytes 98312 | tf_op jit(solution)/shard_map/ppermute | solution.py:275
  30.5 0.7 %collective-permute-start.8 = (f32[2,32,128]{2,1,0:T(8,128)S(1)}, f32[2,32,128]{2,1,0:T(8,128)S(1)}, u32[]{:S(2)}, u32[]{:S(2)}) collective-permute-start(f32[2,32,128]{2,1,0:T(8,128)S(1)} %pad_maximum_fusion.refs_0_), channel_id=1, source_target_pairs={{0,0},{1,7},{2,2},{3,5},{4,4},{5,3},{6,6},{7,1},{8,8},{9,15},{10,1... | collective-permute-start | bytes 98312 | tf_op jit(solution)/shard_map/ppermute | solution.py:275
  31.6 2.0 %collective-permute-start.11 = (f32[32,256]{1,0:T(8,128)S(1)}, f32[32,256]{1,0:T(8,128)S(1)}, u32[]{:S(2)}, u32[]{:S(2)}) collective-permute-start(f32[32,256]{1,0:T(8,128)S(1)} %get-tuple-element.28), channel_id=1, source_target_pairs={{0,0},{1,9},{2,2},{3,11},{4,4},{5,13},{6,6},{7,15},{8,8},{9,1},{10... | collective-permute-start | bytes 98312 | tf_op jit(solution)/shard_map/ppermute | solution.py:285
  32.3 1.4 %collective-permute-start.12 = (f32[32,256]{1,0:T(8,128)S(1)}, f32[32,256]{1,0:T(8,128)S(1)}, u32[]{:S(2)}, u32[]{:S(2)}) collective-permute-start(f32[32,256]{1,0:T(8,128)S(1)} %get-tuple-element.29), channel_id=1, source_target_pairs={{0,0},{1,25},{2,2},{3,27},{4,4},{5,29},{6,6},{7,31},{8,8},{9,17},{... | collective-permute-start | bytes 98312 | tf_op jit(solution)/shard_map/ppermute | solution.py:285
  32.9 0.7 %collective-permute-start.13 = (f32[32,256]{1,0:T(8,128)S(1)}, f32[32,256]{1,0:T(8,128)S(1)}, u32[]{:S(2)}, u32[]{:S(2)}) collective-permute-start(f32[32,256]{1,0:T(8,128)S(1)} %get-tuple-element.30), channel_id=1, source_target_pairs={{0,0},{1,17},{2,2},{3,19},{4,4},{5,21},{6,6},{7,23},{8,8},{9,25},{... | collective-permute-start | bytes 98312 | tf_op jit(solution)/shard_map/ppermute | solution.py:285
  33.7 21.9 %collective-permute-start.14 = (f32[32,384]{1,0:T(8,128)S(1)}, f32[32,384]{1,0:T(8,128)S(1)}, u32[]{:S(2)}, u32[]{:S(2)}) collective-permute-start(f32[32,384]{1,0:T(8,128)S(1)} %moments.1.moments_ref), channel_id=1, source_target_pairs={{0,1},{1,0},{2,3},{3,2},{4,5},{5,4},{6,7},{7,6},{8,9},{9,8},{10,11... | collective-permute-start | bytes 147464 | tf_op jit(solution)/shard_map/ppermute | solution.py:265

commit v8 on v4

--- a/solution.py
+++ b/solution.py
@@ -8,6 +8,7 @@
 
 EVEN_OWNERS = (0, 1, 4, 3, 2, 5, 6, 7)
 ODD_OWNERS = (0, 1, 2, 5, 4, 3, 6, 7)
+PIECE_ROWS = (None, None, None, None, 0, 1, 0, 1)
 LANES = 128
 ROWS = 32
 SLOT = 8
@@ -16,7 +17,7 @@
 VMEM = pl.BlockSpec(memory_space=pltpu.VMEM)
 SMEM = pl.BlockSpec(memory_space=pltpu.SMEM)
 HBM = pl.BlockSpec(memory_space=pltpu.HBM)
-WIDE = pltpu.CompilerParams(vmem_limit_bytes=50 * 1024 * 1024)
+WIDE = pltpu.CompilerParams(vmem_limit_bytes=16 * 1024 * 1024)
 PARAMS = pltpu.CompilerParams(vmem_limit_bytes=16 * 1024 * 1024)
 
 
@@ -43,11 +44,24 @@
     return jnp.where(distance < 1.0, inner, jnp.where(distance < 2.0, outer, 0.0))
 
 
-def mask_kernel(mask_ref, rows_ref, out_ref, mask, rows, sems):
-    stored, band = rows_ref.shape[:2]
-    fetch = pltpu.make_async_copy(mask_ref, mask, sems.at[stored])
+def chosen_row(owner, start, owners, stored):
+    ahead = lax.rem(owner - start + stored * owners, owners)
+    return ahead, lax.rem(start + ahead, stored * owners) // owners
+
+
+def select_kernel(even, odd, owners, starts_ref, rows_ref, out_ref):
+    me = lax.axis_index("dev")
+    owner = lax.bitwise_xor(me, jnp.where(lax.rem(me, 2) == 1, odd, even))
+    for n in range(out_ref.shape[0]):
+        row = chosen_row(owner, starts_ref[n], owners, rows_ref.shape[0])[1]
+        out_ref[n] = rows_ref[row]
+
+
+def mask_kernel(mask_hbm, rows_hbm, out_ref, mask, rows, sems):
+    stored, band = rows.shape[:2]
+    fetch = pltpu.make_async_copy(mask_hbm, mask, sems.at[stored])
     copies = [
-        pltpu.make_async_copy(rows_ref.at[t], rows.at[t], sems.at[t]) for t in range(stored)
+        pltpu.make_async_copy(rows_hbm.at[t], rows.at[t], sems.at[t]) for t in range(stored)
     ]
     fetch.start()
     for copy in copies:
@@ -57,27 +71,31 @@
     for t, copy in enumerate(copies):
         copy.wait()
         for k in range(band):
-            factor = factors[t : t + 1, k : k + 1]
-            out_ref[t, k] = (rows[t, k].astype(jnp.float32) * factor).astype(jnp.bfloat16)
+            factor = jnp.broadcast_to(factors[t : t + 1, k : k + 1], rows.shape[2:])
+            out_ref[t, k] = rows[t, k] * factor.astype(jnp.bfloat16)
 
 
 def field_kernel(
-    after_hbm, near_ref, table_hbm, radius_hbm, harm_hbm,
+    begin, after_hbm, near_ref, table_hbm, radius_hbm, harm_hbm,
     g_ref, hpad_ref, atom_ref, table_ref, radius_ref, harm_ref, sems,
 ):
     batches, near, comps, points = harm_ref.shape
     knots = table_ref.shape[0]
-    moves = ((table_hbm, table_ref), (radius_hbm, radius_ref), (harm_hbm, harm_ref))
+    span = pl.ds(begin, batches)
+    moves = (
+        (table_hbm, table_ref), (radius_hbm.at[span], radius_ref), (harm_hbm.at[span], harm_ref)
+    )
     copies = [pltpu.make_async_copy(a, b, sems.at[n]) for n, (a, b) in enumerate(moves)]
     for copy in copies:
         copy.start()
     lane = lax.broadcasted_iota(jnp.int32, atom_ref.shape, 1)
     atom = jnp.full(atom_ref.shape, -1, jnp.int32)
-    for b in range(batches):
+    for b in range(near_ref.shape[1]):
         for i in range(near):
             atom = jnp.where(lane == b * SLOT + i, near_ref[i, b], atom)
     atom_ref[...] = atom
-    hpad_ref[...] = jnp.zeros(hpad_ref.shape, hpad_ref.dtype)
+    for n in range(batches * near):
+        hpad_ref[n, ROWS // 2 :, :] = jnp.zeros((ROWS // 2, points), jnp.bfloat16)
     knot = lax.broadcasted_iota(jnp.int32, (knots, points), 0).astype(jnp.float32)
     for copy in copies:
         copy.wait()
@@ -95,7 +113,7 @@
             hpad_ref[b * near + i, 0:comps, :] = h
         return carry
 
-    lax.fori_loop(0, batches, body, 0)
+    lax.fori_loop(0, batches, body, 0, unroll=2)
 
 
 def turn_kernel(after_hbm, basis_hbm, part_hbm, phit_ref, part_ref, basis, sems):
@@ -121,7 +139,9 @@
     copies[2].wait()
 
 
-def density_kernel(start_ref, offset_ref, size_ref, atom_ref, phit_ref, part_ref, hpad_ref, *refs):
+def density_kernel(
+    start_ref, offset_ref, size_ref, atom_ref, phit_ref, part_ref, low_ref, high_ref, *refs
+):
     dens_ref, terms_ref, window_ref, w_ref = refs[-4:]
     pieces = refs[:-4]
     owners = window_ref.shape[0]
@@ -129,19 +149,17 @@
     near = part_ref.shape[1]
     if len(pieces) == owners:
         me = lax.axis_index("dev")
-        odd = lax.rem(me, 2)
+        odd = lax.rem(me, 2) == 1
         held = [
-            (piece, lax.bitwise_xor(me, jnp.where(odd == 1, b, a)))
-            for piece, a, b in zip(pieces, EVEN_OWNERS, ODD_OWNERS)
+            (piece, lax.bitwise_xor(me, jnp.where(odd, b, a)), at)
+            for piece, a, b, at in zip(pieces, EVEN_OWNERS, ODD_OWNERS, PIECE_ROWS)
         ]
     else:
-        held = [(pieces[0].at[owner], owner) for owner in range(owners)]
+        held = [(pieces[0].at[owner], owner, None) for owner in range(owners)]
     stored = held[0][0].shape[0]
-    start = start_ref[0]
-    for piece, owner in held:
-        ahead = lax.rem(owner - start + stored * owners, owners)
-        row = lax.rem(start + ahead, stored * owners) // owners
-        window_ref[ahead] = piece[row]
+    for piece, owner, at in held:
+        ahead, row = chosen_row(owner, start_ref[0], owners, stored)
+        window_ref[ahead] = piece[row if at is None else at]
     w_ref[...] = jnp.zeros(w_ref.shape, w_ref.dtype)
     lane = lax.broadcasted_iota(jnp.int32, (1, points), 1)
     zero = jnp.zeros((width, width), jnp.bfloat16)
@@ -169,16 +187,20 @@
         w_ref[b, 0:near, :] = part_ref[b] * row
         return carry
 
-    lax.fori_loop(0, batches, body, 0, unroll=2)
+    lax.fori_loop(0, batches, body, 0, unroll=4)
     weights = w_ref[...].reshape(LANES, points)
     columns = jnp.concatenate(split2(weights), axis=0)
     slot = lax.broadcasted_iota(jnp.int32, (1, 2 * LANES), 1) % LANES
-    cross = dot(hpad_ref[...].reshape(batches * near * ROWS, points), columns, NT)
     terms = jnp.zeros((ROWS, 2 * LANES), jnp.float32)
-    for b in range(batches):
-        for i in range(near):
-            at = (b * near + i) * ROWS
-            terms = terms + jnp.where(slot == b * SLOT + i, cross[at : at + ROWS], 0.0)
+    begin = 0
+    for ref in (low_ref, high_ref):
+        count = ref.shape[0]
+        cross = dot(ref[...].reshape(count * ROWS, points), columns, NT)
+        for n in range(count):
+            b, i = divmod(begin + n, near)
+            here = cross[n * ROWS : (n + 1) * ROWS]
+            terms = terms + jnp.where(slot == b * SLOT + i, here, 0.0)
+        begin = begin + count
     result = terms[:, :LANES] + terms[:, LANES:]
     row_id = lax.broadcasted_iota(jnp.int32, (ROWS, LANES), 0)
     comps = ROWS - 7
@@ -186,20 +208,18 @@
 
 
 def scatter_kernel(comps, atoms, flip, *refs):
-    outs = refs[-4:]
-    pieces = refs[:-4]
+    own, near_a, near_b, far = refs[-4:]
+    pieces = [group.at[m] for group in refs[:-4] for m in range(group.shape[0])]
     row_id = lax.broadcasted_iota(jnp.int32, (3 * atoms, LANES), 0)
     total = jnp.zeros((3 * ROWS, 3 * atoms), jnp.float32)
-    for piece in pieces:
+    for m in range(0, len(pieces), 2):
         left, right = [], []
-        for part in range(piece.shape[0]):
-            values = piece[part]
+        for values in (pieces[m][...], pieces[m + 1][...]):
             chosen = values[comps : comps + 1, :].astype(jnp.int32)
             right.append((row_id == chosen).astype(jnp.float32).astype(jnp.bfloat16))
             left.append(jnp.concatenate(split3(values), axis=0))
         total = total + dot(jnp.concatenate(left, axis=1), jnp.concatenate(right, axis=1), NT)
     sums = total[:ROWS] + total[ROWS : 2 * ROWS] + total[2 * ROWS :]
-    own, near_a, near_b, far = outs
     own[...] = sums
     ahead, back = sums[:, atoms:], sums[:, : 2 * atoms]
     if flip:
@@ -214,11 +234,12 @@
 
 
 def potential_kernel(
-    comps, atoms, flip, size_ref, own_ref, near_a_ref, near_b_ref, fa_ref, fb_ref, atom_ref, g_ref,
-    mom_ref, pot_ref,
+    comps, atoms, flip, size_ref, own_ref, near_a_ref, near_b_ref, fa_ref, fb_ref, atom_ref,
+    low_ref, high_ref, mom_ref, pot_ref,
 ):
     batches, points = pot_ref.shape
-    near = g_ref.shape[0] // batches
+    near = 2 * low_ref.shape[0] // batches
+    fields = [ref.at[n] for ref in (low_ref, high_ref) for n in range(ref.shape[0])]
     own = own_ref[...]
     near_a, near_b = near_a_ref[...], near_b_ref[...]
     if flip:
@@ -250,9 +271,13 @@
         total = jnp.zeros((comps, points), jnp.float32)
         for i in range(near):
             column = chosen[:, b * SLOT + i : b * SLOT + i + 1]
-            total = total + column * g_ref[b * near + i]
+            total = total + column * fields[b * near + i][...]
         row = jnp.sum(total, axis=0, keepdims=True)
         pot_ref[b : b + 1, :] = jnp.where(lane < size_ref[0, b], row, 0.0)
+
+
+def held_in_hbm(*values):
+    return [pltpu.with_memory_space_constraint(value, pltpu.HBM) for value in values]
 
 
 def crossed(value, axis, m):
@@ -293,7 +318,7 @@
 
     masked = pl.pallas_call(
         mask_kernel,
-        out_shape=jax.ShapeDtypeStruct(density_rows.shape, bf16),
+        out_shape=pltpu.VMEM(density_rows.shape, bf16),
         in_specs=[HBM, HBM],
         out_specs=VMEM,
         scratch_shapes=[
@@ -301,35 +326,41 @@
             pltpu.VMEM(density_rows.shape, bf16),
             pltpu.SemaphoreType.DMA((blocks_dev + 1,)),
         ],
-        compiler_params=pltpu.CompilerParams(vmem_limit_bytes=63 * 1024 * 1024),
+        compiler_params=PARAMS,
         name="mask",
-    )(block_mask, density_rows)
-    g, hpad, atom_rows = pl.pallas_call(
-        field_kernel,
-        out_shape=(
-            jax.ShapeDtypeStruct((batches * near, comps, points), f32),
-            jax.ShapeDtypeStruct((batches * near, ROWS, points), bf16),
-            jax.ShapeDtypeStruct((1, LANES), jnp.int32),
-        ),
-        in_specs=[HBM, SMEM] + [HBM] * 3,
-        out_specs=(VMEM,) * 3,
-        scratch_shapes=[
-            pltpu.VMEM(radial_table.shape[::-1], f32),
-            pltpu.VMEM(radius.shape, f32),
-            pltpu.VMEM(harmonics.shape, bf16),
-            pltpu.SemaphoreType.DMA((3,)),
-        ],
-        compiler_params=WIDE,
-        cost_estimate=pl.CostEstimate(flops=2_000_000_000, bytes_accessed=8_000_000, transcendentals=0),
-        name="field",
-    )(masked, atom_near.T, radial_table.T, radius, harmonics)
+    )(*held_in_hbm(block_mask, density_rows))
+
+    half = batches // 2
+
+    def field(begin, after):
+        return pl.pallas_call(
+            functools.partial(field_kernel, begin),
+            out_shape=(
+                pltpu.VMEM((half * near, comps, points), f32),
+                pltpu.VMEM((half * near, ROWS, points), bf16),
+                pltpu.VMEM((1, LANES), jnp.int32),
+            ),
+            in_specs=[HBM, SMEM] + [HBM] * 3,
+            out_specs=(VMEM,) * 3,
+            scratch_shapes=[
+                pltpu.VMEM(radial_table.shape[::-1], f32),
+                pltpu.VMEM((half,) + radius.shape[1:], f32),
+                pltpu.VMEM((half,) + harmonics.shape[1:], bf16),
+                pltpu.SemaphoreType.DMA((3,)),
+            ],
+            compiler_params=WIDE,
+            cost_estimate=pl.CostEstimate(
+                flops=2_000_000_000, bytes_accessed=8_000_000, transcendentals=0
+            ),
+            name="field",
+        )(after, atom_near.T, *held_in_hbm(radial_table.T, radius, harmonics))
 
     def turned_basis(after):
         return pl.pallas_call(
             turn_kernel,
             out_shape=(
-                jax.ShapeDtypeStruct((batches, near_blocks, width, points), bf16),
-                jax.ShapeDtypeStruct(partition.shape, f32),
+                pltpu.VMEM((batches, near_blocks, width, points), bf16),
+                pltpu.VMEM(partition.shape, f32),
             ),
             in_specs=[HBM] * 3,
             out_specs=(VMEM,) * 2,
@@ -339,18 +370,39 @@
                 flops=2_000_000_000, bytes_accessed=8_000_000, transcendentals=0
             ),
             name="turn",
-        )(after, basis_values, partition)
+        )(after, *held_in_hbm(basis_values, partition))
+
+    def selected(even, odd, starts, rows):
+        return pl.pallas_call(
+            functools.partial(select_kernel, even, odd, dev_count),
+            out_shape=pltpu.VMEM((2,) + density_rows.shape[1:], bf16),
+            in_specs=[SMEM, VMEM],
+            out_specs=VMEM,
+            compiler_params=PARAMS,
+            name="select",
+        )(starts, rows)
 
     if dev_count == 8:
+        beside = crossed(window_start, "dev", 1)
+        beside, _ = lax.optimization_barrier((beside, masked))
         first = turned(masked, 4, 2)
-        second = turned(masked, 2, 4)
-        first, g = lax.optimization_barrier((first, g))
-        third = turned(first, 2, 4)
-        phit, weights = turned_basis(first)
+        pair = jnp.concatenate([window_start, beside])
+        starts = turned(pair, 2, 4)
+        g_low, hpad_low, atom_rows = field(0, pair)
+        starts, g_low = lax.optimization_barrier((starts, g_low))
+        chosen = selected(0, 0, starts, masked)
+        second = turned(chosen, 2, 4)
+        g_high, hpad_high, _ = field(half, chosen)
+        first, g_high = lax.optimization_barrier((first, g_high))
+        chosen = selected(4, 2, starts, first)
+        third = turned(chosen, 2, 4)
+        phit, weights = turned_basis(chosen)
         second, phit = lax.optimization_barrier((second, phit))
         sent = (masked, first, second, third)
         pieces = [piece for value in sent for piece in (value, crossed(value, "dev", 1))]
     else:
+        g_low, hpad_low, atom_rows = field(0, masked)
+        g_high, hpad_high, _ = field(half, masked)
         phit, weights = turned_basis(masked)
         pieces = [lax.all_gather(masked, "dev", axis=0)]
 
@@ -360,7 +412,7 @@
             jax.ShapeDtypeStruct((batches, points), f32),
             jax.ShapeDtypeStruct((ROWS, LANES), f32),
         ),
-        in_specs=[SMEM] * 3 + [VMEM] * (4 + len(pieces)),
+        in_specs=[SMEM] * 3 + [VMEM] * (5 + len(pieces)),
         out_specs=(VMEM, VMEM),
         scratch_shapes=[
             pltpu.VMEM((dev_count, band, width, width), bf16),
@@ -370,12 +422,15 @@
         cost_estimate=pl.CostEstimate(flops=2_000_000_000, bytes_accessed=6_000_000, transcendentals=0),
         name="density",
     )(
-        window_start, batch_offsets, batch_sizes, atom_rows, phit, weights, hpad,
+        window_start, batch_offsets, batch_sizes, atom_rows, phit, weights, hpad_low, hpad_high,
         *pieces,
     )
 
-    both = jnp.stack([terms, crossed(terms, "dev", 1)])
-    groups = [both] + [crossed(both, "dev", m) for m in range(2, dev_count, 2)]
+    if dev_count == 8:
+        both = jnp.stack([terms, crossed(terms, "dev", 1)])
+        groups = [both] + [crossed(both, "dev", m) for m in (2, 4, 6)]
+    else:
+        groups = [lax.all_gather(terms, "dev", axis=0)]
     flip = region_count == 4
     own, near_a, near_b, far = pl.pallas_call(
         functools.partial(scatter_kernel, comps, atoms, flip),
@@ -401,11 +456,11 @@
             jax.ShapeDtypeStruct((mine, comps), f32),
             jax.ShapeDtypeStruct((batches, points), f32),
         ),
-        in_specs=[SMEM] + [VMEM] * 7,
+        in_specs=[SMEM] + [VMEM] * 8,
         out_specs=(VMEM, VMEM),
         compiler_params=PARAMS,
         name="potential",
-    )(batch_sizes, own, near_a, near_b, far_a, far_b, atom_rows, g)
+    )(batch_sizes, own, near_a, near_b, far_a, far_b, atom_rows, g_low, g_high)
     return (density, moments.T, potential)
 
 

time: 50 us -> 47.7 us (0.954)
  local copies, waits for them, and re-layouts: 3.56 us -> 0.7 us
  starting transfers between devices: 14.1 us -> 15.2 us
  waiting for transfers between devices: 13.3 us -> 12.4 us
  other arithmetic: 0.01 us -> 0.7 us
    unnamed x16 -> x6, local copies, waits for them, and re-layouts: 3.56 us -> 0.7 us
    ppermute x3 -> x4, waiting for transfers between devices: 3.4 us -> 1.38 us  [turned(): lax.ppermute(value, 'dev', [(i, i ^ (odd if i % 2 else even)) for i in ra...]
    pallas_call x1, Pallas kernels: 5.01 us -> 3.68 us  [per_device(): pl.pallas_call(density_kernel, out_shape=(jax.ShapeDtypeStruct((batches,...]
    ppermute x11 -> x12, waiting for transfers between devices: 9.89 us -> 11 us  [crossed(): lax.ppermute(value, axis, [(i, i ^ m) for i in range(lax.axis_size(axis))])]
    pallas_call x3 -> x6, Pallas kernels: 10.1 us -> 11 us  [the longest x2 5.6 us: field(): pl.pallas_call(functools.partial(field_kernel, begin), out_shape=(pltpu.V...]
    ppermute x3 -> x4, starting transfers between devices: 5.46 us -> 6.25 us  [turned(): lax.ppermute(value, 'dev', [(i, i ^ (odd if i % 2 else even)) for i in ra...]
    concatenate x0 -> x1, other arithmetic: none -> 0.7 us  [per_device(): pair = jnp.concatenate([window_start, beside])]
    ppermute x11 -> x12, starting transfers between devices: 8.6 us -> 8.97 us  [crossed(): lax.ppermute(value, axis, [(i, i ^ m) for i in range(lax.axis_size(axis))])]
  transfers between devices with their start and end apart: 14 -> 16, of which waited for: 8 -> 9; matrix products, arithmetic and copies ran while one was open for 0% -> 1% of each run, Pallas kernels for 16% -> 23%
where the time goes in v8:
time: 47.7 us; the launch traced here: 47.3 us
  Pallas kernels  16.9 us (35%)
  starting transfers between devices  15.2 us (32%)
  waiting for transfers between devices  12.4 us (26%)
  between operations  1.41 us (3%)
  other arithmetic  0.7 us (1%)
  local copies, waits for them, and re-layouts  0.7 us (1%)
    ppermute x12, waiting for transfers between devices, crossed(): lax.ppermute(value, axis, [(i, i ^ m) for i in range(lax.axis_size(axis))])  11 us
    ppermute x12, starting transfers between devices, crossed(): lax.ppermute(value, axis, [(i, i ^ m) for i in range(lax.axis_size(axis))])  8.97 us
    ppermute x4, starting transfers between devices, turned(): lax.ppermute(value, 'dev', [(i, i ^ (odd if i % 2 else even)) for i in ra...  6.25 us
    pallas_call x2, Pallas kernels, field(): pl.pallas_call(functools.partial(field_kernel, begin), out_shape=(pltpu.V...  5.6 us
    pallas_call x1, Pallas kernels, per_device(): pl.pallas_call(density_kernel, out_shape=(jax.ShapeDtypeStruct((batches,...  3.68 us
    pallas_call x1, Pallas kernels, turned_basis(): pl.pallas_call(turn_kernel, out_shape=(pltpu.VMEM((batches, near_blocks,...  2.9 us
    pallas_call x1, Pallas kernels, per_device(): pl.pallas_call(functools.partial(potential_kernel, comps, atoms, flip), o...  1.88 us
    ppermute x4, waiting for transfers between devices, turned(): lax.ppermute(value, 'dev', [(i, i ^ (odd if i % 2 else even)) for i in ra...  1.38 us
  transfers between devices with their start and end apart: 16, of which 9 were waited for; matrix products, arithmetic and copies ran while one was open for 1% of the time, Pallas kernels for 23%

profile of v8, /device:TPU:0, one launch (start us, length us, event | category | flops | bytes accessed | tf_op | source)
XLA Modules:
  0.0 47.3 jit_solution(16356116687887123344)
XLA Ops:
  0.6 0.5 %collective-permute-start = (s32[1]{0:T(128)}, s32[1]{0:T(128)}, u32[]{:S(2)}, u32[]{:S(2)}) collective-permute-start(s32[1]{0:T(128)} %param.14), channel_id=1, source_target_pairs={{0,1},{1,0},{2,3},{3,2},{4,5},{5,4},{6,7},{7,6},{8,9},{9,8},{10,11... | collective-permute-start | bytes 20 | tf_op jit(solution)/shard_map/ppermute | solution.py:284
  1.1 1.3 %mask.1.rows_ref.refs_0_ = bf16[3,4,128,128]{3,2,1,0:T(8,128)(2,1)S(1)} custom-call(s32[3,4]{1,0:T(4,128)} %mask_hbm.1, bf16[3,4,128,128]{3,2,1,0:T(8,128)(2,1)} %rows_hbm.1), custom_call_target="tpu_custom_call" | custom-call | tf_op jit(solution)/shard_map/mask/pallas_call | solution.py:319
  2.5 2.6 %collective-permute-start.3 = (bf16[3,4,128,128]{3,2,1,0:T(8,128)(2,1)S(1)}, bf16[3,4,128,128]{3,2,1,0:T(8,128)(2,1)S(1)}, u32[]{:S(2)}, u32[]{:S(2)}) collective-permute-start(bf16[3,4,128,128]{3,2,1,0:T(8,128)(2,1)S(1)} %mask.1.rows_ref.refs_0_), channel_id=1, source_target_pairs={{0,4},{1,3},{2,6},{3,1},{4,0},{5,7},{6,2},{7,5},{8,12},{9,11},{10,... | collective-permute-start | bytes 1179656 | tf_op jit(solution)/shard_map/ppermute | solution.py:289
  5.7 0.0 collective-permute-done
  5.7 0.7 %pad_add_fusion.after_hbm = s32[2]{0:T(128)S(1)} fusion(s32[1]{0:T(128)} %collective-permute-done, s32[1]{0:T(128)S(6)} %copy.14.start_ref), kind=kLoop, calls=%fused_computation.1 | loop fusion | flops 2 | bytes 16 | tf_op jit(solution)/shard_map/concatenate | solution.py:389
  6.4 1.5 %collective-permute-start.1 = (s32[2]{0:T(128)S(1)}, s32[2]{0:T(128)S(1)}, u32[]{:S(2)}, u32[]{:S(2)}) collective-permute-start(s32[2]{0:T(128)S(1)} %pad_add_fusion.after_hbm), channel_id=1, source_target_pairs={{0,2},{1,5},{2,0},{3,7},{4,6},{5,1},{6,4},{7,3},{8,10},{9,13},{10,... | collective-permute-start | bytes 32 | tf_op jit(solution)/shard_map/ppermute | solution.py:289
  7.9 0.0 copy-start.1
  7.9 0.7 %copy-done.1 = s32[12,6]{0,1:T(8,128)S(1)} copy-done((s32[12,6]{0,1:T(8,128)S(1)}, s32[12,6]{0,1:T(8,128)}, u32[]{:S(2)}) %copy-start.1) | copy-done | bytes 312
  8.6 2.7 %field.2 = (f32[36,25,256]{2,1,0:T(8,128)S(1)}, bf16[36,32,256]{2,1,0:T(8,128)(2,1)S(1)}, s32[1,128]{1,0:T(1,128)S(1)}) custom-call(s32[2]{0:T(128)S(1)} %pad_add_fusion.after_hbm, s32[6,12]{1,0:T(8,128)S(1)} %bitcast.6, f32[16,25]{1,0:T(8,128)} %bitcast.9, f32[12,6,256]{2,1,0:T(8,128)} %radius_hbm.3, bf16[12,6,25,256]{3,2,1,0:T(8,128)(2,1)} %harm_hbm.3), custom_call_target="tpu_custom_call" | custom-call | flops 2000000000 | bytes 8000000 | tf_op jit(solution)/shard_map/field/pallas_call | solution.py:336
  11.3 0.0 collective-permute-done.1.starts_ref
  11.3 0.6 %select.2.after_hbm = bf16[2,4,128,128]{3,2,1,0:T(8,128)(2,1)S(1)} custom-call(s32[2]{0:T(128)S(1)} %collective-permute-done.1.starts_ref, bf16[3,4,128,128]{3,2,1,0:T(8,128)(2,1)S(1)} %mask.1.rows_ref.refs_0_), custom_call_target="tpu_custom_call" | custom-call | tf_op jit(solution)/shard_map/select/pallas_call | solution.py:376
  11.9 0.6 %collective-permute-start.2 = (bf16[2,4,128,128]{3,2,1,0:T(8,128)(2,1)S(1)}, bf16[2,4,128,128]{3,2,1,0:T(8,128)(2,1)S(1)}, u32[]{:S(2)}, u32[]{:S(2)}) collective-permute-start(bf16[2,4,128,128]{3,2,1,0:T(8,128)(2,1)S(1)} %select.2.after_hbm), channel_id=1, source_target_pairs={{0,2},{1,5},{2,0},{3,7},{4,6},{5,1},{6,4},{7,3},{8,10},{9,13},{10,... | collective-permute-start | bytes 786440 | tf_op jit(solution)/shard_map/ppermute | solution.py:289
  12.5 2.9 %field.3 = (f32[36,25,256]{2,1,0:T(8,128)S(1)}, bf16[36,32,256]{2,1,0:T(8,128)(2,1)S(1)}, s32[1,128]{1,0:T(1,128)}) custom-call(bf16[2,4,128,128]{3,2,1,0:T(8,128)(2,1)S(1)} %select.2.after_hbm, s32[6,12]{1,0:T(8,128)S(1)} %bitcast.7, f32[16,25]{1,0:T(8,128)} %bitcast.10, f32[12,6,256]{2,1,0:T(8,128)} %radius_hbm.3, bf16[12,6,25,256]{3,2,1,0:T(8,128)(2,1)} %harm_hbm.3), custom_call_target="tpu_custom_call" | custom-call | flops 2000000000 | bytes 8000000 | tf_op jit(solution)/shard_map/field/pallas_call | solution.py:336
  15.4 0.0 collective-permute-done.3.rows_ref.refs_2_
  15.4 0.6 %select.3.after_hbm = bf16[2,4,128,128]{3,2,1,0:T(8,128)(2,1)S(1)} custom-call(s32[2]{0:T(128)S(1)} %collective-permute-done.1.starts_ref, bf16[3,4,128,128]{3,2,1,0:T(8,128)(2,1)S(1)} %collective-permute-done.3.rows_ref.refs_2_), custom_call_target="tpu_custom_call" | custom-call | tf_op jit(solution)/shard_map/select/pallas_call | solution.py:376
  16.0 0.0 copy-start
  16.0 0.0 copy-start.2
  16.0 1.6 %collective-permute-start.7 = (bf16[2,4,128,128]{3,2,1,0:T(8,128)(2,1)S(1)}, bf16[2,4,128,128]{3,2,1,0:T(8,128)(2,1)S(1)}, u32[]{:S(2)}, u32[]{:S(2)}) collective-permute-start(bf16[2,4,128,128]{3,2,1,0:T(8,128)(2,1)S(1)} %select.3.after_hbm), channel_id=1, source_target_pairs={{0,2},{1,5},{2,0},{3,7},{4,6},{5,1},{6,4},{7,3},{8,10},{9,13},{10,... | collective-permute-start | bytes 786440 | tf_op jit(solution)/shard_map/ppermute | solution.py:289
  17.6 0.0 collective-permute-start.4
  17.6 0.5 %collective-permute-start.5 = (bf16[3,4,128,128]{3,2,1,0:T(8,128)(2,1)S(1)}, bf16[3,4,128,128]{3,2,1,0:T(8,128)(2,1)S(1)}, u32[]{:S(2)}, u32[]{:S(2)}) collective-permute-start(bf16[3,4,128,128]{3,2,1,0:T(8,128)(2,1)S(1)} %collective-permute-done.3.rows_ref.refs_2_), channel_id=1, source_target_pairs={{0,1},{1,0},{2,3},{3,2},{4,5},{5,4},{6,7},{7,6},{8,9},{9,8},{10,11... | collective-permute-start | bytes 1179656 | tf_op jit(solution)/shard_map/ppermute | solution.py:284
  18.1 2.9 %turn.1 = (bf16[12,4,128,256]{3,2,1,0:T(8,128)(2,1)S(1)}, f32[12,6,256]{2,1,0:T(8,128)S(1)}) custom-call(bf16[2,4,128,128]{3,2,1,0:T(8,128)(2,1)S(1)} %select.3.after_hbm, bf16[12,4,256,128]{3,2,1,0:T(8,128)(2,1)} %basis_hbm.1, f32[12,6,256]{2,1,0:T(8,128)} %part_hbm.1), custom_call_target="tpu_custom_call" | custom-call | flops 2000000000 | bytes 8000000 | tf_op jit(solution)/shard_map/turn/pallas_call | solution.py:359
  21.0 0.0 collective-permute-done.2.refs_4_
  21.0 0.1 collective-permute-start.6
  21.1 1.4 %collective-permute-done.7.refs_6_ = bf16[2,4,128,128]{3,2,1,0:T(8,128)(2,1)S(1)} collective-permute-done((bf16[2,4,128,128]{3,2,1,0:T(8,128)(2,1)S(1)}, bf16[2,4,128,128]{3,2,1,0:T(8,128)(2,1)S(1)}, u32[]{:S(2)}, u32[]{:S(2)}) %collective-permute-start.7) | collective-permute-done | bytes 262176 | tf_op jit(solution)/shard_map/ppermute | solution.py:289
  22.5 0.0 collective-permute-start.8
  22.5 0.0 collective-permute-done.4.refs_1_
  22.5 0.1 collective-permute-done.6.refs_5_
  22.6 0.0 collective-permute-done.5.refs_3_
  22.6 1.4 %collective-permute-done.8.refs_7_ = bf16[2,4,128,128]{3,2,1,0:T(8,128)(2,1)S(1)} collective-permute-done((bf16[2,4,128,128]{3,2,1,0:T(8,128)(2,1)S(1)}, bf16[2,4,128,128]{3,2,1,0:T(8,128)(2,1)S(1)}, u32[]{:S(2)}, u32[]{:S(2)}) %collective-permute-start.8) | collective-permute-done | bytes 262176 | tf_op jit(solution)/shard_map/ppermute | solution.py:284
  24.0 0.0 copy-done
  24.0 0.0 copy-done.2
  24.0 3.7 %density.1 = (f32[12,256]{1,0:T(8,128)}, f32[32,128]{1,0:T(8,128)S(1)}) custom-call(s32[1]{0:T(128)S(6)} %copy.14.start_ref, s32[1,12]{1,0:T(1,128)S(1)} %copy-done.2, s32[1,12]{1,0:T(1,128)S(1)} %copy-done, s32[1,128]{1,0:T(1,128)S(1)} %get-tuple-element.26.atom_ref, bf16[12,4,128,256]{3,2,1,0:T(8,128)(2,1)S(1)} %get-tuple-element.32.phit_ref, ...), custom_call_target="tpu_custom_call" | custom-call | flops 2000000000 | bytes 6000000 | tf_op jit(solution)/shard_map/density/pallas_call | solution.py:409
  27.7 0.1 collective-permute-start.9
  27.9 1.0 %collective-permute-done.9 = f32[32,128]{1,0:T(8,128)S(1)} collective-permute-done((f32[32,128]{1,0:T(8,128)S(1)}, f32[32,128]{1,0:T(8,128)S(1)}, u32[]{:S(2)}, u32[]{:S(2)}) %collective-permute-start.9) | collective-permute-done | bytes 16416 | tf_op jit(solution)/shard_map/ppermute | solution.py:284
  28.9 1.4 %collective-permute-start.12 = (f32[2,32,128]{2,1,0:T(8,128)S(1)}, f32[2,32,128]{2,1,0:T(8,128)S(1)}, u32[]{:S(2)}, u32[]{:S(2)}) collective-permute-start(f32[2,32,128]{2,1,0:T(8,128)S(1)} %pad_maximum_fusion.refs_0_), channel_id=1, source_target_pairs={{0,6},{1,7},{2,4},{3,5},{4,2},{5,3},{6,0},{7,1},{8,14},{9,15},{10,... | collective-permute-start | bytes 98312 | tf_op jit(solution)/shard_map/ppermute | solution.py:284
  30.3 1.5 %collective-permute-start.11 = (f32[2,32,128]{2,1,0:T(8,128)S(1)}, f32[2,32,128]{2,1,0:T(8,128)S(1)}, u32[]{:S(2)}, u32[]{:S(2)}) collective-permute-start(f32[2,32,128]{2,1,0:T(8,128)S(1)} %pad_maximum_fusion.refs_0_), channel_id=1, source_target_pairs={{0,4},{1,5},{2,6},{3,7},{4,0},{5,1},{6,2},{7,3},{8,12},{9,13},{10,... | collective-permute-start | bytes 98312 | tf_op jit(solution)/shard_map/ppermute | solution.py:284
  31.9 0.5 %collective-permute-start.10 = (f32[2,32,128]{2,1,0:T(8,128)S(1)}, f32[2,32,128]{2,1,0:T(8,128)S(1)}, u32[]{:S(2)}, u32[]{:S(2)}) collective-permute-start(f32[2,32,128]{2,1,0:T(8,128)S(1)} %pad_maximum_fusion.refs_0_), channel_id=1, source_target_pairs={{0,2},{1,3},{2,0},{3,1},{4,6},{5,7},{6,4},{7,5},{8,10},{9,11},{10,... | collective-permute-start | bytes 98312 | tf_op jit(solution)/shard_map/ppermute | solution.py:284
  32.4 1.3 %collective-permute-done.12.refs_3_ = f32[2,32,128]{2,1,0:T(8,128)S(1)} collective-permute-done((f32[2,32,128]{2,1,0:T(8,128)S(1)}, f32[2,32,128]{2,1,0:T(8,128)S(1)}, u32[]{:S(2)}, u32[]{:S(2)}) %collective-permute-start.12) | collective-permute-done | bytes 32800 | tf_op jit(solution)/shard_map/ppermute | solution.py:284
  33.7 0.5 %collective-permute-done.11.refs_2_ = f32[2,32,128]{2,1,0:T(8,128)S(1)} collective-permute-done((f32[2,32,128]{2,1,0:T(8,128)S(1)}, f32[2,32,128]{2,1,0:T(8,128)S(1)}, u32[]{:S(2)}, u32[]{:S(2)}) %collective-permute-start.11) | collective-permute-done | bytes 32800 | tf_op jit(solution)/shard_map/ppermute | solution.py:284
  34.3 1.5 %collective-permute-done.10.refs_1_ = f32[2,32,128]{2,1,0:T(8,128)S(1)} collective-permute-done((f32[2,32,128]{2,1,0:T(8,128)S(1)}, f32[2,32,128]{2,1,0:T(8,128)S(1)}, u32[]{:S(2)}, u32[]{:S(2)}) %collective-permute-start.10) | collective-permute-done | bytes 32800 | tf_op jit(solution)/shard_map/ppermute | solution.py:284
  35.8 0.4 scatter.1
  36.2 1.6 %collective-permute-start.13 = (f32[32,256]{1,0:T(8,128)S(1)}, f32[32,256]{1,0:T(8,128)S(1)}, u32[]{:S(2)}, u32[]{:S(2)}) collective-permute-start(f32[32,256]{1,0:T(8,128)S(1)} %get-tuple-element.40), channel_id=1, source_target_pairs={{0,8},{8,0},{16,24},{24,16},{1,9},{9,1},{17,25},{25,17},{2,10},{10... | collective-permute-start | bytes 98312 | tf_op jit(solution)/shard_map/ppermute | solution.py:284
  37.8 2.5 %collective-permute-start.14 = (f32[32,256]{1,0:T(8,128)S(1)}, f32[32,256]{1,0:T(8,128)S(1)}, u32[]{:S(2)}, u32[]{:S(2)}) collective-permute-start(f32[32,256]{1,0:T(8,128)S(1)} %get-tuple-element.41), channel_id=1, source_target_pairs={{0,24},{8,16},{16,8},{24,0},{1,25},{9,17},{17,9},{25,1},{2,26},{10... | collective-permute-start | bytes 98312 | tf_op jit(solution)/shard_map/ppermute | solution.py:284
  40.3 0.1 collective-permute-start.15
  40.4 0.0 collective-permute-done.13.near_a_ref
  40.4 3.1 %collective-permute-done.14.near_b_ref = f32[32,256]{1,0:T(8,128)S(1)} collective-permute-done((f32[32,256]{1,0:T(8,128)S(1)}, f32[32,256]{1,0:T(8,128)S(1)}, u32[]{:S(2)}, u32[]{:S(2)}) %collective-permute-start.14) | collective-permute-done | bytes 32800 | tf_op jit(solution)/shard_map/ppermute | solution.py:284
  43.5 1.9 %collective-permute-done.15.fa_ref.fb_ref = f32[32,256]{1,0:T(8,128)S(1)} collective-permute-done((f32[32,256]{1,0:T(8,128)S(1)}, f32[32,256]{1,0:T(8,128)S(1)}, u32[]{:S(2)}, u32[]{:S(2)}) %collective-permute-start.15) | collective-permute-done | bytes 32800 | tf_op jit(solution)/shard_map/ppermute | solution.py:284
  45.4 1.9 %potential.1 = (f32[16,25]{1,0:T(8,128)}, f32[12,256]{1,0:T(8,128)}) custom-call(s32[1,12]{1,0:T(1,128)S(1)} %copy-done, f32[32,384]{1,0:T(8,128)S(1)} %get-tuple-element.39.own_ref, f32[32,256]{1,0:T(8,128)S(1)} %collective-permute-done.13.near_a_ref, f32[32,256]{1,0:T(8,128)S(1)} %collective-permute-done.14.near_b_ref, ...), custom_call_target="tpu_custom_call" | custom-call | tf_op jit(solution)/shard_map/potential/pallas_call | solution.py:453
  (1 shorter events, 0.0 us)
Async XLA Ops:
  0.6 5.1 %collective-permute-start = (s32[1]{0:T(128)}, s32[1]{0:T(128)}, u32[]{:S(2)}, u32[]{:S(2)}) collective-permute-start(s32[1]{0:T(128)} %param.14), channel_id=1, source_target_pairs={{0,1},{1,0},{2,3},{3,2},{4,5},{5,4},{6,7},{7,6},{8,9},{9,8},{10,11... | collective-permute-start | bytes 20 | tf_op jit(solution)/shard_map/ppermute | solution.py:284
  2.5 13.0 %collective-permute-start.3 = (bf16[3,4,128,128]{3,2,1,0:T(8,128)(2,1)S(1)}, bf16[3,4,128,128]{3,2,1,0:T(8,128)(2,1)S(1)}, u32[]{:S(2)}, u32[]{:S(2)}) collective-permute-start(bf16[3,4,128,128]{3,2,1,0:T(8,128)(2,1)S(1)} %mask.1.rows_ref.refs_0_), channel_id=1, source_target_pairs={{0,4},{1,3},{2,6},{3,1},{4,0},{5,7},{6,2},{7,5},{8,12},{9,11},{10,... | collective-permute-start | bytes 1179656 | tf_op jit(solution)/shard_map/ppermute | solution.py:289
  6.4 4.9 %collective-permute-start.1 = (s32[2]{0:T(128)S(1)}, s32[2]{0:T(128)S(1)}, u32[]{:S(2)}, u32[]{:S(2)}) collective-permute-start(s32[2]{0:T(128)S(1)} %pad_add_fusion.after_hbm), channel_id=1, source_target_pairs={{0,2},{1,5},{2,0},{3,7},{4,6},{5,1},{6,4},{7,3},{8,10},{9,13},{10,... | collective-permute-start | bytes 32 | tf_op jit(solution)/shard_map/ppermute | solution.py:289
  7.9 0.7 %copy-start.1 = (s32[12,6]{0,1:T(8,128)S(1)}, s32[12,6]{0,1:T(8,128)}, u32[]{:S(2)}) copy-start(s32[12,6]{0,1:T(8,128)} %param.17) | copy-start | bytes 868
  11.9 9.1 %collective-permute-start.2 = (bf16[2,4,128,128]{3,2,1,0:T(8,128)(2,1)S(1)}, bf16[2,4,128,128]{3,2,1,0:T(8,128)(2,1)S(1)}, u32[]{:S(2)}, u32[]{:S(2)}) collective-permute-start(bf16[2,4,128,128]{3,2,1,0:T(8,128)(2,1)S(1)} %select.2.after_hbm), channel_id=1, source_target_pairs={{0,2},{1,5},{2,0},{3,7},{4,6},{5,1},{6,4},{7,3},{8,10},{9,13},{10,... | collective-permute-start | bytes 786440 | tf_op jit(solution)/shard_map/ppermute | solution.py:289
  16.0 8.0 %copy-start = (s32[1,12]{1,0:T(1,128)S(1)}, s32[1,12]{1,0:T(1,128)}, u32[]{:S(2)}) copy-start(s32[1,12]{1,0:T(1,128)} %size_ref.3) | copy-start | bytes 148
  16.0 8.0 %copy-start.2 = (s32[1,12]{1,0:T(1,128)S(1)}, s32[1,12]{1,0:T(1,128)}, u32[]{:S(2)}) copy-start(s32[1,12]{1,0:T(1,128)} %offset_ref.1) | copy-start | bytes 148
  16.0 6.4 %collective-permute-start.7 = (bf16[2,4,128,128]{3,2,1,0:T(8,128)(2,1)S(1)}, bf16[2,4,128,128]{3,2,1,0:T(8,128)(2,1)S(1)}, u32[]{:S(2)}, u32[]{:S(2)}) collective-permute-start(bf16[2,4,128,128]{3,2,1,0:T(8,128)(2,1)S(1)} %select.3.after_hbm), channel_id=1, source_target_pairs={{0,2},{1,5},{2,0},{3,7},{4,6},{5,1},{6,4},{7,3},{8,10},{9,13},{10,... | collective-permute-start | bytes 786440 | tf_op jit(solution)/shard_map/ppermute | solution.py:289
  17.6 4.9 %collective-permute-start.4 = (bf16[3,4,128,128]{3,2,1,0:T(8,128)(2,1)S(1)}, bf16[3,4,128,128]{3,2,1,0:T(8,128)(2,1)S(1)}, u32[]{:S(2)}, u32[]{:S(2)}) collective-permute-start(bf16[3,4,128,128]{3,2,1,0:T(8,128)(2,1)S(1)} %mask.1.rows_ref.refs_0_), channel_id=1, source_target_pairs={{0,1},{1,0},{2,3},{3,2},{4,5},{5,4},{6,7},{7,6},{8,9},{9,8},{10,11... | collective-permute-start | bytes 1179656 | tf_op jit(solution)/shard_map/ppermute | solution.py:284
  17.6 5.0 %collective-permute-start.5 = (bf16[3,4,128,128]{3,2,1,0:T(8,128)(2,1)S(1)}, bf16[3,4,128,128]{3,2,1,0:T(8,128)(2,1)S(1)}, u32[]{:S(2)}, u32[]{:S(2)}) collective-permute-start(bf16[3,4,128,128]{3,2,1,0:T(8,128)(2,1)S(1)} %collective-permute-done.3.rows_ref.refs_2_), channel_id=1, source_target_pairs={{0,1},{1,0},{2,3},{3,2},{4,5},{5,4},{6,7},{7,6},{8,9},{9,8},{10,11... | collective-permute-start | bytes 1179656 | tf_op jit(solution)/shard_map/ppermute | solution.py:284
  21.0 1.6 %collective-permute-start.6 = (bf16[2,4,128,128]{3,2,1,0:T(8,128)(2,1)S(1)}, bf16[2,4,128,128]{3,2,1,0:T(8,128)(2,1)S(1)}, u32[]{:S(2)}, u32[]{:S(2)}) collective-permute-start(bf16[2,4,128,128]{3,2,1,0:T(8,128)(2,1)S(1)} %collective-permute-done.2.refs_4_), channel_id=1, source_target_pairs={{0,1},{1,0},{2,3},{3,2},{4,5},{5,4},{6,7},{7,6},{8,9},{9,8},{10,11... | collective-permute-start | bytes 786440 | tf_op jit(solution)/shard_map/ppermute | solution.py:284
  22.5 1.5 %collective-permute-start.8 = (bf16[2,4,128,128]{3,2,1,0:T(8,128)(2,1)S(1)}, bf16[2,4,128,128]{3,2,1,0:T(8,128)(2,1)S(1)}, u32[]{:S(2)}, u32[]{:S(2)}) collective-permute-start(bf16[2,4,128,128]{3,2,1,0:T(8,128)(2,1)S(1)} %collective-permute-done.7.refs_6_), channel_id=1, source_target_pairs={{0,1},{1,0},{2,3},{3,2},{4,5},{5,4},{6,7},{7,6},{8,9},{9,8},{10,11... | collective-permute-start | bytes 786440 | tf_op jit(solution)/shard_map/ppermute | solution.py:284
  27.7 1.2 %collective-permute-start.9 = (f32[32,128]{1,0:T(8,128)S(1)}, f32[32,128]{1,0:T(8,128)S(1)}, u32[]{:S(2)}, u32[]{:S(2)}) collective-permute-start(f32[32,128]{1,0:T(8,128)S(1)} %get-tuple-element.38), channel_id=1, source_target_pairs={{0,1},{1,0},{2,3},{3,2},{4,5},{5,4},{6,7},{7,6},{8,9},{9,8},{10,11... | collective-permute-start | bytes 49160 | tf_op jit(solution)/shard_map/ppermute | solution.py:284
  28.9 4.8 %collective-permute-start.12 = (f32[2,32,128]{2,1,0:T(8,128)S(1)}, f32[2,32,128]{2,1,0:T(8,128)S(1)}, u32[]{:S(2)}, u32[]{:S(2)}) collective-permute-start(f32[2,32,128]{2,1,0:T(8,128)S(1)} %pad_maximum_fusion.refs_0_), channel_id=1, source_target_pairs={{0,6},{1,7},{2,4},{3,5},{4,2},{5,3},{6,0},{7,1},{8,14},{9,15},{10,... | collective-permute-start | bytes 98312 | tf_op jit(solution)/shard_map/ppermute | solution.py:284
  30.3 3.9 %collective-permute-start.11 = (f32[2,32,128]{2,1,0:T(8,128)S(1)}, f32[2,32,128]{2,1,0:T(8,128)S(1)}, u32[]{:S(2)}, u32[]{:S(2)}) collective-permute-start(f32[2,32,128]{2,1,0:T(8,128)S(1)} %pad_maximum_fusion.refs_0_), channel_id=1, source_target_pairs={{0,4},{1,5},{2,6},{3,7},{4,0},{5,1},{6,2},{7,3},{8,12},{9,13},{10,... | collective-permute-start | bytes 98312 | tf_op jit(solution)/shard_map/ppermute | solution.py:284
  31.9 3.9 %collective-permute-start.10 = (f32[2,32,128]{2,1,0:T(8,128)S(1)}, f32[2,32,128]{2,1,0:T(8,128)S(1)}, u32[]{:S(2)}, u32[]{:S(2)}) collective-permute-start(f32[2,32,128]{2,1,0:T(8,128)S(1)} %pad_maximum_fusion.refs_0_), channel_id=1, source_target_pairs={{0,2},{1,3},{2,0},{3,1},{4,6},{5,7},{6,4},{7,5},{8,10},{9,11},{10,... | collective-permute-start | bytes 98312 | tf_op jit(solution)/shard_map/ppermute | solution.py:284
  36.2 4.2 %collective-permute-start.13 = (f32[32,256]{1,0:T(8,128)S(1)}, f32[32,256]{1,0:T(8,128)S(1)}, u32[]{:S(2)}, u32[]{:S(2)}) collective-permute-start(f32[32,256]{1,0:T(8,128)S(1)} %get-tuple-element.40), channel_id=1, source_target_pairs={{0,8},{8,0},{16,24},{24,16},{1,9},{9,1},{17,25},{25,17},{2,10},{10... | collective-permute-start | bytes 98312 | tf_op jit(solution)/shard_map/ppermute | solution.py:284
  37.8 5.7 %collective-permute-start.14 = (f32[32,256]{1,0:T(8,128)S(1)}, f32[32,256]{1,0:T(8,128)S(1)}, u32[]{:S(2)}, u32[]{:S(2)}) collective-permute-start(f32[32,256]{1,0:T(8,128)S(1)} %get-tuple-element.41), channel_id=1, source_target_pairs={{0,24},{8,16},{16,8},{24,0},{1,25},{9,17},{17,9},{25,1},{2,26},{10... | collective-permute-start | bytes 98312 | tf_op jit(solution)/shard_map/ppermute | solution.py:284
  40.3 5.2 %collective-permute-start.15 = (f32[32,256]{1,0:T(8,128)S(1)}, f32[32,256]{1,0:T(8,128)S(1)}, u32[]{:S(2)}, u32[]{:S(2)}) collective-permute-start(f32[32,256]{1,0:T(8,128)S(1)} %get-tuple-element.42), channel_id=1, source_target_pairs={{0,16},{8,24},{16,0},{24,8},{1,17},{9,25},{17,1},{25,9},{2,18},{10... | collective-permute-start | bytes 98312 | tf_op jit(solution)/shard_map/ppermute | solution.py:284

commit v9 on v8

--- a/solution.py
+++ b/solution.py
@@ -207,9 +207,8 @@
     terms_ref[...] = jnp.where(row_id == comps, atom_ref[...].astype(jnp.float32), result)
 
 
-def scatter_kernel(comps, atoms, flip, *refs):
-    own, near_a, near_b, far = refs[-4:]
-    pieces = [group.at[m] for group in refs[:-4] for m in range(group.shape[0])]
+def scatter_kernel(comps, atoms, flip, groups, own, send):
+    pieces = [groups.at[m, n] for m in range(groups.shape[0]) for n in range(groups.shape[1])]
     row_id = lax.broadcasted_iota(jnp.int32, (3 * atoms, LANES), 0)
     total = jnp.zeros((3 * ROWS, 3 * atoms), jnp.float32)
     for m in range(0, len(pieces), 2):
@@ -222,35 +221,29 @@
     sums = total[:ROWS] + total[ROWS : 2 * ROWS] + total[2 * ROWS :]
     own[...] = sums
     ahead, back = sums[:, atoms:], sums[:, : 2 * atoms]
+    far = jnp.concatenate([sums[:, :atoms], sums[:, 2 * atoms :]], axis=1)
     if flip:
-        odd = lax.rem(lax.axis_index("region"), 2) == 1
-        near_a[...] = jnp.where(odd, back, ahead)
-        near_b[...] = jnp.where(odd, ahead, back)
+        for slot in range(send.shape[0]):
+            away = lax.rem(slot - lax.axis_index("region") + 4, 4)
+            send[slot] = jnp.where(away == 1, ahead, jnp.where(away == 3, back, far))
     else:
-        near_a[...] = ahead
-        near_b[...] = back
-    far[:, :atoms] = sums[:, :atoms]
-    far[:, atoms:] = sums[:, 2 * atoms :]
+        send[0], send[1], send[2] = ahead, back, far
 
 
 def potential_kernel(
-    comps, atoms, flip, size_ref, own_ref, near_a_ref, near_b_ref, fa_ref, fb_ref, atom_ref,
-    low_ref, high_ref, mom_ref, pot_ref,
+    comps, atoms, flip, size_ref, own_ref, got_ref, atom_ref, low_ref, high_ref, mom_ref, pot_ref
 ):
     batches, points = pot_ref.shape
     near = 2 * low_ref.shape[0] // batches
     fields = [ref.at[n] for ref in (low_ref, high_ref) for n in range(ref.shape[0])]
     own = own_ref[...]
-    near_a, near_b = near_a_ref[...], near_b_ref[...]
+    slots = range(4)
     if flip:
-        odd = lax.rem(lax.axis_index("region"), 2) == 1
-        low = jnp.where(odd, near_a, near_b)
-        high = jnp.where(odd, near_b, near_a)
-    else:
-        low, high = near_a, near_b
-    before = fa_ref[:, atoms:] + low[:, :atoms] + own[:, :atoms]
+        slots = [lax.rem(lax.axis_index("region") + d, 4) for d in (3, 1, 2, 2)]
+    low, high, far_a, far_b = [got_ref[slot] for slot in slots]
+    before = far_a[:, atoms:] + low[:, :atoms] + own[:, :atoms]
     here = low[:, atoms:] + own[:, atoms : 2 * atoms] + high[:, :atoms]
-    after = own[:, 2 * atoms :] + high[:, atoms:] + fb_ref[:, :atoms]
+    after = own[:, 2 * atoms :] + high[:, atoms:] + far_b[:, :atoms]
 
     mine = mom_ref.shape[0]
     want = lax.broadcasted_iota(jnp.int32, (mine, atoms), 0) + lax.axis_index("dev") * mine
@@ -392,13 +385,13 @@
         starts, g_low = lax.optimization_barrier((starts, g_low))
         chosen = selected(0, 0, starts, masked)
         second = turned(chosen, 2, 4)
-        g_high, hpad_high, _ = field(half, chosen)
-        first, g_high = lax.optimization_barrier((first, g_high))
+        first, later, _ = lax.optimization_barrier((first, masked, chosen))
         chosen = selected(4, 2, starts, first)
         third = turned(chosen, 2, 4)
-        phit, weights = turned_basis(chosen)
+        g_high, hpad_high, _ = field(half, chosen)
+        phit, weights = turned_basis(g_high)
         second, phit = lax.optimization_barrier((second, phit))
-        sent = (masked, first, second, third)
+        sent = (later, first, second, third)
         pieces = [piece for value in sent for piece in (value, crossed(value, "dev", 1))]
     else:
         g_low, hpad_low, atom_rows = field(0, masked)
@@ -428,27 +421,28 @@
 
     if dev_count == 8:
         both = jnp.stack([terms, crossed(terms, "dev", 1)])
-        groups = [both] + [crossed(both, "dev", m) for m in (2, 4, 6)]
+        quads = [[i for i in range(dev_count) if i % 2 == core] for core in range(2)]
+        copies = jnp.broadcast_to(both[None], (4,) + both.shape)
+        groups = lax.all_to_all(copies, "dev", 0, 0, axis_index_groups=quads)
     else:
-        groups = [lax.all_gather(terms, "dev", axis=0)]
+        groups = lax.all_gather(terms, "dev", axis=0).reshape(-1, 2, *terms.shape)
     flip = region_count == 4
-    own, near_a, near_b, far = pl.pallas_call(
+    own, send = pl.pallas_call(
         functools.partial(scatter_kernel, comps, atoms, flip),
-        out_shape=tuple(jax.ShapeDtypeStruct((ROWS, n * atoms), f32) for n in (3, 2, 2, 2)),
-        in_specs=[VMEM] * len(groups),
-        out_specs=(VMEM,) * 4,
+        out_shape=(
+            jax.ShapeDtypeStruct((ROWS, 3 * atoms), f32),
+            jax.ShapeDtypeStruct((4 if flip else 3, ROWS, 2 * atoms), f32),
+        ),
+        in_specs=[VMEM],
+        out_specs=(VMEM,) * 2,
         compiler_params=PARAMS,
         name="scatter",
-    )(*groups)
+    )(groups)
     if flip:
-        far_a = far_b = crossed(far, "region", 2)
-        near_a = crossed(near_a, "region", 1)
-        near_b = crossed(near_b, "region", 3)
+        got = lax.all_to_all(send, "region", 0, 0)
     else:
-        far_a = shifted(far, "region", 2)
-        far_b = shifted(far, "region", -2)
-        near_a = shifted(near_a, "region", 1)
-        near_b = shifted(near_b, "region", -1)
+        steps = ((0, 1), (1, -1), (2, 2), (2, -2))
+        got = jnp.stack([shifted(send[slot], "region", step) for slot, step in steps])
 
     moments, potential = pl.pallas_call(
         functools.partial(potential_kernel, comps, atoms, flip),
@@ -456,11 +450,11 @@
             jax.ShapeDtypeStruct((mine, comps), f32),
             jax.ShapeDtypeStruct((batches, points), f32),
         ),
-        in_specs=[SMEM] + [VMEM] * 8,
+        in_specs=[SMEM] + [VMEM] * 5,
         out_specs=(VMEM, VMEM),
         compiler_params=PARAMS,
         name="potential",
-    )(batch_sizes, own, near_a, near_b, far_a, far_b, atom_rows, g_low, g_high)
+    )(batch_sizes, own, got, atom_rows, g_low, g_high)
     return (density, moments.T, potential)
 
 

time: 47.7 us -> 49.1 us (1.029)
  blocking collectives: 0 us -> 18.1 us
  waiting for transfers between devices: 12.4 us -> 2.88 us
  starting transfers between devices: 15.2 us -> 7.83 us
    all_to_all x0 -> x2, blocking collectives: none -> 18.1 us  [the longest x1 10.6 us: per_device(): got = lax.all_to_all(send, 'region', 0, 0)]
    ppermute x12 -> x6, waiting for transfers between devices: 11 us -> 2.87 us  [crossed(): lax.ppermute(value, axis, [(i, i ^ m) for i in range(lax.axis_size(axis))])]
    ppermute x12 -> x6, starting transfers between devices: 8.97 us -> 1.15 us  [crossed(): lax.ppermute(value, axis, [(i, i ^ m) for i in range(lax.axis_size(axis))])]
    ppermute x4, waiting for transfers between devices: 1.38 us -> 0.01 us  [turned(): lax.ppermute(value, 'dev', [(i, i ^ (odd if i % 2 else even)) for i in ra...]
  transfers between devices with their start and end apart: 16 -> 10, of which waited for: 9 -> 4; matrix products, arithmetic and copies ran while one was open for 1% -> 2% of each run, Pallas kernels for 23% -> 20%
where the time goes in v9:
time: 49.1 us; the launch traced here: 48.7 us
  blocking collectives  18.1 us (37%)
  Pallas kernels  17 us (35%)
  starting transfers between devices  7.83 us (16%)
  waiting for transfers between devices  2.88 us (6%)
  between operations  1.4 us (3%)
  other arithmetic  0.76 us (2%)
  local copies, waits for them, and re-layouts  0.71 us (1%)
    all_to_all x1, blocking collectives, per_device(): got = lax.all_to_all(send, 'region', 0, 0)  10.6 us
    all_to_all x1, blocking collectives, per_device(): groups = lax.all_to_all(copies, 'dev', 0, 0, axis_index_groups=quads)  7.54 us
    ppermute x4, starting transfers between devices, turned(): lax.ppermute(value, 'dev', [(i, i ^ (odd if i % 2 else even)) for i in ra...  6.68 us
    pallas_call x2, Pallas kernels, field(): pl.pallas_call(functools.partial(field_kernel, begin), out_shape=(pltpu.V...  5.6 us
    pallas_call x1, Pallas kernels, per_device(): pl.pallas_call(density_kernel, out_shape=(jax.ShapeDtypeStruct((batches,...  3.77 us
    pallas_call x1, Pallas kernels, turned_basis(): pl.pallas_call(turn_kernel, out_shape=(pltpu.VMEM((batches, near_blocks,...  2.91 us
    ppermute x6, waiting for transfers between devices, crossed(): lax.ppermute(value, axis, [(i, i ^ m) for i in range(lax.axis_size(axis))])  2.87 us
    pallas_call x1, Pallas kernels, per_device(): pl.pallas_call(functools.partial(potential_kernel, comps, atoms, flip), o...  1.88 us
  transfers between devices with their start and end apart: 10, of which 4 were waited for; matrix products, arithmetic and copies ran while one was open for 2% of the time, Pallas kernels for 20%

profile of v9, /device:TPU:0, one launch (start us, length us, event | category | flops | bytes accessed | tf_op | source)
XLA Modules:
  0.0 48.7 jit_solution(13338437346791383840)
XLA Ops:
  0.6 1.3 %mask.1.rows_ref.refs_0_ = bf16[3,4,128,128]{3,2,1,0:T(8,128)(2,1)S(1)} custom-call(s32[3,4]{1,0:T(4,128)} %mask_hbm.1, bf16[3,4,128,128]{3,2,1,0:T(8,128)(2,1)} %rows_hbm.1), custom_call_target="tpu_custom_call" | custom-call | tf_op jit(solution)/shard_map/mask/pallas_call | solution.py:312
  1.9 3.0 %collective-permute-start.3 = (bf16[3,4,128,128]{3,2,1,0:T(8,128)(2,1)S(1)}, bf16[3,4,128,128]{3,2,1,0:T(8,128)(2,1)S(1)}, u32[]{:S(2)}, u32[]{:S(2)}) collective-permute-start(bf16[3,4,128,128]{3,2,1,0:T(8,128)(2,1)S(1)} %mask.1.rows_ref.refs_0_), channel_id=1, source_target_pairs={{0,4},{1,3},{2,6},{3,1},{4,0},{5,7},{6,2},{7,5},{8,12},{9,11},{10,... | collective-permute-start | bytes 1179656 | tf_op jit(solution)/shard_map/ppermute | solution.py:282
  5.0 0.0 collective-permute-start
  5.6 0.6 %collective-permute-done = s32[1]{0:T(128)} collective-permute-done((s32[1]{0:T(128)}, s32[1]{0:T(128)}, u32[]{:S(2)}, u32[]{:S(2)}) %collective-permute-start) | collective-permute-done | bytes 36 | tf_op jit(solution)/shard_map/ppermute | solution.py:277
  6.2 0.8 %pad_add_fusion.after_hbm = s32[2]{0:T(128)S(1)} fusion(s32[1]{0:T(128)} %collective-permute-done, s32[1]{0:T(128)S(6)} %copy.14.start_ref), kind=kLoop, calls=%fused_computation.1 | loop fusion | flops 2 | bytes 16 | tf_op jit(solution)/shard_map/concatenate | solution.py:382
  7.0 1.5 %collective-permute-start.1 = (s32[2]{0:T(128)S(1)}, s32[2]{0:T(128)S(1)}, u32[]{:S(2)}, u32[]{:S(2)}) collective-permute-start(s32[2]{0:T(128)S(1)} %pad_add_fusion.after_hbm), channel_id=1, source_target_pairs={{0,2},{1,5},{2,0},{3,7},{4,6},{5,1},{6,4},{7,3},{8,10},{9,13},{10,... | collective-permute-start | bytes 32 | tf_op jit(solution)/shard_map/ppermute | solution.py:282
  8.5 0.0 copy-start.1
  8.5 0.7 %copy-done.1 = s32[12,6]{0,1:T(8,128)S(1)} copy-done((s32[12,6]{0,1:T(8,128)S(1)}, s32[12,6]{0,1:T(8,128)}, u32[]{:S(2)}) %copy-start.1) | copy-done | bytes 312
  9.2 2.7 %field.2 = (f32[36,25,256]{2,1,0:T(8,128)S(1)}, bf16[36,32,256]{2,1,0:T(8,128)(2,1)S(1)}, s32[1,128]{1,0:T(1,128)S(1)}) custom-call(s32[2]{0:T(128)S(1)} %pad_add_fusion.after_hbm, s32[6,12]{1,0:T(8,128)S(1)} %bitcast.6, f32[16,25]{1,0:T(8,128)} %bitcast.9, f32[12,6,256]{2,1,0:T(8,128)} %radius_hbm.3, bf16[12,6,25,256]{3,2,1,0:T(8,128)(2,1)} %harm_hbm.3), custom_call_target="tpu_custom_call" | custom-call | flops 2000000000 | bytes 8000000 | tf_op jit(solution)/shard_map/field/pallas_call | solution.py:329
  11.8 0.0 collective-permute-done.1.starts_ref
  11.8 0.6 %select.2 = bf16[2,4,128,128]{3,2,1,0:T(8,128)(2,1)S(1)} custom-call(s32[2]{0:T(128)S(1)} %collective-permute-done.1.starts_ref, bf16[3,4,128,128]{3,2,1,0:T(8,128)(2,1)S(1)} %mask.1.rows_ref.refs_0_), custom_call_target="tpu_custom_call" | custom-call | tf_op jit(solution)/shard_map/select/pallas_call | solution.py:369
  12.4 0.6 %collective-permute-start.2 = (bf16[2,4,128,128]{3,2,1,0:T(8,128)(2,1)S(1)}, bf16[2,4,128,128]{3,2,1,0:T(8,128)(2,1)S(1)}, u32[]{:S(2)}, u32[]{:S(2)}) collective-permute-start(bf16[2,4,128,128]{3,2,1,0:T(8,128)(2,1)S(1)} %select.2), channel_id=1, source_target_pairs={{0,2},{1,5},{2,0},{3,7},{4,6},{5,1},{6,4},{7,3},{8,10},{9,13},{10,... | collective-permute-start | bytes 786440 | tf_op jit(solution)/shard_map/ppermute | solution.py:282
  13.0 0.0 collective-permute-done.3.rows_ref.refs_2_
  13.0 0.6 %select.3.after_hbm = bf16[2,4,128,128]{3,2,1,0:T(8,128)(2,1)S(1)} custom-call(s32[2]{0:T(128)S(1)} %collective-permute-done.1.starts_ref, bf16[3,4,128,128]{3,2,1,0:T(8,128)(2,1)S(1)} %collective-permute-done.3.rows_ref.refs_2_), custom_call_target="tpu_custom_call" | custom-call | tf_op jit(solution)/shard_map/select/pallas_call | solution.py:369
  13.6 0.1 collective-permute-start.5
  13.7 1.6 %collective-permute-start.7 = (bf16[2,4,128,128]{3,2,1,0:T(8,128)(2,1)S(1)}, bf16[2,4,128,128]{3,2,1,0:T(8,128)(2,1)S(1)}, u32[]{:S(2)}, u32[]{:S(2)}) collective-permute-start(bf16[2,4,128,128]{3,2,1,0:T(8,128)(2,1)S(1)} %select.3.after_hbm), channel_id=1, source_target_pairs={{0,2},{1,5},{2,0},{3,7},{4,6},{5,1},{6,4},{7,3},{8,10},{9,13},{10,... | collective-permute-start | bytes 786440 | tf_op jit(solution)/shard_map/ppermute | solution.py:282
  15.3 2.9 %field.3 = (f32[36,25,256]{2,1,0:T(8,128)S(1)}, bf16[36,32,256]{2,1,0:T(8,128)(2,1)S(1)}, s32[1,128]{1,0:T(1,128)}) custom-call(bf16[2,4,128,128]{3,2,1,0:T(8,128)(2,1)S(1)} %select.3.after_hbm, s32[6,12]{1,0:T(8,128)S(1)} %bitcast.7, f32[16,25]{1,0:T(8,128)} %bitcast.10, f32[12,6,256]{2,1,0:T(8,128)} %radius_hbm.3, bf16[12,6,25,256]{3,2,1,0:T(8,128)(2,1)} %harm_hbm.3), custom_call_target="tpu_custom_call" | custom-call | flops 2000000000 | bytes 8000000 | tf_op jit(solution)/shard_map/field/pallas_call | solution.py:329
  18.2 0.1 collective-permute-start.4
  18.3 0.0 copy-start
  18.3 0.0 copy-start.2
  18.3 2.9 %turn.1 = (bf16[12,4,128,256]{3,2,1,0:T(8,128)(2,1)S(1)}, f32[12,6,256]{2,1,0:T(8,128)S(1)}) custom-call(f32[36,25,256]{2,1,0:T(8,128)S(1)} %get-tuple-element.28.after_hbm.high_ref, bf16[12,4,256,128]{3,2,1,0:T(8,128)(2,1)} %basis_hbm.1, f32[12,6,256]{2,1,0:T(8,128)} %part_hbm.1), custom_call_target="tpu_custom_call" | custom-call | flops 2000000000 | bytes 8000000 | tf_op jit(solution)/shard_map/turn/pallas_call | solution.py:352
  21.2 0.0 collective-permute-done.2.refs_4_
  21.2 0.6 %collective-permute-start.6 = (bf16[2,4,128,128]{3,2,1,0:T(8,128)(2,1)S(1)}, bf16[2,4,128,128]{3,2,1,0:T(8,128)(2,1)S(1)}, u32[]{:S(2)}, u32[]{:S(2)}) collective-permute-start(bf16[2,4,128,128]{3,2,1,0:T(8,128)(2,1)S(1)} %collective-permute-done.2.refs_4_), channel_id=1, source_target_pairs={{0,1},{1,0},{2,3},{3,2},{4,5},{5,4},{6,7},{7,6},{8,9},{9,8},{10,11... | collective-permute-start | bytes 786440 | tf_op jit(solution)/shard_map/ppermute | solution.py:277
  21.8 0.0 collective-permute-done.7.refs_6_
  21.8 0.1 collective-permute-start.8
  21.9 1.1 %collective-permute-done.6.refs_5_ = bf16[2,4,128,128]{3,2,1,0:T(8,128)(2,1)S(1)} collective-permute-done((bf16[2,4,128,128]{3,2,1,0:T(8,128)(2,1)S(1)}, bf16[2,4,128,128]{3,2,1,0:T(8,128)(2,1)S(1)}, u32[]{:S(2)}, u32[]{:S(2)}) %collective-permute-start.6) | collective-permute-done | bytes 262176 | tf_op jit(solution)/shard_map/ppermute | solution.py:277
  23.0 0.0 collective-permute-done.4.refs_1_
  23.0 0.0 collective-permute-done.5.refs_3_
  23.0 0.4 collective-permute-done.8.refs_7_
  23.3 0.0 copy-done
  23.3 0.0 copy-done.2
  23.3 3.8 %density.1 = (f32[12,256]{1,0:T(8,128)}, f32[32,128]{1,0:T(8,128)S(1)}) custom-call(s32[1]{0:T(128)S(6)} %copy.14.start_ref, s32[1,12]{1,0:T(1,128)S(1)} %copy-done.2, s32[1,12]{1,0:T(1,128)S(1)} %copy-done, s32[1,128]{1,0:T(1,128)S(1)} %get-tuple-element.24.atom_ref, bf16[12,4,128,256]{3,2,1,0:T(8,128)(2,1)S(1)} %get-tuple-element.30.phit_ref, ...), custom_call_target="tpu_custom_call" | custom-call | flops 2000000000 | bytes 6000000 | tf_op jit(solution)/shard_map/density/pallas_call | solution.py:402
  27.1 0.4 collective-permute-start.9
  27.5 0.8 %collective-permute-done.9 = f32[32,128]{1,0:T(8,128)S(1)} collective-permute-done((f32[32,128]{1,0:T(8,128)S(1)}, f32[32,128]{1,0:T(8,128)S(1)}, u32[]{:S(2)}, u32[]{:S(2)}) %collective-permute-start.9) | collective-permute-done | bytes 16416 | tf_op jit(solution)/shard_map/ppermute | solution.py:277
  28.3 7.5 %all_to_all.10.groups = f32[4,2,32,128]{3,2,1,0:T(8,128)S(1)} all-to-all(f32[4,2,32,128]{3,2,1,0:T(8,128)S(1)} %broadcast_in_dim.2), channel_id=1, replica_groups={{0,2,4,6},{1,3,5,7},{8,10,12,14},{9,11,13,15},{16,18,20,22},{17,19,21,2..., dimensions={0} | all-to-all | bytes 262144 | tf_op jit(solution)/shard_map/all_to_all | solution.py:426
  35.9 0.4 scatter.1
  36.3 10.6 %all_to_all.11.got_ref = f32[4,32,256]{2,1,0:T(8,128)S(1)} all-to-all(f32[4,32,256]{2,1,0:T(8,128)S(1)} %get-tuple-element.39), channel_id=1, replica_groups=mesh['region'=4,'dev'=8] {'region'}, dimensions={0} | all-to-all | bytes 262144 | tf_op jit(solution)/shard_map/all_to_all | solution.py:442
  46.8 1.9 %potential.1 = (f32[16,25]{1,0:T(8,128)}, f32[12,256]{1,0:T(8,128)}) custom-call(s32[1,12]{1,0:T(1,128)S(1)} %copy-done, f32[32,384]{1,0:T(8,128)S(1)} %get-tuple-element.38.own_ref, f32[4,32,256]{2,1,0:T(8,128)S(1)} %all_to_all.11.got_ref, s32[1,128]{1,0:T(1,128)S(1)} %get-tuple-element.24.atom_ref, f32[36,25,256]{2,1,0:T(8,128)S(1)} %get-tuple-element.40.low_ref, ...), custom_call_target="tpu_custom_call" | custom-call | tf_op jit(solution)/shard_map/potential/pallas_call | solution.py:447
  (2 shorter events, 0.0 us)
Async XLA Ops:
  1.9 11.1 %collective-permute-start.3 = (bf16[3,4,128,128]{3,2,1,0:T(8,128)(2,1)S(1)}, bf16[3,4,128,128]{3,2,1,0:T(8,128)(2,1)S(1)}, u32[]{:S(2)}, u32[]{:S(2)}) collective-permute-start(bf16[3,4,128,128]{3,2,1,0:T(8,128)(2,1)S(1)} %mask.1.rows_ref.refs_0_), channel_id=1, source_target_pairs={{0,4},{1,3},{2,6},{3,1},{4,0},{5,7},{6,2},{7,5},{8,12},{9,11},{10,... | collective-permute-start | bytes 1179656 | tf_op jit(solution)/shard_map/ppermute | solution.py:282
  5.0 1.2 %collective-permute-start = (s32[1]{0:T(128)}, s32[1]{0:T(128)}, u32[]{:S(2)}, u32[]{:S(2)}) collective-permute-start(s32[1]{0:T(128)} %param.14), channel_id=1, source_target_pairs={{0,1},{1,0},{2,3},{3,2},{4,5},{5,4},{6,7},{7,6},{8,9},{9,8},{10,11... | collective-permute-start | bytes 20 | tf_op jit(solution)/shard_map/ppermute | solution.py:277
  7.0 4.9 %collective-permute-start.1 = (s32[2]{0:T(128)S(1)}, s32[2]{0:T(128)S(1)}, u32[]{:S(2)}, u32[]{:S(2)}) collective-permute-start(s32[2]{0:T(128)S(1)} %pad_add_fusion.after_hbm), channel_id=1, source_target_pairs={{0,2},{1,5},{2,0},{3,7},{4,6},{5,1},{6,4},{7,3},{8,10},{9,13},{10,... | collective-permute-start | bytes 32 | tf_op jit(solution)/shard_map/ppermute | solution.py:282
  8.5 0.7 %copy-start.1 = (s32[12,6]{0,1:T(8,128)S(1)}, s32[12,6]{0,1:T(8,128)}, u32[]{:S(2)}) copy-start(s32[12,6]{0,1:T(8,128)} %param.17) | copy-start | bytes 868
  12.4 8.8 %collective-permute-start.2 = (bf16[2,4,128,128]{3,2,1,0:T(8,128)(2,1)S(1)}, bf16[2,4,128,128]{3,2,1,0:T(8,128)(2,1)S(1)}, u32[]{:S(2)}, u32[]{:S(2)}) collective-permute-start(bf16[2,4,128,128]{3,2,1,0:T(8,128)(2,1)S(1)} %select.2), channel_id=1, source_target_pairs={{0,2},{1,5},{2,0},{3,7},{4,6},{5,1},{6,4},{7,3},{8,10},{9,13},{10,... | collective-permute-start | bytes 786440 | tf_op jit(solution)/shard_map/ppermute | solution.py:282
  13.6 9.3 %collective-permute-start.5 = (bf16[3,4,128,128]{3,2,1,0:T(8,128)(2,1)S(1)}, bf16[3,4,128,128]{3,2,1,0:T(8,128)(2,1)S(1)}, u32[]{:S(2)}, u32[]{:S(2)}) collective-permute-start(bf16[3,4,128,128]{3,2,1,0:T(8,128)(2,1)S(1)} %collective-permute-done.3.rows_ref.refs_2_), channel_id=1, source_target_pairs={{0,1},{1,0},{2,3},{3,2},{4,5},{5,4},{6,7},{7,6},{8,9},{9,8},{10,11... | collective-permute-start | bytes 1179656 | tf_op jit(solution)/shard_map/ppermute | solution.py:277
  13.7 8.1 %collective-permute-start.7 = (bf16[2,4,128,128]{3,2,1,0:T(8,128)(2,1)S(1)}, bf16[2,4,128,128]{3,2,1,0:T(8,128)(2,1)S(1)}, u32[]{:S(2)}, u32[]{:S(2)}) collective-permute-start(bf16[2,4,128,128]{3,2,1,0:T(8,128)(2,1)S(1)} %select.3.after_hbm), channel_id=1, source_target_pairs={{0,2},{1,5},{2,0},{3,7},{4,6},{5,1},{6,4},{7,3},{8,10},{9,13},{10,... | collective-permute-start | bytes 786440 | tf_op jit(solution)/shard_map/ppermute | solution.py:282
  18.2 4.8 %collective-permute-start.4 = (bf16[3,4,128,128]{3,2,1,0:T(8,128)(2,1)S(1)}, bf16[3,4,128,128]{3,2,1,0:T(8,128)(2,1)S(1)}, u32[]{:S(2)}, u32[]{:S(2)}) collective-permute-start(bf16[3,4,128,128]{3,2,1,0:T(8,128)(2,1)S(1)} %mask.1.rows_ref.refs_0_), channel_id=1, source_target_pairs={{0,1},{1,0},{2,3},{3,2},{4,5},{5,4},{6,7},{7,6},{8,9},{9,8},{10,11... | collective-permute-start | bytes 1179656 | tf_op jit(solution)/shard_map/ppermute | solution.py:277
  18.3 5.1 %copy-start = (s32[1,12]{1,0:T(1,128)S(1)}, s32[1,12]{1,0:T(1,128)}, u32[]{:S(2)}) copy-start(s32[1,12]{1,0:T(1,128)} %size_ref.3) | copy-start | bytes 148
  18.3 5.0 %copy-start.2 = (s32[1,12]{1,0:T(1,128)S(1)}, s32[1,12]{1,0:T(1,128)}, u32[]{:S(2)}) copy-start(s32[1,12]{1,0:T(1,128)} %offset_ref.1) | copy-start | bytes 148
  21.2 1.7 %collective-permute-start.6 = (bf16[2,4,128,128]{3,2,1,0:T(8,128)(2,1)S(1)}, bf16[2,4,128,128]{3,2,1,0:T(8,128)(2,1)S(1)}, u32[]{:S(2)}, u32[]{:S(2)}) collective-permute-start(bf16[2,4,128,128]{3,2,1,0:T(8,128)(2,1)S(1)} %collective-permute-done.2.refs_4_), channel_id=1, source_target_pairs={{0,1},{1,0},{2,3},{3,2},{4,5},{5,4},{6,7},{7,6},{8,9},{9,8},{10,11... | collective-permute-start | bytes 786440 | tf_op jit(solution)/shard_map/ppermute | solution.py:277
  21.8 1.5 %collective-permute-start.8 = (bf16[2,4,128,128]{3,2,1,0:T(8,128)(2,1)S(1)}, bf16[2,4,128,128]{3,2,1,0:T(8,128)(2,1)S(1)}, u32[]{:S(2)}, u32[]{:S(2)}) collective-permute-start(bf16[2,4,128,128]{3,2,1,0:T(8,128)(2,1)S(1)} %collective-permute-done.7.refs_6_), channel_id=1, source_target_pairs={{0,1},{1,0},{2,3},{3,2},{4,5},{5,4},{6,7},{7,6},{8,9},{9,8},{10,11... | collective-permute-start | bytes 786440 | tf_op jit(solution)/shard_map/ppermute | solution.py:277
  27.1 1.2 %collective-permute-start.9 = (f32[32,128]{1,0:T(8,128)S(1)}, f32[32,128]{1,0:T(8,128)S(1)}, u32[]{:S(2)}, u32[]{:S(2)}) collective-permute-start(f32[32,128]{1,0:T(8,128)S(1)} %get-tuple-element.37), channel_id=1, source_target_pairs={{0,1},{1,0},{2,3},{3,2},{4,5},{5,4},{6,7},{7,6},{8,9},{9,8},{10,11... | collective-permute-start | bytes 49160 | tf_op jit(solution)/shard_map/ppermute | solution.py:277

commit v10 on v8

--- a/solution.py
+++ b/solution.py
@@ -76,8 +76,7 @@
 
 
 def field_kernel(
-    begin, after_hbm, near_ref, table_hbm, radius_hbm, harm_hbm,
-    g_ref, hpad_ref, atom_ref, table_ref, radius_ref, harm_ref, sems,
+    begin, after_hbm, table_hbm, radius_hbm, harm_hbm, g_ref, table_ref, radius_ref, harm_ref, sems
 ):
     batches, near, comps, points = harm_ref.shape
     knots = table_ref.shape[0]
@@ -88,6 +87,39 @@
     copies = [pltpu.make_async_copy(a, b, sems.at[n]) for n, (a, b) in enumerate(moves)]
     for copy in copies:
         copy.start()
+    knot = lax.broadcasted_iota(jnp.int32, (knots, points), 0).astype(jnp.float32)
+    for copy in copies:
+        copy.wait()
+    r_hi, r_lo = split2(table_ref[...].T)
+    coeffs = jnp.concatenate([r_hi, r_hi, r_lo], axis=1)
+
+    def body(b, carry):
+        rows = radius_ref[b]
+        for i in range(near):
+            spline = cubic(jnp.abs(rows[i : i + 1, :] - knot))
+            s_hi, s_lo = split2(spline)
+            radial = dot(coeffs, jnp.concatenate([s_hi, s_lo, s_hi], axis=0))
+            g_ref[b * near + i] = radial * harm_ref[b, i].astype(jnp.float32)
+        return carry
+
+    lax.fori_loop(0, batches, body, 0, unroll=2)
+
+
+def turn_kernel(
+    after_hbm, near_ref, basis_hbm, part_hbm, harm_hbm,
+    phit_ref, part_ref, hpad_ref, atom_ref, basis, harm_ref, sems,
+):
+    batches, near_blocks = basis.shape[:2]
+    near, comps, points = harm_ref.shape[1:]
+    halves = [pl.ds(0, batches // 2), pl.ds(batches // 2, batches - batches // 2)]
+    copies = [
+        pltpu.make_async_copy(basis_hbm.at[half], basis.at[half], sems.at[n])
+        for n, half in enumerate(halves)
+    ]
+    copies.append(pltpu.make_async_copy(harm_hbm, harm_ref, sems.at[2]))
+    copies.append(pltpu.make_async_copy(part_hbm, part_ref, sems.at[3]))
+    for copy in copies:
+        copy.start()
     lane = lax.broadcasted_iota(jnp.int32, atom_ref.shape, 1)
     atom = jnp.full(atom_ref.shape, -1, jnp.int32)
     for b in range(near_ref.shape[1]):
@@ -96,40 +128,15 @@
     atom_ref[...] = atom
     for n in range(batches * near):
         hpad_ref[n, ROWS // 2 :, :] = jnp.zeros((ROWS // 2, points), jnp.bfloat16)
-    knot = lax.broadcasted_iota(jnp.int32, (knots, points), 0).astype(jnp.float32)
-    for copy in copies:
-        copy.wait()
-    r_hi, r_lo = split2(table_ref[...].T)
-    coeffs = jnp.concatenate([r_hi, r_hi, r_lo], axis=1)
-
-    def body(b, carry):
-        rows = radius_ref[b]
-        for i in range(near):
-            spline = cubic(jnp.abs(rows[i : i + 1, :] - knot))
-            s_hi, s_lo = split2(spline)
-            radial = dot(coeffs, jnp.concatenate([s_hi, s_lo, s_hi], axis=0))
-            h = harm_ref[b, i]
-            g_ref[b * near + i] = radial * h.astype(jnp.float32)
-            hpad_ref[b * near + i, 0:comps, :] = h
-        return carry
-
-    lax.fori_loop(0, batches, body, 0, unroll=2)
-
-
-def turn_kernel(after_hbm, basis_hbm, part_hbm, phit_ref, part_ref, basis, sems):
-    batches, near_blocks = basis.shape[:2]
-    halves = [pl.ds(0, batches // 2), pl.ds(batches // 2, batches - batches // 2)]
-    copies = [
-        pltpu.make_async_copy(basis_hbm.at[half], basis.at[half], sems.at[n])
-        for n, half in enumerate(halves)
-    ]
-    copies.append(pltpu.make_async_copy(part_hbm, part_ref, sems.at[2]))
-    for copy in copies:
-        copy.start()
 
     def turn(b, carry):
         for j in range(near_blocks):
             phit_ref[b, j] = basis[b, j].T
+        return carry
+
+    def pad(b, carry):
+        for i in range(near):
+            hpad_ref[b * near + i, 0:comps, :] = harm_ref[b, i]
         return carry
 
     copies[0].wait()
@@ -137,10 +144,12 @@
     copies[1].wait()
     lax.fori_loop(batches // 2, batches, turn, 0)
     copies[2].wait()
+    lax.fori_loop(0, batches, pad, 0)
+    copies[3].wait()
 
 
 def density_kernel(
-    start_ref, offset_ref, size_ref, atom_ref, phit_ref, part_ref, low_ref, high_ref, *refs
+    start_ref, offset_ref, size_ref, atom_ref, phit_ref, part_ref, hpad_ref, *refs
 ):
     dens_ref, terms_ref, window_ref, w_ref = refs[-4:]
     pieces = refs[:-4]
@@ -166,20 +175,19 @@
 
     def body(b, carry):
         first = offset_ref[0, b]
+        left = []
+        for j in range(near_blocks):
+            row = [
+                window_ref[first + j, f - j + 1] if 0 <= f - j + 1 < 4 else zero
+                for f in range(near_blocks)
+            ]
+            left.append(jnp.concatenate(row, axis=1))
+        right = phit_ref[b].reshape(near_blocks * width, points)
+        mixed = dot(jnp.concatenate(left, axis=0), right)
         total = jnp.zeros((width, points), jnp.float32)
-        for q, js in ((0, (0, 1, 2)), (2, (0, 1, 2, 3))):
-            left = []
-            for j in js:
-                pair = [
-                    window_ref[first + j, f - j + 1] if 0 <= f - j + 1 < 4 else zero
-                    for f in (q, q + 1)
-                ]
-                left.append(jnp.concatenate(pair, axis=1))
-            right = jnp.concatenate([phit_ref[b, q], phit_ref[b, q + 1]], axis=0)
-            mixed = dot(jnp.concatenate(left, axis=0), right)
-            for at, j in enumerate(js):
-                part = mixed[at * width : (at + 1) * width]
-                total = total + part * phit_ref[b, j].astype(jnp.float32)
+        for j in range(near_blocks):
+            part = mixed[j * width : (j + 1) * width]
+            total = total + part * phit_ref[b, j].astype(jnp.float32)
         summed = jnp.sum(total, axis=0, keepdims=True)
         alive = lane < size_ref[0, b]
         row = jnp.where(alive, summed, 0.0)
@@ -192,15 +200,11 @@
     columns = jnp.concatenate(split2(weights), axis=0)
     slot = lax.broadcasted_iota(jnp.int32, (1, 2 * LANES), 1) % LANES
     terms = jnp.zeros((ROWS, 2 * LANES), jnp.float32)
-    begin = 0
-    for ref in (low_ref, high_ref):
-        count = ref.shape[0]
-        cross = dot(ref[...].reshape(count * ROWS, points), columns, NT)
-        for n in range(count):
-            b, i = divmod(begin + n, near)
-            here = cross[n * ROWS : (n + 1) * ROWS]
-            terms = terms + jnp.where(slot == b * SLOT + i, here, 0.0)
-        begin = begin + count
+    cross = dot(hpad_ref[...].reshape(batches * near * ROWS, points), columns, NT)
+    for n in range(batches * near):
+        b, i = divmod(n, near)
+        here = cross[n * ROWS : (n + 1) * ROWS]
+        terms = terms + jnp.where(slot == b * SLOT + i, here, 0.0)
     result = terms[:, :LANES] + terms[:, LANES:]
     row_id = lax.broadcasted_iota(jnp.int32, (ROWS, LANES), 0)
     comps = ROWS - 7
@@ -331,17 +335,14 @@
     )(*held_in_hbm(block_mask, density_rows))
 
     half = batches // 2
+    work = pl.CostEstimate(flops=2_000_000_000, bytes_accessed=8_000_000, transcendentals=0)
 
     def field(begin, after):
         return pl.pallas_call(
             functools.partial(field_kernel, begin),
-            out_shape=(
-                pltpu.VMEM((half * near, comps, points), f32),
-                pltpu.VMEM((half * near, ROWS, points), bf16),
-                pltpu.VMEM((1, LANES), jnp.int32),
-            ),
-            in_specs=[HBM, SMEM] + [HBM] * 3,
-            out_specs=(VMEM,) * 3,
+            out_shape=pltpu.VMEM((half * near, comps, points), f32),
+            in_specs=[HBM] * 4,
+            out_specs=VMEM,
             scratch_shapes=[
                 pltpu.VMEM(radial_table.shape[::-1], f32),
                 pltpu.VMEM((half,) + radius.shape[1:], f32),
@@ -349,11 +350,9 @@
                 pltpu.SemaphoreType.DMA((3,)),
             ],
             compiler_params=WIDE,
-            cost_estimate=pl.CostEstimate(
-                flops=2_000_000_000, bytes_accessed=8_000_000, transcendentals=0
-            ),
+            cost_estimate=work,
             name="field",
-        )(after, atom_near.T, *held_in_hbm(radial_table.T, radius, harmonics))
+        )(after, *held_in_hbm(radial_table.T, radius, harmonics))
 
     def turned_basis(after):
         return pl.pallas_call(
@@ -361,16 +360,20 @@
             out_shape=(
                 pltpu.VMEM((batches, near_blocks, width, points), bf16),
                 pltpu.VMEM(partition.shape, f32),
+                pltpu.VMEM((batches * near, ROWS, points), bf16),
+                pltpu.VMEM((1, LANES), jnp.int32),
             ),
-            in_specs=[HBM] * 3,
-            out_specs=(VMEM,) * 2,
-            scratch_shapes=[pltpu.VMEM(basis_values.shape, bf16), pltpu.SemaphoreType.DMA((3,))],
+            in_specs=[HBM, SMEM] + [HBM] * 3,
+            out_specs=(VMEM,) * 4,
+            scratch_shapes=[
+                pltpu.VMEM(basis_values.shape, bf16),
+                pltpu.VMEM(harmonics.shape, bf16),
+                pltpu.SemaphoreType.DMA((4,)),
+            ],
             compiler_params=WIDE,
-            cost_estimate=pl.CostEstimate(
-                flops=2_000_000_000, bytes_accessed=8_000_000, transcendentals=0
-            ),
+            cost_estimate=work,
             name="turn",
-        )(after, *held_in_hbm(basis_values, partition))
+        )(after, atom_near.T, *held_in_hbm(basis_values, partition, harmonics))
 
     def selected(even, odd, starts, rows):
         return pl.pallas_call(
@@ -388,31 +391,26 @@
         first = turned(masked, 4, 2)
         pair = jnp.concatenate([window_start, beside])
         starts = turned(pair, 2, 4)
-        g_low, hpad_low, atom_rows = field(0, pair)
-        starts, g_low = lax.optimization_barrier((starts, g_low))
         chosen = selected(0, 0, starts, masked)
         second = turned(chosen, 2, 4)
-        g_high, hpad_high, _ = field(half, chosen)
-        first, g_high = lax.optimization_barrier((first, g_high))
+        first, later, _ = lax.optimization_barrier((first, masked, chosen))
         chosen = selected(4, 2, starts, first)
         third = turned(chosen, 2, 4)
-        phit, weights = turned_basis(chosen)
+        phit, weights, hpad, atom_rows = turned_basis(chosen)
         second, phit = lax.optimization_barrier((second, phit))
-        sent = (masked, first, second, third)
+        sent = (later, first, second, third)
         pieces = [piece for value in sent for piece in (value, crossed(value, "dev", 1))]
     else:
-        g_low, hpad_low, atom_rows = field(0, masked)
-        g_high, hpad_high, _ = field(half, masked)
-        phit, weights = turned_basis(masked)
+        phit, weights, hpad, atom_rows = turned_basis(masked)
         pieces = [lax.all_gather(masked, "dev", axis=0)]
 
     density, terms = pl.pallas_call(
         density_kernel,
         out_shape=(
-            jax.ShapeDtypeStruct((batches, points), f32),
-            jax.ShapeDtypeStruct((ROWS, LANES), f32),
+            pltpu.VMEM((batches, points), f32),
+            pltpu.VMEM((ROWS, LANES), f32),
         ),
-        in_specs=[SMEM] * 3 + [VMEM] * (5 + len(pieces)),
+        in_specs=[SMEM] * 3 + [VMEM] * (4 + len(pieces)),
         out_specs=(VMEM, VMEM),
         scratch_shapes=[
             pltpu.VMEM((dev_count, band, width, width), bf16),
@@ -422,7 +420,7 @@
         cost_estimate=pl.CostEstimate(flops=2_000_000_000, bytes_accessed=6_000_000, transcendentals=0),
         name="density",
     )(
-        window_start, batch_offsets, batch_sizes, atom_rows, phit, weights, hpad_low, hpad_high,
+        window_start, batch_offsets, batch_sizes, atom_rows, phit, weights, hpad,
         *pieces,
     )
 
@@ -431,6 +429,8 @@
         groups = [both] + [crossed(both, "dev", m) for m in (2, 4, 6)]
     else:
         groups = [lax.all_gather(terms, "dev", axis=0)]
+    g_low = field(0, groups[0])
+    *groups, g_low = lax.optimization_barrier((*groups, g_low))
     flip = region_count == 4
     own, near_a, near_b, far = pl.pallas_call(
         functools.partial(scatter_kernel, comps, atoms, flip),
@@ -440,15 +440,20 @@
         compiler_params=PARAMS,
         name="scatter",
     )(*groups)
+    g_high = field(half, own)
     if flip:
+        near_a = crossed(near_a, "region", 1)
         far_a = far_b = crossed(far, "region", 2)
-        near_a = crossed(near_a, "region", 1)
         near_b = crossed(near_b, "region", 3)
     else:
         far_a = shifted(far, "region", 2)
         far_b = shifted(far, "region", -2)
         near_a = shifted(near_a, "region", 1)
         near_b = shifted(near_b, "region", -1)
+
+    near_a, near_b, far_a, far_b, g_high = lax.optimization_barrier(
+        (near_a, near_b, far_a, far_b, g_high)
+    )
 
     moments, potential = pl.pallas_call(
         functools.partial(potential_kernel, comps, atoms, flip),

time: 47.7 us -> 45.3 us (0.950)
  waiting for transfers between devices: 12.4 us -> 11.1 us
  Pallas kernels: 16.9 us -> 16 us
    ppermute x12, waiting for transfers between devices: 11 us -> 6.79 us  [crossed(): lax.ppermute(value, axis, [(i, i ^ m) for i in range(lax.axis_size(axis))])]
    ppermute x4, waiting for transfers between devices: 1.38 us -> 4.29 us  [turned(): lax.ppermute(value, 'dev', [(i, i ^ (odd if i % 2 else even)) for i in ra...]
    pallas_call x3, Pallas kernels: 9.28 us -> 7.68 us  [the longest x2 4.14 us: field(): pl.pallas_call(functools.partial(field_kernel, begin), out_shape=pltpu.VM...]
    pallas_call x1, Pallas kernels: 2.9 us -> 3.64 us  [turned_basis(): pl.pallas_call(turn_kernel, out_shape=(pltpu.VMEM((batches, near_blocks,...]
  transfers between devices with their start and end apart: 16 -> 16, of which waited for: 9 -> 8; matrix products, arithmetic and copies ran while one was open for 1% -> 3% of each run, Pallas kernels for 23% -> 20%
where the time goes in v10:
time: 45.3 us; the launch traced here: 45.1 us
  Pallas kernels  16 us (35%)
  starting transfers between devices  15.2 us (34%)
  waiting for transfers between devices  11.1 us (25%)
  between operations  1.42 us (3%)
  other arithmetic  0.7 us (2%)
  local copies, waits for them, and re-layouts  0.62 us (1%)
    ppermute x12, starting transfers between devices, crossed(): lax.ppermute(value, axis, [(i, i ^ m) for i in range(lax.axis_size(axis))])  8.52 us
    ppermute x12, waiting for transfers between devices, crossed(): lax.ppermute(value, axis, [(i, i ^ m) for i in range(lax.axis_size(axis))])  6.79 us
    ppermute x4, starting transfers between devices, turned(): lax.ppermute(value, 'dev', [(i, i ^ (odd if i % 2 else even)) for i in ra...  6.68 us
    ppermute x4, waiting for transfers between devices, turned(): lax.ppermute(value, 'dev', [(i, i ^ (odd if i % 2 else even)) for i in ra...  4.29 us
    pallas_call x2, Pallas kernels, field(): pl.pallas_call(functools.partial(field_kernel, begin), out_shape=pltpu.VM...  4.14 us
    pallas_call x1, Pallas kernels, turned_basis(): pl.pallas_call(turn_kernel, out_shape=(pltpu.VMEM((batches, near_blocks,...  3.64 us
    pallas_call x1, Pallas kernels, per_device(): pl.pallas_call(density_kernel, out_shape=(pltpu.VMEM((batches, points), f...  3.54 us
    pallas_call x1, Pallas kernels, per_device(): pl.pallas_call(functools.partial(potential_kernel, comps, atoms, flip), o...  1.88 us
  transfers between devices with their start and end apart: 16, of which 8 were waited for; matrix products, arithmetic and copies ran while one was open for 3% of the time, Pallas kernels for 20%

profile of v10, /device:TPU:0, one launch (start us, length us, event | category | flops | bytes accessed | tf_op | source)
XLA Modules:
  0.0 45.1 jit_solution(3687909852389592344)
XLA Ops:
  0.6 0.0 copy-start.1
  0.6 1.3 %mask.1.rows_ref.refs_0_ = bf16[3,4,128,128]{3,2,1,0:T(8,128)(2,1)S(1)} custom-call(s32[3,4]{1,0:T(4,128)} %mask_hbm.1, bf16[3,4,128,128]{3,2,1,0:T(8,128)(2,1)} %rows_hbm.1), custom_call_target="tpu_custom_call" | custom-call | tf_op jit(solution)/shard_map/mask/pallas_call | solution.py:323
  2.0 3.0 %collective-permute-start.2 = (bf16[3,4,128,128]{3,2,1,0:T(8,128)(2,1)S(1)}, bf16[3,4,128,128]{3,2,1,0:T(8,128)(2,1)S(1)}, u32[]{:S(2)}, u32[]{:S(2)}) collective-permute-start(bf16[3,4,128,128]{3,2,1,0:T(8,128)(2,1)S(1)} %mask.1.rows_ref.refs_0_), channel_id=1, source_target_pairs={{0,4},{1,3},{2,6},{3,1},{4,0},{5,7},{6,2},{7,5},{8,12},{9,11},{10,... | collective-permute-start | bytes 1179656 | tf_op jit(solution)/shard_map/ppermute | solution.py:293
  5.0 0.0 collective-permute-start
  5.6 0.6 %collective-permute-done = s32[1]{0:T(128)} collective-permute-done((s32[1]{0:T(128)}, s32[1]{0:T(128)}, u32[]{:S(2)}, u32[]{:S(2)}) %collective-permute-start) | collective-permute-done | bytes 36 | tf_op jit(solution)/shard_map/ppermute | solution.py:288
  6.2 0.7 %pad_add_fusion = s32[2]{0:T(128)S(1)} fusion(s32[1]{0:T(128)} %collective-permute-done, s32[1]{0:T(128)S(6)} %copy.15.start_ref), kind=kLoop, calls=%fused_computation.1 | loop fusion | flops 2 | bytes 16 | tf_op jit(solution)/shard_map/concatenate | solution.py:392
  6.9 1.5 %collective-permute-start.1 = (s32[2]{0:T(128)S(1)}, s32[2]{0:T(128)S(1)}, u32[]{:S(2)}, u32[]{:S(2)}) collective-permute-start(s32[2]{0:T(128)S(1)} %pad_add_fusion), channel_id=1, source_target_pairs={{0,2},{1,5},{2,0},{3,7},{4,6},{5,1},{6,4},{7,3},{8,10},{9,13},{10,... | collective-permute-start | bytes 32 | tf_op jit(solution)/shard_map/ppermute | solution.py:293
  8.4 2.0 %collective-permute-done.1.starts_ref = s32[2]{0:T(128)S(1)} collective-permute-done((s32[2]{0:T(128)S(1)}, s32[2]{0:T(128)S(1)}, u32[]{:S(2)}, u32[]{:S(2)}) %collective-permute-start.1) | collective-permute-done | bytes 40 | tf_op jit(solution)/shard_map/ppermute | solution.py:293
  10.5 0.6 %select.2 = bf16[2,4,128,128]{3,2,1,0:T(8,128)(2,1)S(1)} custom-call(s32[2]{0:T(128)S(1)} %collective-permute-done.1.starts_ref, bf16[3,4,128,128]{3,2,1,0:T(8,128)(2,1)S(1)} %mask.1.rows_ref.refs_0_), custom_call_target="tpu_custom_call" | custom-call | tf_op jit(solution)/shard_map/select/pallas_call | solution.py:379
  11.1 1.6 %collective-permute-start.3 = (bf16[2,4,128,128]{3,2,1,0:T(8,128)(2,1)S(1)}, bf16[2,4,128,128]{3,2,1,0:T(8,128)(2,1)S(1)}, u32[]{:S(2)}, u32[]{:S(2)}) collective-permute-start(bf16[2,4,128,128]{3,2,1,0:T(8,128)(2,1)S(1)} %select.2), channel_id=1, source_target_pairs={{0,2},{1,5},{2,0},{3,7},{4,6},{5,1},{6,4},{7,3},{8,10},{9,13},{10,... | collective-permute-start | bytes 786440 | tf_op jit(solution)/shard_map/ppermute | solution.py:293
  12.6 0.0 collective-permute-done.2.rows_ref.refs_2_
  12.6 0.6 %select.3.after_hbm = bf16[2,4,128,128]{3,2,1,0:T(8,128)(2,1)S(1)} custom-call(s32[2]{0:T(128)S(1)} %collective-permute-done.1.starts_ref, bf16[3,4,128,128]{3,2,1,0:T(8,128)(2,1)S(1)} %collective-permute-done.2.rows_ref.refs_2_), custom_call_target="tpu_custom_call" | custom-call | tf_op jit(solution)/shard_map/select/pallas_call | solution.py:379
  13.2 0.6 %collective-permute-start.7 = (bf16[2,4,128,128]{3,2,1,0:T(8,128)(2,1)S(1)}, bf16[2,4,128,128]{3,2,1,0:T(8,128)(2,1)S(1)}, u32[]{:S(2)}, u32[]{:S(2)}) collective-permute-start(bf16[2,4,128,128]{3,2,1,0:T(8,128)(2,1)S(1)} %select.3.after_hbm), channel_id=1, source_target_pairs={{0,2},{1,5},{2,0},{3,7},{4,6},{5,1},{6,4},{7,3},{8,10},{9,13},{10,... | collective-permute-start | bytes 786440 | tf_op jit(solution)/shard_map/ppermute | solution.py:293
  13.8 0.0 collective-permute-start.5
  13.8 0.5 %collective-permute-start.4 = (bf16[3,4,128,128]{3,2,1,0:T(8,128)(2,1)S(1)}, bf16[3,4,128,128]{3,2,1,0:T(8,128)(2,1)S(1)}, u32[]{:S(2)}, u32[]{:S(2)}) collective-permute-start(bf16[3,4,128,128]{3,2,1,0:T(8,128)(2,1)S(1)} %mask.1.rows_ref.refs_0_), channel_id=1, source_target_pairs={{0,1},{1,0},{2,3},{3,2},{4,5},{5,4},{6,7},{7,6},{8,9},{9,8},{10,11... | collective-permute-start | bytes 1179656 | tf_op jit(solution)/shard_map/ppermute | solution.py:288
  14.3 0.0 copy-done.1
  14.3 0.0 copy-start
  14.3 0.0 copy-start.2
  14.3 3.6 %turn.1 = (bf16[12,4,128,256]{3,2,1,0:T(8,128)(2,1)S(1)}, f32[12,6,256]{2,1,0:T(8,128)S(1)}, bf16[72,32,256]{2,1,0:T(8,128)(2,1)S(1)}, s32[1,128]{1,0:T(1,128)S(1)}) custom-call(bf16[2,4,128,128]{3,2,1,0:T(8,128)(2,1)S(1)} %select.3.after_hbm, s32[6,12]{1,0:T(8,128)S(1)} %bitcast.6, bf16[12,4,256,128]{3,2,1,0:T(8,128)(2,1)} %basis_hbm.1, ...), custom_call_target="tpu_custom_call" | custom-call | flops 2000000000 | bytes 8000000 | tf_op jit(solution)/shard_map/turn/pallas_call | solution.py:358
  18.0 0.0 collective-permute-done.3.refs_4_
  18.0 0.1 collective-permute-start.6
  18.1 2.2 %collective-permute-done.7.refs_6_ = bf16[2,4,128,128]{3,2,1,0:T(8,128)(2,1)S(1)} collective-permute-done((bf16[2,4,128,128]{3,2,1,0:T(8,128)(2,1)S(1)}, bf16[2,4,128,128]{3,2,1,0:T(8,128)(2,1)S(1)}, u32[]{:S(2)}, u32[]{:S(2)}) %collective-permute-start.7) | collective-permute-done | bytes 262176 | tf_op jit(solution)/shard_map/ppermute | solution.py:293
  20.3 0.0 collective-permute-start.8
  20.3 0.0 collective-permute-done.6.refs_5_
  20.3 0.0 collective-permute-done.4.refs_1_
  20.3 0.0 collective-permute-done.5.refs_3_
  20.3 1.5 %collective-permute-done.8.refs_7_ = bf16[2,4,128,128]{3,2,1,0:T(8,128)(2,1)S(1)} collective-permute-done((bf16[2,4,128,128]{3,2,1,0:T(8,128)(2,1)S(1)}, bf16[2,4,128,128]{3,2,1,0:T(8,128)(2,1)S(1)}, u32[]{:S(2)}, u32[]{:S(2)}) %collective-permute-start.8) | collective-permute-done | bytes 262176 | tf_op jit(solution)/shard_map/ppermute | solution.py:288
  21.8 0.0 copy-done
  21.9 0.0 copy-done.2
  21.9 3.5 %density.1 = (f32[12,256]{1,0:T(8,128)S(1)}, f32[32,128]{1,0:T(8,128)S(1)}) custom-call(s32[1]{0:T(128)S(6)} %copy.15.start_ref, s32[1,12]{1,0:T(1,128)S(1)} %copy-done.2, s32[1,12]{1,0:T(1,128)S(1)} %copy-done, s32[1,128]{1,0:T(1,128)S(1)} %get-tuple-element.32.atom_ref, bf16[12,4,128,256]{3,2,1,0:T(8,128)(2,1)S(1)} %get-tuple-element.34.phit_ref, ...), custom_call_target="tpu_custom_call" | custom-call | flops 2000000000 | bytes 6000000 | tf_op jit(solution)/shard_map/density/pallas_call | solution.py:407
  25.4 0.2 collective-permute-start.9
  25.6 0.6 %copy.14 = f32[12,256]{1,0:T(8,128)} copy(f32[12,256]{1,0:T(8,128)S(1)} %get-tuple-element.57) | data formatting | bytes 24576
  26.2 0.4 collective-permute-done.9
  26.7 1.5 %collective-permute-start.12 = (f32[2,32,128]{2,1,0:T(8,128)S(1)}, f32[2,32,128]{2,1,0:T(8,128)S(1)}, u32[]{:S(2)}, u32[]{:S(2)}) collective-permute-start(f32[2,32,128]{2,1,0:T(8,128)S(1)} %pad_maximum_fusion.after_hbm.refs_0_), channel_id=1, source_target_pairs={{0,6},{1,7},{2,4},{3,5},{4,2},{5,3},{6,0},{7,1},{8,14},{9,15},{10,... | collective-permute-start | bytes 98312 | tf_op jit(solution)/shard_map/ppermute | solution.py:288
  28.1 1.5 %collective-permute-start.11 = (f32[2,32,128]{2,1,0:T(8,128)S(1)}, f32[2,32,128]{2,1,0:T(8,128)S(1)}, u32[]{:S(2)}, u32[]{:S(2)}) collective-permute-start(f32[2,32,128]{2,1,0:T(8,128)S(1)} %pad_maximum_fusion.after_hbm.refs_0_), channel_id=1, source_target_pairs={{0,4},{1,5},{2,6},{3,7},{4,0},{5,1},{6,2},{7,3},{8,12},{9,13},{10,... | collective-permute-start | bytes 98312 | tf_op jit(solution)/shard_map/ppermute | solution.py:288
  29.6 0.5 %collective-permute-start.10 = (f32[2,32,128]{2,1,0:T(8,128)S(1)}, f32[2,32,128]{2,1,0:T(8,128)S(1)}, u32[]{:S(2)}, u32[]{:S(2)}) collective-permute-start(f32[2,32,128]{2,1,0:T(8,128)S(1)} %pad_maximum_fusion.after_hbm.refs_0_), channel_id=1, source_target_pairs={{0,2},{1,3},{2,0},{3,1},{4,6},{5,7},{6,4},{7,5},{8,10},{9,11},{10,... | collective-permute-start | bytes 98312 | tf_op jit(solution)/shard_map/ppermute | solution.py:288
  30.1 2.1 %field.2.low_ref = f32[36,25,256]{2,1,0:T(8,128)S(1)} custom-call(f32[2,32,128]{2,1,0:T(8,128)S(1)} %pad_maximum_fusion.after_hbm.refs_0_, f32[16,25]{1,0:T(8,128)} %bitcast.8, f32[12,6,256]{2,1,0:T(8,128)} %radius_hbm.3, bf16[12,6,25,256]{3,2,1,0:T(8,128)(2,1)} %harm_hbm.5), custom_call_target="tpu_custom_call" | custom-call | flops 2000000000 | bytes 8000000 | tf_op jit(solution)/shard_map/field/pallas_call | solution.py:341
  32.2 0.0 collective-permute-done.12.refs_3_
  32.2 0.0 collective-permute-done.11.refs_2_
  32.2 1.3 %collective-permute-done.10.refs_1_ = f32[2,32,128]{2,1,0:T(8,128)S(1)} collective-permute-done((f32[2,32,128]{2,1,0:T(8,128)S(1)}, f32[2,32,128]{2,1,0:T(8,128)S(1)}, u32[]{:S(2)}, u32[]{:S(2)}) %collective-permute-start.10) | collective-permute-done | bytes 32800 | tf_op jit(solution)/shard_map/ppermute | solution.py:288
  33.5 0.4 scatter.1
  33.9 1.6 %collective-permute-start.13 = (f32[32,256]{1,0:T(8,128)S(1)}, f32[32,256]{1,0:T(8,128)S(1)}, u32[]{:S(2)}, u32[]{:S(2)}) collective-permute-start(f32[32,256]{1,0:T(8,128)S(1)} %get-tuple-element.46), channel_id=1, source_target_pairs={{0,8},{8,0},{16,24},{24,16},{1,9},{9,1},{17,25},{25,17},{2,10},{10... | collective-permute-start | bytes 98312 | tf_op jit(solution)/shard_map/ppermute | solution.py:288
  35.5 2.5 %collective-permute-start.14 = (f32[32,256]{1,0:T(8,128)S(1)}, f32[32,256]{1,0:T(8,128)S(1)}, u32[]{:S(2)}, u32[]{:S(2)}) collective-permute-start(f32[32,256]{1,0:T(8,128)S(1)} %get-tuple-element.47), channel_id=1, source_target_pairs={{0,24},{8,16},{16,8},{24,0},{1,25},{9,17},{17,9},{25,1},{2,26},{10... | collective-permute-start | bytes 98312 | tf_op jit(solution)/shard_map/ppermute | solution.py:288
  38.0 0.1 collective-permute-start.15
  38.1 2.1 %field.3.high_ref = f32[36,25,256]{2,1,0:T(8,128)S(1)} custom-call(f32[32,384]{1,0:T(8,128)S(1)} %get-tuple-element.45.after_hbm.own_ref, f32[16,25]{1,0:T(8,128)} %bitcast.9, f32[12,6,256]{2,1,0:T(8,128)} %radius_hbm.3, bf16[12,6,25,256]{3,2,1,0:T(8,128)(2,1)} %harm_hbm.5), custom_call_target="tpu_custom_call" | custom-call | flops 2000000000 | bytes 8000000 | tf_op jit(solution)/shard_map/field/pallas_call | solution.py:341
  40.2 0.0 collective-permute-done.13.near_a_ref
  40.2 1.0 %collective-permute-done.14.near_b_ref = f32[32,256]{1,0:T(8,128)S(1)} collective-permute-done((f32[32,256]{1,0:T(8,128)S(1)}, f32[32,256]{1,0:T(8,128)S(1)}, u32[]{:S(2)}, u32[]{:S(2)}) %collective-permute-start.14) | collective-permute-done | bytes 32800 | tf_op jit(solution)/shard_map/ppermute | solution.py:288
  41.2 1.9 %collective-permute-done.15.fa_ref.fb_ref = f32[32,256]{1,0:T(8,128)S(1)} collective-permute-done((f32[32,256]{1,0:T(8,128)S(1)}, f32[32,256]{1,0:T(8,128)S(1)}, u32[]{:S(2)}, u32[]{:S(2)}) %collective-permute-start.15) | collective-permute-done | bytes 32800 | tf_op jit(solution)/shard_map/ppermute | solution.py:288
  43.2 1.9 %potential.1 = (f32[16,25]{1,0:T(8,128)}, f32[12,256]{1,0:T(8,128)}) custom-call(s32[1,12]{1,0:T(1,128)S(1)} %copy-done, f32[32,384]{1,0:T(8,128)S(1)} %get-tuple-element.45.after_hbm.own_ref, f32[32,256]{1,0:T(8,128)S(1)} %collective-permute-done.13.near_a_ref, f32[32,256]{1,0:T(8,128)S(1)} %collective-permute-done.14.near_b_ref, ...), custom_call_target="tpu_custom_call" | custom-call | tf_op jit(solution)/shard_map/potential/pallas_call | solution.py:458
  (1 shorter events, 0.0 us)
Async XLA Ops:
  0.6 13.7 %copy-start.1 = (s32[12,6]{0,1:T(8,128)S(1)}, s32[12,6]{0,1:T(8,128)}, u32[]{:S(2)}) copy-start(s32[12,6]{0,1:T(8,128)} %param.17) | copy-start | bytes 868
  2.0 10.7 %collective-permute-start.2 = (bf16[3,4,128,128]{3,2,1,0:T(8,128)(2,1)S(1)}, bf16[3,4,128,128]{3,2,1,0:T(8,128)(2,1)S(1)}, u32[]{:S(2)}, u32[]{:S(2)}) collective-permute-start(bf16[3,4,128,128]{3,2,1,0:T(8,128)(2,1)S(1)} %mask.1.rows_ref.refs_0_), channel_id=1, source_target_pairs={{0,4},{1,3},{2,6},{3,1},{4,0},{5,7},{6,2},{7,5},{8,12},{9,11},{10,... | collective-permute-start | bytes 1179656 | tf_op jit(solution)/shard_map/ppermute | solution.py:293
  5.0 1.2 %collective-permute-start = (s32[1]{0:T(128)}, s32[1]{0:T(128)}, u32[]{:S(2)}, u32[]{:S(2)}) collective-permute-start(s32[1]{0:T(128)} %param.14), channel_id=1, source_target_pairs={{0,1},{1,0},{2,3},{3,2},{4,5},{5,4},{6,7},{7,6},{8,9},{9,8},{10,11... | collective-permute-start | bytes 20 | tf_op jit(solution)/shard_map/ppermute | solution.py:288
  6.9 3.5 %collective-permute-start.1 = (s32[2]{0:T(128)S(1)}, s32[2]{0:T(128)S(1)}, u32[]{:S(2)}, u32[]{:S(2)}) collective-permute-start(s32[2]{0:T(128)S(1)} %pad_add_fusion), channel_id=1, source_target_pairs={{0,2},{1,5},{2,0},{3,7},{4,6},{5,1},{6,4},{7,3},{8,10},{9,13},{10,... | collective-permute-start | bytes 32 | tf_op jit(solution)/shard_map/ppermute | solution.py:293
  11.1 6.9 %collective-permute-start.3 = (bf16[2,4,128,128]{3,2,1,0:T(8,128)(2,1)S(1)}, bf16[2,4,128,128]{3,2,1,0:T(8,128)(2,1)S(1)}, u32[]{:S(2)}, u32[]{:S(2)}) collective-permute-start(bf16[2,4,128,128]{3,2,1,0:T(8,128)(2,1)S(1)} %select.2), channel_id=1, source_target_pairs={{0,2},{1,5},{2,0},{3,7},{4,6},{5,1},{6,4},{7,3},{8,10},{9,13},{10,... | collective-permute-start | bytes 786440 | tf_op jit(solution)/shard_map/ppermute | solution.py:293
  13.2 7.1 %collective-permute-start.7 = (bf16[2,4,128,128]{3,2,1,0:T(8,128)(2,1)S(1)}, bf16[2,4,128,128]{3,2,1,0:T(8,128)(2,1)S(1)}, u32[]{:S(2)}, u32[]{:S(2)}) collective-permute-start(bf16[2,4,128,128]{3,2,1,0:T(8,128)(2,1)S(1)} %select.3.after_hbm), channel_id=1, source_target_pairs={{0,2},{1,5},{2,0},{3,7},{4,6},{5,1},{6,4},{7,3},{8,10},{9,13},{10,... | collective-permute-start | bytes 786440 | tf_op jit(solution)/shard_map/ppermute | solution.py:293
  13.8 6.5 %collective-permute-start.5 = (bf16[3,4,128,128]{3,2,1,0:T(8,128)(2,1)S(1)}, bf16[3,4,128,128]{3,2,1,0:T(8,128)(2,1)S(1)}, u32[]{:S(2)}, u32[]{:S(2)}) collective-permute-start(bf16[3,4,128,128]{3,2,1,0:T(8,128)(2,1)S(1)} %collective-permute-done.2.rows_ref.refs_2_), channel_id=1, source_target_pairs={{0,1},{1,0},{2,3},{3,2},{4,5},{5,4},{6,7},{7,6},{8,9},{9,8},{10,11... | collective-permute-start | bytes 1179656 | tf_op jit(solution)/shard_map/ppermute | solution.py:288
  13.8 6.5 %collective-permute-start.4 = (bf16[3,4,128,128]{3,2,1,0:T(8,128)(2,1)S(1)}, bf16[3,4,128,128]{3,2,1,0:T(8,128)(2,1)S(1)}, u32[]{:S(2)}, u32[]{:S(2)}) collective-permute-start(bf16[3,4,128,128]{3,2,1,0:T(8,128)(2,1)S(1)} %mask.1.rows_ref.refs_0_), channel_id=1, source_target_pairs={{0,1},{1,0},{2,3},{3,2},{4,5},{5,4},{6,7},{7,6},{8,9},{9,8},{10,11... | collective-permute-start | bytes 1179656 | tf_op jit(solution)/shard_map/ppermute | solution.py:288
  14.3 7.5 %copy-start = (s32[1,12]{1,0:T(1,128)S(1)}, s32[1,12]{1,0:T(1,128)}, u32[]{:S(2)}) copy-start(s32[1,12]{1,0:T(1,128)} %size_ref.3) | copy-start | bytes 148
  14.3 7.5 %copy-start.2 = (s32[1,12]{1,0:T(1,128)S(1)}, s32[1,12]{1,0:T(1,128)}, u32[]{:S(2)}) copy-start(s32[1,12]{1,0:T(1,128)} %offset_ref.1) | copy-start | bytes 148
  18.0 2.3 %collective-permute-start.6 = (bf16[2,4,128,128]{3,2,1,0:T(8,128)(2,1)S(1)}, bf16[2,4,128,128]{3,2,1,0:T(8,128)(2,1)S(1)}, u32[]{:S(2)}, u32[]{:S(2)}) collective-permute-start(bf16[2,4,128,128]{3,2,1,0:T(8,128)(2,1)S(1)} %collective-permute-done.3.refs_4_), channel_id=1, source_target_pairs={{0,1},{1,0},{2,3},{3,2},{4,5},{5,4},{6,7},{7,6},{8,9},{9,8},{10,11... | collective-permute-start | bytes 786440 | tf_op jit(solution)/shard_map/ppermute | solution.py:288
  20.3 1.5 %collective-permute-start.8 = (bf16[2,4,128,128]{3,2,1,0:T(8,128)(2,1)S(1)}, bf16[2,4,128,128]{3,2,1,0:T(8,128)(2,1)S(1)}, u32[]{:S(2)}, u32[]{:S(2)}) collective-permute-start(bf16[2,4,128,128]{3,2,1,0:T(8,128)(2,1)S(1)} %collective-permute-done.7.refs_6_), channel_id=1, source_target_pairs={{0,1},{1,0},{2,3},{3,2},{4,5},{5,4},{6,7},{7,6},{8,9},{9,8},{10,11... | collective-permute-start | bytes 786440 | tf_op jit(solution)/shard_map/ppermute | solution.py:288
  25.4 1.2 %collective-permute-start.9 = (f32[32,128]{1,0:T(8,128)S(1)}, f32[32,128]{1,0:T(8,128)S(1)}, u32[]{:S(2)}, u32[]{:S(2)}) collective-permute-start(f32[32,128]{1,0:T(8,128)S(1)} %get-tuple-element.40), channel_id=1, source_target_pairs={{0,1},{1,0},{2,3},{3,2},{4,5},{5,4},{6,7},{7,6},{8,9},{9,8},{10,11... | collective-permute-start | bytes 49160 | tf_op jit(solution)/shard_map/ppermute | solution.py:288
  26.7 5.6 %collective-permute-start.12 = (f32[2,32,128]{2,1,0:T(8,128)S(1)}, f32[2,32,128]{2,1,0:T(8,128)S(1)}, u32[]{:S(2)}, u32[]{:S(2)}) collective-permute-start(f32[2,32,128]{2,1,0:T(8,128)S(1)} %pad_maximum_fusion.after_hbm.refs_0_), channel_id=1, source_target_pairs={{0,6},{1,7},{2,4},{3,5},{4,2},{5,3},{6,0},{7,1},{8,14},{9,15},{10,... | collective-permute-start | bytes 98312 | tf_op jit(solution)/shard_map/ppermute | solution.py:288
  28.1 4.1 %collective-permute-start.11 = (f32[2,32,128]{2,1,0:T(8,128)S(1)}, f32[2,32,128]{2,1,0:T(8,128)S(1)}, u32[]{:S(2)}, u32[]{:S(2)}) collective-permute-start(f32[2,32,128]{2,1,0:T(8,128)S(1)} %pad_maximum_fusion.after_hbm.refs_0_), channel_id=1, source_target_pairs={{0,4},{1,5},{2,6},{3,7},{4,0},{5,1},{6,2},{7,3},{8,12},{9,13},{10,... | collective-permute-start | bytes 98312 | tf_op jit(solution)/shard_map/ppermute | solution.py:288
  29.6 3.9 %collective-permute-start.10 = (f32[2,32,128]{2,1,0:T(8,128)S(1)}, f32[2,32,128]{2,1,0:T(8,128)S(1)}, u32[]{:S(2)}, u32[]{:S(2)}) collective-permute-start(f32[2,32,128]{2,1,0:T(8,128)S(1)} %pad_maximum_fusion.after_hbm.refs_0_), channel_id=1, source_target_pairs={{0,2},{1,3},{2,0},{3,1},{4,6},{5,7},{6,4},{7,5},{8,10},{9,11},{10,... | collective-permute-start | bytes 98312 | tf_op jit(solution)/shard_map/ppermute | solution.py:288
  33.9 6.3 %collective-permute-start.13 = (f32[32,256]{1,0:T(8,128)S(1)}, f32[32,256]{1,0:T(8,128)S(1)}, u32[]{:S(2)}, u32[]{:S(2)}) collective-permute-start(f32[32,256]{1,0:T(8,128)S(1)} %get-tuple-element.46), channel_id=1, source_target_pairs={{0,8},{8,0},{16,24},{24,16},{1,9},{9,1},{17,25},{25,17},{2,10},{10... | collective-permute-start | bytes 98312 | tf_op jit(solution)/shard_map/ppermute | solution.py:288
  35.5 5.7 %collective-permute-start.14 = (f32[32,256]{1,0:T(8,128)S(1)}, f32[32,256]{1,0:T(8,128)S(1)}, u32[]{:S(2)}, u32[]{:S(2)}) collective-permute-start(f32[32,256]{1,0:T(8,128)S(1)} %get-tuple-element.47), channel_id=1, source_target_pairs={{0,24},{8,16},{16,8},{24,0},{1,25},{9,17},{17,9},{25,1},{2,26},{10... | collective-permute-start | bytes 98312 | tf_op jit(solution)/shard_map/ppermute | solution.py:288
  38.0 5.2 %collective-permute-start.15 = (f32[32,256]{1,0:T(8,128)S(1)}, f32[32,256]{1,0:T(8,128)S(1)}, u32[]{:S(2)}, u32[]{:S(2)}) collective-permute-start(f32[32,256]{1,0:T(8,128)S(1)} %get-tuple-element.48), channel_id=1, source_target_pairs={{0,16},{8,24},{16,0},{24,8},{1,17},{9,25},{17,1},{25,9},{2,18},{10... | collective-permute-start | bytes 98312 | tf_op jit(solution)/shard_map/ppermute | solution.py:288

commit v11 on v10

--- a/solution.py
+++ b/solution.py
@@ -49,11 +49,11 @@
     return ahead, lax.rem(start + ahead, stored * owners) // owners
 
 
-def select_kernel(even, odd, owners, starts_ref, rows_ref, out_ref):
+def select_kernel(even, odd, owners, start_ref, beside_ref, rows_ref, out_ref):
     me = lax.axis_index("dev")
     owner = lax.bitwise_xor(me, jnp.where(lax.rem(me, 2) == 1, odd, even))
-    for n in range(out_ref.shape[0]):
-        row = chosen_row(owner, starts_ref[n], owners, rows_ref.shape[0])[1]
+    for n, ref in enumerate((start_ref, beside_ref)):
+        row = chosen_row(owner, ref[0], owners, rows_ref.shape[0])[1]
         out_ref[n] = rows_ref[row]
 
 
@@ -238,7 +238,7 @@
 
 
 def potential_kernel(
-    comps, atoms, flip, size_ref, own_ref, near_a_ref, near_b_ref, fa_ref, fb_ref, atom_ref,
+    comps, atoms, flip, size_ref, own_ref, near_b_ref, fa_ref, fb_ref, near_a_ref, atom_ref,
     low_ref, high_ref, mom_ref, pot_ref,
 ):
     batches, points = pot_ref.shape
@@ -379,18 +379,15 @@
         return pl.pallas_call(
             functools.partial(select_kernel, even, odd, dev_count),
             out_shape=pltpu.VMEM((2,) + density_rows.shape[1:], bf16),
-            in_specs=[SMEM, VMEM],
+            in_specs=[SMEM, SMEM, VMEM],
             out_specs=VMEM,
             compiler_params=PARAMS,
             name="select",
-        )(starts, rows)
+        )(*starts, rows)
 
     if dev_count == 8:
-        beside = crossed(window_start, "dev", 1)
-        beside, _ = lax.optimization_barrier((beside, masked))
+        starts = (turned(window_start, 2, 4), turned(window_start, 5, 3))
         first = turned(masked, 4, 2)
-        pair = jnp.concatenate([window_start, beside])
-        starts = turned(pair, 2, 4)
         chosen = selected(0, 0, starts, masked)
         second = turned(chosen, 2, 4)
         first, later, _ = lax.optimization_barrier((first, masked, chosen))
@@ -442,17 +439,17 @@
     )(*groups)
     g_high = field(half, own)
     if flip:
+        near_b = crossed(near_b, "region", 3)
+        far_a = far_b = crossed(far, "region", 2)
         near_a = crossed(near_a, "region", 1)
-        far_a = far_b = crossed(far, "region", 2)
-        near_b = crossed(near_b, "region", 3)
     else:
         far_a = shifted(far, "region", 2)
         far_b = shifted(far, "region", -2)
         near_a = shifted(near_a, "region", 1)
         near_b = shifted(near_b, "region", -1)
 
-    near_a, near_b, far_a, far_b, g_high = lax.optimization_barrier(
-        (near_a, near_b, far_a, far_b, g_high)
+    near_b, far_a, far_b, near_a, g_high = lax.optimization_barrier(
+        (near_b, far_a, far_b, near_a, g_high)
     )
 
     moments, potential = pl.pallas_call(
@@ -465,7 +462,7 @@
         out_specs=(VMEM, VMEM),
         compiler_params=PARAMS,
         name="potential",
-    )(batch_sizes, own, near_a, near_b, far_a, far_b, atom_rows, g_low, g_high)
+    )(batch_sizes, own, near_b, far_a, far_b, near_a, atom_rows, g_low, g_high)
     return (density, moments.T, potential)
 
 

time: 45.3 us -> 45.1 us (level)
  Pallas kernels: 16 us -> 17.5 us
  waiting for transfers between devices: 11.1 us -> 9.6 us
  other arithmetic: 0.7 us -> 0.01 us
  starting transfers between devices: 15.2 us -> 15.7 us
    ppermute x12 -> x11, waiting for transfers between devices: 6.79 us -> 4.47 us  [crossed(): lax.ppermute(value, axis, [(i, i ^ m) for i in range(lax.axis_size(axis))])]
    pallas_call x2, Pallas kernels: 1.17 us -> 2.59 us  [selected(): pl.pallas_call(functools.partial(select_kernel, even, odd, dev_count), ou...]
    ppermute x4 -> x5, waiting for transfers between devices: 4.29 us -> 5.13 us  [turned(): lax.ppermute(value, 'dev', [(i, i ^ (odd if i % 2 else even)) for i in ra...]
    concatenate x1 -> x0, other arithmetic: 0.7 us -> none  [per_device(): pair = jnp.concatenate([window_start, beside])]
    ppermute x12 -> x11, starting transfers between devices: 8.52 us -> 9.03 us  [crossed(): lax.ppermute(value, axis, [(i, i ^ m) for i in range(lax.axis_size(axis))])]
    ppermute x4 -> x5, starting transfers between devices: 6.68 us -> 6.68 us  [turned(): lax.ppermute(value, 'dev', [(i, i ^ (odd if i % 2 else even)) for i in ra...]
  transfers between devices with their start and end apart: 16 -> 16, of which waited for: 8 -> 8; matrix products, arithmetic and copies ran while one was open for 3% -> 1% of each run, Pallas kernels for 20% -> 23%
where the time goes in v11:
time: 45.1 us; the launch traced here: 44.8 us
  Pallas kernels  17.5 us (39%)
  starting transfers between devices  15.7 us (35%)
  waiting for transfers between devices  9.6 us (21%)
  between operations  1.42 us (3%)
  local copies, waits for them, and re-layouts  0.62 us (1%)
    ppermute x11, starting transfers between devices, crossed(): lax.ppermute(value, axis, [(i, i ^ m) for i in range(lax.axis_size(axis))])  9.03 us
    ppermute x5, starting transfers between devices, turned(): lax.ppermute(value, 'dev', [(i, i ^ (odd if i % 2 else even)) for i in ra...  6.68 us
    ppermute x5, waiting for transfers between devices, turned(): lax.ppermute(value, 'dev', [(i, i ^ (odd if i % 2 else even)) for i in ra...  5.13 us
    ppermute x11, waiting for transfers between devices, crossed(): lax.ppermute(value, axis, [(i, i ^ m) for i in range(lax.axis_size(axis))])  4.47 us
    pallas_call x2, Pallas kernels, field(): pl.pallas_call(functools.partial(field_kernel, begin), out_shape=pltpu.VM...  4.14 us
    pallas_call x1, Pallas kernels, turned_basis(): pl.pallas_call(turn_kernel, out_shape=(pltpu.VMEM((batches, near_blocks,...  3.64 us
    pallas_call x1, Pallas kernels, per_device(): pl.pallas_call(density_kernel, out_shape=(pltpu.VMEM((batches, points), f...  3.54 us
    pallas_call x2, Pallas kernels, selected(): pl.pallas_call(functools.partial(select_kernel, even, odd, dev_count), ou...  2.59 us
  transfers between devices with their start and end apart: 16, of which 8 were waited for; matrix products, arithmetic and copies ran while one was open for 1% of the time, Pallas kernels for 23%

profile of v11, /device:TPU:0, one launch (start us, length us, event | category | flops | bytes accessed | tf_op | source)
XLA Modules:
  0.0 44.8 jit_solution(764607467141510090)
XLA Ops:
  0.6 0.0 copy-start.1
  0.6 1.3 %mask.1.rows_ref.refs_0_ = bf16[3,4,128,128]{3,2,1,0:T(8,128)(2,1)S(1)} custom-call(s32[3,4]{1,0:T(4,128)} %mask_hbm.1, bf16[3,4,128,128]{3,2,1,0:T(8,128)(2,1)} %rows_hbm.1), custom_call_target="tpu_custom_call" | custom-call | tf_op jit(solution)/shard_map/mask/pallas_call | solution.py:323
  2.0 3.0 %collective-permute-start.2 = (bf16[3,4,128,128]{3,2,1,0:T(8,128)(2,1)S(1)}, bf16[3,4,128,128]{3,2,1,0:T(8,128)(2,1)S(1)}, u32[]{:S(2)}, u32[]{:S(2)}) collective-permute-start(bf16[3,4,128,128]{3,2,1,0:T(8,128)(2,1)S(1)} %mask.1.rows_ref.refs_0_), channel_id=1, source_target_pairs={{0,4},{1,3},{2,6},{3,1},{4,0},{5,7},{6,2},{7,5},{8,12},{9,11},{10,... | collective-permute-start | bytes 1179656 | tf_op jit(solution)/shard_map/ppermute | solution.py:293
  5.0 1.5 %collective-permute-start = (s32[1]{0:T(128)}, s32[1]{0:T(128)}, u32[]{:S(2)}, u32[]{:S(2)}) collective-permute-start(s32[1]{0:T(128)} %param.14), channel_id=1, source_target_pairs={{0,2},{1,5},{2,0},{3,7},{4,6},{5,1},{6,4},{7,3},{8,10},{9,13},{10,... | collective-permute-start | bytes 20 | tf_op jit(solution)/shard_map/ppermute | solution.py:293
  6.5 0.0 collective-permute-start.1
  6.5 2.2 %collective-permute-done.start_ref = s32[1]{0:T(128)} collective-permute-done((s32[1]{0:T(128)}, s32[1]{0:T(128)}, u32[]{:S(2)}, u32[]{:S(2)}) %collective-permute-start) | collective-permute-done | bytes 36 | tf_op jit(solution)/shard_map/ppermute | solution.py:293
  8.7 1.6 %collective-permute-done.1.beside_ref = s32[1]{0:T(128)} collective-permute-done((s32[1]{0:T(128)}, s32[1]{0:T(128)}, u32[]{:S(2)}, u32[]{:S(2)}) %collective-permute-start.1) | collective-permute-done | bytes 36 | tf_op jit(solution)/shard_map/ppermute | solution.py:293
  10.3 1.3 %select.2 = bf16[2,4,128,128]{3,2,1,0:T(8,128)(2,1)S(1)} custom-call(s32[1]{0:T(128)} %collective-permute-done.start_ref, s32[1]{0:T(128)} %collective-permute-done.1.beside_ref, bf16[3,4,128,128]{3,2,1,0:T(8,128)(2,1)S(1)} %mask.1.rows_ref.refs_0_), custom_call_target="tpu_custom_call" | custom-call | tf_op jit(solution)/shard_map/select/pallas_call | solution.py:379
  11.6 1.6 %collective-permute-start.3 = (bf16[2,4,128,128]{3,2,1,0:T(8,128)(2,1)S(1)}, bf16[2,4,128,128]{3,2,1,0:T(8,128)(2,1)S(1)}, u32[]{:S(2)}, u32[]{:S(2)}) collective-permute-start(bf16[2,4,128,128]{3,2,1,0:T(8,128)(2,1)S(1)} %select.2), channel_id=1, source_target_pairs={{0,2},{1,5},{2,0},{3,7},{4,6},{5,1},{6,4},{7,3},{8,10},{9,13},{10,... | collective-permute-start | bytes 786440 | tf_op jit(solution)/shard_map/ppermute | solution.py:293
  13.2 0.0 collective-permute-done.2.rows_ref.refs_2_
  13.2 1.3 %select.3.after_hbm = bf16[2,4,128,128]{3,2,1,0:T(8,128)(2,1)S(1)} custom-call(s32[1]{0:T(128)} %collective-permute-done.start_ref, s32[1]{0:T(128)} %collective-permute-done.1.beside_ref, bf16[3,4,128,128]{3,2,1,0:T(8,128)(2,1)S(1)} %collective-permute-done.2.rows_ref.refs_2_), custom_call_target="tpu_custom_call" | custom-call | tf_op jit(solution)/shard_map/select/pallas_call | solution.py:379
  14.5 0.6 %collective-permute-start.7 = (bf16[2,4,128,128]{3,2,1,0:T(8,128)(2,1)S(1)}, bf16[2,4,128,128]{3,2,1,0:T(8,128)(2,1)S(1)}, u32[]{:S(2)}, u32[]{:S(2)}) collective-permute-start(bf16[2,4,128,128]{3,2,1,0:T(8,128)(2,1)S(1)} %select.3.after_hbm), channel_id=1, source_target_pairs={{0,2},{1,5},{2,0},{3,7},{4,6},{5,1},{6,4},{7,3},{8,10},{9,13},{10,... | collective-permute-start | bytes 786440 | tf_op jit(solution)/shard_map/ppermute | solution.py:293
  15.1 0.3 collective-permute-start.5
  15.4 0.2 collective-permute-start.4
  15.6 0.0 copy-done.1
  15.6 0.0 copy-start
  15.6 0.0 copy-start.2
  15.6 3.6 %turn.1 = (bf16[12,4,128,256]{3,2,1,0:T(8,128)(2,1)S(1)}, f32[12,6,256]{2,1,0:T(8,128)S(1)}, bf16[72,32,256]{2,1,0:T(8,128)(2,1)S(1)}, s32[1,128]{1,0:T(1,128)S(1)}) custom-call(bf16[2,4,128,128]{3,2,1,0:T(8,128)(2,1)S(1)} %select.3.after_hbm, s32[6,12]{1,0:T(8,128)S(1)} %bitcast.6, bf16[12,4,256,128]{3,2,1,0:T(8,128)(2,1)} %basis_hbm.1, ...), custom_call_target="tpu_custom_call" | custom-call | flops 2000000000 | bytes 8000000 | tf_op jit(solution)/shard_map/turn/pallas_call | solution.py:358
  19.3 0.0 collective-permute-done.3.refs_4_
  19.3 0.4 collective-permute-start.6
  19.6 1.3 %collective-permute-done.7.refs_6_ = bf16[2,4,128,128]{3,2,1,0:T(8,128)(2,1)S(1)} collective-permute-done((bf16[2,4,128,128]{3,2,1,0:T(8,128)(2,1)S(1)}, bf16[2,4,128,128]{3,2,1,0:T(8,128)(2,1)S(1)}, u32[]{:S(2)}, u32[]{:S(2)}) %collective-permute-start.7) | collective-permute-done | bytes 262176 | tf_op jit(solution)/shard_map/ppermute | solution.py:293
  20.9 0.0 collective-permute-start.8
  21.6 0.0 collective-permute-done.6.refs_5_
  21.6 0.0 collective-permute-done.4.refs_1_
  21.6 0.0 collective-permute-done.5.refs_3_
  21.6 0.8 %collective-permute-done.8.refs_7_ = bf16[2,4,128,128]{3,2,1,0:T(8,128)(2,1)S(1)} collective-permute-done((bf16[2,4,128,128]{3,2,1,0:T(8,128)(2,1)S(1)}, bf16[2,4,128,128]{3,2,1,0:T(8,128)(2,1)S(1)}, u32[]{:S(2)}, u32[]{:S(2)}) %collective-permute-start.8) | collective-permute-done | bytes 262176 | tf_op jit(solution)/shard_map/ppermute | solution.py:288
  22.5 0.0 copy-done
  22.5 0.0 copy-done.2
  22.5 3.5 %density.1 = (f32[12,256]{1,0:T(8,128)S(1)}, f32[32,128]{1,0:T(8,128)S(1)}) custom-call(s32[1]{0:T(128)S(6)} %copy.15.start_ref, s32[1,12]{1,0:T(1,128)S(1)} %copy-done.2, s32[1,12]{1,0:T(1,128)S(1)} %copy-done, s32[1,128]{1,0:T(1,128)S(1)} %get-tuple-element.30.atom_ref, bf16[12,4,128,256]{3,2,1,0:T(8,128)(2,1)S(1)} %get-tuple-element.32.phit_ref, ...), custom_call_target="tpu_custom_call" | custom-call | flops 2000000000 | bytes 6000000 | tf_op jit(solution)/shard_map/density/pallas_call | solution.py:404
  26.0 0.2 collective-permute-start.9
  26.2 0.6 %copy.14 = f32[12,256]{1,0:T(8,128)} copy(f32[12,256]{1,0:T(8,128)S(1)} %get-tuple-element.55) | data formatting | bytes 24576
  26.8 0.4 collective-permute-done.9
  27.3 2.1 %collective-permute-start.12 = (f32[2,32,128]{2,1,0:T(8,128)S(1)}, f32[2,32,128]{2,1,0:T(8,128)S(1)}, u32[]{:S(2)}, u32[]{:S(2)}) collective-permute-start(f32[2,32,128]{2,1,0:T(8,128)S(1)} %pad_maximum_fusion.after_hbm.refs_0_), channel_id=1, source_target_pairs={{0,6},{1,7},{2,4},{3,5},{4,2},{5,3},{6,0},{7,1},{8,14},{9,15},{10,... | collective-permute-start | bytes 98312 | tf_op jit(solution)/shard_map/ppermute | solution.py:288
  29.4 0.8 %collective-permute-start.11 = (f32[2,32,128]{2,1,0:T(8,128)S(1)}, f32[2,32,128]{2,1,0:T(8,128)S(1)}, u32[]{:S(2)}, u32[]{:S(2)}) collective-permute-start(f32[2,32,128]{2,1,0:T(8,128)S(1)} %pad_maximum_fusion.after_hbm.refs_0_), channel_id=1, source_target_pairs={{0,4},{1,5},{2,6},{3,7},{4,0},{5,1},{6,2},{7,3},{8,12},{9,13},{10,... | collective-permute-start | bytes 98312 | tf_op jit(solution)/shard_map/ppermute | solution.py:288
  30.2 0.6 %collective-permute-start.10 = (f32[2,32,128]{2,1,0:T(8,128)S(1)}, f32[2,32,128]{2,1,0:T(8,128)S(1)}, u32[]{:S(2)}, u32[]{:S(2)}) collective-permute-start(f32[2,32,128]{2,1,0:T(8,128)S(1)} %pad_maximum_fusion.after_hbm.refs_0_), channel_id=1, source_target_pairs={{0,2},{1,3},{2,0},{3,1},{4,6},{5,7},{6,4},{7,5},{8,10},{9,11},{10,... | collective-permute-start | bytes 98312 | tf_op jit(solution)/shard_map/ppermute | solution.py:288
  30.8 2.1 %field.2.low_ref = f32[36,25,256]{2,1,0:T(8,128)S(1)} custom-call(f32[2,32,128]{2,1,0:T(8,128)S(1)} %pad_maximum_fusion.after_hbm.refs_0_, f32[16,25]{1,0:T(8,128)} %bitcast.8, f32[12,6,256]{2,1,0:T(8,128)} %radius_hbm.3, bf16[12,6,25,256]{3,2,1,0:T(8,128)(2,1)} %harm_hbm.5), custom_call_target="tpu_custom_call" | custom-call | flops 2000000000 | bytes 8000000 | tf_op jit(solution)/shard_map/field/pallas_call | solution.py:341
  32.8 0.0 collective-permute-done.12.refs_3_
  32.8 0.4 %collective-permute-done.11.refs_2_ = f32[2,32,128]{2,1,0:T(8,128)S(1)} collective-permute-done((f32[2,32,128]{2,1,0:T(8,128)S(1)}, f32[2,32,128]{2,1,0:T(8,128)S(1)}, u32[]{:S(2)}, u32[]{:S(2)}) %collective-permute-start.11) | collective-permute-done | bytes 32800 | tf_op jit(solution)/shard_map/ppermute | solution.py:288
  33.3 0.8 %collective-permute-done.10.refs_1_ = f32[2,32,128]{2,1,0:T(8,128)S(1)} collective-permute-done((f32[2,32,128]{2,1,0:T(8,128)S(1)}, f32[2,32,128]{2,1,0:T(8,128)S(1)}, u32[]{:S(2)}, u32[]{:S(2)}) %collective-permute-start.10) | collective-permute-done | bytes 32800 | tf_op jit(solution)/shard_map/ppermute | solution.py:288
  34.1 0.4 scatter.1
  34.5 3.7 %collective-permute-start.13 = (f32[32,256]{1,0:T(8,128)S(1)}, f32[32,256]{1,0:T(8,128)S(1)}, u32[]{:S(2)}, u32[]{:S(2)}) collective-permute-start(f32[32,256]{1,0:T(8,128)S(1)} %get-tuple-element.44), channel_id=1, source_target_pairs={{0,24},{8,16},{16,8},{24,0},{1,25},{9,17},{17,9},{25,1},{2,26},{10... | collective-permute-start | bytes 98312 | tf_op jit(solution)/shard_map/ppermute | solution.py:288
  38.1 0.0 collective-permute-start.14
  38.1 0.8 %collective-permute-start.15 = (f32[32,256]{1,0:T(8,128)S(1)}, f32[32,256]{1,0:T(8,128)S(1)}, u32[]{:S(2)}, u32[]{:S(2)}) collective-permute-start(f32[32,256]{1,0:T(8,128)S(1)} %get-tuple-element.46), channel_id=1, source_target_pairs={{0,8},{8,0},{16,24},{24,16},{1,9},{9,1},{17,25},{25,17},{2,10},{10... | collective-permute-start | bytes 98312 | tf_op jit(solution)/shard_map/ppermute | solution.py:288
  38.9 2.1 %field.3.high_ref = f32[36,25,256]{2,1,0:T(8,128)S(1)} custom-call(f32[32,384]{1,0:T(8,128)S(1)} %get-tuple-element.43.after_hbm.own_ref, f32[16,25]{1,0:T(8,128)} %bitcast.9, f32[12,6,256]{2,1,0:T(8,128)} %radius_hbm.3, bf16[12,6,25,256]{3,2,1,0:T(8,128)(2,1)} %harm_hbm.5), custom_call_target="tpu_custom_call" | custom-call | flops 2000000000 | bytes 8000000 | tf_op jit(solution)/shard_map/field/pallas_call | solution.py:341
  41.0 0.0 collective-permute-done.13.near_b_ref
  41.0 1.9 %collective-permute-done.14.fa_ref.fb_ref = f32[32,256]{1,0:T(8,128)S(1)} collective-permute-done((f32[32,256]{1,0:T(8,128)S(1)}, f32[32,256]{1,0:T(8,128)S(1)}, u32[]{:S(2)}, u32[]{:S(2)}) %collective-permute-start.14) | collective-permute-done | bytes 32800 | tf_op jit(solution)/shard_map/ppermute | solution.py:288
  42.9 0.0 collective-permute-done.15.near_a_ref
  42.9 1.9 %potential.1 = (f32[16,25]{1,0:T(8,128)}, f32[12,256]{1,0:T(8,128)}) custom-call(s32[1,12]{1,0:T(1,128)S(1)} %copy-done, f32[32,384]{1,0:T(8,128)S(1)} %get-tuple-element.43.after_hbm.own_ref, f32[32,256]{1,0:T(8,128)S(1)} %collective-permute-done.13.near_b_ref, f32[32,256]{1,0:T(8,128)S(1)} %collective-permute-done.14.fa_ref.fb_ref, ...), custom_call_target="tpu_custom_call" | custom-call | tf_op jit(solution)/shard_map/potential/pallas_call | solution.py:455
  (1 shorter events, 0.0 us)
Async XLA Ops:
  0.6 15.0 %copy-start.1 = (s32[12,6]{0,1:T(8,128)S(1)}, s32[12,6]{0,1:T(8,128)}, u32[]{:S(2)}) copy-start(s32[12,6]{0,1:T(8,128)} %param.17) | copy-start | bytes 868
  2.0 11.2 %collective-permute-start.2 = (bf16[3,4,128,128]{3,2,1,0:T(8,128)(2,1)S(1)}, bf16[3,4,128,128]{3,2,1,0:T(8,128)(2,1)S(1)}, u32[]{:S(2)}, u32[]{:S(2)}) collective-permute-start(bf16[3,4,128,128]{3,2,1,0:T(8,128)(2,1)S(1)} %mask.1.rows_ref.refs_0_), channel_id=1, source_target_pairs={{0,4},{1,3},{2,6},{3,1},{4,0},{5,7},{6,2},{7,5},{8,12},{9,11},{10,... | collective-permute-start | bytes 1179656 | tf_op jit(solution)/shard_map/ppermute | solution.py:293
  5.0 3.7 %collective-permute-start = (s32[1]{0:T(128)}, s32[1]{0:T(128)}, u32[]{:S(2)}, u32[]{:S(2)}) collective-permute-start(s32[1]{0:T(128)} %param.14), channel_id=1, source_target_pairs={{0,2},{1,5},{2,0},{3,7},{4,6},{5,1},{6,4},{7,3},{8,10},{9,13},{10,... | collective-permute-start | bytes 20 | tf_op jit(solution)/shard_map/ppermute | solution.py:293
  6.5 3.8 %collective-permute-start.1 = (s32[1]{0:T(128)}, s32[1]{0:T(128)}, u32[]{:S(2)}, u32[]{:S(2)}) collective-permute-start(s32[1]{0:T(128)} %param.14), channel_id=1, source_target_pairs={{0,5},{1,2},{2,7},{3,0},{4,1},{5,6},{6,3},{7,4},{8,13},{9,10},{10,... | collective-permute-start | bytes 20 | tf_op jit(solution)/shard_map/ppermute | solution.py:293
  11.6 7.6 %collective-permute-start.3 = (bf16[2,4,128,128]{3,2,1,0:T(8,128)(2,1)S(1)}, bf16[2,4,128,128]{3,2,1,0:T(8,128)(2,1)S(1)}, u32[]{:S(2)}, u32[]{:S(2)}) collective-permute-start(bf16[2,4,128,128]{3,2,1,0:T(8,128)(2,1)S(1)} %select.2), channel_id=1, source_target_pairs={{0,2},{1,5},{2,0},{3,7},{4,6},{5,1},{6,4},{7,3},{8,10},{9,13},{10,... | collective-permute-start | bytes 786440 | tf_op jit(solution)/shard_map/ppermute | solution.py:293
  14.5 6.4 %collective-permute-start.7 = (bf16[2,4,128,128]{3,2,1,0:T(8,128)(2,1)S(1)}, bf16[2,4,128,128]{3,2,1,0:T(8,128)(2,1)S(1)}, u32[]{:S(2)}, u32[]{:S(2)}) collective-permute-start(bf16[2,4,128,128]{3,2,1,0:T(8,128)(2,1)S(1)} %select.3.after_hbm), channel_id=1, source_target_pairs={{0,2},{1,5},{2,0},{3,7},{4,6},{5,1},{6,4},{7,3},{8,10},{9,13},{10,... | collective-permute-start | bytes 786440 | tf_op jit(solution)/shard_map/ppermute | solution.py:293
  15.1 6.5 %collective-permute-start.5 = (bf16[3,4,128,128]{3,2,1,0:T(8,128)(2,1)S(1)}, bf16[3,4,128,128]{3,2,1,0:T(8,128)(2,1)S(1)}, u32[]{:S(2)}, u32[]{:S(2)}) collective-permute-start(bf16[3,4,128,128]{3,2,1,0:T(8,128)(2,1)S(1)} %collective-permute-done.2.rows_ref.refs_2_), channel_id=1, source_target_pairs={{0,1},{1,0},{2,3},{3,2},{4,5},{5,4},{6,7},{7,6},{8,9},{9,8},{10,11... | collective-permute-start | bytes 1179656 | tf_op jit(solution)/shard_map/ppermute | solution.py:288
  15.4 6.2 %collective-permute-start.4 = (bf16[3,4,128,128]{3,2,1,0:T(8,128)(2,1)S(1)}, bf16[3,4,128,128]{3,2,1,0:T(8,128)(2,1)S(1)}, u32[]{:S(2)}, u32[]{:S(2)}) collective-permute-start(bf16[3,4,128,128]{3,2,1,0:T(8,128)(2,1)S(1)} %mask.1.rows_ref.refs_0_), channel_id=1, source_target_pairs={{0,1},{1,0},{2,3},{3,2},{4,5},{5,4},{6,7},{7,6},{8,9},{9,8},{10,11... | collective-permute-start | bytes 1179656 | tf_op jit(solution)/shard_map/ppermute | solution.py:288
  15.6 6.9 %copy-start = (s32[1,12]{1,0:T(1,128)S(1)}, s32[1,12]{1,0:T(1,128)}, u32[]{:S(2)}) copy-start(s32[1,12]{1,0:T(1,128)} %size_ref.3) | copy-start | bytes 148
  15.6 6.9 %copy-start.2 = (s32[1,12]{1,0:T(1,128)S(1)}, s32[1,12]{1,0:T(1,128)}, u32[]{:S(2)}) copy-start(s32[1,12]{1,0:T(1,128)} %offset_ref.1) | copy-start | bytes 148
  19.3 2.3 %collective-permute-start.6 = (bf16[2,4,128,128]{3,2,1,0:T(8,128)(2,1)S(1)}, bf16[2,4,128,128]{3,2,1,0:T(8,128)(2,1)S(1)}, u32[]{:S(2)}, u32[]{:S(2)}) collective-permute-start(bf16[2,4,128,128]{3,2,1,0:T(8,128)(2,1)S(1)} %collective-permute-done.3.refs_4_), channel_id=1, source_target_pairs={{0,1},{1,0},{2,3},{3,2},{4,5},{5,4},{6,7},{7,6},{8,9},{9,8},{10,11... | collective-permute-start | bytes 786440 | tf_op jit(solution)/shard_map/ppermute | solution.py:288
  20.9 1.5 %collective-permute-start.8 = (bf16[2,4,128,128]{3,2,1,0:T(8,128)(2,1)S(1)}, bf16[2,4,128,128]{3,2,1,0:T(8,128)(2,1)S(1)}, u32[]{:S(2)}, u32[]{:S(2)}) collective-permute-start(bf16[2,4,128,128]{3,2,1,0:T(8,128)(2,1)S(1)} %collective-permute-done.7.refs_6_), channel_id=1, source_target_pairs={{0,1},{1,0},{2,3},{3,2},{4,5},{5,4},{6,7},{7,6},{8,9},{9,8},{10,11... | collective-permute-start | bytes 786440 | tf_op jit(solution)/shard_map/ppermute | solution.py:288
  26.0 1.2 %collective-permute-start.9 = (f32[32,128]{1,0:T(8,128)S(1)}, f32[32,128]{1,0:T(8,128)S(1)}, u32[]{:S(2)}, u32[]{:S(2)}) collective-permute-start(f32[32,128]{1,0:T(8,128)S(1)} %get-tuple-element.38), channel_id=1, source_target_pairs={{0,1},{1,0},{2,3},{3,2},{4,5},{5,4},{6,7},{7,6},{8,9},{9,8},{10,11... | collective-permute-start | bytes 49160 | tf_op jit(solution)/shard_map/ppermute | solution.py:288
  27.3 5.6 %collective-permute-start.12 = (f32[2,32,128]{2,1,0:T(8,128)S(1)}, f32[2,32,128]{2,1,0:T(8,128)S(1)}, u32[]{:S(2)}, u32[]{:S(2)}) collective-permute-start(f32[2,32,128]{2,1,0:T(8,128)S(1)} %pad_maximum_fusion.after_hbm.refs_0_), channel_id=1, source_target_pairs={{0,6},{1,7},{2,4},{3,5},{4,2},{5,3},{6,0},{7,1},{8,14},{9,15},{10,... | collective-permute-start | bytes 98312 | tf_op jit(solution)/shard_map/ppermute | solution.py:288
  29.4 3.9 %collective-permute-start.11 = (f32[2,32,128]{2,1,0:T(8,128)S(1)}, f32[2,32,128]{2,1,0:T(8,128)S(1)}, u32[]{:S(2)}, u32[]{:S(2)}) collective-permute-start(f32[2,32,128]{2,1,0:T(8,128)S(1)} %pad_maximum_fusion.after_hbm.refs_0_), channel_id=1, source_target_pairs={{0,4},{1,5},{2,6},{3,7},{4,0},{5,1},{6,2},{7,3},{8,12},{9,13},{10,... | collective-permute-start | bytes 98312 | tf_op jit(solution)/shard_map/ppermute | solution.py:288
  30.2 3.9 %collective-permute-start.10 = (f32[2,32,128]{2,1,0:T(8,128)S(1)}, f32[2,32,128]{2,1,0:T(8,128)S(1)}, u32[]{:S(2)}, u32[]{:S(2)}) collective-permute-start(f32[2,32,128]{2,1,0:T(8,128)S(1)} %pad_maximum_fusion.after_hbm.refs_0_), channel_id=1, source_target_pairs={{0,2},{1,3},{2,0},{3,1},{4,6},{5,7},{6,4},{7,5},{8,10},{9,11},{10,... | collective-permute-start | bytes 98312 | tf_op jit(solution)/shard_map/ppermute | solution.py:288
  34.5 6.5 %collective-permute-start.13 = (f32[32,256]{1,0:T(8,128)S(1)}, f32[32,256]{1,0:T(8,128)S(1)}, u32[]{:S(2)}, u32[]{:S(2)}) collective-permute-start(f32[32,256]{1,0:T(8,128)S(1)} %get-tuple-element.44), channel_id=1, source_target_pairs={{0,24},{8,16},{16,8},{24,0},{1,25},{9,17},{17,9},{25,1},{2,26},{10... | collective-permute-start | bytes 98312 | tf_op jit(solution)/shard_map/ppermute | solution.py:288
  38.1 4.8 %collective-permute-start.14 = (f32[32,256]{1,0:T(8,128)S(1)}, f32[32,256]{1,0:T(8,128)S(1)}, u32[]{:S(2)}, u32[]{:S(2)}) collective-permute-start(f32[32,256]{1,0:T(8,128)S(1)} %get-tuple-element.45), channel_id=1, source_target_pairs={{0,16},{8,24},{16,0},{24,8},{1,17},{9,25},{17,1},{25,9},{2,18},{10... | collective-permute-start | bytes 98312 | tf_op jit(solution)/shard_map/ppermute | solution.py:288
  38.1 4.8 %collective-permute-start.15 = (f32[32,256]{1,0:T(8,128)S(1)}, f32[32,256]{1,0:T(8,128)S(1)}, u32[]{:S(2)}, u32[]{:S(2)}) collective-permute-start(f32[32,256]{1,0:T(8,128)S(1)} %get-tuple-element.46), channel_id=1, source_target_pairs={{0,8},{8,0},{16,24},{24,16},{1,9},{9,1},{17,25},{25,17},{2,10},{10... | collective-permute-start | bytes 98312 | tf_op jit(solution)/shard_map/ppermute | solution.py:288

commit v12 on v11

--- a/solution.py
+++ b/solution.py
@@ -49,11 +49,11 @@
     return ahead, lax.rem(start + ahead, stored * owners) // owners
 
 
-def select_kernel(even, odd, owners, start_ref, beside_ref, rows_ref, out_ref):
+def select_kernel(even, odd, owners, starts_ref, rows_ref, out_ref):
     me = lax.axis_index("dev")
     owner = lax.bitwise_xor(me, jnp.where(lax.rem(me, 2) == 1, odd, even))
-    for n, ref in enumerate((start_ref, beside_ref)):
-        row = chosen_row(owner, ref[0], owners, rows_ref.shape[0])[1]
+    for n in range(out_ref.shape[0]):
+        row = chosen_row(owner, starts_ref[n], owners, rows_ref.shape[0])[1]
         out_ref[n] = rows_ref[row]
 
 
@@ -320,6 +320,7 @@
     atoms = mine * dev_count
     f32, bf16 = jnp.float32, jnp.bfloat16
 
+    work = pl.CostEstimate(flops=2_000_000_000, bytes_accessed=8_000_000, transcendentals=0)
     masked = pl.pallas_call(
         mask_kernel,
         out_shape=pltpu.VMEM(density_rows.shape, bf16),
@@ -331,11 +332,11 @@
             pltpu.SemaphoreType.DMA((blocks_dev + 1,)),
         ],
         compiler_params=PARAMS,
+        cost_estimate=work,
         name="mask",
     )(*held_in_hbm(block_mask, density_rows))
 
     half = batches // 2
-    work = pl.CostEstimate(flops=2_000_000_000, bytes_accessed=8_000_000, transcendentals=0)
 
     def field(begin, after):
         return pl.pallas_call(
@@ -379,15 +380,17 @@
         return pl.pallas_call(
             functools.partial(select_kernel, even, odd, dev_count),
             out_shape=pltpu.VMEM((2,) + density_rows.shape[1:], bf16),
-            in_specs=[SMEM, SMEM, VMEM],
+            in_specs=[SMEM, VMEM],
             out_specs=VMEM,
             compiler_params=PARAMS,
             name="select",
-        )(*starts, rows)
+        )(starts, rows)
 
     if dev_count == 8:
-        starts = (turned(window_start, 2, 4), turned(window_start, 5, 3))
-        first = turned(masked, 4, 2)
+        beside = crossed(window_start, "dev", 1)
+        beside, rows = lax.optimization_barrier((beside, masked))
+        first = turned(rows, 4, 2)
+        starts = turned(jnp.concatenate([window_start, beside]), 2, 4)
         chosen = selected(0, 0, starts, masked)
         second = turned(chosen, 2, 4)
         first, later, _ = lax.optimization_barrier((first, masked, chosen))

time: 45.1 us -> 44.2 us (0.980)
  Pallas kernels: 17.5 us -> 16 us
  other arithmetic: 0.01 us -> 0.71 us
    pallas_call x2, Pallas kernels: 2.59 us -> 1.17 us  [selected(): pl.pallas_call(functools.partial(select_kernel, even, odd, dev_count), ou...]
    ppermute x5 -> x4, waiting for transfers between devices: 5.13 us -> 4.26 us  [turned(): lax.ppermute(value, 'dev', [(i, i ^ (odd if i % 2 else even)) for i in ra...]
    ppermute x11 -> x12, waiting for transfers between devices: 4.47 us -> 5.2 us  [crossed(): lax.ppermute(value, axis, [(i, i ^ m) for i in range(lax.axis_size(axis))])]
    concatenate x0 -> x1, other arithmetic: none -> 0.7 us  [per_device(): starts = turned(jnp.concatenate([window_start, beside]), 2, 4)]
    ppermute x5 -> x4, starting transfers between devices: 6.68 us -> 6.35 us  [turned(): lax.ppermute(value, 'dev', [(i, i ^ (odd if i % 2 else even)) for i in ra...]
    ppermute x11 -> x12, starting transfers between devices: 9.03 us -> 9.24 us  [crossed(): lax.ppermute(value, axis, [(i, i ^ m) for i in range(lax.axis_size(axis))])]
  transfers between devices with their start and end apart: 16 -> 16, of which waited for: 8 -> 6; matrix products, arithmetic and copies ran while one was open for 1% -> 3% of each run, Pallas kernels for 23% -> 23%
where the time goes in v12:
time: 44.2 us; the launch traced here: 43.8 us
  Pallas kernels  16 us (36%)
  starting transfers between devices  15.6 us (35%)
  waiting for transfers between devices  9.46 us (21%)
  between operations  1.42 us (3%)
  other arithmetic  0.71 us (2%)
  local copies, waits for them, and re-layouts  0.62 us (1%)
    ppermute x12, starting transfers between devices, crossed(): lax.ppermute(value, axis, [(i, i ^ m) for i in range(lax.axis_size(axis))])  9.24 us
    ppermute x4, starting transfers between devices, turned(): lax.ppermute(value, 'dev', [(i, i ^ (odd if i % 2 else even)) for i in ra...  6.35 us
    ppermute x12, waiting for transfers between devices, crossed(): lax.ppermute(value, axis, [(i, i ^ m) for i in range(lax.axis_size(axis))])  5.2 us
    ppermute x4, waiting for transfers between devices, turned(): lax.ppermute(value, 'dev', [(i, i ^ (odd if i % 2 else even)) for i in ra...  4.26 us
    pallas_call x2, Pallas kernels, field(): pl.pallas_call(functools.partial(field_kernel, begin), out_shape=pltpu.VM...  4.14 us
    pallas_call x1, Pallas kernels, turned_basis(): pl.pallas_call(turn_kernel, out_shape=(pltpu.VMEM((batches, near_blocks,...  3.64 us
    pallas_call x1, Pallas kernels, per_device(): pl.pallas_call(density_kernel, out_shape=(pltpu.VMEM((batches, points), f...  3.54 us
    pallas_call x1, Pallas kernels, per_device(): pl.pallas_call(functools.partial(potential_kernel, comps, atoms, flip), o...  1.88 us
  transfers between devices with their start and end apart: 16, of which 6 were waited for; matrix products, arithmetic and copies ran while one was open for 3% of the time, Pallas kernels for 23%

profile of v12, /device:TPU:0, one launch (start us, length us, event | category | flops | bytes accessed | tf_op | source)
XLA Modules:
  0.0 43.8 jit_solution(4886534404238442806)
XLA Ops:
  0.6 0.5 %collective-permute-start = (s32[1]{0:T(128)}, s32[1]{0:T(128)}, u32[]{:S(2)}, u32[]{:S(2)}) collective-permute-start(s32[1]{0:T(128)} %param.14), channel_id=1, source_target_pairs={{0,1},{1,0},{2,3},{3,2},{4,5},{5,4},{6,7},{7,6},{8,9},{9,8},{10,11... | collective-permute-start | bytes 20 | tf_op jit(solution)/shard_map/ppermute | solution.py:288
  1.1 1.3 %mask.1.rows_ref.refs_0_ = bf16[3,4,128,128]{3,2,1,0:T(8,128)(2,1)S(1)} custom-call(s32[3,4]{1,0:T(4,128)} %mask_hbm.1, bf16[3,4,128,128]{3,2,1,0:T(8,128)(2,1)} %rows_hbm.1), custom_call_target="tpu_custom_call" | custom-call | flops 2000000000 | bytes 8000000 | tf_op jit(solution)/shard_map/mask/pallas_call | solution.py:324
  2.5 0.0 copy-start.1
  2.5 0.0 collective-permute-done
  2.5 2.6 %collective-permute-start.2 = (bf16[3,4,128,128]{3,2,1,0:T(8,128)(2,1)S(1)}, bf16[3,4,128,128]{3,2,1,0:T(8,128)(2,1)S(1)}, u32[]{:S(2)}, u32[]{:S(2)}) collective-permute-start(bf16[3,4,128,128]{3,2,1,0:T(8,128)(2,1)S(1)} %mask.1.rows_ref.refs_0_), channel_id=1, source_target_pairs={{0,4},{1,3},{2,6},{3,1},{4,0},{5,7},{6,2},{7,5},{8,12},{9,11},{10,... | collective-permute-start | bytes 1179656 | tf_op jit(solution)/shard_map/ppermute | solution.py:293
  5.7 0.7 %pad_add_fusion = s32[2]{0:T(128)S(1)} fusion(s32[1]{0:T(128)} %collective-permute-done, s32[1]{0:T(128)S(6)} %copy.15.start_ref), kind=kLoop, calls=%fused_computation.1 | loop fusion | flops 2 | bytes 16 | tf_op jit(solution)/shard_map/concatenate | solution.py:393
  6.4 1.5 %collective-permute-start.1 = (s32[2]{0:T(128)S(1)}, s32[2]{0:T(128)S(1)}, u32[]{:S(2)}, u32[]{:S(2)}) collective-permute-start(s32[2]{0:T(128)S(1)} %pad_add_fusion), channel_id=1, source_target_pairs={{0,2},{1,5},{2,0},{3,7},{4,6},{5,1},{6,4},{7,3},{8,10},{9,13},{10,... | collective-permute-start | bytes 32 | tf_op jit(solution)/shard_map/ppermute | solution.py:293
  7.9 2.1 %collective-permute-done.1.starts_ref = s32[2]{0:T(128)S(1)} collective-permute-done((s32[2]{0:T(128)S(1)}, s32[2]{0:T(128)S(1)}, u32[]{:S(2)}, u32[]{:S(2)}) %collective-permute-start.1) | collective-permute-done | bytes 40 | tf_op jit(solution)/shard_map/ppermute | solution.py:293
  10.1 0.6 %select.2 = bf16[2,4,128,128]{3,2,1,0:T(8,128)(2,1)S(1)} custom-call(s32[2]{0:T(128)S(1)} %collective-permute-done.1.starts_ref, bf16[3,4,128,128]{3,2,1,0:T(8,128)(2,1)S(1)} %mask.1.rows_ref.refs_0_), custom_call_target="tpu_custom_call" | custom-call | tf_op jit(solution)/shard_map/select/pallas_call | solution.py:380
  10.6 1.6 %collective-permute-start.3 = (bf16[2,4,128,128]{3,2,1,0:T(8,128)(2,1)S(1)}, bf16[2,4,128,128]{3,2,1,0:T(8,128)(2,1)S(1)}, u32[]{:S(2)}, u32[]{:S(2)}) collective-permute-start(bf16[2,4,128,128]{3,2,1,0:T(8,128)(2,1)S(1)} %select.2), channel_id=1, source_target_pairs={{0,2},{1,5},{2,0},{3,7},{4,6},{5,1},{6,4},{7,3},{8,10},{9,13},{10,... | collective-permute-start | bytes 786440 | tf_op jit(solution)/shard_map/ppermute | solution.py:293
  12.2 0.0 collective-permute-done.2.rows_ref.refs_2_
  12.2 0.6 %select.3.after_hbm = bf16[2,4,128,128]{3,2,1,0:T(8,128)(2,1)S(1)} custom-call(s32[2]{0:T(128)S(1)} %collective-permute-done.1.starts_ref, bf16[3,4,128,128]{3,2,1,0:T(8,128)(2,1)S(1)} %collective-permute-done.2.rows_ref.refs_2_), custom_call_target="tpu_custom_call" | custom-call | tf_op jit(solution)/shard_map/select/pallas_call | solution.py:380
  12.8 0.7 %collective-permute-start.7 = (bf16[2,4,128,128]{3,2,1,0:T(8,128)(2,1)S(1)}, bf16[2,4,128,128]{3,2,1,0:T(8,128)(2,1)S(1)}, u32[]{:S(2)}, u32[]{:S(2)}) collective-permute-start(bf16[2,4,128,128]{3,2,1,0:T(8,128)(2,1)S(1)} %select.3.after_hbm), channel_id=1, source_target_pairs={{0,2},{1,5},{2,0},{3,7},{4,6},{5,1},{6,4},{7,3},{8,10},{9,13},{10,... | collective-permute-start | bytes 786440 | tf_op jit(solution)/shard_map/ppermute | solution.py:293
  13.5 0.0 collective-permute-start.5
  13.5 0.5 %collective-permute-start.4 = (bf16[3,4,128,128]{3,2,1,0:T(8,128)(2,1)S(1)}, bf16[3,4,128,128]{3,2,1,0:T(8,128)(2,1)S(1)}, u32[]{:S(2)}, u32[]{:S(2)}) collective-permute-start(bf16[3,4,128,128]{3,2,1,0:T(8,128)(2,1)S(1)} %mask.1.rows_ref.refs_0_), channel_id=1, source_target_pairs={{0,1},{1,0},{2,3},{3,2},{4,5},{5,4},{6,7},{7,6},{8,9},{9,8},{10,11... | collective-permute-start | bytes 1179656 | tf_op jit(solution)/shard_map/ppermute | solution.py:288
  14.0 0.0 copy-done.1
  14.0 0.0 copy-start
  14.0 0.0 copy-start.2
  14.0 3.6 %turn.1 = (bf16[12,4,128,256]{3,2,1,0:T(8,128)(2,1)S(1)}, f32[12,6,256]{2,1,0:T(8,128)S(1)}, bf16[72,32,256]{2,1,0:T(8,128)(2,1)S(1)}, s32[1,128]{1,0:T(1,128)S(1)}) custom-call(bf16[2,4,128,128]{3,2,1,0:T(8,128)(2,1)S(1)} %select.3.after_hbm, s32[6,12]{1,0:T(8,128)S(1)} %bitcast.6, bf16[12,4,256,128]{3,2,1,0:T(8,128)(2,1)} %basis_hbm.1, ...), custom_call_target="tpu_custom_call" | custom-call | flops 2000000000 | bytes 8000000 | tf_op jit(solution)/shard_map/turn/pallas_call | solution.py:359
  17.7 0.0 collective-permute-done.3.refs_4_
  17.7 0.1 collective-permute-start.6
  17.8 2.1 %collective-permute-done.7.refs_6_ = bf16[2,4,128,128]{3,2,1,0:T(8,128)(2,1)S(1)} collective-permute-done((bf16[2,4,128,128]{3,2,1,0:T(8,128)(2,1)S(1)}, bf16[2,4,128,128]{3,2,1,0:T(8,128)(2,1)S(1)}, u32[]{:S(2)}, u32[]{:S(2)}) %collective-permute-start.7) | collective-permute-done | bytes 262176 | tf_op jit(solution)/shard_map/ppermute | solution.py:293
  19.9 0.0 collective-permute-start.8
  19.9 0.0 collective-permute-done.6.refs_5_
  19.9 0.0 collective-permute-done.4.refs_1_
  19.9 0.0 collective-permute-done.5.refs_3_
  19.9 1.5 %collective-permute-done.8.refs_7_ = bf16[2,4,128,128]{3,2,1,0:T(8,128)(2,1)S(1)} collective-permute-done((bf16[2,4,128,128]{3,2,1,0:T(8,128)(2,1)S(1)}, bf16[2,4,128,128]{3,2,1,0:T(8,128)(2,1)S(1)}, u32[]{:S(2)}, u32[]{:S(2)}) %collective-permute-start.8) | collective-permute-done | bytes 262176 | tf_op jit(solution)/shard_map/ppermute | solution.py:288
  21.4 0.0 copy-done
  21.4 0.0 copy-done.2
  21.4 3.5 %density.1 = (f32[12,256]{1,0:T(8,128)S(1)}, f32[32,128]{1,0:T(8,128)S(1)}) custom-call(s32[1]{0:T(128)S(6)} %copy.15.start_ref, s32[1,12]{1,0:T(1,128)S(1)} %copy-done.2, s32[1,12]{1,0:T(1,128)S(1)} %copy-done, s32[1,128]{1,0:T(1,128)S(1)} %get-tuple-element.34.atom_ref, bf16[12,4,128,256]{3,2,1,0:T(8,128)(2,1)S(1)} %get-tuple-element.36.phit_ref, ...), custom_call_target="tpu_custom_call" | custom-call | flops 2000000000 | bytes 6000000 | tf_op jit(solution)/shard_map/density/pallas_call | solution.py:407
  25.0 0.2 collective-permute-start.9
  25.2 0.6 %copy.14 = f32[12,256]{1,0:T(8,128)} copy(f32[12,256]{1,0:T(8,128)S(1)} %get-tuple-element.59) | data formatting | bytes 24576
  25.8 0.5 %collective-permute-done.9 = f32[32,128]{1,0:T(8,128)S(1)} collective-permute-done((f32[32,128]{1,0:T(8,128)S(1)}, f32[32,128]{1,0:T(8,128)S(1)}, u32[]{:S(2)}, u32[]{:S(2)}) %collective-permute-start.9) | collective-permute-done | bytes 16416 | tf_op jit(solution)/shard_map/ppermute | solution.py:288
  26.2 1.4 %collective-permute-start.12 = (f32[2,32,128]{2,1,0:T(8,128)S(1)}, f32[2,32,128]{2,1,0:T(8,128)S(1)}, u32[]{:S(2)}, u32[]{:S(2)}) collective-permute-start(f32[2,32,128]{2,1,0:T(8,128)S(1)} %pad_maximum_fusion.after_hbm.refs_0_), channel_id=1, source_target_pairs={{0,6},{1,7},{2,4},{3,5},{4,2},{5,3},{6,0},{7,1},{8,14},{9,15},{10,... | collective-permute-start | bytes 98312 | tf_op jit(solution)/shard_map/ppermute | solution.py:288
  27.7 1.5 %collective-permute-start.11 = (f32[2,32,128]{2,1,0:T(8,128)S(1)}, f32[2,32,128]{2,1,0:T(8,128)S(1)}, u32[]{:S(2)}, u32[]{:S(2)}) collective-permute-start(f32[2,32,128]{2,1,0:T(8,128)S(1)} %pad_maximum_fusion.after_hbm.refs_0_), channel_id=1, source_target_pairs={{0,4},{1,5},{2,6},{3,7},{4,0},{5,1},{6,2},{7,3},{8,12},{9,13},{10,... | collective-permute-start | bytes 98312 | tf_op jit(solution)/shard_map/ppermute | solution.py:288
  29.2 0.5 %collective-permute-start.10 = (f32[2,32,128]{2,1,0:T(8,128)S(1)}, f32[2,32,128]{2,1,0:T(8,128)S(1)}, u32[]{:S(2)}, u32[]{:S(2)}) collective-permute-start(f32[2,32,128]{2,1,0:T(8,128)S(1)} %pad_maximum_fusion.after_hbm.refs_0_), channel_id=1, source_target_pairs={{0,2},{1,3},{2,0},{3,1},{4,6},{5,7},{6,4},{7,5},{8,10},{9,11},{10,... | collective-permute-start | bytes 98312 | tf_op jit(solution)/shard_map/ppermute | solution.py:288
  29.7 2.1 %field.2.low_ref = f32[36,25,256]{2,1,0:T(8,128)S(1)} custom-call(f32[2,32,128]{2,1,0:T(8,128)S(1)} %pad_maximum_fusion.after_hbm.refs_0_, f32[16,25]{1,0:T(8,128)} %bitcast.8, f32[12,6,256]{2,1,0:T(8,128)} %radius_hbm.3, bf16[12,6,25,256]{3,2,1,0:T(8,128)(2,1)} %harm_hbm.5), custom_call_target="tpu_custom_call" | custom-call | flops 2000000000 | bytes 8000000 | tf_op jit(solution)/shard_map/field/pallas_call | solution.py:342
  31.8 0.0 collective-permute-done.12.refs_3_
  31.8 0.0 collective-permute-done.11.refs_2_
  31.8 1.3 %collective-permute-done.10.refs_1_ = f32[2,32,128]{2,1,0:T(8,128)S(1)} collective-permute-done((f32[2,32,128]{2,1,0:T(8,128)S(1)}, f32[2,32,128]{2,1,0:T(8,128)S(1)}, u32[]{:S(2)}, u32[]{:S(2)}) %collective-permute-start.10) | collective-permute-done | bytes 32800 | tf_op jit(solution)/shard_map/ppermute | solution.py:288
  33.1 0.4 scatter.1
  33.5 3.7 %collective-permute-start.13 = (f32[32,256]{1,0:T(8,128)S(1)}, f32[32,256]{1,0:T(8,128)S(1)}, u32[]{:S(2)}, u32[]{:S(2)}) collective-permute-start(f32[32,256]{1,0:T(8,128)S(1)} %get-tuple-element.48), channel_id=1, source_target_pairs={{0,24},{8,16},{16,8},{24,0},{1,25},{9,17},{17,9},{25,1},{2,26},{10... | collective-permute-start | bytes 98312 | tf_op jit(solution)/shard_map/ppermute | solution.py:288
  37.1 0.0 collective-permute-start.14
  37.1 0.8 %collective-permute-start.15 = (f32[32,256]{1,0:T(8,128)S(1)}, f32[32,256]{1,0:T(8,128)S(1)}, u32[]{:S(2)}, u32[]{:S(2)}) collective-permute-start(f32[32,256]{1,0:T(8,128)S(1)} %get-tuple-element.50), channel_id=1, source_target_pairs={{0,8},{8,0},{16,24},{24,16},{1,9},{9,1},{17,25},{25,17},{2,10},{10... | collective-permute-start | bytes 98312 | tf_op jit(solution)/shard_map/ppermute | solution.py:288
  37.9 2.1 %field.3.high_ref = f32[36,25,256]{2,1,0:T(8,128)S(1)} custom-call(f32[32,384]{1,0:T(8,128)S(1)} %get-tuple-element.47.after_hbm.own_ref, f32[16,25]{1,0:T(8,128)} %bitcast.9, f32[12,6,256]{2,1,0:T(8,128)} %radius_hbm.3, bf16[12,6,25,256]{3,2,1,0:T(8,128)(2,1)} %harm_hbm.5), custom_call_target="tpu_custom_call" | custom-call | flops 2000000000 | bytes 8000000 | tf_op jit(solution)/shard_map/field/pallas_call | solution.py:342
  40.0 0.0 collective-permute-done.13.near_b_ref
  40.0 1.9 %collective-permute-done.14.fa_ref.fb_ref = f32[32,256]{1,0:T(8,128)S(1)} collective-permute-done((f32[32,256]{1,0:T(8,128)S(1)}, f32[32,256]{1,0:T(8,128)S(1)}, u32[]{:S(2)}, u32[]{:S(2)}) %collective-permute-start.14) | collective-permute-done | bytes 32800 | tf_op jit(solution)/shard_map/ppermute | solution.py:288
  42.0 0.0 collective-permute-done.15.near_a_ref
  42.0 1.9 %potential.1 = (f32[16,25]{1,0:T(8,128)}, f32[12,256]{1,0:T(8,128)}) custom-call(s32[1,12]{1,0:T(1,128)S(1)} %copy-done, f32[32,384]{1,0:T(8,128)S(1)} %get-tuple-element.47.after_hbm.own_ref, f32[32,256]{1,0:T(8,128)S(1)} %collective-permute-done.13.near_b_ref, f32[32,256]{1,0:T(8,128)S(1)} %collective-permute-done.14.fa_ref.fb_ref, ...), custom_call_target="tpu_custom_call" | custom-call | tf_op jit(solution)/shard_map/potential/pallas_call | solution.py:458
  (1 shorter events, 0.0 us)
Async XLA Ops:
  0.6 1.8 %collective-permute-start = (s32[1]{0:T(128)}, s32[1]{0:T(128)}, u32[]{:S(2)}, u32[]{:S(2)}) collective-permute-start(s32[1]{0:T(128)} %param.14), channel_id=1, source_target_pairs={{0,1},{1,0},{2,3},{3,2},{4,5},{5,4},{6,7},{7,6},{8,9},{9,8},{10,11... | collective-permute-start | bytes 20 | tf_op jit(solution)/shard_map/ppermute | solution.py:288
  2.5 11.5 %copy-start.1 = (s32[12,6]{0,1:T(8,128)S(1)}, s32[12,6]{0,1:T(8,128)}, u32[]{:S(2)}) copy-start(s32[12,6]{0,1:T(8,128)} %param.17) | copy-start | bytes 868
  2.5 9.7 %collective-permute-start.2 = (bf16[3,4,128,128]{3,2,1,0:T(8,128)(2,1)S(1)}, bf16[3,4,128,128]{3,2,1,0:T(8,128)(2,1)S(1)}, u32[]{:S(2)}, u32[]{:S(2)}) collective-permute-start(bf16[3,4,128,128]{3,2,1,0:T(8,128)(2,1)S(1)} %mask.1.rows_ref.refs_0_), channel_id=1, source_target_pairs={{0,4},{1,3},{2,6},{3,1},{4,0},{5,7},{6,2},{7,5},{8,12},{9,11},{10,... | collective-permute-start | bytes 1179656 | tf_op jit(solution)/shard_map/ppermute | solution.py:293
  6.4 3.6 %collective-permute-start.1 = (s32[2]{0:T(128)S(1)}, s32[2]{0:T(128)S(1)}, u32[]{:S(2)}, u32[]{:S(2)}) collective-permute-start(s32[2]{0:T(128)S(1)} %pad_add_fusion), channel_id=1, source_target_pairs={{0,2},{1,5},{2,0},{3,7},{4,6},{5,1},{6,4},{7,3},{8,10},{9,13},{10,... | collective-permute-start | bytes 32 | tf_op jit(solution)/shard_map/ppermute | solution.py:293
  10.6 7.0 %collective-permute-start.3 = (bf16[2,4,128,128]{3,2,1,0:T(8,128)(2,1)S(1)}, bf16[2,4,128,128]{3,2,1,0:T(8,128)(2,1)S(1)}, u32[]{:S(2)}, u32[]{:S(2)}) collective-permute-start(bf16[2,4,128,128]{3,2,1,0:T(8,128)(2,1)S(1)} %select.2), channel_id=1, source_target_pairs={{0,2},{1,5},{2,0},{3,7},{4,6},{5,1},{6,4},{7,3},{8,10},{9,13},{10,... | collective-permute-start | bytes 786440 | tf_op jit(solution)/shard_map/ppermute | solution.py:293
  12.8 7.1 %collective-permute-start.7 = (bf16[2,4,128,128]{3,2,1,0:T(8,128)(2,1)S(1)}, bf16[2,4,128,128]{3,2,1,0:T(8,128)(2,1)S(1)}, u32[]{:S(2)}, u32[]{:S(2)}) collective-permute-start(bf16[2,4,128,128]{3,2,1,0:T(8,128)(2,1)S(1)} %select.3.after_hbm), channel_id=1, source_target_pairs={{0,2},{1,5},{2,0},{3,7},{4,6},{5,1},{6,4},{7,3},{8,10},{9,13},{10,... | collective-permute-start | bytes 786440 | tf_op jit(solution)/shard_map/ppermute | solution.py:293
  13.5 6.4 %collective-permute-start.5 = (bf16[3,4,128,128]{3,2,1,0:T(8,128)(2,1)S(1)}, bf16[3,4,128,128]{3,2,1,0:T(8,128)(2,1)S(1)}, u32[]{:S(2)}, u32[]{:S(2)}) collective-permute-start(bf16[3,4,128,128]{3,2,1,0:T(8,128)(2,1)S(1)} %collective-permute-done.2.rows_ref.refs_2_), channel_id=1, source_target_pairs={{0,1},{1,0},{2,3},{3,2},{4,5},{5,4},{6,7},{7,6},{8,9},{9,8},{10,11... | collective-permute-start | bytes 1179656 | tf_op jit(solution)/shard_map/ppermute | solution.py:288
  13.5 6.4 %collective-permute-start.4 = (bf16[3,4,128,128]{3,2,1,0:T(8,128)(2,1)S(1)}, bf16[3,4,128,128]{3,2,1,0:T(8,128)(2,1)S(1)}, u32[]{:S(2)}, u32[]{:S(2)}) collective-permute-start(bf16[3,4,128,128]{3,2,1,0:T(8,128)(2,1)S(1)} %mask.1.rows_ref.refs_0_), channel_id=1, source_target_pairs={{0,1},{1,0},{2,3},{3,2},{4,5},{5,4},{6,7},{7,6},{8,9},{9,8},{10,11... | collective-permute-start | bytes 1179656 | tf_op jit(solution)/shard_map/ppermute | solution.py:288
  14.0 7.4 %copy-start = (s32[1,12]{1,0:T(1,128)S(1)}, s32[1,12]{1,0:T(1,128)}, u32[]{:S(2)}) copy-start(s32[1,12]{1,0:T(1,128)} %size_ref.3) | copy-start | bytes 148
  14.0 7.4 %copy-start.2 = (s32[1,12]{1,0:T(1,128)S(1)}, s32[1,12]{1,0:T(1,128)}, u32[]{:S(2)}) copy-start(s32[1,12]{1,0:T(1,128)} %offset_ref.1) | copy-start | bytes 148
  17.7 2.2 %collective-permute-start.6 = (bf16[2,4,128,128]{3,2,1,0:T(8,128)(2,1)S(1)}, bf16[2,4,128,128]{3,2,1,0:T(8,128)(2,1)S(1)}, u32[]{:S(2)}, u32[]{:S(2)}) collective-permute-start(bf16[2,4,128,128]{3,2,1,0:T(8,128)(2,1)S(1)} %collective-permute-done.3.refs_4_), channel_id=1, source_target_pairs={{0,1},{1,0},{2,3},{3,2},{4,5},{5,4},{6,7},{7,6},{8,9},{9,8},{10,11... | collective-permute-start | bytes 786440 | tf_op jit(solution)/shard_map/ppermute | solution.py:288
  19.9 1.5 %collective-permute-start.8 = (bf16[2,4,128,128]{3,2,1,0:T(8,128)(2,1)S(1)}, bf16[2,4,128,128]{3,2,1,0:T(8,128)(2,1)S(1)}, u32[]{:S(2)}, u32[]{:S(2)}) collective-permute-start(bf16[2,4,128,128]{3,2,1,0:T(8,128)(2,1)S(1)} %collective-permute-done.7.refs_6_), channel_id=1, source_target_pairs={{0,1},{1,0},{2,3},{3,2},{4,5},{5,4},{6,7},{7,6},{8,9},{9,8},{10,11... | collective-permute-start | bytes 786440 | tf_op jit(solution)/shard_map/ppermute | solution.py:288
  25.0 1.2 %collective-permute-start.9 = (f32[32,128]{1,0:T(8,128)S(1)}, f32[32,128]{1,0:T(8,128)S(1)}, u32[]{:S(2)}, u32[]{:S(2)}) collective-permute-start(f32[32,128]{1,0:T(8,128)S(1)} %get-tuple-element.42), channel_id=1, source_target_pairs={{0,1},{1,0},{2,3},{3,2},{4,5},{5,4},{6,7},{7,6},{8,9},{9,8},{10,11... | collective-permute-start | bytes 49160 | tf_op jit(solution)/shard_map/ppermute | solution.py:288
  26.2 5.6 %collective-permute-start.12 = (f32[2,32,128]{2,1,0:T(8,128)S(1)}, f32[2,32,128]{2,1,0:T(8,128)S(1)}, u32[]{:S(2)}, u32[]{:S(2)}) collective-permute-start(f32[2,32,128]{2,1,0:T(8,128)S(1)} %pad_maximum_fusion.after_hbm.refs_0_), channel_id=1, source_target_pairs={{0,6},{1,7},{2,4},{3,5},{4,2},{5,3},{6,0},{7,1},{8,14},{9,15},{10,... | collective-permute-start | bytes 98312 | tf_op jit(solution)/shard_map/ppermute | solution.py:288
  27.7 4.2 %collective-permute-start.11 = (f32[2,32,128]{2,1,0:T(8,128)S(1)}, f32[2,32,128]{2,1,0:T(8,128)S(1)}, u32[]{:S(2)}, u32[]{:S(2)}) collective-permute-start(f32[2,32,128]{2,1,0:T(8,128)S(1)} %pad_maximum_fusion.after_hbm.refs_0_), channel_id=1, source_target_pairs={{0,4},{1,5},{2,6},{3,7},{4,0},{5,1},{6,2},{7,3},{8,12},{9,13},{10,... | collective-permute-start | bytes 98312 | tf_op jit(solution)/shard_map/ppermute | solution.py:288
  29.2 3.9 %collective-permute-start.10 = (f32[2,32,128]{2,1,0:T(8,128)S(1)}, f32[2,32,128]{2,1,0:T(8,128)S(1)}, u32[]{:S(2)}, u32[]{:S(2)}) collective-permute-start(f32[2,32,128]{2,1,0:T(8,128)S(1)} %pad_maximum_fusion.after_hbm.refs_0_), channel_id=1, source_target_pairs={{0,2},{1,3},{2,0},{3,1},{4,6},{5,7},{6,4},{7,5},{8,10},{9,11},{10,... | collective-permute-start | bytes 98312 | tf_op jit(solution)/shard_map/ppermute | solution.py:288
  33.5 6.5 %collective-permute-start.13 = (f32[32,256]{1,0:T(8,128)S(1)}, f32[32,256]{1,0:T(8,128)S(1)}, u32[]{:S(2)}, u32[]{:S(2)}) collective-permute-start(f32[32,256]{1,0:T(8,128)S(1)} %get-tuple-element.48), channel_id=1, source_target_pairs={{0,24},{8,16},{16,8},{24,0},{1,25},{9,17},{17,9},{25,1},{2,26},{10... | collective-permute-start | bytes 98312 | tf_op jit(solution)/shard_map/ppermute | solution.py:288
  37.1 4.8 %collective-permute-start.14 = (f32[32,256]{1,0:T(8,128)S(1)}, f32[32,256]{1,0:T(8,128)S(1)}, u32[]{:S(2)}, u32[]{:S(2)}) collective-permute-start(f32[32,256]{1,0:T(8,128)S(1)} %get-tuple-element.49), channel_id=1, source_target_pairs={{0,16},{8,24},{16,0},{24,8},{1,17},{9,25},{17,1},{25,9},{2,18},{10... | collective-permute-start | bytes 98312 | tf_op jit(solution)/shard_map/ppermute | solution.py:288
  37.1 4.8 %collective-permute-start.15 = (f32[32,256]{1,0:T(8,128)S(1)}, f32[32,256]{1,0:T(8,128)S(1)}, u32[]{:S(2)}, u32[]{:S(2)}) collective-permute-start(f32[32,256]{1,0:T(8,128)S(1)} %get-tuple-element.50), channel_id=1, source_target_pairs={{0,8},{8,0},{16,24},{24,16},{1,9},{9,1},{17,25},{25,17},{2,10},{10... | collective-permute-start | bytes 98312 | tf_op jit(solution)/shard_map/ppermute | solution.py:288

commit v13 on v12

--- a/solution.py
+++ b/solution.py
@@ -76,7 +76,8 @@
 
 
 def field_kernel(
-    begin, after_hbm, table_hbm, radius_hbm, harm_hbm, g_ref, table_ref, radius_ref, harm_ref, sems
+    begin, after_hbm, alive_ref, table_hbm, radius_hbm, harm_hbm,
+    g_ref, table_ref, radius_ref, harm_ref, sems,
 ):
     batches, near, comps, points = harm_ref.shape
     knots = table_ref.shape[0]
@@ -95,19 +96,20 @@
 
     def body(b, carry):
         rows = radius_ref[b]
+        alive = alive_ref[pl.ds(begin + b, 1), :]
         for i in range(near):
             spline = cubic(jnp.abs(rows[i : i + 1, :] - knot))
             s_hi, s_lo = split2(spline)
             radial = dot(coeffs, jnp.concatenate([s_hi, s_lo, s_hi], axis=0))
-            g_ref[b * near + i] = radial * harm_ref[b, i].astype(jnp.float32)
+            g_ref[b * near + i] = radial * (harm_ref[b, i].astype(jnp.float32) * alive)
         return carry
 
     lax.fori_loop(0, batches, body, 0, unroll=2)
 
 
 def turn_kernel(
-    after_hbm, near_ref, basis_hbm, part_hbm, harm_hbm,
-    phit_ref, part_ref, hpad_ref, atom_ref, basis, harm_ref, sems,
+    after_hbm, near_ref, size_ref, basis_hbm, part_hbm, harm_hbm,
+    phit_ref, part_ref, hpad_ref, atom_ref, alive_ref, basis, harm_ref, sems,
 ):
     batches, near_blocks = basis.shape[:2]
     near, comps, points = harm_ref.shape[1:]
@@ -126,6 +128,9 @@
         for i in range(near):
             atom = jnp.where(lane == b * SLOT + i, near_ref[i, b], atom)
     atom_ref[...] = atom
+    point = lax.broadcasted_iota(jnp.int32, (1, points), 1)
+    for b in range(batches):
+        alive_ref[b : b + 1, :] = (point < size_ref[0, b]).astype(jnp.float32)
     for n in range(batches * near):
         hpad_ref[n, ROWS // 2 :, :] = jnp.zeros((ROWS // 2, points), jnp.bfloat16)
 
@@ -149,7 +154,7 @@
 
 
 def density_kernel(
-    start_ref, offset_ref, size_ref, atom_ref, phit_ref, part_ref, hpad_ref, *refs
+    start_ref, offset_ref, atom_ref, alive_ref, phit_ref, part_ref, hpad_ref, *refs
 ):
     dens_ref, terms_ref, window_ref, w_ref = refs[-4:]
     pieces = refs[:-4]
@@ -170,7 +175,6 @@
         ahead, row = chosen_row(owner, start_ref[0], owners, stored)
         window_ref[ahead] = piece[row if at is None else at]
     w_ref[...] = jnp.zeros(w_ref.shape, w_ref.dtype)
-    lane = lax.broadcasted_iota(jnp.int32, (1, points), 1)
     zero = jnp.zeros((width, width), jnp.bfloat16)
 
     def body(b, carry):
@@ -189,13 +193,13 @@
             part = mixed[j * width : (j + 1) * width]
             total = total + part * phit_ref[b, j].astype(jnp.float32)
         summed = jnp.sum(total, axis=0, keepdims=True)
-        alive = lane < size_ref[0, b]
-        row = jnp.where(alive, summed, 0.0)
+        row = summed * alive_ref[pl.ds(b, 1), :]
         dens_ref[pl.ds(b, 1), :] = row
         w_ref[b, 0:near, :] = part_ref[b] * row
         return carry
 
-    lax.fori_loop(0, batches, body, 0, unroll=4)
+    for b in range(batches):
+        body(b, 0)
     weights = w_ref[...].reshape(LANES, points)
     columns = jnp.concatenate(split2(weights), axis=0)
     slot = lax.broadcasted_iota(jnp.int32, (1, 2 * LANES), 1) % LANES
@@ -238,7 +242,7 @@
 
 
 def potential_kernel(
-    comps, atoms, flip, size_ref, own_ref, near_b_ref, fa_ref, fb_ref, near_a_ref, atom_ref,
+    comps, atoms, flip, own_ref, near_b_ref, fa_ref, fb_ref, near_a_ref, atom_ref,
     low_ref, high_ref, mom_ref, pot_ref,
 ):
     batches, points = pot_ref.shape
@@ -270,14 +274,12 @@
     got = dot(jnp.concatenate(split3(moments), axis=0), pick)
     chosen = got[:ROWS] + got[ROWS : 2 * ROWS] + got[2 * ROWS :]
     chosen = chosen[:comps]
-    lane = lax.broadcasted_iota(jnp.int32, (1, points), 1)
     for b in range(batches):
         total = jnp.zeros((comps, points), jnp.float32)
         for i in range(near):
             column = chosen[:, b * SLOT + i : b * SLOT + i + 1]
             total = total + column * fields[b * near + i][...]
-        row = jnp.sum(total, axis=0, keepdims=True)
-        pot_ref[b : b + 1, :] = jnp.where(lane < size_ref[0, b], row, 0.0)
+        pot_ref[b : b + 1, :] = jnp.sum(total, axis=0, keepdims=True)
 
 
 def held_in_hbm(*values):
@@ -342,7 +344,7 @@
         return pl.pallas_call(
             functools.partial(field_kernel, begin),
             out_shape=pltpu.VMEM((half * near, comps, points), f32),
-            in_specs=[HBM] * 4,
+            in_specs=[HBM, VMEM] + [HBM] * 3,
             out_specs=VMEM,
             scratch_shapes=[
                 pltpu.VMEM(radial_table.shape[::-1], f32),
@@ -353,7 +355,7 @@
             compiler_params=WIDE,
             cost_estimate=work,
             name="field",
-        )(after, *held_in_hbm(radial_table.T, radius, harmonics))
+        )(after, alive, *held_in_hbm(radial_table.T, radius, harmonics))
 
     def turned_basis(after):
         return pl.pallas_call(
@@ -363,9 +365,10 @@
                 pltpu.VMEM(partition.shape, f32),
                 pltpu.VMEM((batches * near, ROWS, points), bf16),
                 pltpu.VMEM((1, LANES), jnp.int32),
+                pltpu.VMEM((batches, points), f32),
             ),
-            in_specs=[HBM, SMEM] + [HBM] * 3,
-            out_specs=(VMEM,) * 4,
+            in_specs=[HBM, SMEM, SMEM] + [HBM] * 3,
+            out_specs=(VMEM,) * 5,
             scratch_shapes=[
                 pltpu.VMEM(basis_values.shape, bf16),
                 pltpu.VMEM(harmonics.shape, bf16),
@@ -374,7 +377,7 @@
             compiler_params=WIDE,
             cost_estimate=work,
             name="turn",
-        )(after, atom_near.T, *held_in_hbm(basis_values, partition, harmonics))
+        )(after, atom_near.T, batch_sizes, *held_in_hbm(basis_values, partition, harmonics))
 
     def selected(even, odd, starts, rows):
         return pl.pallas_call(
@@ -396,12 +399,12 @@
         first, later, _ = lax.optimization_barrier((first, masked, chosen))
         chosen = selected(4, 2, starts, first)
         third = turned(chosen, 2, 4)
-        phit, weights, hpad, atom_rows = turned_basis(chosen)
+        phit, weights, hpad, atom_rows, alive = turned_basis(chosen)
         second, phit = lax.optimization_barrier((second, phit))
         sent = (later, first, second, third)
         pieces = [piece for value in sent for piece in (value, crossed(value, "dev", 1))]
     else:
-        phit, weights, hpad, atom_rows = turned_basis(masked)
+        phit, weights, hpad, atom_rows, alive = turned_basis(masked)
         pieces = [lax.all_gather(masked, "dev", axis=0)]
 
     density, terms = pl.pallas_call(
@@ -410,7 +413,7 @@
             pltpu.VMEM((batches, points), f32),
             pltpu.VMEM((ROWS, LANES), f32),
         ),
-        in_specs=[SMEM] * 3 + [VMEM] * (4 + len(pieces)),
+        in_specs=[SMEM] * 2 + [VMEM] * (5 + len(pieces)),
         out_specs=(VMEM, VMEM),
         scratch_shapes=[
             pltpu.VMEM((dev_count, band, width, width), bf16),
@@ -420,7 +423,7 @@
         cost_estimate=pl.CostEstimate(flops=2_000_000_000, bytes_accessed=6_000_000, transcendentals=0),
         name="density",
     )(
-        window_start, batch_offsets, batch_sizes, atom_rows, phit, weights, hpad,
+        window_start, batch_offsets, atom_rows, alive, phit, weights, hpad,
         *pieces,
     )
 
@@ -461,11 +464,11 @@
             jax.ShapeDtypeStruct((mine, comps), f32),
             jax.ShapeDtypeStruct((batches, points), f32),
         ),
-        in_specs=[SMEM] + [VMEM] * 8,
+        in_specs=[VMEM] * 8,
         out_specs=(VMEM, VMEM),
         compiler_params=PARAMS,
         name="potential",
-    )(batch_sizes, own, near_b, far_a, far_b, near_a, atom_rows, g_low, g_high)
+    )(own, near_b, far_a, far_b, near_a, atom_rows, g_low, g_high)
     return (density, moments.T, potential)
 
 

time: 44.2 us -> 43.2 us (0.977)
  Pallas kernels: 16 us -> 15.1 us
    pallas_call x1, Pallas kernels: 1.88 us -> 1.34 us  [per_device(): pl.pallas_call(functools.partial(potential_kernel, comps, atoms, flip), o...]
  transfers between devices with their start and end apart: 16 -> 16, of which waited for: 6 -> 6; matrix products, arithmetic and copies ran while one was open for 3% -> 3% of each run, Pallas kernels for 23% -> 24%
where the time goes in v13:
time: 43.2 us; the launch traced here: 42.9 us
  starting transfers between devices  15.6 us (36%)
  Pallas kernels  15.1 us (35%)
  waiting for transfers between devices  9.42 us (22%)
  between operations  1.43 us (3%)
  other arithmetic  0.71 us (2%)
  local copies, waits for them, and re-layouts  0.62 us (1%)
    ppermute x12, starting transfers between devices, crossed(): lax.ppermute(value, axis, [(i, i ^ m) for i in range(lax.axis_size(axis))])  9.26 us
    ppermute x4, starting transfers between devices, turned(): lax.ppermute(value, 'dev', [(i, i ^ (odd if i % 2 else even)) for i in ra...  6.35 us
    ppermute x12, waiting for transfers between devices, crossed(): lax.ppermute(value, axis, [(i, i ^ m) for i in range(lax.axis_size(axis))])  5.18 us
    ppermute x4, waiting for transfers between devices, turned(): lax.ppermute(value, 'dev', [(i, i ^ (odd if i % 2 else even)) for i in ra...  4.24 us
    pallas_call x2, Pallas kernels, field(): pl.pallas_call(functools.partial(field_kernel, begin), out_shape=pltpu.VM...  4.14 us
    pallas_call x1, Pallas kernels, turned_basis(): pl.pallas_call(turn_kernel, out_shape=(pltpu.VMEM((batches, near_blocks,...  3.65 us
    pallas_call x1, Pallas kernels, per_device(): pl.pallas_call(density_kernel, out_shape=(pltpu.VMEM((batches, points), f...  3.16 us
    pallas_call x1, Pallas kernels, per_device(): pl.pallas_call(functools.partial(potential_kernel, comps, atoms, flip), o...  1.34 us
  transfers between devices with their start and end apart: 16, of which 6 were waited for; matrix products, arithmetic and copies ran while one was open for 3% of the time, Pallas kernels for 24%

profile of v13, /device:TPU:0, one launch (start us, length us, event | category | flops | bytes accessed | tf_op | source)
XLA Modules:
  0.0 42.9 jit_solution(4662338615683661570)
XLA Ops:
  0.6 0.5 %collective-permute-start = (s32[1]{0:T(128)}, s32[1]{0:T(128)}, u32[]{:S(2)}, u32[]{:S(2)}) collective-permute-start(s32[1]{0:T(128)} %param.14), channel_id=1, source_target_pairs={{0,1},{1,0},{2,3},{3,2},{4,5},{5,4},{6,7},{7,6},{8,9},{9,8},{10,11... | collective-permute-start | bytes 20 | tf_op jit(solution)/shard_map/ppermute | solution.py:290
  1.1 1.3 %mask.1.rows_ref.refs_0_ = bf16[3,4,128,128]{3,2,1,0:T(8,128)(2,1)S(1)} custom-call(s32[3,4]{1,0:T(4,128)} %mask_hbm.1, bf16[3,4,128,128]{3,2,1,0:T(8,128)(2,1)} %rows_hbm.1), custom_call_target="tpu_custom_call" | custom-call | flops 2000000000 | bytes 8000000 | tf_op jit(solution)/shard_map/mask/pallas_call | solution.py:326
  2.5 0.0 copy-start
  2.5 0.0 copy-start.1
  2.5 0.0 collective-permute-done
  2.5 2.6 %collective-permute-start.2 = (bf16[3,4,128,128]{3,2,1,0:T(8,128)(2,1)S(1)}, bf16[3,4,128,128]{3,2,1,0:T(8,128)(2,1)S(1)}, u32[]{:S(2)}, u32[]{:S(2)}) collective-permute-start(bf16[3,4,128,128]{3,2,1,0:T(8,128)(2,1)S(1)} %mask.1.rows_ref.refs_0_), channel_id=1, source_target_pairs={{0,4},{1,3},{2,6},{3,1},{4,0},{5,7},{6,2},{7,5},{8,12},{9,11},{10,... | collective-permute-start | bytes 1179656 | tf_op jit(solution)/shard_map/ppermute | solution.py:295
  5.7 0.7 %pad_add_fusion = s32[2]{0:T(128)S(1)} fusion(s32[1]{0:T(128)} %collective-permute-done, s32[1]{0:T(128)S(6)} %copy.15.start_ref), kind=kLoop, calls=%fused_computation.1 | loop fusion | flops 2 | bytes 16 | tf_op jit(solution)/shard_map/concatenate | solution.py:396
  6.4 1.5 %collective-permute-start.1 = (s32[2]{0:T(128)S(1)}, s32[2]{0:T(128)S(1)}, u32[]{:S(2)}, u32[]{:S(2)}) collective-permute-start(s32[2]{0:T(128)S(1)} %pad_add_fusion), channel_id=1, source_target_pairs={{0,2},{1,5},{2,0},{3,7},{4,6},{5,1},{6,4},{7,3},{8,10},{9,13},{10,... | collective-permute-start | bytes 32 | tf_op jit(solution)/shard_map/ppermute | solution.py:295
  7.9 2.1 %collective-permute-done.1.starts_ref = s32[2]{0:T(128)S(1)} collective-permute-done((s32[2]{0:T(128)S(1)}, s32[2]{0:T(128)S(1)}, u32[]{:S(2)}, u32[]{:S(2)}) %collective-permute-start.1) | collective-permute-done | bytes 40 | tf_op jit(solution)/shard_map/ppermute | solution.py:295
  10.1 0.6 %select.2 = bf16[2,4,128,128]{3,2,1,0:T(8,128)(2,1)S(1)} custom-call(s32[2]{0:T(128)S(1)} %collective-permute-done.1.starts_ref, bf16[3,4,128,128]{3,2,1,0:T(8,128)(2,1)S(1)} %mask.1.rows_ref.refs_0_), custom_call_target="tpu_custom_call" | custom-call | tf_op jit(solution)/shard_map/select/pallas_call | solution.py:383
  10.7 1.6 %collective-permute-start.3 = (bf16[2,4,128,128]{3,2,1,0:T(8,128)(2,1)S(1)}, bf16[2,4,128,128]{3,2,1,0:T(8,128)(2,1)S(1)}, u32[]{:S(2)}, u32[]{:S(2)}) collective-permute-start(bf16[2,4,128,128]{3,2,1,0:T(8,128)(2,1)S(1)} %select.2), channel_id=1, source_target_pairs={{0,2},{1,5},{2,0},{3,7},{4,6},{5,1},{6,4},{7,3},{8,10},{9,13},{10,... | collective-permute-start | bytes 786440 | tf_op jit(solution)/shard_map/ppermute | solution.py:295
  12.2 0.0 collective-permute-done.2.rows_ref.refs_2_
  12.2 0.6 %select.3.after_hbm = bf16[2,4,128,128]{3,2,1,0:T(8,128)(2,1)S(1)} custom-call(s32[2]{0:T(128)S(1)} %collective-permute-done.1.starts_ref, bf16[3,4,128,128]{3,2,1,0:T(8,128)(2,1)S(1)} %collective-permute-done.2.rows_ref.refs_2_), custom_call_target="tpu_custom_call" | custom-call | tf_op jit(solution)/shard_map/select/pallas_call | solution.py:383
  12.8 0.7 %collective-permute-start.7 = (bf16[2,4,128,128]{3,2,1,0:T(8,128)(2,1)S(1)}, bf16[2,4,128,128]{3,2,1,0:T(8,128)(2,1)S(1)}, u32[]{:S(2)}, u32[]{:S(2)}) collective-permute-start(bf16[2,4,128,128]{3,2,1,0:T(8,128)(2,1)S(1)} %select.3.after_hbm), channel_id=1, source_target_pairs={{0,2},{1,5},{2,0},{3,7},{4,6},{5,1},{6,4},{7,3},{8,10},{9,13},{10,... | collective-permute-start | bytes 786440 | tf_op jit(solution)/shard_map/ppermute | solution.py:295
  13.5 0.0 collective-permute-start.5
  13.5 0.5 %collective-permute-start.4 = (bf16[3,4,128,128]{3,2,1,0:T(8,128)(2,1)S(1)}, bf16[3,4,128,128]{3,2,1,0:T(8,128)(2,1)S(1)}, u32[]{:S(2)}, u32[]{:S(2)}) collective-permute-start(bf16[3,4,128,128]{3,2,1,0:T(8,128)(2,1)S(1)} %mask.1.rows_ref.refs_0_), channel_id=1, source_target_pairs={{0,1},{1,0},{2,3},{3,2},{4,5},{5,4},{6,7},{7,6},{8,9},{9,8},{10,11... | collective-permute-start | bytes 1179656 | tf_op jit(solution)/shard_map/ppermute | solution.py:290
  14.0 0.0 copy-done
  14.0 0.0 copy-done.1
  14.0 0.0 copy-start.2
  14.0 3.7 %turn.1 = (bf16[12,4,128,256]{3,2,1,0:T(8,128)(2,1)S(1)}, f32[12,6,256]{2,1,0:T(8,128)S(1)}, bf16[72,32,256]{2,1,0:T(8,128)(2,1)S(1)}, s32[1,128]{1,0:T(1,128)S(1)}, f32[12,256]{1,0:T(8,128)S(1)}) custom-call(bf16[2,4,128,128]{3,2,1,0:T(8,128)(2,1)S(1)} %select.3.after_hbm, s32[6,12]{1,0:T(8,128)S(1)} %bitcast.6, s32[1,12]{1,0:T(1,128)S(1)} %copy-done.1, ...), custom_call_target="tpu_custom_call" | custom-call | flops 2000000000 | bytes 8000000 | tf_op jit(solution)/shard_map/turn/pallas_call | solution.py:361
  17.7 0.0 collective-permute-done.3.refs_4_
  17.7 0.1 collective-permute-start.6
  17.8 2.1 %collective-permute-done.7.refs_6_ = bf16[2,4,128,128]{3,2,1,0:T(8,128)(2,1)S(1)} collective-permute-done((bf16[2,4,128,128]{3,2,1,0:T(8,128)(2,1)S(1)}, bf16[2,4,128,128]{3,2,1,0:T(8,128)(2,1)S(1)}, u32[]{:S(2)}, u32[]{:S(2)}) %collective-permute-start.7) | collective-permute-done | bytes 262176 | tf_op jit(solution)/shard_map/ppermute | solution.py:295
  19.9 0.0 collective-permute-start.8
  19.9 0.0 collective-permute-done.6.refs_5_
  19.9 0.0 collective-permute-done.4.refs_1_
  19.9 0.0 collective-permute-done.5.refs_3_
  19.9 1.5 %collective-permute-done.8.refs_7_ = bf16[2,4,128,128]{3,2,1,0:T(8,128)(2,1)S(1)} collective-permute-done((bf16[2,4,128,128]{3,2,1,0:T(8,128)(2,1)S(1)}, bf16[2,4,128,128]{3,2,1,0:T(8,128)(2,1)S(1)}, u32[]{:S(2)}, u32[]{:S(2)}) %collective-permute-start.8) | collective-permute-done | bytes 262176 | tf_op jit(solution)/shard_map/ppermute | solution.py:290
  21.4 0.0 copy-done.2
  21.4 3.2 %density.1 = (f32[12,256]{1,0:T(8,128)S(1)}, f32[32,128]{1,0:T(8,128)S(1)}) custom-call(s32[1]{0:T(128)S(6)} %copy.15.start_ref, s32[1,12]{1,0:T(1,128)S(1)} %copy-done.2, s32[1,128]{1,0:T(1,128)S(1)} %get-tuple-element.35.atom_ref, f32[12,256]{1,0:T(8,128)S(1)} %get-tuple-element.36.alive_ref, bf16[12,4,128,256]{3,2,1,0:T(8,128)(2,1)S(1)} %get-tuple-element.38.phit_ref, ...), custom_call_target="tpu_custom_call" | custom-call | flops 2000000000 | bytes 6000000 | tf_op jit(solution)/shard_map/density/pallas_call | solution.py:410
  24.6 0.2 collective-permute-start.9
  24.8 0.6 %copy.14 = f32[12,256]{1,0:T(8,128)} copy(f32[12,256]{1,0:T(8,128)S(1)} %get-tuple-element.61) | data formatting | bytes 24576
  25.4 0.4 %collective-permute-done.9 = f32[32,128]{1,0:T(8,128)S(1)} collective-permute-done((f32[32,128]{1,0:T(8,128)S(1)}, f32[32,128]{1,0:T(8,128)S(1)}, u32[]{:S(2)}, u32[]{:S(2)}) %collective-permute-start.9) | collective-permute-done | bytes 16416 | tf_op jit(solution)/shard_map/ppermute | solution.py:290
  25.9 1.4 %collective-permute-start.12 = (f32[2,32,128]{2,1,0:T(8,128)S(1)}, f32[2,32,128]{2,1,0:T(8,128)S(1)}, u32[]{:S(2)}, u32[]{:S(2)}) collective-permute-start(f32[2,32,128]{2,1,0:T(8,128)S(1)} %pad_maximum_fusion.after_hbm.refs_0_), channel_id=1, source_target_pairs={{0,6},{1,7},{2,4},{3,5},{4,2},{5,3},{6,0},{7,1},{8,14},{9,15},{10,... | collective-permute-start | bytes 98312 | tf_op jit(solution)/shard_map/ppermute | solution.py:290
  27.3 1.5 %collective-permute-start.11 = (f32[2,32,128]{2,1,0:T(8,128)S(1)}, f32[2,32,128]{2,1,0:T(8,128)S(1)}, u32[]{:S(2)}, u32[]{:S(2)}) collective-permute-start(f32[2,32,128]{2,1,0:T(8,128)S(1)} %pad_maximum_fusion.after_hbm.refs_0_), channel_id=1, source_target_pairs={{0,4},{1,5},{2,6},{3,7},{4,0},{5,1},{6,2},{7,3},{8,12},{9,13},{10,... | collective-permute-start | bytes 98312 | tf_op jit(solution)/shard_map/ppermute | solution.py:290
  28.8 0.5 %collective-permute-start.10 = (f32[2,32,128]{2,1,0:T(8,128)S(1)}, f32[2,32,128]{2,1,0:T(8,128)S(1)}, u32[]{:S(2)}, u32[]{:S(2)}) collective-permute-start(f32[2,32,128]{2,1,0:T(8,128)S(1)} %pad_maximum_fusion.after_hbm.refs_0_), channel_id=1, source_target_pairs={{0,2},{1,3},{2,0},{3,1},{4,6},{5,7},{6,4},{7,5},{8,10},{9,11},{10,... | collective-permute-start | bytes 98312 | tf_op jit(solution)/shard_map/ppermute | solution.py:290
  29.4 2.1 %field.2.low_ref = f32[36,25,256]{2,1,0:T(8,128)S(1)} custom-call(f32[2,32,128]{2,1,0:T(8,128)S(1)} %pad_maximum_fusion.after_hbm.refs_0_, f32[12,256]{1,0:T(8,128)S(1)} %get-tuple-element.36.alive_ref, f32[16,25]{1,0:T(8,128)} %bitcast.8, f32[12,6,256]{2,1,0:T(8,128)} %radius_hbm.3, bf16[12,6,25,256]{3,2,1,0:T(8,128)(2,1)} %harm_hbm.5), custom_call_target="tpu_custom_call" | custom-call | flops 2000000000 | bytes 8000000 | tf_op jit(solution)/shard_map/field/pallas_call | solution.py:344
  31.4 0.0 collective-permute-done.12.refs_3_
  31.4 0.0 collective-permute-done.11.refs_2_
  31.5 1.3 %collective-permute-done.10.refs_1_ = f32[2,32,128]{2,1,0:T(8,128)S(1)} collective-permute-done((f32[2,32,128]{2,1,0:T(8,128)S(1)}, f32[2,32,128]{2,1,0:T(8,128)S(1)}, u32[]{:S(2)}, u32[]{:S(2)}) %collective-permute-start.10) | collective-permute-done | bytes 32800 | tf_op jit(solution)/shard_map/ppermute | solution.py:290
  32.7 0.4 scatter.1
  33.1 3.7 %collective-permute-start.13 = (f32[32,256]{1,0:T(8,128)S(1)}, f32[32,256]{1,0:T(8,128)S(1)}, u32[]{:S(2)}, u32[]{:S(2)}) collective-permute-start(f32[32,256]{1,0:T(8,128)S(1)} %get-tuple-element.50), channel_id=1, source_target_pairs={{0,24},{8,16},{16,8},{24,0},{1,25},{9,17},{17,9},{25,1},{2,26},{10... | collective-permute-start | bytes 98312 | tf_op jit(solution)/shard_map/ppermute | solution.py:290
  36.8 0.0 collective-permute-start.14
  36.8 0.8 %collective-permute-start.15 = (f32[32,256]{1,0:T(8,128)S(1)}, f32[32,256]{1,0:T(8,128)S(1)}, u32[]{:S(2)}, u32[]{:S(2)}) collective-permute-start(f32[32,256]{1,0:T(8,128)S(1)} %get-tuple-element.52), channel_id=1, source_target_pairs={{0,8},{8,0},{16,24},{24,16},{1,9},{9,1},{17,25},{25,17},{2,10},{10... | collective-permute-start | bytes 98312 | tf_op jit(solution)/shard_map/ppermute | solution.py:290
  37.6 2.1 %field.3.high_ref = f32[36,25,256]{2,1,0:T(8,128)S(1)} custom-call(f32[32,384]{1,0:T(8,128)S(1)} %get-tuple-element.49.after_hbm.own_ref, f32[12,256]{1,0:T(8,128)S(1)} %get-tuple-element.36.alive_ref, f32[16,25]{1,0:T(8,128)} %bitcast.9, f32[12,6,256]{2,1,0:T(8,128)} %radius_hbm.3, bf16[12,6,25,256]{3,2,1,0:T(8,128)(2,1)} %harm_hbm.5), custom_call_target="tpu_custom_call" | custom-call | flops 2000000000 | bytes 8000000 | tf_op jit(solution)/shard_map/field/pallas_call | solution.py:344
  39.6 0.0 collective-permute-done.13.near_b_ref
  39.6 1.9 %collective-permute-done.14.fa_ref.fb_ref = f32[32,256]{1,0:T(8,128)S(1)} collective-permute-done((f32[32,256]{1,0:T(8,128)S(1)}, f32[32,256]{1,0:T(8,128)S(1)}, u32[]{:S(2)}, u32[]{:S(2)}) %collective-permute-start.14) | collective-permute-done | bytes 32800 | tf_op jit(solution)/shard_map/ppermute | solution.py:290
  41.6 0.0 collective-permute-done.15.near_a_ref
  41.6 1.3 %potential.1 = (f32[16,25]{1,0:T(8,128)}, f32[12,256]{1,0:T(8,128)}) custom-call(f32[32,384]{1,0:T(8,128)S(1)} %get-tuple-element.49.after_hbm.own_ref, f32[32,256]{1,0:T(8,128)S(1)} %collective-permute-done.13.near_b_ref, f32[32,256]{1,0:T(8,128)S(1)} %collective-permute-done.14.fa_ref.fb_ref, f32[32,256]{1,0:T(8,128)S(1)} %collective-permute-done.14.fa_ref.fb_ref, ...), custom_call_target="tpu_custom_call" | custom-call | tf_op jit(solution)/shard_map/potential/pallas_call | solution.py:461
  (1 shorter events, 0.0 us)
Async XLA Ops:
  0.6 1.9 %collective-permute-start = (s32[1]{0:T(128)}, s32[1]{0:T(128)}, u32[]{:S(2)}, u32[]{:S(2)}) collective-permute-start(s32[1]{0:T(128)} %param.14), channel_id=1, source_target_pairs={{0,1},{1,0},{2,3},{3,2},{4,5},{5,4},{6,7},{7,6},{8,9},{9,8},{10,11... | collective-permute-start | bytes 20 | tf_op jit(solution)/shard_map/ppermute | solution.py:290
  2.5 11.6 %copy-start = (s32[12,6]{0,1:T(8,128)S(1)}, s32[12,6]{0,1:T(8,128)}, u32[]{:S(2)}) copy-start(s32[12,6]{0,1:T(8,128)} %param.17) | copy-start | bytes 868
  2.5 11.6 %copy-start.1 = (s32[1,12]{1,0:T(1,128)S(1)}, s32[1,12]{1,0:T(1,128)}, u32[]{:S(2)}) copy-start(s32[1,12]{1,0:T(1,128)} %size_ref.1) | copy-start | bytes 148
  2.5 9.7 %collective-permute-start.2 = (bf16[3,4,128,128]{3,2,1,0:T(8,128)(2,1)S(1)}, bf16[3,4,128,128]{3,2,1,0:T(8,128)(2,1)S(1)}, u32[]{:S(2)}, u32[]{:S(2)}) collective-permute-start(bf16[3,4,128,128]{3,2,1,0:T(8,128)(2,1)S(1)} %mask.1.rows_ref.refs_0_), channel_id=1, source_target_pairs={{0,4},{1,3},{2,6},{3,1},{4,0},{5,7},{6,2},{7,5},{8,12},{9,11},{10,... | collective-permute-start | bytes 1179656 | tf_op jit(solution)/shard_map/ppermute | solution.py:295
  6.4 3.6 %collective-permute-start.1 = (s32[2]{0:T(128)S(1)}, s32[2]{0:T(128)S(1)}, u32[]{:S(2)}, u32[]{:S(2)}) collective-permute-start(s32[2]{0:T(128)S(1)} %pad_add_fusion), channel_id=1, source_target_pairs={{0,2},{1,5},{2,0},{3,7},{4,6},{5,1},{6,4},{7,3},{8,10},{9,13},{10,... | collective-permute-start | bytes 32 | tf_op jit(solution)/shard_map/ppermute | solution.py:295
  10.7 7.0 %collective-permute-start.3 = (bf16[2,4,128,128]{3,2,1,0:T(8,128)(2,1)S(1)}, bf16[2,4,128,128]{3,2,1,0:T(8,128)(2,1)S(1)}, u32[]{:S(2)}, u32[]{:S(2)}) collective-permute-start(bf16[2,4,128,128]{3,2,1,0:T(8,128)(2,1)S(1)} %select.2), channel_id=1, source_target_pairs={{0,2},{1,5},{2,0},{3,7},{4,6},{5,1},{6,4},{7,3},{8,10},{9,13},{10,... | collective-permute-start | bytes 786440 | tf_op jit(solution)/shard_map/ppermute | solution.py:295
  12.8 7.1 %collective-permute-start.7 = (bf16[2,4,128,128]{3,2,1,0:T(8,128)(2,1)S(1)}, bf16[2,4,128,128]{3,2,1,0:T(8,128)(2,1)S(1)}, u32[]{:S(2)}, u32[]{:S(2)}) collective-permute-start(bf16[2,4,128,128]{3,2,1,0:T(8,128)(2,1)S(1)} %select.3.after_hbm), channel_id=1, source_target_pairs={{0,2},{1,5},{2,0},{3,7},{4,6},{5,1},{6,4},{7,3},{8,10},{9,13},{10,... | collective-permute-start | bytes 786440 | tf_op jit(solution)/shard_map/ppermute | solution.py:295
  13.5 6.4 %collective-permute-start.5 = (bf16[3,4,128,128]{3,2,1,0:T(8,128)(2,1)S(1)}, bf16[3,4,128,128]{3,2,1,0:T(8,128)(2,1)S(1)}, u32[]{:S(2)}, u32[]{:S(2)}) collective-permute-start(bf16[3,4,128,128]{3,2,1,0:T(8,128)(2,1)S(1)} %collective-permute-done.2.rows_ref.refs_2_), channel_id=1, source_target_pairs={{0,1},{1,0},{2,3},{3,2},{4,5},{5,4},{6,7},{7,6},{8,9},{9,8},{10,11... | collective-permute-start | bytes 1179656 | tf_op jit(solution)/shard_map/ppermute | solution.py:290
  13.5 6.4 %collective-permute-start.4 = (bf16[3,4,128,128]{3,2,1,0:T(8,128)(2,1)S(1)}, bf16[3,4,128,128]{3,2,1,0:T(8,128)(2,1)S(1)}, u32[]{:S(2)}, u32[]{:S(2)}) collective-permute-start(bf16[3,4,128,128]{3,2,1,0:T(8,128)(2,1)S(1)} %mask.1.rows_ref.refs_0_), channel_id=1, source_target_pairs={{0,1},{1,0},{2,3},{3,2},{4,5},{5,4},{6,7},{7,6},{8,9},{9,8},{10,11... | collective-permute-start | bytes 1179656 | tf_op jit(solution)/shard_map/ppermute | solution.py:290
  14.0 7.4 %copy-start.2 = (s32[1,12]{1,0:T(1,128)S(1)}, s32[1,12]{1,0:T(1,128)}, u32[]{:S(2)}) copy-start(s32[1,12]{1,0:T(1,128)} %offset_ref.1) | copy-start | bytes 148
  17.7 2.2 %collective-permute-start.6 = (bf16[2,4,128,128]{3,2,1,0:T(8,128)(2,1)S(1)}, bf16[2,4,128,128]{3,2,1,0:T(8,128)(2,1)S(1)}, u32[]{:S(2)}, u32[]{:S(2)}) collective-permute-start(bf16[2,4,128,128]{3,2,1,0:T(8,128)(2,1)S(1)} %collective-permute-done.3.refs_4_), channel_id=1, source_target_pairs={{0,1},{1,0},{2,3},{3,2},{4,5},{5,4},{6,7},{7,6},{8,9},{9,8},{10,11... | collective-permute-start | bytes 786440 | tf_op jit(solution)/shard_map/ppermute | solution.py:290
  19.9 1.5 %collective-permute-start.8 = (bf16[2,4,128,128]{3,2,1,0:T(8,128)(2,1)S(1)}, bf16[2,4,128,128]{3,2,1,0:T(8,128)(2,1)S(1)}, u32[]{:S(2)}, u32[]{:S(2)}) collective-permute-start(bf16[2,4,128,128]{3,2,1,0:T(8,128)(2,1)S(1)} %collective-permute-done.7.refs_6_), channel_id=1, source_target_pairs={{0,1},{1,0},{2,3},{3,2},{4,5},{5,4},{6,7},{7,6},{8,9},{9,8},{10,11... | collective-permute-start | bytes 786440 | tf_op jit(solution)/shard_map/ppermute | solution.py:290
  24.6 1.2 %collective-permute-start.9 = (f32[32,128]{1,0:T(8,128)S(1)}, f32[32,128]{1,0:T(8,128)S(1)}, u32[]{:S(2)}, u32[]{:S(2)}) collective-permute-start(f32[32,128]{1,0:T(8,128)S(1)} %get-tuple-element.44), channel_id=1, source_target_pairs={{0,1},{1,0},{2,3},{3,2},{4,5},{5,4},{6,7},{7,6},{8,9},{9,8},{10,11... | collective-permute-start | bytes 49160 | tf_op jit(solution)/shard_map/ppermute | solution.py:290
  25.9 5.6 %collective-permute-start.12 = (f32[2,32,128]{2,1,0:T(8,128)S(1)}, f32[2,32,128]{2,1,0:T(8,128)S(1)}, u32[]{:S(2)}, u32[]{:S(2)}) collective-permute-start(f32[2,32,128]{2,1,0:T(8,128)S(1)} %pad_maximum_fusion.after_hbm.refs_0_), channel_id=1, source_target_pairs={{0,6},{1,7},{2,4},{3,5},{4,2},{5,3},{6,0},{7,1},{8,14},{9,15},{10,... | collective-permute-start | bytes 98312 | tf_op jit(solution)/shard_map/ppermute | solution.py:290
  27.3 4.2 %collective-permute-start.11 = (f32[2,32,128]{2,1,0:T(8,128)S(1)}, f32[2,32,128]{2,1,0:T(8,128)S(1)}, u32[]{:S(2)}, u32[]{:S(2)}) collective-permute-start(f32[2,32,128]{2,1,0:T(8,128)S(1)} %pad_maximum_fusion.after_hbm.refs_0_), channel_id=1, source_target_pairs={{0,4},{1,5},{2,6},{3,7},{4,0},{5,1},{6,2},{7,3},{8,12},{9,13},{10,... | collective-permute-start | bytes 98312 | tf_op jit(solution)/shard_map/ppermute | solution.py:290
  28.8 3.9 %collective-permute-start.10 = (f32[2,32,128]{2,1,0:T(8,128)S(1)}, f32[2,32,128]{2,1,0:T(8,128)S(1)}, u32[]{:S(2)}, u32[]{:S(2)}) collective-permute-start(f32[2,32,128]{2,1,0:T(8,128)S(1)} %pad_maximum_fusion.after_hbm.refs_0_), channel_id=1, source_target_pairs={{0,2},{1,3},{2,0},{3,1},{4,6},{5,7},{6,4},{7,5},{8,10},{9,11},{10,... | collective-permute-start | bytes 98312 | tf_op jit(solution)/shard_map/ppermute | solution.py:290
  33.1 6.5 %collective-permute-start.13 = (f32[32,256]{1,0:T(8,128)S(1)}, f32[32,256]{1,0:T(8,128)S(1)}, u32[]{:S(2)}, u32[]{:S(2)}) collective-permute-start(f32[32,256]{1,0:T(8,128)S(1)} %get-tuple-element.50), channel_id=1, source_target_pairs={{0,24},{8,16},{16,8},{24,0},{1,25},{9,17},{17,9},{25,1},{2,26},{10... | collective-permute-start | bytes 98312 | tf_op jit(solution)/shard_map/ppermute | solution.py:290
  36.8 4.8 %collective-permute-start.14 = (f32[32,256]{1,0:T(8,128)S(1)}, f32[32,256]{1,0:T(8,128)S(1)}, u32[]{:S(2)}, u32[]{:S(2)}) collective-permute-start(f32[32,256]{1,0:T(8,128)S(1)} %get-tuple-element.51), channel_id=1, source_target_pairs={{0,16},{8,24},{16,0},{24,8},{1,17},{9,25},{17,1},{25,9},{2,18},{10... | collective-permute-start | bytes 98312 | tf_op jit(solution)/shard_map/ppermute | solution.py:290
  36.8 4.8 %collective-permute-start.15 = (f32[32,256]{1,0:T(8,128)S(1)}, f32[32,256]{1,0:T(8,128)S(1)}, u32[]{:S(2)}, u32[]{:S(2)}) collective-permute-start(f32[32,256]{1,0:T(8,128)S(1)} %get-tuple-element.52), channel_id=1, source_target_pairs={{0,8},{8,0},{16,24},{24,16},{1,9},{9,1},{17,25},{25,17},{2,10},{10... | collective-permute-start | bytes 98312 | tf_op jit(solution)/shard_map/ppermute | solution.py:290

commit v14 on v13

--- a/solution.py
+++ b/solution.py
@@ -108,8 +108,8 @@
 
 
 def turn_kernel(
-    after_hbm, near_ref, size_ref, basis_hbm, part_hbm, harm_hbm,
-    phit_ref, part_ref, hpad_ref, atom_ref, alive_ref, basis, harm_ref, sems,
+    after_hbm, near_ref, size_ref, start_ref, offset_ref, basis_hbm, part_hbm, harm_hbm,
+    phit_ref, part_ref, hpad_ref, atom_ref, alive_ref, place_ref, basis, harm_ref, sems,
 ):
     batches, near_blocks = basis.shape[:2]
     near, comps, points = harm_ref.shape[1:]
@@ -128,6 +128,10 @@
         for i in range(near):
             atom = jnp.where(lane == b * SLOT + i, near_ref[i, b], atom)
     atom_ref[...] = atom
+    place = jnp.full(place_ref.shape, start_ref[0], jnp.int32)
+    for b in range(batches):
+        place = jnp.where(lane == b + 1, offset_ref[0, b], place)
+    place_ref[...] = place
     point = lax.broadcasted_iota(jnp.int32, (1, points), 1)
     for b in range(batches):
         alive_ref[b : b + 1, :] = (point < size_ref[0, b]).astype(jnp.float32)
@@ -154,7 +158,7 @@
 
 
 def density_kernel(
-    start_ref, offset_ref, atom_ref, alive_ref, phit_ref, part_ref, hpad_ref, *refs
+    place_ref, atom_ref, alive_ref, phit_ref, part_ref, hpad_ref, *refs
 ):
     dens_ref, terms_ref, window_ref, w_ref = refs[-4:]
     pieces = refs[:-4]
@@ -172,13 +176,13 @@
         held = [(pieces[0].at[owner], owner, None) for owner in range(owners)]
     stored = held[0][0].shape[0]
     for piece, owner, at in held:
-        ahead, row = chosen_row(owner, start_ref[0], owners, stored)
+        ahead, row = chosen_row(owner, place_ref[0, 0], owners, stored)
         window_ref[ahead] = piece[row if at is None else at]
     w_ref[...] = jnp.zeros(w_ref.shape, w_ref.dtype)
     zero = jnp.zeros((width, width), jnp.bfloat16)
 
     def body(b, carry):
-        first = offset_ref[0, b]
+        first = place_ref[0, b + 1]
         left = []
         for j in range(near_blocks):
             row = [
@@ -215,63 +219,46 @@
     terms_ref[...] = jnp.where(row_id == comps, atom_ref[...].astype(jnp.float32), result)
 
 
-def scatter_kernel(comps, atoms, flip, *refs):
-    own, near_a, near_b, far = refs[-4:]
-    pieces = [group.at[m] for group in refs[:-4] for m in range(group.shape[0])]
+def scatter_kernel(comps, atoms, steps, *refs):
+    pieces, sums = refs[:-1], refs[-1]
     row_id = lax.broadcasted_iota(jnp.int32, (3 * atoms, LANES), 0)
+    region = lax.axis_index("region")
     total = jnp.zeros((3 * ROWS, 3 * atoms), jnp.float32)
-    for m in range(0, len(pieces), 2):
+    for n in range(0, len(pieces), 2):
         left, right = [], []
-        for values in (pieces[m][...], pieces[m + 1][...]):
+        for piece, step in zip(pieces[n : n + 2], steps[n : n + 2]):
+            values = piece[...]
             chosen = values[comps : comps + 1, :].astype(jnp.int32)
+            if step:
+                away = lax.rem(lax.bitwise_xor(region, step) - region + 4, 4)
+                chosen = lax.rem(chosen + away * atoms, 4 * atoms)
             right.append((row_id == chosen).astype(jnp.float32).astype(jnp.bfloat16))
             left.append(jnp.concatenate(split3(values), axis=0))
         total = total + dot(jnp.concatenate(left, axis=1), jnp.concatenate(right, axis=1), NT)
-    sums = total[:ROWS] + total[ROWS : 2 * ROWS] + total[2 * ROWS :]
-    own[...] = sums
-    ahead, back = sums[:, atoms:], sums[:, : 2 * atoms]
-    if flip:
-        odd = lax.rem(lax.axis_index("region"), 2) == 1
-        near_a[...] = jnp.where(odd, back, ahead)
-        near_b[...] = jnp.where(odd, ahead, back)
-    else:
-        near_a[...] = ahead
-        near_b[...] = back
-    far[:, :atoms] = sums[:, :atoms]
-    far[:, atoms:] = sums[:, 2 * atoms :]
-
-
-def potential_kernel(
-    comps, atoms, flip, own_ref, near_b_ref, fa_ref, fb_ref, near_a_ref, atom_ref,
-    low_ref, high_ref, mom_ref, pot_ref,
-):
+    sums[...] = total[:ROWS] + total[ROWS : 2 * ROWS] + total[2 * ROWS :]
+
+
+def potential_kernel(comps, atoms, atom_ref, low_ref, high_ref, *refs):
+    mom_ref, pot_ref = refs[-2:]
     batches, points = pot_ref.shape
     near = 2 * low_ref.shape[0] // batches
     fields = [ref.at[n] for ref in (low_ref, high_ref) for n in range(ref.shape[0])]
-    own = own_ref[...]
-    near_a, near_b = near_a_ref[...], near_b_ref[...]
-    if flip:
-        odd = lax.rem(lax.axis_index("region"), 2) == 1
-        low = jnp.where(odd, near_a, near_b)
-        high = jnp.where(odd, near_b, near_a)
-    else:
-        low, high = near_a, near_b
-    before = fa_ref[:, atoms:] + low[:, :atoms] + own[:, :atoms]
-    here = low[:, atoms:] + own[:, atoms : 2 * atoms] + high[:, :atoms]
-    after = own[:, 2 * atoms :] + high[:, atoms:] + fb_ref[:, :atoms]
+    moments = refs[0][...]
+    for ref in refs[1:-2]:
+        moments = moments + ref[...]
+    parts = jnp.concatenate(split3(moments), axis=0)
 
     mine = mom_ref.shape[0]
     want = lax.broadcasted_iota(jnp.int32, (mine, atoms), 0) + lax.axis_index("dev") * mine
     keep = want == lax.broadcasted_iota(jnp.int32, (mine, atoms), 1)
     keep = keep.astype(jnp.float32).astype(jnp.bfloat16)
-    taken = dot(keep, jnp.concatenate(split3(here), axis=0), NT)
+    taken = dot(keep, parts[:, atoms : 2 * atoms], NT)
     taken = taken[:, :ROWS] + taken[:, ROWS : 2 * ROWS] + taken[:, 2 * ROWS :]
     mom_ref[...] = taken[:, :comps]
 
-    moments = jnp.concatenate([before, here, after], axis=1)
     row_id = lax.broadcasted_iota(jnp.int32, (3 * atoms, LANES), 0)
     pick = (row_id == atom_ref[...]).astype(jnp.float32).astype(jnp.bfloat16)
-    got = dot(jnp.concatenate(split3(moments), axis=0), pick)
+    got = dot(parts, pick)
     chosen = got[:ROWS] + got[ROWS : 2 * ROWS] + got[2 * ROWS :]
     chosen = chosen[:comps]
     for b in range(batches):
@@ -366,9 +353,10 @@
                 pltpu.VMEM((batches * near, ROWS, points), bf16),
                 pltpu.VMEM((1, LANES), jnp.int32),
                 pltpu.VMEM((batches, points), f32),
+                pltpu.VMEM((1, LANES), jnp.int32),
             ),
-            in_specs=[HBM, SMEM, SMEM] + [HBM] * 3,
-            out_specs=(VMEM,) * 5,
+            in_specs=[HBM] + [SMEM] * 4 + [HBM] * 3,
+            out_specs=(VMEM,) * 6,
             scratch_shapes=[
                 pltpu.VMEM(basis_values.shape, bf16),
                 pltpu.VMEM(harmonics.shape, bf16),
@@ -377,7 +365,10 @@
             compiler_params=WIDE,
             cost_estimate=work,
             name="turn",
-        )(after, atom_near.T, batch_sizes, *held_in_hbm(basis_values, partition, harmonics))
+        )(
+            after, atom_near.T, batch_sizes, window_start, batch_offsets,
+            *held_in_hbm(basis_values, partition, harmonics),
+        )
 
     def selected(even, odd, starts, rows):
         return pl.pallas_call(
@@ -399,12 +390,12 @@
         first, later, _ = lax.optimization_barrier((first, masked, chosen))
         chosen = selected(4, 2, starts, first)
         third = turned(chosen, 2, 4)
-        phit, weights, hpad, atom_rows, alive = turned_basis(chosen)
+        phit, weights, hpad, atom_rows, alive, places = turned_basis(chosen)
         second, phit = lax.optimization_barrier((second, phit))
         sent = (later, first, second, third)
         pieces = [piece for value in sent for piece in (value, crossed(value, "dev", 1))]
     else:
-        phit, weights, hpad, atom_rows, alive = turned_basis(masked)
+        phit, weights, hpad, atom_rows, alive, places = turned_basis(masked)
         pieces = [lax.all_gather(masked, "dev", axis=0)]
 
     density, terms = pl.pallas_call(
@@ -413,7 +404,7 @@
             pltpu.VMEM((batches, points), f32),
             pltpu.VMEM((ROWS, LANES), f32),
         ),
-        in_specs=[SMEM] * 2 + [VMEM] * (5 + len(pieces)),
+        in_specs=[SMEM] + [VMEM] * (5 + len(pieces)),
         out_specs=(VMEM, VMEM),
         scratch_shapes=[
             pltpu.VMEM((dev_count, band, width, width), bf16),
@@ -423,52 +414,52 @@
         cost_estimate=pl.CostEstimate(flops=2_000_000_000, bytes_accessed=6_000_000, transcendentals=0),
         name="density",
     )(
-        window_start, batch_offsets, atom_rows, alive, phit, weights, hpad,
+        places, atom_rows, alive, phit, weights, hpad,
         *pieces,
     )
 
-    if dev_count == 8:
-        both = jnp.stack([terms, crossed(terms, "dev", 1)])
-        groups = [both] + [crossed(both, "dev", m) for m in (2, 4, 6)]
+    def scattered(steps, pieces):
+        return pl.pallas_call(
+            functools.partial(scatter_kernel, comps, atoms, steps),
+            out_shape=jax.ShapeDtypeStruct((ROWS, 3 * atoms), f32),
+            in_specs=[VMEM] * len(pieces),
+            out_specs=VMEM,
+            compiler_params=PARAMS,
+            name="scatter",
+        )(*pieces)
+
+    g_low = field(0, terms)
+    if dev_count == 8 and region_count == 4:
+        steps = (1, 2, 3)
+        others = [crossed(terms, "region", m) for m in steps]
+        *others, g_low = lax.optimization_barrier((*others, g_low))
+        sums = scattered((0,) + steps, [terms] + others)
+        sums = sums + crossed(sums, "dev", 1)
+        groups = [sums] + [crossed(sums, "dev", m) for m in (2, 4, 6)]
+        g_high = field(half, sums)
+        *groups, g_high = lax.optimization_barrier((*groups, g_high))
     else:
-        groups = [lax.all_gather(terms, "dev", axis=0)]
-    g_low = field(0, groups[0])
-    *groups, g_low = lax.optimization_barrier((*groups, g_low))
-    flip = region_count == 4
-    own, near_a, near_b, far = pl.pallas_call(
-        functools.partial(scatter_kernel, comps, atoms, flip),
-        out_shape=tuple(jax.ShapeDtypeStruct((ROWS, n * atoms), f32) for n in (3, 2, 2, 2)),
-        in_specs=[VMEM] * len(groups),
-        out_specs=(VMEM,) * 4,
-        compiler_params=PARAMS,
-        name="scatter",
-    )(*groups)
-    g_high = field(half, own)
-    if flip:
-        near_b = crossed(near_b, "region", 3)
-        far_a = far_b = crossed(far, "region", 2)
-        near_a = crossed(near_a, "region", 1)
-    else:
-        far_a = shifted(far, "region", 2)
-        far_b = shifted(far, "region", -2)
-        near_a = shifted(near_a, "region", 1)
-        near_b = shifted(near_b, "region", -1)
-
-    near_b, far_a, far_b, near_a, g_high = lax.optimization_barrier(
-        (near_b, far_a, far_b, near_a, g_high)
-    )
+        gathered = lax.all_gather(terms, "dev", axis=0)
+        sums = scattered((0,) * dev_count, [gathered[m] for m in range(dev_count)])
+        before, here, after = [sums[:, n * atoms : (n + 1) * atoms] for n in range(3)]
+        low, high = shifted(sums, "region", 1), shifted(sums, "region", -1)
+        before = before + low[:, atoms : 2 * atoms] + shifted(after, "region", 2)
+        here = here + low[:, 2 * atoms :] + high[:, :atoms]
+        after = after + high[:, atoms : 2 * atoms] + shifted(sums[:, :atoms], "region", -2)
+        groups = [jnp.concatenate([before, here, after], axis=1)]
+        g_high = field(half, terms)
 
     moments, potential = pl.pallas_call(
-        functools.partial(potential_kernel, comps, atoms, flip),
+        functools.partial(potential_kernel, comps, atoms),
         out_shape=(
             jax.ShapeDtypeStruct((mine, comps), f32),
             jax.ShapeDtypeStruct((batches, points), f32),
         ),
-        in_specs=[VMEM] * 8,
+        in_specs=[VMEM] * (3 + len(groups)),
         out_specs=(VMEM, VMEM),
         compiler_params=PARAMS,
         name="potential",
-    )(own, near_b, far_a, far_b, near_a, atom_rows, g_low, g_high)
+    )(atom_rows, g_low, g_high, *groups)
     return (density, moments.T, potential)
 
 

time: 43.2 us -> 43.3 us (level)
  transfers between devices with their start and end apart: 16 -> 16, of which waited for: 6 -> 7; matrix products, arithmetic and copies ran while one was open for 3% -> 3% of each run, Pallas kernels for 24% -> 24%
where the time goes in v14:
time: 43.3 us; the launch traced here: 43 us
  starting transfers between devices  15.5 us (36%)
  Pallas kernels  15.1 us (35%)
  waiting for transfers between devices  9.6 us (22%)
  between operations  1.43 us (3%)
  other arithmetic  0.71 us (2%)
  local copies, waits for them, and re-layouts  0.63 us (1%)
    ppermute x12, starting transfers between devices, crossed(): lax.ppermute(value, axis, [(i, i ^ m) for i in range(lax.axis_size(axis))])  9.16 us
    ppermute x4, starting transfers between devices, turned(): lax.ppermute(value, 'dev', [(i, i ^ (odd if i % 2 else even)) for i in ra...  6.35 us
    ppermute x12, waiting for transfers between devices, crossed(): lax.ppermute(value, axis, [(i, i ^ m) for i in range(lax.axis_size(axis))])  5.38 us
    ppermute x4, waiting for transfers between devices, turned(): lax.ppermute(value, 'dev', [(i, i ^ (odd if i % 2 else even)) for i in ra...  4.22 us
    pallas_call x2, Pallas kernels, field(): pl.pallas_call(functools.partial(field_kernel, begin), out_shape=pltpu.VM...  4.14 us
    pallas_call x1, Pallas kernels, turned_basis(): pl.pallas_call(turn_kernel, out_shape=(pltpu.VMEM((batches, near_blocks,...  3.67 us
    pallas_call x1, Pallas kernels, per_device(): pl.pallas_call(density_kernel, out_shape=(pltpu.VMEM((batches, points), f...  3.19 us
    pallas_call x1, Pallas kernels, per_device(): pl.pallas_call(functools.partial(potential_kernel, comps, atoms), out_sha...  1.33 us
  transfers between devices with their start and end apart: 16, of which 7 were waited for; matrix products, arithmetic and copies ran while one was open for 3% of the time, Pallas kernels for 24%

profile of v14, /device:TPU:0, one launch (start us, length us, event | category | flops | bytes accessed | tf_op | source)
XLA Modules:
  0.0 43.0 jit_solution(17606838932179779166)
XLA Ops:
  0.6 0.5 %collective-permute-start = (s32[1]{0:T(128)}, s32[1]{0:T(128)}, u32[]{:S(2)}, u32[]{:S(2)}) collective-permute-start(s32[1]{0:T(128)} %param.14), channel_id=1, source_target_pairs={{0,1},{1,0},{2,3},{3,2},{4,5},{5,4},{6,7},{7,6},{8,9},{9,8},{10,11... | collective-permute-start | bytes 20 | tf_op jit(solution)/shard_map/ppermute | solution.py:277
  1.1 1.3 %mask.1.rows_ref.refs_0_ = bf16[3,4,128,128]{3,2,1,0:T(8,128)(2,1)S(1)} custom-call(s32[3,4]{1,0:T(4,128)} %mask_hbm.1, bf16[3,4,128,128]{3,2,1,0:T(8,128)(2,1)} %rows_hbm.1), custom_call_target="tpu_custom_call" | custom-call | flops 2000000000 | bytes 8000000 | tf_op jit(solution)/shard_map/mask/pallas_call | solution.py:313
  2.5 0.0 copy-start
  2.5 0.0 copy-start.1
  2.5 0.0 copy-start.2
  2.5 0.0 collective-permute-done
  2.5 2.6 %collective-permute-start.2 = (bf16[3,4,128,128]{3,2,1,0:T(8,128)(2,1)S(1)}, bf16[3,4,128,128]{3,2,1,0:T(8,128)(2,1)S(1)}, u32[]{:S(2)}, u32[]{:S(2)}) collective-permute-start(bf16[3,4,128,128]{3,2,1,0:T(8,128)(2,1)S(1)} %mask.1.rows_ref.refs_0_), channel_id=1, source_target_pairs={{0,4},{1,3},{2,6},{3,1},{4,0},{5,7},{6,2},{7,5},{8,12},{9,11},{10,... | collective-permute-start | bytes 1179656 | tf_op jit(solution)/shard_map/ppermute | solution.py:282
  5.8 0.7 %pad_add_fusion = s32[2]{0:T(128)S(1)} fusion(s32[1]{0:T(128)} %collective-permute-done, s32[1]{0:T(128)S(6)} %copy.15.start_ref), kind=kLoop, calls=%fused_computation | loop fusion | flops 2 | bytes 16 | tf_op jit(solution)/shard_map/concatenate | solution.py:387
  6.5 1.5 %collective-permute-start.1 = (s32[2]{0:T(128)S(1)}, s32[2]{0:T(128)S(1)}, u32[]{:S(2)}, u32[]{:S(2)}) collective-permute-start(s32[2]{0:T(128)S(1)} %pad_add_fusion), channel_id=1, source_target_pairs={{0,2},{1,5},{2,0},{3,7},{4,6},{5,1},{6,4},{7,3},{8,10},{9,13},{10,... | collective-permute-start | bytes 32 | tf_op jit(solution)/shard_map/ppermute | solution.py:282
  8.0 2.1 %collective-permute-done.1.starts_ref = s32[2]{0:T(128)S(1)} collective-permute-done((s32[2]{0:T(128)S(1)}, s32[2]{0:T(128)S(1)}, u32[]{:S(2)}, u32[]{:S(2)}) %collective-permute-start.1) | collective-permute-done | bytes 40 | tf_op jit(solution)/shard_map/ppermute | solution.py:282
  10.1 0.6 %select.2 = bf16[2,4,128,128]{3,2,1,0:T(8,128)(2,1)S(1)} custom-call(s32[2]{0:T(128)S(1)} %collective-permute-done.1.starts_ref, bf16[3,4,128,128]{3,2,1,0:T(8,128)(2,1)S(1)} %mask.1.rows_ref.refs_0_), custom_call_target="tpu_custom_call" | custom-call | tf_op jit(solution)/shard_map/select/pallas_call | solution.py:374
  10.7 1.6 %collective-permute-start.3 = (bf16[2,4,128,128]{3,2,1,0:T(8,128)(2,1)S(1)}, bf16[2,4,128,128]{3,2,1,0:T(8,128)(2,1)S(1)}, u32[]{:S(2)}, u32[]{:S(2)}) collective-permute-start(bf16[2,4,128,128]{3,2,1,0:T(8,128)(2,1)S(1)} %select.2), channel_id=1, source_target_pairs={{0,2},{1,5},{2,0},{3,7},{4,6},{5,1},{6,4},{7,3},{8,10},{9,13},{10,... | collective-permute-start | bytes 786440 | tf_op jit(solution)/shard_map/ppermute | solution.py:282
  12.2 0.0 collective-permute-done.2.rows_ref.refs_2_
  12.2 0.6 %select.3.after_hbm = bf16[2,4,128,128]{3,2,1,0:T(8,128)(2,1)S(1)} custom-call(s32[2]{0:T(128)S(1)} %collective-permute-done.1.starts_ref, bf16[3,4,128,128]{3,2,1,0:T(8,128)(2,1)S(1)} %collective-permute-done.2.rows_ref.refs_2_), custom_call_target="tpu_custom_call" | custom-call | tf_op jit(solution)/shard_map/select/pallas_call | solution.py:374
  12.8 0.7 %collective-permute-start.7 = (bf16[2,4,128,128]{3,2,1,0:T(8,128)(2,1)S(1)}, bf16[2,4,128,128]{3,2,1,0:T(8,128)(2,1)S(1)}, u32[]{:S(2)}, u32[]{:S(2)}) collective-permute-start(bf16[2,4,128,128]{3,2,1,0:T(8,128)(2,1)S(1)} %select.3.after_hbm), channel_id=1, source_target_pairs={{0,2},{1,5},{2,0},{3,7},{4,6},{5,1},{6,4},{7,3},{8,10},{9,13},{10,... | collective-permute-start | bytes 786440 | tf_op jit(solution)/shard_map/ppermute | solution.py:282
  13.5 0.0 collective-permute-start.5
  13.5 0.5 %collective-permute-start.4 = (bf16[3,4,128,128]{3,2,1,0:T(8,128)(2,1)S(1)}, bf16[3,4,128,128]{3,2,1,0:T(8,128)(2,1)S(1)}, u32[]{:S(2)}, u32[]{:S(2)}) collective-permute-start(bf16[3,4,128,128]{3,2,1,0:T(8,128)(2,1)S(1)} %mask.1.rows_ref.refs_0_), channel_id=1, source_target_pairs={{0,1},{1,0},{2,3},{3,2},{4,5},{5,4},{6,7},{7,6},{8,9},{9,8},{10,11... | collective-permute-start | bytes 1179656 | tf_op jit(solution)/shard_map/ppermute | solution.py:277
  14.0 0.0 copy-done
  14.0 0.0 copy-done.1
  14.0 0.0 copy-done.2
  14.0 3.7 %turn.1 = (bf16[12,4,128,256]{3,2,1,0:T(8,128)(2,1)S(1)}, f32[12,6,256]{2,1,0:T(8,128)S(1)}, bf16[72,32,256]{2,1,0:T(8,128)(2,1)S(1)}, s32[1,128]{1,0:T(1,128)S(...) custom-call(bf16[2,4,128,128]{3,2,1,0:T(8,128)(2,1)S(1)} %select.3.after_hbm, s32[6,12]{1,0:T(8,128)S(1)} %bitcast.3, ...), custom_call_target="tpu_custom_call" | custom-call | flops 2000000000 | bytes 8000000 | tf_op jit(solution)/shard_map/turn/pallas_call | solution.py:348
  17.7 0.0 collective-permute-done.3.refs_4_
  17.7 0.1 collective-permute-start.6
  17.8 2.1 %collective-permute-done.7.refs_6_ = bf16[2,4,128,128]{3,2,1,0:T(8,128)(2,1)S(1)} collective-permute-done((bf16[2,4,128,128]{3,2,1,0:T(8,128)(2,1)S(1)}, bf16[2,4,128,128]{3,2,1,0:T(8,128)(2,1)S(1)}, u32[]{:S(2)}, u32[]{:S(2)}) %collective-permute-start.7) | collective-permute-done | bytes 262176 | tf_op jit(solution)/shard_map/ppermute | solution.py:282
  19.9 0.0 collective-permute-start.8
  19.9 0.0 collective-permute-done.6.refs_5_
  19.9 0.0 collective-permute-done.4.refs_1_
  19.9 0.0 collective-permute-done.5.refs_3_
  19.9 1.5 %collective-permute-done.8.refs_7_ = bf16[2,4,128,128]{3,2,1,0:T(8,128)(2,1)S(1)} collective-permute-done((bf16[2,4,128,128]{3,2,1,0:T(8,128)(2,1)S(1)}, bf16[2,4,128,128]{3,2,1,0:T(8,128)(2,1)S(1)}, u32[]{:S(2)}, u32[]{:S(2)}) %collective-permute-start.8) | collective-permute-done | bytes 262176 | tf_op jit(solution)/shard_map/ppermute | solution.py:277
  21.4 3.2 %density.1 = (f32[12,256]{1,0:T(8,128)S(1)}, f32[32,128]{1,0:T(8,128)S(1)}) custom-call(s32[1,128]{1,0:T(1,128)S(1)} %get-tuple-element.31.place_ref, s32[1,128]{1,0:T(1,128)S(1)} %get-tuple-element.32.atom_ref, f32[12,256]{1,0:T(8,128)S(1)} %get-tuple-element.33.alive_ref, bf16[12,4,128,256]{3,2,1,0:T(8,128)(2,1)S(1)} %get-tuple-element.35.phit_ref, ...), custom_call_target="tpu_custom_call" | custom-call | flops 2000000000 | bytes 6000000 | tf_op jit(solution)/shard_map/density/pallas_call | solution.py:401
  24.6 3.7 %collective-permute-start.11 = (f32[32,128]{1,0:T(8,128)S(1)}, f32[32,128]{1,0:T(8,128)S(1)}, u32[]{:S(2)}, u32[]{:S(2)}) collective-permute-start(f32[32,128]{1,0:T(8,128)S(1)} %get-tuple-element.41.after_hbm.refs_0_), channel_id=1, source_target_pairs={{0,24},{8,16},{16,8},{24,0},{1,25},{9,17},{17,9},{25,1},{2,26},{10... | collective-permute-start | bytes 49160 | tf_op jit(solution)/shard_map/ppermute | solution.py:277
  28.3 0.0 collective-permute-start.10
  28.3 0.8 %collective-permute-start.9 = (f32[32,128]{1,0:T(8,128)S(1)}, f32[32,128]{1,0:T(8,128)S(1)}, u32[]{:S(2)}, u32[]{:S(2)}) collective-permute-start(f32[32,128]{1,0:T(8,128)S(1)} %get-tuple-element.41.after_hbm.refs_0_), channel_id=1, source_target_pairs={{0,8},{8,0},{16,24},{24,16},{1,9},{9,1},{17,25},{25,17},{2,10},{10... | collective-permute-start | bytes 49160 | tf_op jit(solution)/shard_map/ppermute | solution.py:277
  29.1 2.1 %field.2.low_ref = f32[36,25,256]{2,1,0:T(8,128)S(1)} custom-call(f32[32,128]{1,0:T(8,128)S(1)} %get-tuple-element.41.after_hbm.refs_0_, f32[12,256]{1,0:T(8,128)S(1)} %get-tuple-element.33.alive_ref, f32[16,25]{1,0:T(8,128)} %bitcast.4, f32[12,6,256]{2,1,0:T(8,128)} %radius_hbm.3, bf16[12,6,25,256]{3,2,1,0:T(8,128)(2,1)} %harm_hbm.5), custom_call_target="tpu_custom_call" | custom-call | flops 2000000000 | bytes 8000000 | tf_op jit(solution)/shard_map/field/pallas_call | solution.py:331
  31.2 0.0 collective-permute-done.11.refs_3_
  31.2 1.8 %collective-permute-done.10.refs_2_ = f32[32,128]{1,0:T(8,128)S(1)} collective-permute-done((f32[32,128]{1,0:T(8,128)S(1)}, f32[32,128]{1,0:T(8,128)S(1)}, u32[]{:S(2)}, u32[]{:S(2)}) %collective-permute-start.10) | collective-permute-done | bytes 16416 | tf_op jit(solution)/shard_map/ppermute | solution.py:277
  33.0 0.0 collective-permute-done.9.refs_1_
  33.0 0.3 scatter.1
  33.2 0.0 collective-permute-start.12
  33.3 0.6 %copy.14 = f32[12,256]{1,0:T(8,128)} copy(f32[12,256]{1,0:T(8,128)S(1)} %get-tuple-element.53) | data formatting | bytes 24576
  33.9 0.6 %collective-permute-done.12 = f32[32,384]{1,0:T(8,128)S(1)} collective-permute-done((f32[32,384]{1,0:T(8,128)S(1)}, f32[32,384]{1,0:T(8,128)S(1)}, u32[]{:S(2)}, u32[]{:S(2)}) %collective-permute-start.12) | collective-permute-done | bytes 49184 | tf_op jit(solution)/shard_map/ppermute | solution.py:277
  34.5 1.5 %collective-permute-start.15 = (f32[32,384]{1,0:T(8,128)S(1)}, f32[32,384]{1,0:T(8,128)S(1)}, u32[]{:S(2)}, u32[]{:S(2)}) collective-permute-start(f32[32,384]{1,0:T(8,128)S(1)} %add.3.after_hbm.refs_0_), channel_id=1, source_target_pairs={{0,6},{1,7},{2,4},{3,5},{4,2},{5,3},{6,0},{7,1},{8,14},{9,15},{10,... | collective-permute-start | bytes 147464 | tf_op jit(solution)/shard_map/ppermute | solution.py:277
  36.0 1.5 %collective-permute-start.14 = (f32[32,384]{1,0:T(8,128)S(1)}, f32[32,384]{1,0:T(8,128)S(1)}, u32[]{:S(2)}, u32[]{:S(2)}) collective-permute-start(f32[32,384]{1,0:T(8,128)S(1)} %add.3.after_hbm.refs_0_), channel_id=1, source_target_pairs={{0,4},{1,5},{2,6},{3,7},{4,0},{5,1},{6,2},{7,3},{8,12},{9,13},{10,... | collective-permute-start | bytes 147464 | tf_op jit(solution)/shard_map/ppermute | solution.py:277
  37.5 0.5 %collective-permute-start.13 = (f32[32,384]{1,0:T(8,128)S(1)}, f32[32,384]{1,0:T(8,128)S(1)}, u32[]{:S(2)}, u32[]{:S(2)}) collective-permute-start(f32[32,384]{1,0:T(8,128)S(1)} %add.3.after_hbm.refs_0_), channel_id=1, source_target_pairs={{0,2},{1,3},{2,0},{3,1},{4,6},{5,7},{6,4},{7,5},{8,10},{9,11},{10,... | collective-permute-start | bytes 147464 | tf_op jit(solution)/shard_map/ppermute | solution.py:277
  38.1 2.1 %field.3.high_ref = f32[36,25,256]{2,1,0:T(8,128)S(1)} custom-call(f32[32,384]{1,0:T(8,128)S(1)} %add.3.after_hbm.refs_0_, f32[12,256]{1,0:T(8,128)S(1)} %get-tuple-element.33.alive_ref, f32[16,25]{1,0:T(8,128)} %bitcast.5, f32[12,6,256]{2,1,0:T(8,128)} %radius_hbm.3, bf16[12,6,25,256]{3,2,1,0:T(8,128)(2,1)} %harm_hbm.5), custom_call_target="tpu_custom_call" | custom-call | flops 2000000000 | bytes 8000000 | tf_op jit(solution)/shard_map/field/pallas_call | solution.py:331
  40.2 0.0 collective-permute-done.15.refs_3_
  40.2 0.1 collective-permute-done.14.refs_2_
  40.3 1.3 %collective-permute-done.13.refs_1_ = f32[32,384]{1,0:T(8,128)S(1)} collective-permute-done((f32[32,384]{1,0:T(8,128)S(1)}, f32[32,384]{1,0:T(8,128)S(1)}, u32[]{:S(2)}, u32[]{:S(2)}) %collective-permute-start.13) | collective-permute-done | bytes 49184 | tf_op jit(solution)/shard_map/ppermute | solution.py:277
  41.6 1.3 %potential.1 = (f32[16,25]{1,0:T(8,128)}, f32[12,256]{1,0:T(8,128)}) custom-call(s32[1,128]{1,0:T(1,128)S(1)} %get-tuple-element.32.atom_ref, f32[36,25,256]{2,1,0:T(8,128)S(1)} %field.2.low_ref, f32[36,25,256]{2,1,0:T(8,128)S(1)} %field.3.high_ref, f32[32,384]{1,0:T(8,128)S(1)} %add.3.after_hbm.refs_0_, f32[32,384]{1,0:T(8,128)S(1)} %collective-permute-done.13.refs_1_, ...), custom_call_target="tpu_custom_call" | custom-call | tf_op jit(solution)/shard_map/potential/pallas_call | solution.py:452
  (1 shorter events, 0.0 us)
Async XLA Ops:
  0.6 1.9 %collective-permute-start = (s32[1]{0:T(128)}, s32[1]{0:T(128)}, u32[]{:S(2)}, u32[]{:S(2)}) collective-permute-start(s32[1]{0:T(128)} %param.14), channel_id=1, source_target_pairs={{0,1},{1,0},{2,3},{3,2},{4,5},{5,4},{6,7},{7,6},{8,9},{9,8},{10,11... | collective-permute-start | bytes 20 | tf_op jit(solution)/shard_map/ppermute | solution.py:277
  2.5 11.6 %copy-start = (s32[12,6]{0,1:T(8,128)S(1)}, s32[12,6]{0,1:T(8,128)}, u32[]{:S(2)}) copy-start(s32[12,6]{0,1:T(8,128)} %param.17) | copy-start | bytes 868
  2.5 11.6 %copy-start.1 = (s32[1,12]{1,0:T(1,128)S(1)}, s32[1,12]{1,0:T(1,128)}, u32[]{:S(2)}) copy-start(s32[1,12]{1,0:T(1,128)} %size_ref.1) | copy-start | bytes 148
  2.5 11.6 %copy-start.2 = (s32[1,12]{1,0:T(1,128)S(1)}, s32[1,12]{1,0:T(1,128)}, u32[]{:S(2)}) copy-start(s32[1,12]{1,0:T(1,128)} %offset_ref.1) | copy-start | bytes 148
  2.5 9.7 %collective-permute-start.2 = (bf16[3,4,128,128]{3,2,1,0:T(8,128)(2,1)S(1)}, bf16[3,4,128,128]{3,2,1,0:T(8,128)(2,1)S(1)}, u32[]{:S(2)}, u32[]{:S(2)}) collective-permute-start(bf16[3,4,128,128]{3,2,1,0:T(8,128)(2,1)S(1)} %mask.1.rows_ref.refs_0_), channel_id=1, source_target_pairs={{0,4},{1,3},{2,6},{3,1},{4,0},{5,7},{6,2},{7,5},{8,12},{9,11},{10,... | collective-permute-start | bytes 1179656 | tf_op jit(solution)/shard_map/ppermute | solution.py:282
  6.5 3.6 %collective-permute-start.1 = (s32[2]{0:T(128)S(1)}, s32[2]{0:T(128)S(1)}, u32[]{:S(2)}, u32[]{:S(2)}) collective-permute-start(s32[2]{0:T(128)S(1)} %pad_add_fusion), channel_id=1, source_target_pairs={{0,2},{1,5},{2,0},{3,7},{4,6},{5,1},{6,4},{7,3},{8,10},{9,13},{10,... | collective-permute-start | bytes 32 | tf_op jit(solution)/shard_map/ppermute | solution.py:282
  10.7 7.1 %collective-permute-start.3 = (bf16[2,4,128,128]{3,2,1,0:T(8,128)(2,1)S(1)}, bf16[2,4,128,128]{3,2,1,0:T(8,128)(2,1)S(1)}, u32[]{:S(2)}, u32[]{:S(2)}) collective-permute-start(bf16[2,4,128,128]{3,2,1,0:T(8,128)(2,1)S(1)} %select.2), channel_id=1, source_target_pairs={{0,2},{1,5},{2,0},{3,7},{4,6},{5,1},{6,4},{7,3},{8,10},{9,13},{10,... | collective-permute-start | bytes 786440 | tf_op jit(solution)/shard_map/ppermute | solution.py:282
  12.8 7.1 %collective-permute-start.7 = (bf16[2,4,128,128]{3,2,1,0:T(8,128)(2,1)S(1)}, bf16[2,4,128,128]{3,2,1,0:T(8,128)(2,1)S(1)}, u32[]{:S(2)}, u32[]{:S(2)}) collective-permute-start(bf16[2,4,128,128]{3,2,1,0:T(8,128)(2,1)S(1)} %select.3.after_hbm), channel_id=1, source_target_pairs={{0,2},{1,5},{2,0},{3,7},{4,6},{5,1},{6,4},{7,3},{8,10},{9,13},{10,... | collective-permute-start | bytes 786440 | tf_op jit(solution)/shard_map/ppermute | solution.py:282
  13.5 6.4 %collective-permute-start.5 = (bf16[3,4,128,128]{3,2,1,0:T(8,128)(2,1)S(1)}, bf16[3,4,128,128]{3,2,1,0:T(8,128)(2,1)S(1)}, u32[]{:S(2)}, u32[]{:S(2)}) collective-permute-start(bf16[3,4,128,128]{3,2,1,0:T(8,128)(2,1)S(1)} %collective-permute-done.2.rows_ref.refs_2_), channel_id=1, source_target_pairs={{0,1},{1,0},{2,3},{3,2},{4,5},{5,4},{6,7},{7,6},{8,9},{9,8},{10,11... | collective-permute-start | bytes 1179656 | tf_op jit(solution)/shard_map/ppermute | solution.py:277
  13.5 6.4 %collective-permute-start.4 = (bf16[3,4,128,128]{3,2,1,0:T(8,128)(2,1)S(1)}, bf16[3,4,128,128]{3,2,1,0:T(8,128)(2,1)S(1)}, u32[]{:S(2)}, u32[]{:S(2)}) collective-permute-start(bf16[3,4,128,128]{3,2,1,0:T(8,128)(2,1)S(1)} %mask.1.rows_ref.refs_0_), channel_id=1, source_target_pairs={{0,1},{1,0},{2,3},{3,2},{4,5},{5,4},{6,7},{7,6},{8,9},{9,8},{10,11... | collective-permute-start | bytes 1179656 | tf_op jit(solution)/shard_map/ppermute | solution.py:277
  17.7 2.2 %collective-permute-start.6 = (bf16[2,4,128,128]{3,2,1,0:T(8,128)(2,1)S(1)}, bf16[2,4,128,128]{3,2,1,0:T(8,128)(2,1)S(1)}, u32[]{:S(2)}, u32[]{:S(2)}) collective-permute-start(bf16[2,4,128,128]{3,2,1,0:T(8,128)(2,1)S(1)} %collective-permute-done.3.refs_4_), channel_id=1, source_target_pairs={{0,1},{1,0},{2,3},{3,2},{4,5},{5,4},{6,7},{7,6},{8,9},{9,8},{10,11... | collective-permute-start | bytes 786440 | tf_op jit(solution)/shard_map/ppermute | solution.py:277
  19.9 1.5 %collective-permute-start.8 = (bf16[2,4,128,128]{3,2,1,0:T(8,128)(2,1)S(1)}, bf16[2,4,128,128]{3,2,1,0:T(8,128)(2,1)S(1)}, u32[]{:S(2)}, u32[]{:S(2)}) collective-permute-start(bf16[2,4,128,128]{3,2,1,0:T(8,128)(2,1)S(1)} %collective-permute-done.7.refs_6_), channel_id=1, source_target_pairs={{0,1},{1,0},{2,3},{3,2},{4,5},{5,4},{6,7},{7,6},{8,9},{9,8},{10,11... | collective-permute-start | bytes 786440 | tf_op jit(solution)/shard_map/ppermute | solution.py:277
  24.6 6.5 %collective-permute-start.11 = (f32[32,128]{1,0:T(8,128)S(1)}, f32[32,128]{1,0:T(8,128)S(1)}, u32[]{:S(2)}, u32[]{:S(2)}) collective-permute-start(f32[32,128]{1,0:T(8,128)S(1)} %get-tuple-element.41.after_hbm.refs_0_), channel_id=1, source_target_pairs={{0,24},{8,16},{16,8},{24,0},{1,25},{9,17},{17,9},{25,1},{2,26},{10... | collective-permute-start | bytes 49160 | tf_op jit(solution)/shard_map/ppermute | solution.py:277
  28.3 4.6 %collective-permute-start.10 = (f32[32,128]{1,0:T(8,128)S(1)}, f32[32,128]{1,0:T(8,128)S(1)}, u32[]{:S(2)}, u32[]{:S(2)}) collective-permute-start(f32[32,128]{1,0:T(8,128)S(1)} %get-tuple-element.41.after_hbm.refs_0_), channel_id=1, source_target_pairs={{0,16},{8,24},{16,0},{24,8},{1,17},{9,25},{17,1},{25,9},{2,18},{10... | collective-permute-start | bytes 49160 | tf_op jit(solution)/shard_map/ppermute | solution.py:277
  28.3 4.6 %collective-permute-start.9 = (f32[32,128]{1,0:T(8,128)S(1)}, f32[32,128]{1,0:T(8,128)S(1)}, u32[]{:S(2)}, u32[]{:S(2)}) collective-permute-start(f32[32,128]{1,0:T(8,128)S(1)} %get-tuple-element.41.after_hbm.refs_0_), channel_id=1, source_target_pairs={{0,8},{8,0},{16,24},{24,16},{1,9},{9,1},{17,25},{25,17},{2,10},{10... | collective-permute-start | bytes 49160 | tf_op jit(solution)/shard_map/ppermute | solution.py:277
  33.2 1.3 %collective-permute-start.12 = (f32[32,384]{1,0:T(8,128)S(1)}, f32[32,384]{1,0:T(8,128)S(1)}, u32[]{:S(2)}, u32[]{:S(2)}) collective-permute-start(f32[32,384]{1,0:T(8,128)S(1)} %scatter.1), channel_id=1, source_target_pairs={{0,1},{1,0},{2,3},{3,2},{4,5},{5,4},{6,7},{7,6},{8,9},{9,8},{10,11... | collective-permute-start | bytes 147464 | tf_op jit(solution)/shard_map/ppermute | solution.py:277
  34.5 5.6 %collective-permute-start.15 = (f32[32,384]{1,0:T(8,128)S(1)}, f32[32,384]{1,0:T(8,128)S(1)}, u32[]{:S(2)}, u32[]{:S(2)}) collective-permute-start(f32[32,384]{1,0:T(8,128)S(1)} %add.3.after_hbm.refs_0_), channel_id=1, source_target_pairs={{0,6},{1,7},{2,4},{3,5},{4,2},{5,3},{6,0},{7,1},{8,14},{9,15},{10,... | collective-permute-start | bytes 147464 | tf_op jit(solution)/shard_map/ppermute | solution.py:277
  36.0 4.3 %collective-permute-start.14 = (f32[32,384]{1,0:T(8,128)S(1)}, f32[32,384]{1,0:T(8,128)S(1)}, u32[]{:S(2)}, u32[]{:S(2)}) collective-permute-start(f32[32,384]{1,0:T(8,128)S(1)} %add.3.after_hbm.refs_0_), channel_id=1, source_target_pairs={{0,4},{1,5},{2,6},{3,7},{4,0},{5,1},{6,2},{7,3},{8,12},{9,13},{10,... | collective-permute-start | bytes 147464 | tf_op jit(solution)/shard_map/ppermute | solution.py:277
  37.5 4.1 %collective-permute-start.13 = (f32[32,384]{1,0:T(8,128)S(1)}, f32[32,384]{1,0:T(8,128)S(1)}, u32[]{:S(2)}, u32[]{:S(2)}) collective-permute-start(f32[32,384]{1,0:T(8,128)S(1)} %add.3.after_hbm.refs_0_), channel_id=1, source_target_pairs={{0,2},{1,3},{2,0},{3,1},{4,6},{5,7},{6,4},{7,5},{8,10},{9,11},{10,... | collective-permute-start | bytes 147464 | tf_op jit(solution)/shard_map/ppermute | solution.py:277

commit v15 on v13

--- a/solution.py
+++ b/solution.py
@@ -52,9 +52,21 @@
 def select_kernel(even, odd, owners, starts_ref, rows_ref, out_ref):
     me = lax.axis_index("dev")
     owner = lax.bitwise_xor(me, jnp.where(lax.rem(me, 2) == 1, odd, even))
+    stored, band, width = rows_ref.shape[:3]
+    starts = starts_ref[...]
+    reach = starts + lax.bitwise_and(owner - starts, owners - 1)
+    reach = jnp.where(reach >= stored * owners, reach - stored * owners, reach)
     for n in range(out_ref.shape[0]):
-        row = chosen_row(owner, starts_ref[n], owners, rows_ref.shape[0])[1]
-        out_ref[n] = rows_ref[row]
+        spot = jnp.broadcast_to(reach[:, n : n + 1], (width, width))
+        factors = [
+            jnp.where((spot >= t * owners) & (spot < (t + 1) * owners), 1.0, 0.0).astype(jnp.bfloat16)
+            for t in range(stored)
+        ]
+        for k in range(band):
+            total = rows_ref[0, k] * factors[0]
+            for t in range(1, stored):
+                total = total + rows_ref[t, k] * factors[t]
+            out_ref[n, k] = total
 
 
 def mask_kernel(mask_hbm, rows_hbm, out_ref, mask, rows, sems):
@@ -383,17 +395,18 @@
         return pl.pallas_call(
             functools.partial(select_kernel, even, odd, dev_count),
             out_shape=pltpu.VMEM((2,) + density_rows.shape[1:], bf16),
-            in_specs=[SMEM, VMEM],
+            in_specs=[VMEM, VMEM],
             out_specs=VMEM,
             compiler_params=PARAMS,
             name="select",
         )(starts, rows)
 
     if dev_count == 8:
-        beside = crossed(window_start, "dev", 1)
+        opening = window_start[None]
+        beside = crossed(opening, "dev", 1)
         beside, rows = lax.optimization_barrier((beside, masked))
         first = turned(rows, 4, 2)
-        starts = turned(jnp.concatenate([window_start, beside]), 2, 4)
+        starts = turned(jnp.concatenate([opening, beside], axis=1), 2, 4)
         chosen = selected(0, 0, starts, masked)
         second = turned(chosen, 2, 4)
         first, later, _ = lax.optimization_barrier((first, masked, chosen))

time: 43.2 us -> 42.9 us (level)
  Pallas kernels: 15.1 us -> 14.3 us
  starting transfers between devices: 15.6 us -> 16.3 us
    pallas_call x2, Pallas kernels: 1.17 us -> 0.37 us  [selected(): pl.pallas_call(functools.partial(select_kernel, even, odd, dev_count), ou...]
    ppermute x4, starting transfers between devices: 6.35 us -> 7.03 us  [turned(): lax.ppermute(value, 'dev', [(i, i ^ (odd if i % 2 else even)) for i in ra...]
  transfers between devices with their start and end apart: 16 -> 16, of which waited for: 6 -> 6; matrix products, arithmetic and copies ran while one was open for 3% -> 3% of each run, Pallas kernels for 24% -> 22%
where the time goes in v15:
time: 42.9 us; the launch traced here: 42.5 us
  starting transfers between devices  16.3 us (38%)
  Pallas kernels  14.3 us (33%)
  waiting for transfers between devices  9.15 us (21%)
  between operations  1.42 us (3%)
  other arithmetic  0.7 us (2%)
  local copies, waits for them, and re-layouts  0.62 us (1%)
    ppermute x12, starting transfers between devices, crossed(): lax.ppermute(value, axis, [(i, i ^ m) for i in range(lax.axis_size(axis))])  9.27 us
    ppermute x4, starting transfers between devices, turned(): lax.ppermute(value, 'dev', [(i, i ^ (odd if i % 2 else even)) for i in ra...  7.03 us
    ppermute x12, waiting for transfers between devices, crossed(): lax.ppermute(value, axis, [(i, i ^ m) for i in range(lax.axis_size(axis))])  5.18 us
    pallas_call x2, Pallas kernels, field(): pl.pallas_call(functools.partial(field_kernel, begin), out_shape=pltpu.VM...  4.14 us
    ppermute x4, waiting for transfers between devices, turned(): lax.ppermute(value, 'dev', [(i, i ^ (odd if i % 2 else even)) for i in ra...  3.97 us
    pallas_call x1, Pallas kernels, turned_basis(): pl.pallas_call(turn_kernel, out_shape=(pltpu.VMEM((batches, near_blocks,...  3.65 us
    pallas_call x1, Pallas kernels, per_device(): pl.pallas_call(density_kernel, out_shape=(pltpu.VMEM((batches, points), f...  3.15 us
    pallas_call x1, Pallas kernels, per_device(): pl.pallas_call(functools.partial(potential_kernel, comps, atoms, flip), o...  1.34 us
  transfers between devices with their start and end apart: 16, of which 6 were waited for; matrix products, arithmetic and copies ran while one was open for 3% of the time, Pallas kernels for 22%

profile of v15, /device:TPU:0, one launch (start us, length us, event | category | flops | bytes accessed | tf_op | source)
XLA Modules:
  0.0 42.5 jit_solution(8601587468640051874)
XLA Ops:
  0.6 0.5 %collective-permute-start = (s32[1,1]{1,0:T(1,128)}, s32[1,1]{1,0:T(1,128)}, u32[]{:S(2)}, u32[]{:S(2)}) collective-permute-start(s32[1,1]{1,0:T(1,128)} %bitcast), channel_id=1, source_target_pairs={{0,1},{1,0},{2,3},{3,2},{4,5},{5,4},{6,7},{7,6},{8,9},{9,8},{10,11... | collective-permute-start | bytes 20 | tf_op jit(solution)/shard_map/ppermute | solution.py:302
  1.1 1.3 %mask.1.rows_ref.refs_0_ = bf16[3,4,128,128]{3,2,1,0:T(8,128)(2,1)S(1)} custom-call(s32[3,4]{1,0:T(4,128)} %mask_hbm.1, bf16[3,4,128,128]{3,2,1,0:T(8,128)(2,1)} %rows_hbm.1), custom_call_target="tpu_custom_call" | custom-call | flops 2000000000 | bytes 8000000 | tf_op jit(solution)/shard_map/mask/pallas_call | solution.py:338
  2.5 0.0 copy-start
  2.5 0.0 copy-start.1
  2.5 0.0 collective-permute-done
  2.5 2.6 %collective-permute-start.2 = (bf16[3,4,128,128]{3,2,1,0:T(8,128)(2,1)S(1)}, bf16[3,4,128,128]{3,2,1,0:T(8,128)(2,1)S(1)}, u32[]{:S(2)}, u32[]{:S(2)}) collective-permute-start(bf16[3,4,128,128]{3,2,1,0:T(8,128)(2,1)S(1)} %mask.1.rows_ref.refs_0_), channel_id=1, source_target_pairs={{0,4},{1,3},{2,6},{3,1},{4,0},{5,7},{6,2},{7,5},{8,12},{9,11},{10,... | collective-permute-start | bytes 1179656 | tf_op jit(solution)/shard_map/ppermute | solution.py:307
  5.7 0.7 %pad_add_fusion = s32[1,2]{1,0:T(1,128)S(1)} fusion(s32[1,1]{1,0:T(1,128)} %collective-permute-done, s32[1,1]{1,0:T(1,128)} %bitcast.6), kind=kLoop, calls=%fused_computation.1 | loop fusion | flops 2 | bytes 16 | tf_op jit(solution)/shard_map/concatenate | solution.py:409
  6.4 1.5 %collective-permute-start.1 = (s32[1,2]{1,0:T(1,128)S(1)}, s32[1,2]{1,0:T(1,128)S(1)}, u32[]{:S(2)}, u32[]{:S(2)}) collective-permute-start(s32[1,2]{1,0:T(1,128)S(1)} %pad_add_fusion), channel_id=1, source_target_pairs={{0,2},{1,5},{2,0},{3,7},{4,6},{5,1},{6,4},{7,3},{8,10},{9,13},{10,... | collective-permute-start | bytes 32 | tf_op jit(solution)/shard_map/ppermute | solution.py:307
  7.9 2.1 %collective-permute-done.1.starts_ref = s32[1,2]{1,0:T(1,128)S(1)} collective-permute-done((s32[1,2]{1,0:T(1,128)S(1)}, s32[1,2]{1,0:T(1,128)S(1)}, u32[]{:S(2)}, u32[]{:S(2)}) %collective-permute-start.1) | collective-permute-done | bytes 40 | tf_op jit(solution)/shard_map/ppermute | solution.py:307
  10.1 0.2 select.2
  10.2 1.6 %collective-permute-start.3 = (bf16[2,4,128,128]{3,2,1,0:T(8,128)(2,1)S(1)}, bf16[2,4,128,128]{3,2,1,0:T(8,128)(2,1)S(1)}, u32[]{:S(2)}, u32[]{:S(2)}) collective-permute-start(bf16[2,4,128,128]{3,2,1,0:T(8,128)(2,1)S(1)} %select.2), channel_id=1, source_target_pairs={{0,2},{1,5},{2,0},{3,7},{4,6},{5,1},{6,4},{7,3},{8,10},{9,13},{10,... | collective-permute-start | bytes 786440 | tf_op jit(solution)/shard_map/ppermute | solution.py:307
  11.8 0.0 collective-permute-done.2.rows_ref.refs_2_
  11.8 0.2 select.3.after_hbm
  12.0 1.4 %collective-permute-start.7 = (bf16[2,4,128,128]{3,2,1,0:T(8,128)(2,1)S(1)}, bf16[2,4,128,128]{3,2,1,0:T(8,128)(2,1)S(1)}, u32[]{:S(2)}, u32[]{:S(2)}) collective-permute-start(bf16[2,4,128,128]{3,2,1,0:T(8,128)(2,1)S(1)} %select.3.after_hbm), channel_id=1, source_target_pairs={{0,2},{1,5},{2,0},{3,7},{4,6},{5,1},{6,4},{7,3},{8,10},{9,13},{10,... | collective-permute-start | bytes 786440 | tf_op jit(solution)/shard_map/ppermute | solution.py:307
  13.4 0.0 collective-permute-start.5
  13.4 0.5 %collective-permute-start.4 = (bf16[3,4,128,128]{3,2,1,0:T(8,128)(2,1)S(1)}, bf16[3,4,128,128]{3,2,1,0:T(8,128)(2,1)S(1)}, u32[]{:S(2)}, u32[]{:S(2)}) collective-permute-start(bf16[3,4,128,128]{3,2,1,0:T(8,128)(2,1)S(1)} %mask.1.rows_ref.refs_0_), channel_id=1, source_target_pairs={{0,1},{1,0},{2,3},{3,2},{4,5},{5,4},{6,7},{7,6},{8,9},{9,8},{10,11... | collective-permute-start | bytes 1179656 | tf_op jit(solution)/shard_map/ppermute | solution.py:302
  13.9 0.0 copy-done
  13.9 0.0 copy-done.1
  13.9 0.0 copy-start.2
  13.9 3.7 %turn.1 = (bf16[12,4,128,256]{3,2,1,0:T(8,128)(2,1)S(1)}, f32[12,6,256]{2,1,0:T(8,128)S(1)}, bf16[72,32,256]{2,1,0:T(8,128)(2,1)S(1)}, s32[1,128]{1,0:T(1,128)S(1)}, f32[12,256]{1,0:T(8,128)S(1)}) custom-call(bf16[2,4,128,128]{3,2,1,0:T(8,128)(2,1)S(1)} %select.3.after_hbm, s32[6,12]{1,0:T(8,128)S(1)} %bitcast.8, s32[1,12]{1,0:T(1,128)S(1)} %copy-done.1, ...), custom_call_target="tpu_custom_call" | custom-call | flops 2000000000 | bytes 8000000 | tf_op jit(solution)/shard_map/turn/pallas_call | solution.py:373
  17.6 0.0 collective-permute-done.3.refs_4_
  17.6 0.1 collective-permute-start.6
  17.7 1.8 %collective-permute-done.7.refs_6_ = bf16[2,4,128,128]{3,2,1,0:T(8,128)(2,1)S(1)} collective-permute-done((bf16[2,4,128,128]{3,2,1,0:T(8,128)(2,1)S(1)}, bf16[2,4,128,128]{3,2,1,0:T(8,128)(2,1)S(1)}, u32[]{:S(2)}, u32[]{:S(2)}) %collective-permute-start.7) | collective-permute-done | bytes 262176 | tf_op jit(solution)/shard_map/ppermute | solution.py:307
  19.5 0.0 collective-permute-start.8
  19.5 0.0 collective-permute-done.6.refs_5_
  19.5 0.0 collective-permute-done.4.refs_1_
  19.5 0.0 collective-permute-done.5.refs_3_
  19.5 1.5 %collective-permute-done.8.refs_7_ = bf16[2,4,128,128]{3,2,1,0:T(8,128)(2,1)S(1)} collective-permute-done((bf16[2,4,128,128]{3,2,1,0:T(8,128)(2,1)S(1)}, bf16[2,4,128,128]{3,2,1,0:T(8,128)(2,1)S(1)}, u32[]{:S(2)}, u32[]{:S(2)}) %collective-permute-start.8) | collective-permute-done | bytes 262176 | tf_op jit(solution)/shard_map/ppermute | solution.py:302
  21.0 0.0 copy-done.2
  21.0 3.2 %density.1 = (f32[12,256]{1,0:T(8,128)S(1)}, f32[32,128]{1,0:T(8,128)S(1)}) custom-call(s32[1]{0:T(128)} %copy.15.start_ref, s32[1,12]{1,0:T(1,128)S(1)} %copy-done.2, s32[1,128]{1,0:T(1,128)S(1)} %get-tuple-element.35.atom_ref, f32[12,256]{1,0:T(8,128)S(1)} %get-tuple-element.36.alive_ref, bf16[12,4,128,256]{3,2,1,0:T(8,128)(2,1)S(1)} %get-tuple-element.38.phit_ref, ...), custom_call_target="tpu_custom_call" | custom-call | flops 2000000000 | bytes 6000000 | tf_op jit(solution)/shard_map/density/pallas_call | solution.py:423
  24.2 0.2 collective-permute-start.9
  24.4 0.6 %copy.14 = f32[12,256]{1,0:T(8,128)} copy(f32[12,256]{1,0:T(8,128)S(1)} %get-tuple-element.61) | data formatting | bytes 24576
  25.0 0.4 %collective-permute-done.9 = f32[32,128]{1,0:T(8,128)S(1)} collective-permute-done((f32[32,128]{1,0:T(8,128)S(1)}, f32[32,128]{1,0:T(8,128)S(1)}, u32[]{:S(2)}, u32[]{:S(2)}) %collective-permute-start.9) | collective-permute-done | bytes 16416 | tf_op jit(solution)/shard_map/ppermute | solution.py:302
  25.5 1.4 %collective-permute-start.12 = (f32[2,32,128]{2,1,0:T(8,128)S(1)}, f32[2,32,128]{2,1,0:T(8,128)S(1)}, u32[]{:S(2)}, u32[]{:S(2)}) collective-permute-start(f32[2,32,128]{2,1,0:T(8,128)S(1)} %pad_maximum_fusion.after_hbm.refs_0_), channel_id=1, source_target_pairs={{0,6},{1,7},{2,4},{3,5},{4,2},{5,3},{6,0},{7,1},{8,14},{9,15},{10,... | collective-permute-start | bytes 98312 | tf_op jit(solution)/shard_map/ppermute | solution.py:302
  26.9 1.5 %collective-permute-start.11 = (f32[2,32,128]{2,1,0:T(8,128)S(1)}, f32[2,32,128]{2,1,0:T(8,128)S(1)}, u32[]{:S(2)}, u32[]{:S(2)}) collective-permute-start(f32[2,32,128]{2,1,0:T(8,128)S(1)} %pad_maximum_fusion.after_hbm.refs_0_), channel_id=1, source_target_pairs={{0,4},{1,5},{2,6},{3,7},{4,0},{5,1},{6,2},{7,3},{8,12},{9,13},{10,... | collective-permute-start | bytes 98312 | tf_op jit(solution)/shard_map/ppermute | solution.py:302
  28.4 0.5 %collective-permute-start.10 = (f32[2,32,128]{2,1,0:T(8,128)S(1)}, f32[2,32,128]{2,1,0:T(8,128)S(1)}, u32[]{:S(2)}, u32[]{:S(2)}) collective-permute-start(f32[2,32,128]{2,1,0:T(8,128)S(1)} %pad_maximum_fusion.after_hbm.refs_0_), channel_id=1, source_target_pairs={{0,2},{1,3},{2,0},{3,1},{4,6},{5,7},{6,4},{7,5},{8,10},{9,11},{10,... | collective-permute-start | bytes 98312 | tf_op jit(solution)/shard_map/ppermute | solution.py:302
  28.9 2.1 %field.2.low_ref = f32[36,25,256]{2,1,0:T(8,128)S(1)} custom-call(f32[2,32,128]{2,1,0:T(8,128)S(1)} %pad_maximum_fusion.after_hbm.refs_0_, f32[12,256]{1,0:T(8,128)S(1)} %get-tuple-element.36.alive_ref, f32[16,25]{1,0:T(8,128)} %bitcast.10, f32[12,6,256]{2,1,0:T(8,128)} %radius_hbm.3, bf16[12,6,25,256]{3,2,1,0:T(8,128)(2,1)} %harm_hbm.5), custom_call_target="tpu_custom_call" | custom-call | flops 2000000000 | bytes 8000000 | tf_op jit(solution)/shard_map/field/pallas_call | solution.py:356
  31.0 0.0 collective-permute-done.12.refs_3_
  31.0 0.0 collective-permute-done.11.refs_2_
  31.0 1.3 %collective-permute-done.10.refs_1_ = f32[2,32,128]{2,1,0:T(8,128)S(1)} collective-permute-done((f32[2,32,128]{2,1,0:T(8,128)S(1)}, f32[2,32,128]{2,1,0:T(8,128)S(1)}, u32[]{:S(2)}, u32[]{:S(2)}) %collective-permute-start.10) | collective-permute-done | bytes 32800 | tf_op jit(solution)/shard_map/ppermute | solution.py:302
  32.3 0.4 scatter.1
  32.7 3.7 %collective-permute-start.13 = (f32[32,256]{1,0:T(8,128)S(1)}, f32[32,256]{1,0:T(8,128)S(1)}, u32[]{:S(2)}, u32[]{:S(2)}) collective-permute-start(f32[32,256]{1,0:T(8,128)S(1)} %get-tuple-element.50), channel_id=1, source_target_pairs={{0,24},{8,16},{16,8},{24,0},{1,25},{9,17},{17,9},{25,1},{2,26},{10... | collective-permute-start | bytes 98312 | tf_op jit(solution)/shard_map/ppermute | solution.py:302
  36.4 0.0 collective-permute-start.14
  36.4 0.8 %collective-permute-start.15 = (f32[32,256]{1,0:T(8,128)S(1)}, f32[32,256]{1,0:T(8,128)S(1)}, u32[]{:S(2)}, u32[]{:S(2)}) collective-permute-start(f32[32,256]{1,0:T(8,128)S(1)} %get-tuple-element.52), channel_id=1, source_target_pairs={{0,8},{8,0},{16,24},{24,16},{1,9},{9,1},{17,25},{25,17},{2,10},{10... | collective-permute-start | bytes 98312 | tf_op jit(solution)/shard_map/ppermute | solution.py:302
  37.2 2.1 %field.3.high_ref = f32[36,25,256]{2,1,0:T(8,128)S(1)} custom-call(f32[32,384]{1,0:T(8,128)S(1)} %get-tuple-element.49.after_hbm.own_ref, f32[12,256]{1,0:T(8,128)S(1)} %get-tuple-element.36.alive_ref, f32[16,25]{1,0:T(8,128)} %bitcast.11, f32[12,6,256]{2,1,0:T(8,128)} %radius_hbm.3, bf16[12,6,25,256]{3,2,1,0:T(8,128)(2,1)} %harm_hbm.5), custom_call_target="tpu_custom_call" | custom-call | flops 2000000000 | bytes 8000000 | tf_op jit(solution)/shard_map/field/pallas_call | solution.py:356
  39.2 0.0 collective-permute-done.13.near_b_ref
  39.2 1.9 %collective-permute-done.14.fa_ref.fb_ref = f32[32,256]{1,0:T(8,128)S(1)} collective-permute-done((f32[32,256]{1,0:T(8,128)S(1)}, f32[32,256]{1,0:T(8,128)S(1)}, u32[]{:S(2)}, u32[]{:S(2)}) %collective-permute-start.14) | collective-permute-done | bytes 32800 | tf_op jit(solution)/shard_map/ppermute | solution.py:302
  41.2 0.0 collective-permute-done.15.near_a_ref
  41.2 1.3 %potential.1 = (f32[16,25]{1,0:T(8,128)}, f32[12,256]{1,0:T(8,128)}) custom-call(f32[32,384]{1,0:T(8,128)S(1)} %get-tuple-element.49.after_hbm.own_ref, f32[32,256]{1,0:T(8,128)S(1)} %collective-permute-done.13.near_b_ref, f32[32,256]{1,0:T(8,128)S(1)} %collective-permute-done.14.fa_ref.fb_ref, f32[32,256]{1,0:T(8,128)S(1)} %collective-permute-done.14.fa_ref.fb_ref, ...), custom_call_target="tpu_custom_call" | custom-call | tf_op jit(solution)/shard_map/potential/pallas_call | solution.py:474
  (1 shorter events, 0.0 us)
Async XLA Ops:
  0.6 1.9 %collective-permute-start = (s32[1,1]{1,0:T(1,128)}, s32[1,1]{1,0:T(1,128)}, u32[]{:S(2)}, u32[]{:S(2)}) collective-permute-start(s32[1,1]{1,0:T(1,128)} %bitcast), channel_id=1, source_target_pairs={{0,1},{1,0},{2,3},{3,2},{4,5},{5,4},{6,7},{7,6},{8,9},{9,8},{10,11... | collective-permute-start | bytes 20 | tf_op jit(solution)/shard_map/ppermute | solution.py:302
  2.5 11.4 %copy-start = (s32[12,6]{0,1:T(8,128)S(1)}, s32[12,6]{0,1:T(8,128)}, u32[]{:S(2)}) copy-start(s32[12,6]{0,1:T(8,128)} %param.17) | copy-start | bytes 868
  2.5 11.4 %copy-start.1 = (s32[1,12]{1,0:T(1,128)S(1)}, s32[1,12]{1,0:T(1,128)}, u32[]{:S(2)}) copy-start(s32[1,12]{1,0:T(1,128)} %size_ref.1) | copy-start | bytes 148
  2.5 9.3 %collective-permute-start.2 = (bf16[3,4,128,128]{3,2,1,0:T(8,128)(2,1)S(1)}, bf16[3,4,128,128]{3,2,1,0:T(8,128)(2,1)S(1)}, u32[]{:S(2)}, u32[]{:S(2)}) collective-permute-start(bf16[3,4,128,128]{3,2,1,0:T(8,128)(2,1)S(1)} %mask.1.rows_ref.refs_0_), channel_id=1, source_target_pairs={{0,4},{1,3},{2,6},{3,1},{4,0},{5,7},{6,2},{7,5},{8,12},{9,11},{10,... | collective-permute-start | bytes 1179656 | tf_op jit(solution)/shard_map/ppermute | solution.py:307
  6.4 3.6 %collective-permute-start.1 = (s32[1,2]{1,0:T(1,128)S(1)}, s32[1,2]{1,0:T(1,128)S(1)}, u32[]{:S(2)}, u32[]{:S(2)}) collective-permute-start(s32[1,2]{1,0:T(1,128)S(1)} %pad_add_fusion), channel_id=1, source_target_pairs={{0,2},{1,5},{2,0},{3,7},{4,6},{5,1},{6,4},{7,3},{8,10},{9,13},{10,... | collective-permute-start | bytes 32 | tf_op jit(solution)/shard_map/ppermute | solution.py:307
  10.2 7.3 %collective-permute-start.3 = (bf16[2,4,128,128]{3,2,1,0:T(8,128)(2,1)S(1)}, bf16[2,4,128,128]{3,2,1,0:T(8,128)(2,1)S(1)}, u32[]{:S(2)}, u32[]{:S(2)}) collective-permute-start(bf16[2,4,128,128]{3,2,1,0:T(8,128)(2,1)S(1)} %select.2), channel_id=1, source_target_pairs={{0,2},{1,5},{2,0},{3,7},{4,6},{5,1},{6,4},{7,3},{8,10},{9,13},{10,... | collective-permute-start | bytes 786440 | tf_op jit(solution)/shard_map/ppermute | solution.py:307
  12.0 7.5 %collective-permute-start.7 = (bf16[2,4,128,128]{3,2,1,0:T(8,128)(2,1)S(1)}, bf16[2,4,128,128]{3,2,1,0:T(8,128)(2,1)S(1)}, u32[]{:S(2)}, u32[]{:S(2)}) collective-permute-start(bf16[2,4,128,128]{3,2,1,0:T(8,128)(2,1)S(1)} %select.3.after_hbm), channel_id=1, source_target_pairs={{0,2},{1,5},{2,0},{3,7},{4,6},{5,1},{6,4},{7,3},{8,10},{9,13},{10,... | collective-permute-start | bytes 786440 | tf_op jit(solution)/shard_map/ppermute | solution.py:307
  13.4 6.1 %collective-permute-start.5 = (bf16[3,4,128,128]{3,2,1,0:T(8,128)(2,1)S(1)}, bf16[3,4,128,128]{3,2,1,0:T(8,128)(2,1)S(1)}, u32[]{:S(2)}, u32[]{:S(2)}) collective-permute-start(bf16[3,4,128,128]{3,2,1,0:T(8,128)(2,1)S(1)} %collective-permute-done.2.rows_ref.refs_2_), channel_id=1, source_target_pairs={{0,1},{1,0},{2,3},{3,2},{4,5},{5,4},{6,7},{7,6},{8,9},{9,8},{10,11... | collective-permute-start | bytes 1179656 | tf_op jit(solution)/shard_map/ppermute | solution.py:302
  13.4 6.1 %collective-permute-start.4 = (bf16[3,4,128,128]{3,2,1,0:T(8,128)(2,1)S(1)}, bf16[3,4,128,128]{3,2,1,0:T(8,128)(2,1)S(1)}, u32[]{:S(2)}, u32[]{:S(2)}) collective-permute-start(bf16[3,4,128,128]{3,2,1,0:T(8,128)(2,1)S(1)} %mask.1.rows_ref.refs_0_), channel_id=1, source_target_pairs={{0,1},{1,0},{2,3},{3,2},{4,5},{5,4},{6,7},{7,6},{8,9},{9,8},{10,11... | collective-permute-start | bytes 1179656 | tf_op jit(solution)/shard_map/ppermute | solution.py:302
  13.9 7.1 %copy-start.2 = (s32[1,12]{1,0:T(1,128)S(1)}, s32[1,12]{1,0:T(1,128)}, u32[]{:S(2)}) copy-start(s32[1,12]{1,0:T(1,128)} %offset_ref.1) | copy-start | bytes 148
  17.6 1.9 %collective-permute-start.6 = (bf16[2,4,128,128]{3,2,1,0:T(8,128)(2,1)S(1)}, bf16[2,4,128,128]{3,2,1,0:T(8,128)(2,1)S(1)}, u32[]{:S(2)}, u32[]{:S(2)}) collective-permute-start(bf16[2,4,128,128]{3,2,1,0:T(8,128)(2,1)S(1)} %collective-permute-done.3.refs_4_), channel_id=1, source_target_pairs={{0,1},{1,0},{2,3},{3,2},{4,5},{5,4},{6,7},{7,6},{8,9},{9,8},{10,11... | collective-permute-start | bytes 786440 | tf_op jit(solution)/shard_map/ppermute | solution.py:302
  19.5 1.5 %collective-permute-start.8 = (bf16[2,4,128,128]{3,2,1,0:T(8,128)(2,1)S(1)}, bf16[2,4,128,128]{3,2,1,0:T(8,128)(2,1)S(1)}, u32[]{:S(2)}, u32[]{:S(2)}) collective-permute-start(bf16[2,4,128,128]{3,2,1,0:T(8,128)(2,1)S(1)} %collective-permute-done.7.refs_6_), channel_id=1, source_target_pairs={{0,1},{1,0},{2,3},{3,2},{4,5},{5,4},{6,7},{7,6},{8,9},{9,8},{10,11... | collective-permute-start | bytes 786440 | tf_op jit(solution)/shard_map/ppermute | solution.py:302
  24.2 1.2 %collective-permute-start.9 = (f32[32,128]{1,0:T(8,128)S(1)}, f32[32,128]{1,0:T(8,128)S(1)}, u32[]{:S(2)}, u32[]{:S(2)}) collective-permute-start(f32[32,128]{1,0:T(8,128)S(1)} %get-tuple-element.44), channel_id=1, source_target_pairs={{0,1},{1,0},{2,3},{3,2},{4,5},{5,4},{6,7},{7,6},{8,9},{9,8},{10,11... | collective-permute-start | bytes 49160 | tf_op jit(solution)/shard_map/ppermute | solution.py:302
  25.5 5.6 %collective-permute-start.12 = (f32[2,32,128]{2,1,0:T(8,128)S(1)}, f32[2,32,128]{2,1,0:T(8,128)S(1)}, u32[]{:S(2)}, u32[]{:S(2)}) collective-permute-start(f32[2,32,128]{2,1,0:T(8,128)S(1)} %pad_maximum_fusion.after_hbm.refs_0_), channel_id=1, source_target_pairs={{0,6},{1,7},{2,4},{3,5},{4,2},{5,3},{6,0},{7,1},{8,14},{9,15},{10,... | collective-permute-start | bytes 98312 | tf_op jit(solution)/shard_map/ppermute | solution.py:302
  26.9 4.1 %collective-permute-start.11 = (f32[2,32,128]{2,1,0:T(8,128)S(1)}, f32[2,32,128]{2,1,0:T(8,128)S(1)}, u32[]{:S(2)}, u32[]{:S(2)}) collective-permute-start(f32[2,32,128]{2,1,0:T(8,128)S(1)} %pad_maximum_fusion.after_hbm.refs_0_), channel_id=1, source_target_pairs={{0,4},{1,5},{2,6},{3,7},{4,0},{5,1},{6,2},{7,3},{8,12},{9,13},{10,... | collective-permute-start | bytes 98312 | tf_op jit(solution)/shard_map/ppermute | solution.py:302
  28.4 3.9 %collective-permute-start.10 = (f32[2,32,128]{2,1,0:T(8,128)S(1)}, f32[2,32,128]{2,1,0:T(8,128)S(1)}, u32[]{:S(2)}, u32[]{:S(2)}) collective-permute-start(f32[2,32,128]{2,1,0:T(8,128)S(1)} %pad_maximum_fusion.after_hbm.refs_0_), channel_id=1, source_target_pairs={{0,2},{1,3},{2,0},{3,1},{4,6},{5,7},{6,4},{7,5},{8,10},{9,11},{10,... | collective-permute-start | bytes 98312 | tf_op jit(solution)/shard_map/ppermute | solution.py:302
  32.7 6.5 %collective-permute-start.13 = (f32[32,256]{1,0:T(8,128)S(1)}, f32[32,256]{1,0:T(8,128)S(1)}, u32[]{:S(2)}, u32[]{:S(2)}) collective-permute-start(f32[32,256]{1,0:T(8,128)S(1)} %get-tuple-element.50), channel_id=1, source_target_pairs={{0,24},{8,16},{16,8},{24,0},{1,25},{9,17},{17,9},{25,1},{2,26},{10... | collective-permute-start | bytes 98312 | tf_op jit(solution)/shard_map/ppermute | solution.py:302
  36.4 4.8 %collective-permute-start.14 = (f32[32,256]{1,0:T(8,128)S(1)}, f32[32,256]{1,0:T(8,128)S(1)}, u32[]{:S(2)}, u32[]{:S(2)}) collective-permute-start(f32[32,256]{1,0:T(8,128)S(1)} %get-tuple-element.51), channel_id=1, source_target_pairs={{0,16},{8,24},{16,0},{24,8},{1,17},{9,25},{17,1},{25,9},{2,18},{10... | collective-permute-start | bytes 98312 | tf_op jit(solution)/shard_map/ppermute | solution.py:302
  36.4 4.8 %collective-permute-start.15 = (f32[32,256]{1,0:T(8,128)S(1)}, f32[32,256]{1,0:T(8,128)S(1)}, u32[]{:S(2)}, u32[]{:S(2)}) collective-permute-start(f32[32,256]{1,0:T(8,128)S(1)} %get-tuple-element.52), channel_id=1, source_target_pairs={{0,8},{8,0},{16,24},{24,16},{1,9},{9,1},{17,25},{25,17},{2,10},{10... | collective-permute-start | bytes 98312 | tf_op jit(solution)/shard_map/ppermute | solution.py:302

commit v16 on v15

--- a/solution.py
+++ b/solution.py
@@ -49,7 +49,16 @@
     return ahead, lax.rem(start + ahead, stored * owners) // owners
 
 
-def select_kernel(even, odd, owners, starts_ref, rows_ref, out_ref):
+def select_kernel(even, odd, owners, starts_ref, mask_ref, raw_ref, out_ref, rows_ref):
+    factors = mask_ref[...].astype(jnp.float32)
+    for t in range(raw_ref.shape[0]):
+        for k in range(raw_ref.shape[1]):
+            factor = jnp.broadcast_to(factors[t : t + 1, k : k + 1], raw_ref.shape[2:])
+            rows_ref[t, k] = raw_ref[t, k] * factor.astype(jnp.bfloat16)
+    pick_rows(even, odd, owners, starts_ref, rows_ref, out_ref)
+
+
+def pick_rows(even, odd, owners, starts_ref, rows_ref, out_ref):
     me = lax.axis_index("dev")
     owner = lax.bitwise_xor(me, jnp.where(lax.rem(me, 2) == 1, odd, even))
     stored, band, width = rows_ref.shape[:3]
@@ -391,26 +400,30 @@
             name="turn",
         )(after, atom_near.T, batch_sizes, *held_in_hbm(basis_values, partition, harmonics))
 
-    def selected(even, odd, starts, rows):
+    def selected(even, odd, starts, rows, mask=None):
+        picked = pltpu.VMEM((2,) + density_rows.shape[1:], bf16)
+        kernel = pick_rows if mask is None else select_kernel
+        operands = (starts, rows) if mask is None else (starts, mask, rows)
         return pl.pallas_call(
-            functools.partial(select_kernel, even, odd, dev_count),
-            out_shape=pltpu.VMEM((2,) + density_rows.shape[1:], bf16),
-            in_specs=[VMEM, VMEM],
-            out_specs=VMEM,
+            functools.partial(kernel, even, odd, dev_count),
+            out_shape=picked if mask is None else (picked, pltpu.VMEM(density_rows.shape, bf16)),
+            in_specs=[VMEM] * len(operands),
+            out_specs=VMEM if mask is None else (VMEM, VMEM),
             compiler_params=PARAMS,
             name="select",
-        )(starts, rows)
+        )(*operands)
 
     if dev_count == 8:
         opening = window_start[None]
+        first = turned(density_rows, 4, 2)
         beside = crossed(opening, "dev", 1)
-        beside, rows = lax.optimization_barrier((beside, masked))
-        first = turned(rows, 4, 2)
+        beside, masked = lax.optimization_barrier((beside, masked))
         starts = turned(jnp.concatenate([opening, beside], axis=1), 2, 4)
+        first_mask = turned(block_mask, 4, 2)
         chosen = selected(0, 0, starts, masked)
         second = turned(chosen, 2, 4)
-        first, later, _ = lax.optimization_barrier((first, masked, chosen))
-        chosen = selected(4, 2, starts, first)
+        first, later, first_mask, _ = lax.optimization_barrier((first, masked, first_mask, chosen))
+        chosen, first = selected(4, 2, starts, first, first_mask)
         third = turned(chosen, 2, 4)
         phit, weights, hpad, atom_rows, alive = turned_basis(chosen)
         second, phit = lax.optimization_barrier((second, phit))

time: 42.9 us -> 43.2 us (level)
  waiting for transfers between devices: 9.15 us -> 9.8 us
    ppermute x4 -> x5, waiting for transfers between devices: 3.97 us -> 5.13 us  [turned(): lax.ppermute(value, 'dev', [(i, i ^ (odd if i % 2 else even)) for i in ra...]
    ppermute x12, starting transfers between devices: 9.27 us -> 8.73 us  [crossed(): lax.ppermute(value, axis, [(i, i ^ m) for i in range(lax.axis_size(axis))])]
    ppermute x12, waiting for transfers between devices: 5.18 us -> 4.67 us  [crossed(): lax.ppermute(value, axis, [(i, i ^ m) for i in range(lax.axis_size(axis))])]
    ppermute x4 -> x5, starting transfers between devices: 7.03 us -> 7.19 us  [turned(): lax.ppermute(value, 'dev', [(i, i ^ (odd if i % 2 else even)) for i in ra...]
  transfers between devices with their start and end apart: 16 -> 17, of which waited for: 6 -> 7; matrix products, arithmetic and copies ran while one was open for 3% -> 3% of each run, Pallas kernels for 22% -> 22%
where the time goes in v16:
time: 43.2 us; the launch traced here: 42.9 us
  starting transfers between devices  15.9 us (37%)
  Pallas kernels  14.4 us (33%)
  waiting for transfers between devices  9.8 us (23%)
  between operations  1.42 us (3%)
  other arithmetic  0.7 us (2%)
  local copies, waits for them, and re-layouts  0.62 us (1%)
    ppermute x12, starting transfers between devices, crossed(): lax.ppermute(value, axis, [(i, i ^ m) for i in range(lax.axis_size(axis))])  8.73 us
    ppermute x5, starting transfers between devices, turned(): lax.ppermute(value, 'dev', [(i, i ^ (odd if i % 2 else even)) for i in ra...  7.19 us
    ppermute x5, waiting for transfers between devices, turned(): lax.ppermute(value, 'dev', [(i, i ^ (odd if i % 2 else even)) for i in ra...  5.13 us
    ppermute x12, waiting for transfers between devices, crossed(): lax.ppermute(value, axis, [(i, i ^ m) for i in range(lax.axis_size(axis))])  4.67 us
    pallas_call x2, Pallas kernels, field(): pl.pallas_call(functools.partial(field_kernel, begin), out_shape=pltpu.VM...  4.14 us
    pallas_call x1, Pallas kernels, turned_basis(): pl.pallas_call(turn_kernel, out_shape=(pltpu.VMEM((batches, near_blocks,...  3.65 us
    pallas_call x1, Pallas kernels, per_device(): pl.pallas_call(density_kernel, out_shape=(pltpu.VMEM((batches, points), f...  3.17 us
    pallas_call x1, Pallas kernels, per_device(): pl.pallas_call(functools.partial(potential_kernel, comps, atoms, flip), o...  1.34 us
  transfers between devices with their start and end apart: 17, of which 7 were waited for; matrix products, arithmetic and copies ran while one was open for 3% of the time, Pallas kernels for 22%

profile of v16, /device:TPU:0, one launch (start us, length us, event | category | flops | bytes accessed | tf_op | source)
XLA Modules:
  0.0 42.9 jit_solution(8486820863408286766)
XLA Ops:
  0.6 3.0 %collective-permute-start.2 = (bf16[3,4,128,128]{3,2,1,0:T(8,128)(2,1)}, bf16[3,4,128,128]{3,2,1,0:T(8,128)(2,1)S(1)}, u32[]{:S(2)}, u32[]{:S(2)}) collective-permute-start(bf16[3,4,128,128]{3,2,1,0:T(8,128)(2,1)} %rows_hbm.1), channel_id=1, source_target_pairs={{0,4},{1,3},{2,6},{3,1},{4,0},{5,7},{6,2},{7,5},{8,12},{9,11},{10,... | collective-permute-start | bytes 1179656 | tf_op jit(solution)/shard_map/ppermute | solution.py:316
  3.7 0.0 collective-permute-start
  3.7 1.0 %collective-permute-start.3 = (s32[3,4]{1,0:T(4,128)}, s32[3,4]{1,0:T(4,128)S(1)}, u32[]{:S(2)}, u32[]{:S(2)}) collective-permute-start(s32[3,4]{1,0:T(4,128)} %mask_hbm.1), channel_id=1, source_target_pairs={{0,4},{1,3},{2,6},{3,1},{4,0},{5,7},{6,2},{7,5},{8,12},{9,11},{10,... | collective-permute-start | bytes 152 | tf_op jit(solution)/shard_map/ppermute | solution.py:316
  5.4 0.0 copy-start
  5.4 0.0 copy-start.1
  5.4 1.3 %mask.1.rows_ref.refs_0_ = bf16[3,4,128,128]{3,2,1,0:T(8,128)(2,1)S(1)} custom-call(s32[3,4]{1,0:T(4,128)} %mask_hbm.1, bf16[3,4,128,128]{3,2,1,0:T(8,128)(2,1)} %rows_hbm.1), custom_call_target="tpu_custom_call" | custom-call | flops 2000000000 | bytes 8000000 | tf_op jit(solution)/shard_map/mask/pallas_call | solution.py:347
  6.7 0.0 collective-permute-done
  6.7 0.7 %pad_add_fusion = s32[1,2]{1,0:T(1,128)S(1)} fusion(s32[1,1]{1,0:T(1,128)} %collective-permute-done, s32[1,1]{1,0:T(1,128)} %bitcast.6), kind=kLoop, calls=%fused_computation.1 | loop fusion | flops 2 | bytes 16 | tf_op jit(solution)/shard_map/concatenate | solution.py:421
  7.4 1.0 %collective-permute-start.1 = (s32[1,2]{1,0:T(1,128)S(1)}, s32[1,2]{1,0:T(1,128)S(1)}, u32[]{:S(2)}, u32[]{:S(2)}) collective-permute-start(s32[1,2]{1,0:T(1,128)S(1)} %pad_add_fusion), channel_id=1, source_target_pairs={{0,2},{1,5},{2,0},{3,7},{4,6},{5,1},{6,4},{7,3},{8,10},{9,13},{10,... | collective-permute-start | bytes 32 | tf_op jit(solution)/shard_map/ppermute | solution.py:316
  8.4 2.6 %collective-permute-done.1.starts_ref = s32[1,2]{1,0:T(1,128)S(1)} collective-permute-done((s32[1,2]{1,0:T(1,128)S(1)}, s32[1,2]{1,0:T(1,128)S(1)}, u32[]{:S(2)}, u32[]{:S(2)}) %collective-permute-start.1) | collective-permute-done | bytes 40 | tf_op jit(solution)/shard_map/ppermute | solution.py:316
  11.0 0.2 select.2
  11.1 1.0 %collective-permute-start.4 = (bf16[2,4,128,128]{3,2,1,0:T(8,128)(2,1)S(1)}, bf16[2,4,128,128]{3,2,1,0:T(8,128)(2,1)S(1)}, u32[]{:S(2)}, u32[]{:S(2)}) collective-permute-start(bf16[2,4,128,128]{3,2,1,0:T(8,128)(2,1)S(1)} %select.2), channel_id=1, source_target_pairs={{0,2},{1,5},{2,0},{3,7},{4,6},{5,1},{6,4},{7,3},{8,10},{9,13},{10,... | collective-permute-start | bytes 786440 | tf_op jit(solution)/shard_map/ppermute | solution.py:316
  12.2 0.0 collective-permute-done.3.mask_ref
  12.2 0.0 collective-permute-done.2.raw_ref
  12.2 0.3 select.3
  12.4 1.1 %collective-permute-start.8 = (bf16[2,4,128,128]{3,2,1,0:T(8,128)(2,1)S(1)}, bf16[2,4,128,128]{3,2,1,0:T(8,128)(2,1)S(1)}, u32[]{:S(2)}, u32[]{:S(2)}) collective-permute-start(bf16[2,4,128,128]{3,2,1,0:T(8,128)(2,1)S(1)} %get-tuple-element.39.after_hbm), channel_id=1, source_target_pairs={{0,2},{1,5},{2,0},{3,7},{4,6},{5,1},{6,4},{7,3},{8,10},{9,13},{10,... | collective-permute-start | bytes 786440 | tf_op jit(solution)/shard_map/ppermute | solution.py:316
  13.6 0.0 collective-permute-start.6
  13.6 0.5 %collective-permute-start.5 = (bf16[3,4,128,128]{3,2,1,0:T(8,128)(2,1)S(1)}, bf16[3,4,128,128]{3,2,1,0:T(8,128)(2,1)S(1)}, u32[]{:S(2)}, u32[]{:S(2)}) collective-permute-start(bf16[3,4,128,128]{3,2,1,0:T(8,128)(2,1)S(1)} %mask.1.rows_ref.refs_0_), channel_id=1, source_target_pairs={{0,1},{1,0},{2,3},{3,2},{4,5},{5,4},{6,7},{7,6},{8,9},{9,8},{10,11... | collective-permute-start | bytes 1179656 | tf_op jit(solution)/shard_map/ppermute | solution.py:311
  14.1 0.0 copy-done
  14.1 0.0 copy-done.1
  14.1 0.0 copy-start.2
  14.1 3.7 %turn.1 = (bf16[12,4,128,256]{3,2,1,0:T(8,128)(2,1)S(1)}, f32[12,6,256]{2,1,0:T(8,128)S(1)}, bf16[72,32,256]{2,1,0:T(8,128)(2,1)S(1)}, s32[1,128]{1,0:T(1,128)S(1)}, f32[12,256]{1,0:T(8,128)S(1)}) custom-call(bf16[2,4,128,128]{3,2,1,0:T(8,128)(2,1)S(1)} %get-tuple-element.39.after_hbm, s32[6,12]{1,0:T(8,128)S(1)} %bitcast.8, s32[1,12]{1,0:T(1,128)S(1)} %copy-done.1, ...), custom_call_target="tpu_custom_call" | custom-call | flops 2000000000 | bytes 8000000 | tf_op jit(solution)/shard_map/turn/pallas_call | solution.py:382
  17.8 0.0 collective-permute-done.4.refs_4_
  17.8 0.1 collective-permute-start.7
  17.9 2.5 %collective-permute-done.8.refs_6_ = bf16[2,4,128,128]{3,2,1,0:T(8,128)(2,1)S(1)} collective-permute-done((bf16[2,4,128,128]{3,2,1,0:T(8,128)(2,1)S(1)}, bf16[2,4,128,128]{3,2,1,0:T(8,128)(2,1)S(1)}, u32[]{:S(2)}, u32[]{:S(2)}) %collective-permute-start.8) | collective-permute-done | bytes 262176 | tf_op jit(solution)/shard_map/ppermute | solution.py:316
  20.4 0.0 collective-permute-start.9
  20.4 0.0 collective-permute-done.7.refs_5_
  20.4 0.0 collective-permute-done.6.refs_3_
  20.4 0.0 collective-permute-done.5.refs_1_
  20.4 1.5 %collective-permute-done.9.refs_7_ = bf16[2,4,128,128]{3,2,1,0:T(8,128)(2,1)S(1)} collective-permute-done((bf16[2,4,128,128]{3,2,1,0:T(8,128)(2,1)S(1)}, bf16[2,4,128,128]{3,2,1,0:T(8,128)(2,1)S(1)}, u32[]{:S(2)}, u32[]{:S(2)}) %collective-permute-start.9) | collective-permute-done | bytes 262176 | tf_op jit(solution)/shard_map/ppermute | solution.py:311
  21.9 0.0 copy-done.2
  21.9 3.2 %density.1 = (f32[12,256]{1,0:T(8,128)S(1)}, f32[32,128]{1,0:T(8,128)S(1)}) custom-call(s32[1]{0:T(128)} %copy.15.start_ref, s32[1,12]{1,0:T(1,128)S(1)} %copy-done.2, s32[1,128]{1,0:T(1,128)S(1)} %get-tuple-element.40.atom_ref, f32[12,256]{1,0:T(8,128)S(1)} %get-tuple-element.41.alive_ref, bf16[12,4,128,256]{3,2,1,0:T(8,128)(2,1)S(1)} %get-tuple-element.43.phit_ref, ...), custom_call_target="tpu_custom_call" | custom-call | flops 2000000000 | bytes 6000000 | tf_op jit(solution)/shard_map/density/pallas_call | solution.py:436
  25.1 0.2 collective-permute-start.10
  25.3 0.6 %copy.14 = f32[12,256]{1,0:T(8,128)} copy(f32[12,256]{1,0:T(8,128)S(1)} %get-tuple-element.67) | data formatting | bytes 24576
  25.9 0.5 %collective-permute-done.10 = f32[32,128]{1,0:T(8,128)S(1)} collective-permute-done((f32[32,128]{1,0:T(8,128)S(1)}, f32[32,128]{1,0:T(8,128)S(1)}, u32[]{:S(2)}, u32[]{:S(2)}) %collective-permute-start.10) | collective-permute-done | bytes 16416 | tf_op jit(solution)/shard_map/ppermute | solution.py:311
  26.4 1.9 %collective-permute-start.13 = (f32[2,32,128]{2,1,0:T(8,128)S(1)}, f32[2,32,128]{2,1,0:T(8,128)S(1)}, u32[]{:S(2)}, u32[]{:S(2)}) collective-permute-start(f32[2,32,128]{2,1,0:T(8,128)S(1)} %pad_maximum_fusion.after_hbm.refs_0_), channel_id=1, source_target_pairs={{0,6},{1,7},{2,4},{3,5},{4,2},{5,3},{6,0},{7,1},{8,14},{9,15},{10,... | collective-permute-start | bytes 98312 | tf_op jit(solution)/shard_map/ppermute | solution.py:311
  28.3 0.5 %collective-permute-start.12 = (f32[2,32,128]{2,1,0:T(8,128)S(1)}, f32[2,32,128]{2,1,0:T(8,128)S(1)}, u32[]{:S(2)}, u32[]{:S(2)}) collective-permute-start(f32[2,32,128]{2,1,0:T(8,128)S(1)} %pad_maximum_fusion.after_hbm.refs_0_), channel_id=1, source_target_pairs={{0,4},{1,5},{2,6},{3,7},{4,0},{5,1},{6,2},{7,3},{8,12},{9,13},{10,... | collective-permute-start | bytes 98312 | tf_op jit(solution)/shard_map/ppermute | solution.py:311
  28.8 1.1 %collective-permute-start.11 = (f32[2,32,128]{2,1,0:T(8,128)S(1)}, f32[2,32,128]{2,1,0:T(8,128)S(1)}, u32[]{:S(2)}, u32[]{:S(2)}) collective-permute-start(f32[2,32,128]{2,1,0:T(8,128)S(1)} %pad_maximum_fusion.after_hbm.refs_0_), channel_id=1, source_target_pairs={{0,2},{1,3},{2,0},{3,1},{4,6},{5,7},{6,4},{7,5},{8,10},{9,11},{10,... | collective-permute-start | bytes 98312 | tf_op jit(solution)/shard_map/ppermute | solution.py:311
  29.9 2.1 %field.2.low_ref = f32[36,25,256]{2,1,0:T(8,128)S(1)} custom-call(f32[2,32,128]{2,1,0:T(8,128)S(1)} %pad_maximum_fusion.after_hbm.refs_0_, f32[12,256]{1,0:T(8,128)S(1)} %get-tuple-element.41.alive_ref, f32[16,25]{1,0:T(8,128)} %bitcast.10, f32[12,6,256]{2,1,0:T(8,128)} %radius_hbm.3, bf16[12,6,25,256]{3,2,1,0:T(8,128)(2,1)} %harm_hbm.5), custom_call_target="tpu_custom_call" | custom-call | flops 2000000000 | bytes 8000000 | tf_op jit(solution)/shard_map/field/pallas_call | solution.py:365
  31.9 0.0 collective-permute-done.13.refs_3_
  31.9 0.2 collective-permute-done.12.refs_2_
  32.2 0.5 %collective-permute-done.11.refs_1_ = f32[2,32,128]{2,1,0:T(8,128)S(1)} collective-permute-done((f32[2,32,128]{2,1,0:T(8,128)S(1)}, f32[2,32,128]{2,1,0:T(8,128)S(1)}, u32[]{:S(2)}, u32[]{:S(2)}) %collective-permute-start.11) | collective-permute-done | bytes 32800 | tf_op jit(solution)/shard_map/ppermute | solution.py:311
  32.7 0.4 scatter.1
  33.1 3.7 %collective-permute-start.14 = (f32[32,256]{1,0:T(8,128)S(1)}, f32[32,256]{1,0:T(8,128)S(1)}, u32[]{:S(2)}, u32[]{:S(2)}) collective-permute-start(f32[32,256]{1,0:T(8,128)S(1)} %get-tuple-element.56), channel_id=1, source_target_pairs={{0,24},{8,16},{16,8},{24,0},{1,25},{9,17},{17,9},{25,1},{2,26},{10... | collective-permute-start | bytes 98312 | tf_op jit(solution)/shard_map/ppermute | solution.py:311
  36.7 0.0 collective-permute-start.15
  36.7 0.8 %collective-permute-start.16 = (f32[32,256]{1,0:T(8,128)S(1)}, f32[32,256]{1,0:T(8,128)S(1)}, u32[]{:S(2)}, u32[]{:S(2)}) collective-permute-start(f32[32,256]{1,0:T(8,128)S(1)} %get-tuple-element.58), channel_id=1, source_target_pairs={{0,8},{8,0},{16,24},{24,16},{1,9},{9,1},{17,25},{25,17},{2,10},{10... | collective-permute-start | bytes 98312 | tf_op jit(solution)/shard_map/ppermute | solution.py:311
  37.5 2.1 %field.3.high_ref = f32[36,25,256]{2,1,0:T(8,128)S(1)} custom-call(f32[32,384]{1,0:T(8,128)S(1)} %get-tuple-element.55.after_hbm.own_ref, f32[12,256]{1,0:T(8,128)S(1)} %get-tuple-element.41.alive_ref, f32[16,25]{1,0:T(8,128)} %bitcast.11, f32[12,6,256]{2,1,0:T(8,128)} %radius_hbm.3, bf16[12,6,25,256]{3,2,1,0:T(8,128)(2,1)} %harm_hbm.5), custom_call_target="tpu_custom_call" | custom-call | flops 2000000000 | bytes 8000000 | tf_op jit(solution)/shard_map/field/pallas_call | solution.py:365
  39.6 0.0 collective-permute-done.14.near_b_ref
  39.6 1.9 %collective-permute-done.15.fa_ref.fb_ref = f32[32,256]{1,0:T(8,128)S(1)} collective-permute-done((f32[32,256]{1,0:T(8,128)S(1)}, f32[32,256]{1,0:T(8,128)S(1)}, u32[]{:S(2)}, u32[]{:S(2)}) %collective-permute-start.15) | collective-permute-done | bytes 32800 | tf_op jit(solution)/shard_map/ppermute | solution.py:311
  41.5 0.0 collective-permute-done.16.near_a_ref
  41.6 1.3 %potential.1 = (f32[16,25]{1,0:T(8,128)}, f32[12,256]{1,0:T(8,128)}) custom-call(f32[32,384]{1,0:T(8,128)S(1)} %get-tuple-element.55.after_hbm.own_ref, f32[32,256]{1,0:T(8,128)S(1)} %collective-permute-done.14.near_b_ref, f32[32,256]{1,0:T(8,128)S(1)} %collective-permute-done.15.fa_ref.fb_ref, f32[32,256]{1,0:T(8,128)S(1)} %collective-permute-done.15.fa_ref.fb_ref, ...), custom_call_target="tpu_custom_call" | custom-call | tf_op jit(solution)/shard_map/potential/pallas_call | solution.py:487
  (1 shorter events, 0.0 us)
Async XLA Ops:
  0.6 11.5 %collective-permute-start.2 = (bf16[3,4,128,128]{3,2,1,0:T(8,128)(2,1)}, bf16[3,4,128,128]{3,2,1,0:T(8,128)(2,1)S(1)}, u32[]{:S(2)}, u32[]{:S(2)}) collective-permute-start(bf16[3,4,128,128]{3,2,1,0:T(8,128)(2,1)} %rows_hbm.1), channel_id=1, source_target_pairs={{0,4},{1,3},{2,6},{3,1},{4,0},{5,7},{6,2},{7,5},{8,12},{9,11},{10,... | collective-permute-start | bytes 1179656 | tf_op jit(solution)/shard_map/ppermute | solution.py:316
  3.7 3.0 %collective-permute-start = (s32[1,1]{1,0:T(1,128)}, s32[1,1]{1,0:T(1,128)}, u32[]{:S(2)}, u32[]{:S(2)}) collective-permute-start(s32[1,1]{1,0:T(1,128)} %bitcast), channel_id=1, source_target_pairs={{0,1},{1,0},{2,3},{3,2},{4,5},{5,4},{6,7},{7,6},{8,9},{9,8},{10,11... | collective-permute-start | bytes 20 | tf_op jit(solution)/shard_map/ppermute | solution.py:311
  3.7 8.5 %collective-permute-start.3 = (s32[3,4]{1,0:T(4,128)}, s32[3,4]{1,0:T(4,128)S(1)}, u32[]{:S(2)}, u32[]{:S(2)}) collective-permute-start(s32[3,4]{1,0:T(4,128)} %mask_hbm.1), channel_id=1, source_target_pairs={{0,4},{1,3},{2,6},{3,1},{4,0},{5,7},{6,2},{7,5},{8,12},{9,11},{10,... | collective-permute-start | bytes 152 | tf_op jit(solution)/shard_map/ppermute | solution.py:316
  5.4 8.7 %copy-start = (s32[12,6]{0,1:T(8,128)S(1)}, s32[12,6]{0,1:T(8,128)}, u32[]{:S(2)}) copy-start(s32[12,6]{0,1:T(8,128)} %param.17) | copy-start | bytes 868
  5.4 8.7 %copy-start.1 = (s32[1,12]{1,0:T(1,128)S(1)}, s32[1,12]{1,0:T(1,128)}, u32[]{:S(2)}) copy-start(s32[1,12]{1,0:T(1,128)} %size_ref.1) | copy-start | bytes 148
  7.4 3.5 %collective-permute-start.1 = (s32[1,2]{1,0:T(1,128)S(1)}, s32[1,2]{1,0:T(1,128)S(1)}, u32[]{:S(2)}, u32[]{:S(2)}) collective-permute-start(s32[1,2]{1,0:T(1,128)S(1)} %pad_add_fusion), channel_id=1, source_target_pairs={{0,2},{1,5},{2,0},{3,7},{4,6},{5,1},{6,4},{7,3},{8,10},{9,13},{10,... | collective-permute-start | bytes 32 | tf_op jit(solution)/shard_map/ppermute | solution.py:316
  11.1 6.6 %collective-permute-start.4 = (bf16[2,4,128,128]{3,2,1,0:T(8,128)(2,1)S(1)}, bf16[2,4,128,128]{3,2,1,0:T(8,128)(2,1)S(1)}, u32[]{:S(2)}, u32[]{:S(2)}) collective-permute-start(bf16[2,4,128,128]{3,2,1,0:T(8,128)(2,1)S(1)} %select.2), channel_id=1, source_target_pairs={{0,2},{1,5},{2,0},{3,7},{4,6},{5,1},{6,4},{7,3},{8,10},{9,13},{10,... | collective-permute-start | bytes 786440 | tf_op jit(solution)/shard_map/ppermute | solution.py:316
  12.4 8.0 %collective-permute-start.8 = (bf16[2,4,128,128]{3,2,1,0:T(8,128)(2,1)S(1)}, bf16[2,4,128,128]{3,2,1,0:T(8,128)(2,1)S(1)}, u32[]{:S(2)}, u32[]{:S(2)}) collective-permute-start(bf16[2,4,128,128]{3,2,1,0:T(8,128)(2,1)S(1)} %get-tuple-element.39.after_hbm), channel_id=1, source_target_pairs={{0,2},{1,5},{2,0},{3,7},{4,6},{5,1},{6,4},{7,3},{8,10},{9,13},{10,... | collective-permute-start | bytes 786440 | tf_op jit(solution)/shard_map/ppermute | solution.py:316
  13.6 6.8 %collective-permute-start.6 = (bf16[3,4,128,128]{3,2,1,0:T(8,128)(2,1)S(1)}, bf16[3,4,128,128]{3,2,1,0:T(8,128)(2,1)S(1)}, u32[]{:S(2)}, u32[]{:S(2)}) collective-permute-start(bf16[3,4,128,128]{3,2,1,0:T(8,128)(2,1)S(1)} %get-tuple-element.47.refs_2_), channel_id=1, source_target_pairs={{0,1},{1,0},{2,3},{3,2},{4,5},{5,4},{6,7},{7,6},{8,9},{9,8},{10,11... | collective-permute-start | bytes 1179656 | tf_op jit(solution)/shard_map/ppermute | solution.py:311
  13.6 6.8 %collective-permute-start.5 = (bf16[3,4,128,128]{3,2,1,0:T(8,128)(2,1)S(1)}, bf16[3,4,128,128]{3,2,1,0:T(8,128)(2,1)S(1)}, u32[]{:S(2)}, u32[]{:S(2)}) collective-permute-start(bf16[3,4,128,128]{3,2,1,0:T(8,128)(2,1)S(1)} %mask.1.rows_ref.refs_0_), channel_id=1, source_target_pairs={{0,1},{1,0},{2,3},{3,2},{4,5},{5,4},{6,7},{7,6},{8,9},{9,8},{10,11... | collective-permute-start | bytes 1179656 | tf_op jit(solution)/shard_map/ppermute | solution.py:311
  14.1 7.8 %copy-start.2 = (s32[1,12]{1,0:T(1,128)S(1)}, s32[1,12]{1,0:T(1,128)}, u32[]{:S(2)}) copy-start(s32[1,12]{1,0:T(1,128)} %offset_ref.1) | copy-start | bytes 148
  17.8 2.6 %collective-permute-start.7 = (bf16[2,4,128,128]{3,2,1,0:T(8,128)(2,1)S(1)}, bf16[2,4,128,128]{3,2,1,0:T(8,128)(2,1)S(1)}, u32[]{:S(2)}, u32[]{:S(2)}) collective-permute-start(bf16[2,4,128,128]{3,2,1,0:T(8,128)(2,1)S(1)} %collective-permute-done.4.refs_4_), channel_id=1, source_target_pairs={{0,1},{1,0},{2,3},{3,2},{4,5},{5,4},{6,7},{7,6},{8,9},{9,8},{10,11... | collective-permute-start | bytes 786440 | tf_op jit(solution)/shard_map/ppermute | solution.py:311
  20.4 1.5 %collective-permute-start.9 = (bf16[2,4,128,128]{3,2,1,0:T(8,128)(2,1)S(1)}, bf16[2,4,128,128]{3,2,1,0:T(8,128)(2,1)S(1)}, u32[]{:S(2)}, u32[]{:S(2)}) collective-permute-start(bf16[2,4,128,128]{3,2,1,0:T(8,128)(2,1)S(1)} %collective-permute-done.8.refs_6_), channel_id=1, source_target_pairs={{0,1},{1,0},{2,3},{3,2},{4,5},{5,4},{6,7},{7,6},{8,9},{9,8},{10,11... | collective-permute-start | bytes 786440 | tf_op jit(solution)/shard_map/ppermute | solution.py:311
  25.1 1.2 %collective-permute-start.10 = (f32[32,128]{1,0:T(8,128)S(1)}, f32[32,128]{1,0:T(8,128)S(1)}, u32[]{:S(2)}, u32[]{:S(2)}) collective-permute-start(f32[32,128]{1,0:T(8,128)S(1)} %get-tuple-element.50), channel_id=1, source_target_pairs={{0,1},{1,0},{2,3},{3,2},{4,5},{5,4},{6,7},{7,6},{8,9},{9,8},{10,11... | collective-permute-start | bytes 49160 | tf_op jit(solution)/shard_map/ppermute | solution.py:311
  26.4 5.6 %collective-permute-start.13 = (f32[2,32,128]{2,1,0:T(8,128)S(1)}, f32[2,32,128]{2,1,0:T(8,128)S(1)}, u32[]{:S(2)}, u32[]{:S(2)}) collective-permute-start(f32[2,32,128]{2,1,0:T(8,128)S(1)} %pad_maximum_fusion.after_hbm.refs_0_), channel_id=1, source_target_pairs={{0,6},{1,7},{2,4},{3,5},{4,2},{5,3},{6,0},{7,1},{8,14},{9,15},{10,... | collective-permute-start | bytes 98312 | tf_op jit(solution)/shard_map/ppermute | solution.py:311
  28.3 3.9 %collective-permute-start.12 = (f32[2,32,128]{2,1,0:T(8,128)S(1)}, f32[2,32,128]{2,1,0:T(8,128)S(1)}, u32[]{:S(2)}, u32[]{:S(2)}) collective-permute-start(f32[2,32,128]{2,1,0:T(8,128)S(1)} %pad_maximum_fusion.after_hbm.refs_0_), channel_id=1, source_target_pairs={{0,4},{1,5},{2,6},{3,7},{4,0},{5,1},{6,2},{7,3},{8,12},{9,13},{10,... | collective-permute-start | bytes 98312 | tf_op jit(solution)/shard_map/ppermute | solution.py:311
  28.8 3.9 %collective-permute-start.11 = (f32[2,32,128]{2,1,0:T(8,128)S(1)}, f32[2,32,128]{2,1,0:T(8,128)S(1)}, u32[]{:S(2)}, u32[]{:S(2)}) collective-permute-start(f32[2,32,128]{2,1,0:T(8,128)S(1)} %pad_maximum_fusion.after_hbm.refs_0_), channel_id=1, source_target_pairs={{0,2},{1,3},{2,0},{3,1},{4,6},{5,7},{6,4},{7,5},{8,10},{9,11},{10,... | collective-permute-start | bytes 98312 | tf_op jit(solution)/shard_map/ppermute | solution.py:311
  33.1 6.5 %collective-permute-start.14 = (f32[32,256]{1,0:T(8,128)S(1)}, f32[32,256]{1,0:T(8,128)S(1)}, u32[]{:S(2)}, u32[]{:S(2)}) collective-permute-start(f32[32,256]{1,0:T(8,128)S(1)} %get-tuple-element.56), channel_id=1, source_target_pairs={{0,24},{8,16},{16,8},{24,0},{1,25},{9,17},{17,9},{25,1},{2,26},{10... | collective-permute-start | bytes 98312 | tf_op jit(solution)/shard_map/ppermute | solution.py:311
  36.7 4.8 %collective-permute-start.15 = (f32[32,256]{1,0:T(8,128)S(1)}, f32[32,256]{1,0:T(8,128)S(1)}, u32[]{:S(2)}, u32[]{:S(2)}) collective-permute-start(f32[32,256]{1,0:T(8,128)S(1)} %get-tuple-element.57), channel_id=1, source_target_pairs={{0,16},{8,24},{16,0},{24,8},{1,17},{9,25},{17,1},{25,9},{2,18},{10... | collective-permute-start | bytes 98312 | tf_op jit(solution)/shard_map/ppermute | solution.py:311
  36.7 4.8 %collective-permute-start.16 = (f32[32,256]{1,0:T(8,128)S(1)}, f32[32,256]{1,0:T(8,128)S(1)}, u32[]{:S(2)}, u32[]{:S(2)}) collective-permute-start(f32[32,256]{1,0:T(8,128)S(1)} %get-tuple-element.58), channel_id=1, source_target_pairs={{0,8},{8,0},{16,24},{24,16},{1,9},{9,1},{17,25},{25,17},{2,10},{10... | collective-permute-start | bytes 98312 | tf_op jit(solution)/shard_map/ppermute | solution.py:311

commit v17 on v15

--- a/solution.py
+++ b/solution.py
@@ -254,7 +254,7 @@
 
 
 def potential_kernel(
-    comps, atoms, flip, own_ref, near_b_ref, fa_ref, fb_ref, near_a_ref, atom_ref,
+    comps, atoms, flip, own_ref, fa_ref, fb_ref, near_b_ref, near_a_ref, atom_ref,
     low_ref, high_ref, mom_ref, pot_ref,
 ):
     batches, points = pot_ref.shape
@@ -458,8 +458,8 @@
     )(*groups)
     g_high = field(half, own)
     if flip:
+        far_a = far_b = crossed(far, "region", 2)
         near_b = crossed(near_b, "region", 3)
-        far_a = far_b = crossed(far, "region", 2)
         near_a = crossed(near_a, "region", 1)
     else:
         far_a = shifted(far, "region", 2)
@@ -467,8 +467,8 @@
         near_a = shifted(near_a, "region", 1)
         near_b = shifted(near_b, "region", -1)
 
-    near_b, far_a, far_b, near_a, g_high = lax.optimization_barrier(
-        (near_b, far_a, far_b, near_a, g_high)
+    far_a, far_b, near_b, near_a, g_high = lax.optimization_barrier(
+        (far_a, far_b, near_b, near_a, g_high)
     )
 
     moments, potential = pl.pallas_call(
@@ -481,7 +481,7 @@
         out_specs=(VMEM, VMEM),
         compiler_params=PARAMS,
         name="potential",
-    )(own, near_b, far_a, far_b, near_a, atom_rows, g_low, g_high)
+    )(own, far_a, far_b, near_b, near_a, atom_rows, g_low, g_high)
     return (density, moments.T, potential)
 
 

time: 42.9 us -> 42.7 us (level)
  no operation moved by 1% of the time
where the time goes in v17:
time: 42.7 us; the launch traced here: 42.4 us
  starting transfers between devices  16.1 us (38%)
  Pallas kernels  14.3 us (33%)
  waiting for transfers between devices  9.26 us (22%)
  between operations  1.42 us (3%)
  other arithmetic  0.7 us (2%)
  local copies, waits for them, and re-layouts  0.62 us (1%)
    ppermute x12, starting transfers between devices, crossed(): lax.ppermute(value, axis, [(i, i ^ m) for i in range(lax.axis_size(axis))])  9.05 us
    ppermute x4, starting transfers between devices, turned(): lax.ppermute(value, 'dev', [(i, i ^ (odd if i % 2 else even)) for i in ra...  7.03 us
    ppermute x12, waiting for transfers between devices, crossed(): lax.ppermute(value, axis, [(i, i ^ m) for i in range(lax.axis_size(axis))])  5.3 us
    pallas_call x2, Pallas kernels, field(): pl.pallas_call(functools.partial(field_kernel, begin), out_shape=pltpu.VM...  4.15 us
    ppermute x4, waiting for transfers between devices, turned(): lax.ppermute(value, 'dev', [(i, i ^ (odd if i % 2 else even)) for i in ra...  3.97 us
    pallas_call x1, Pallas kernels, turned_basis(): pl.pallas_call(turn_kernel, out_shape=(pltpu.VMEM((batches, near_blocks,...  3.65 us
    pallas_call x1, Pallas kernels, per_device(): pl.pallas_call(density_kernel, out_shape=(pltpu.VMEM((batches, points), f...  3.16 us
    pallas_call x1, Pallas kernels, per_device(): pl.pallas_call(functools.partial(potential_kernel, comps, atoms, flip), o...  1.34 us
  transfers between devices with their start and end apart: 16, of which 6 were waited for; matrix products, arithmetic and copies ran while one was open for 3% of the time, Pallas kernels for 22%

profile of v17, /device:TPU:0, one launch (start us, length us, event | category | flops | bytes accessed | tf_op | source)
XLA Modules:
  0.0 42.4 jit_solution(10823929492022059777)
XLA Ops:
  0.6 0.5 %collective-permute-start = (s32[1,1]{1,0:T(1,128)}, s32[1,1]{1,0:T(1,128)}, u32[]{:S(2)}, u32[]{:S(2)}) collective-permute-start(s32[1,1]{1,0:T(1,128)} %bitcast), channel_id=1, source_target_pairs={{0,1},{1,0},{2,3},{3,2},{4,5},{5,4},{6,7},{7,6},{8,9},{9,8},{10,11... | collective-permute-start | bytes 20 | tf_op jit(solution)/shard_map/ppermute | solution.py:302
  1.1 1.3 %mask.1.rows_ref.refs_0_ = bf16[3,4,128,128]{3,2,1,0:T(8,128)(2,1)S(1)} custom-call(s32[3,4]{1,0:T(4,128)} %mask_hbm.1, bf16[3,4,128,128]{3,2,1,0:T(8,128)(2,1)} %rows_hbm.1), custom_call_target="tpu_custom_call" | custom-call | flops 2000000000 | bytes 8000000 | tf_op jit(solution)/shard_map/mask/pallas_call | solution.py:338
  2.5 0.0 copy-start
  2.5 0.0 copy-start.1
  2.5 0.0 collective-permute-done
  2.5 2.6 %collective-permute-start.2 = (bf16[3,4,128,128]{3,2,1,0:T(8,128)(2,1)S(1)}, bf16[3,4,128,128]{3,2,1,0:T(8,128)(2,1)S(1)}, u32[]{:S(2)}, u32[]{:S(2)}) collective-permute-start(bf16[3,4,128,128]{3,2,1,0:T(8,128)(2,1)S(1)} %mask.1.rows_ref.refs_0_), channel_id=1, source_target_pairs={{0,4},{1,3},{2,6},{3,1},{4,0},{5,7},{6,2},{7,5},{8,12},{9,11},{10,... | collective-permute-start | bytes 1179656 | tf_op jit(solution)/shard_map/ppermute | solution.py:307
  5.7 0.7 %pad_add_fusion = s32[1,2]{1,0:T(1,128)S(1)} fusion(s32[1,1]{1,0:T(1,128)} %collective-permute-done, s32[1,1]{1,0:T(1,128)} %bitcast.6), kind=kLoop, calls=%fused_computation.1 | loop fusion | flops 2 | bytes 16 | tf_op jit(solution)/shard_map/concatenate | solution.py:409
  6.4 1.5 %collective-permute-start.1 = (s32[1,2]{1,0:T(1,128)S(1)}, s32[1,2]{1,0:T(1,128)S(1)}, u32[]{:S(2)}, u32[]{:S(2)}) collective-permute-start(s32[1,2]{1,0:T(1,128)S(1)} %pad_add_fusion), channel_id=1, source_target_pairs={{0,2},{1,5},{2,0},{3,7},{4,6},{5,1},{6,4},{7,3},{8,10},{9,13},{10,... | collective-permute-start | bytes 32 | tf_op jit(solution)/shard_map/ppermute | solution.py:307
  7.9 2.1 %collective-permute-done.1.starts_ref = s32[1,2]{1,0:T(1,128)S(1)} collective-permute-done((s32[1,2]{1,0:T(1,128)S(1)}, s32[1,2]{1,0:T(1,128)S(1)}, u32[]{:S(2)}, u32[]{:S(2)}) %collective-permute-start.1) | collective-permute-done | bytes 40 | tf_op jit(solution)/shard_map/ppermute | solution.py:307
  10.1 0.2 select.2
  10.2 1.6 %collective-permute-start.3 = (bf16[2,4,128,128]{3,2,1,0:T(8,128)(2,1)S(1)}, bf16[2,4,128,128]{3,2,1,0:T(8,128)(2,1)S(1)}, u32[]{:S(2)}, u32[]{:S(2)}) collective-permute-start(bf16[2,4,128,128]{3,2,1,0:T(8,128)(2,1)S(1)} %select.2), channel_id=1, source_target_pairs={{0,2},{1,5},{2,0},{3,7},{4,6},{5,1},{6,4},{7,3},{8,10},{9,13},{10,... | collective-permute-start | bytes 786440 | tf_op jit(solution)/shard_map/ppermute | solution.py:307
  11.8 0.0 collective-permute-done.2.rows_ref.refs_2_
  11.8 0.2 select.3.after_hbm
  12.0 1.4 %collective-permute-start.7 = (bf16[2,4,128,128]{3,2,1,0:T(8,128)(2,1)S(1)}, bf16[2,4,128,128]{3,2,1,0:T(8,128)(2,1)S(1)}, u32[]{:S(2)}, u32[]{:S(2)}) collective-permute-start(bf16[2,4,128,128]{3,2,1,0:T(8,128)(2,1)S(1)} %select.3.after_hbm), channel_id=1, source_target_pairs={{0,2},{1,5},{2,0},{3,7},{4,6},{5,1},{6,4},{7,3},{8,10},{9,13},{10,... | collective-permute-start | bytes 786440 | tf_op jit(solution)/shard_map/ppermute | solution.py:307
  13.4 0.0 collective-permute-start.5
  13.4 0.5 %collective-permute-start.4 = (bf16[3,4,128,128]{3,2,1,0:T(8,128)(2,1)S(1)}, bf16[3,4,128,128]{3,2,1,0:T(8,128)(2,1)S(1)}, u32[]{:S(2)}, u32[]{:S(2)}) collective-permute-start(bf16[3,4,128,128]{3,2,1,0:T(8,128)(2,1)S(1)} %mask.1.rows_ref.refs_0_), channel_id=1, source_target_pairs={{0,1},{1,0},{2,3},{3,2},{4,5},{5,4},{6,7},{7,6},{8,9},{9,8},{10,11... | collective-permute-start | bytes 1179656 | tf_op jit(solution)/shard_map/ppermute | solution.py:302
  13.9 0.0 copy-done
  13.9 0.0 copy-done.1
  13.9 0.0 copy-start.2
  13.9 3.7 %turn.1 = (bf16[12,4,128,256]{3,2,1,0:T(8,128)(2,1)S(1)}, f32[12,6,256]{2,1,0:T(8,128)S(1)}, bf16[72,32,256]{2,1,0:T(8,128)(2,1)S(1)}, s32[1,128]{1,0:T(1,128)S(1)}, f32[12,256]{1,0:T(8,128)S(1)}) custom-call(bf16[2,4,128,128]{3,2,1,0:T(8,128)(2,1)S(1)} %select.3.after_hbm, s32[6,12]{1,0:T(8,128)S(1)} %bitcast.8, s32[1,12]{1,0:T(1,128)S(1)} %copy-done.1, ...), custom_call_target="tpu_custom_call" | custom-call | flops 2000000000 | bytes 8000000 | tf_op jit(solution)/shard_map/turn/pallas_call | solution.py:373
  17.6 0.0 collective-permute-done.3.refs_4_
  17.6 0.1 collective-permute-start.6
  17.7 1.8 %collective-permute-done.7.refs_6_ = bf16[2,4,128,128]{3,2,1,0:T(8,128)(2,1)S(1)} collective-permute-done((bf16[2,4,128,128]{3,2,1,0:T(8,128)(2,1)S(1)}, bf16[2,4,128,128]{3,2,1,0:T(8,128)(2,1)S(1)}, u32[]{:S(2)}, u32[]{:S(2)}) %collective-permute-start.7) | collective-permute-done | bytes 262176 | tf_op jit(solution)/shard_map/ppermute | solution.py:307
  19.5 0.0 collective-permute-start.8
  19.5 0.0 collective-permute-done.6.refs_5_
  19.5 0.0 collective-permute-done.4.refs_1_
  19.5 0.0 collective-permute-done.5.refs_3_
  19.5 1.5 %collective-permute-done.8.refs_7_ = bf16[2,4,128,128]{3,2,1,0:T(8,128)(2,1)S(1)} collective-permute-done((bf16[2,4,128,128]{3,2,1,0:T(8,128)(2,1)S(1)}, bf16[2,4,128,128]{3,2,1,0:T(8,128)(2,1)S(1)}, u32[]{:S(2)}, u32[]{:S(2)}) %collective-permute-start.8) | collective-permute-done | bytes 262176 | tf_op jit(solution)/shard_map/ppermute | solution.py:302
  21.0 0.0 copy-done.2
  21.0 3.2 %density.1 = (f32[12,256]{1,0:T(8,128)S(1)}, f32[32,128]{1,0:T(8,128)S(1)}) custom-call(s32[1]{0:T(128)} %copy.15.start_ref, s32[1,12]{1,0:T(1,128)S(1)} %copy-done.2, s32[1,128]{1,0:T(1,128)S(1)} %get-tuple-element.35.atom_ref, f32[12,256]{1,0:T(8,128)S(1)} %get-tuple-element.36.alive_ref, bf16[12,4,128,256]{3,2,1,0:T(8,128)(2,1)S(1)} %get-tuple-element.38.phit_ref, ...), custom_call_target="tpu_custom_call" | custom-call | flops 2000000000 | bytes 6000000 | tf_op jit(solution)/shard_map/density/pallas_call | solution.py:423
  24.2 0.2 collective-permute-start.9
  24.4 0.6 %copy.14 = f32[12,256]{1,0:T(8,128)} copy(f32[12,256]{1,0:T(8,128)S(1)} %get-tuple-element.61) | data formatting | bytes 24576
  25.0 0.4 %collective-permute-done.9 = f32[32,128]{1,0:T(8,128)S(1)} collective-permute-done((f32[32,128]{1,0:T(8,128)S(1)}, f32[32,128]{1,0:T(8,128)S(1)}, u32[]{:S(2)}, u32[]{:S(2)}) %collective-permute-start.9) | collective-permute-done | bytes 16416 | tf_op jit(solution)/shard_map/ppermute | solution.py:302
  25.5 1.4 %collective-permute-start.12 = (f32[2,32,128]{2,1,0:T(8,128)S(1)}, f32[2,32,128]{2,1,0:T(8,128)S(1)}, u32[]{:S(2)}, u32[]{:S(2)}) collective-permute-start(f32[2,32,128]{2,1,0:T(8,128)S(1)} %pad_maximum_fusion.after_hbm.refs_0_), channel_id=1, source_target_pairs={{0,6},{1,7},{2,4},{3,5},{4,2},{5,3},{6,0},{7,1},{8,14},{9,15},{10,... | collective-permute-start | bytes 98312 | tf_op jit(solution)/shard_map/ppermute | solution.py:302
  26.9 1.5 %collective-permute-start.11 = (f32[2,32,128]{2,1,0:T(8,128)S(1)}, f32[2,32,128]{2,1,0:T(8,128)S(1)}, u32[]{:S(2)}, u32[]{:S(2)}) collective-permute-start(f32[2,32,128]{2,1,0:T(8,128)S(1)} %pad_maximum_fusion.after_hbm.refs_0_), channel_id=1, source_target_pairs={{0,4},{1,5},{2,6},{3,7},{4,0},{5,1},{6,2},{7,3},{8,12},{9,13},{10,... | collective-permute-start | bytes 98312 | tf_op jit(solution)/shard_map/ppermute | solution.py:302
  28.4 0.5 %collective-permute-start.10 = (f32[2,32,128]{2,1,0:T(8,128)S(1)}, f32[2,32,128]{2,1,0:T(8,128)S(1)}, u32[]{:S(2)}, u32[]{:S(2)}) collective-permute-start(f32[2,32,128]{2,1,0:T(8,128)S(1)} %pad_maximum_fusion.after_hbm.refs_0_), channel_id=1, source_target_pairs={{0,2},{1,3},{2,0},{3,1},{4,6},{5,7},{6,4},{7,5},{8,10},{9,11},{10,... | collective-permute-start | bytes 98312 | tf_op jit(solution)/shard_map/ppermute | solution.py:302
  28.9 2.1 %field.2.low_ref = f32[36,25,256]{2,1,0:T(8,128)S(1)} custom-call(f32[2,32,128]{2,1,0:T(8,128)S(1)} %pad_maximum_fusion.after_hbm.refs_0_, f32[12,256]{1,0:T(8,128)S(1)} %get-tuple-element.36.alive_ref, f32[16,25]{1,0:T(8,128)} %bitcast.10, f32[12,6,256]{2,1,0:T(8,128)} %radius_hbm.3, bf16[12,6,25,256]{3,2,1,0:T(8,128)(2,1)} %harm_hbm.5), custom_call_target="tpu_custom_call" | custom-call | flops 2000000000 | bytes 8000000 | tf_op jit(solution)/shard_map/field/pallas_call | solution.py:356
  31.0 0.0 collective-permute-done.12.refs_3_
  31.0 0.0 collective-permute-done.11.refs_2_
  31.0 1.3 %collective-permute-done.10.refs_1_ = f32[2,32,128]{2,1,0:T(8,128)S(1)} collective-permute-done((f32[2,32,128]{2,1,0:T(8,128)S(1)}, f32[2,32,128]{2,1,0:T(8,128)S(1)}, u32[]{:S(2)}, u32[]{:S(2)}) %collective-permute-start.10) | collective-permute-done | bytes 32800 | tf_op jit(solution)/shard_map/ppermute | solution.py:302
  32.3 0.4 scatter.1
  32.7 2.7 %collective-permute-start.13 = (f32[32,256]{1,0:T(8,128)S(1)}, f32[32,256]{1,0:T(8,128)S(1)}, u32[]{:S(2)}, u32[]{:S(2)}) collective-permute-start(f32[32,256]{1,0:T(8,128)S(1)} %get-tuple-element.50), channel_id=1, source_target_pairs={{0,16},{8,24},{16,0},{24,8},{1,17},{9,25},{17,1},{25,9},{2,18},{10... | collective-permute-start | bytes 98312 | tf_op jit(solution)/shard_map/ppermute | solution.py:302
  35.4 1.3 %collective-permute-start.14 = (f32[32,256]{1,0:T(8,128)S(1)}, f32[32,256]{1,0:T(8,128)S(1)}, u32[]{:S(2)}, u32[]{:S(2)}) collective-permute-start(f32[32,256]{1,0:T(8,128)S(1)} %get-tuple-element.51), channel_id=1, source_target_pairs={{0,24},{8,16},{16,8},{24,0},{1,25},{9,17},{17,9},{25,1},{2,26},{10... | collective-permute-start | bytes 98312 | tf_op jit(solution)/shard_map/ppermute | solution.py:302
  36.7 0.2 collective-permute-start.15
  36.9 2.1 %field.3.high_ref = f32[36,25,256]{2,1,0:T(8,128)S(1)} custom-call(f32[32,384]{1,0:T(8,128)S(1)} %get-tuple-element.49.after_hbm.own_ref, f32[12,256]{1,0:T(8,128)S(1)} %get-tuple-element.36.alive_ref, f32[16,25]{1,0:T(8,128)} %bitcast.11, f32[12,6,256]{2,1,0:T(8,128)} %radius_hbm.3, bf16[12,6,25,256]{3,2,1,0:T(8,128)(2,1)} %harm_hbm.5), custom_call_target="tpu_custom_call" | custom-call | flops 2000000000 | bytes 8000000 | tf_op jit(solution)/shard_map/field/pallas_call | solution.py:356
  39.0 0.0 collective-permute-done.13.fa_ref.fb_ref
  39.0 2.0 %collective-permute-done.14.near_b_ref = f32[32,256]{1,0:T(8,128)S(1)} collective-permute-done((f32[32,256]{1,0:T(8,128)S(1)}, f32[32,256]{1,0:T(8,128)S(1)}, u32[]{:S(2)}, u32[]{:S(2)}) %collective-permute-start.14) | collective-permute-done | bytes 32800 | tf_op jit(solution)/shard_map/ppermute | solution.py:302
  41.1 0.0 collective-permute-done.15.near_a_ref
  41.1 1.3 %potential.1 = (f32[16,25]{1,0:T(8,128)}, f32[12,256]{1,0:T(8,128)}) custom-call(f32[32,384]{1,0:T(8,128)S(1)} %get-tuple-element.49.after_hbm.own_ref, f32[32,256]{1,0:T(8,128)S(1)} %collective-permute-done.13.fa_ref.fb_ref, f32[32,256]{1,0:T(8,128)S(1)} %collective-permute-done.13.fa_ref.fb_ref, f32[32,256]{1,0:T(8,128)S(1)} %collective-permute-done.14.near_b_ref, ...), custom_call_target="tpu_custom_call" | custom-call | tf_op jit(solution)/shard_map/potential/pallas_call | solution.py:474
  (1 shorter events, 0.0 us)
Async XLA Ops:
  0.6 1.9 %collective-permute-start = (s32[1,1]{1,0:T(1,128)}, s32[1,1]{1,0:T(1,128)}, u32[]{:S(2)}, u32[]{:S(2)}) collective-permute-start(s32[1,1]{1,0:T(1,128)} %bitcast), channel_id=1, source_target_pairs={{0,1},{1,0},{2,3},{3,2},{4,5},{5,4},{6,7},{7,6},{8,9},{9,8},{10,11... | collective-permute-start | bytes 20 | tf_op jit(solution)/shard_map/ppermute | solution.py:302
  2.5 11.4 %copy-start = (s32[12,6]{0,1:T(8,128)S(1)}, s32[12,6]{0,1:T(8,128)}, u32[]{:S(2)}) copy-start(s32[12,6]{0,1:T(8,128)} %param.17) | copy-start | bytes 868
  2.5 11.4 %copy-start.1 = (s32[1,12]{1,0:T(1,128)S(1)}, s32[1,12]{1,0:T(1,128)}, u32[]{:S(2)}) copy-start(s32[1,12]{1,0:T(1,128)} %size_ref.1) | copy-start | bytes 148
  2.5 9.3 %collective-permute-start.2 = (bf16[3,4,128,128]{3,2,1,0:T(8,128)(2,1)S(1)}, bf16[3,4,128,128]{3,2,1,0:T(8,128)(2,1)S(1)}, u32[]{:S(2)}, u32[]{:S(2)}) collective-permute-start(bf16[3,4,128,128]{3,2,1,0:T(8,128)(2,1)S(1)} %mask.1.rows_ref.refs_0_), channel_id=1, source_target_pairs={{0,4},{1,3},{2,6},{3,1},{4,0},{5,7},{6,2},{7,5},{8,12},{9,11},{10,... | collective-permute-start | bytes 1179656 | tf_op jit(solution)/shard_map/ppermute | solution.py:307
  6.4 3.6 %collective-permute-start.1 = (s32[1,2]{1,0:T(1,128)S(1)}, s32[1,2]{1,0:T(1,128)S(1)}, u32[]{:S(2)}, u32[]{:S(2)}) collective-permute-start(s32[1,2]{1,0:T(1,128)S(1)} %pad_add_fusion), channel_id=1, source_target_pairs={{0,2},{1,5},{2,0},{3,7},{4,6},{5,1},{6,4},{7,3},{8,10},{9,13},{10,... | collective-permute-start | bytes 32 | tf_op jit(solution)/shard_map/ppermute | solution.py:307
  10.2 7.3 %collective-permute-start.3 = (bf16[2,4,128,128]{3,2,1,0:T(8,128)(2,1)S(1)}, bf16[2,4,128,128]{3,2,1,0:T(8,128)(2,1)S(1)}, u32[]{:S(2)}, u32[]{:S(2)}) collective-permute-start(bf16[2,4,128,128]{3,2,1,0:T(8,128)(2,1)S(1)} %select.2), channel_id=1, source_target_pairs={{0,2},{1,5},{2,0},{3,7},{4,6},{5,1},{6,4},{7,3},{8,10},{9,13},{10,... | collective-permute-start | bytes 786440 | tf_op jit(solution)/shard_map/ppermute | solution.py:307
  12.0 7.5 %collective-permute-start.7 = (bf16[2,4,128,128]{3,2,1,0:T(8,128)(2,1)S(1)}, bf16[2,4,128,128]{3,2,1,0:T(8,128)(2,1)S(1)}, u32[]{:S(2)}, u32[]{:S(2)}) collective-permute-start(bf16[2,4,128,128]{3,2,1,0:T(8,128)(2,1)S(1)} %select.3.after_hbm), channel_id=1, source_target_pairs={{0,2},{1,5},{2,0},{3,7},{4,6},{5,1},{6,4},{7,3},{8,10},{9,13},{10,... | collective-permute-start | bytes 786440 | tf_op jit(solution)/shard_map/ppermute | solution.py:307
  13.4 6.1 %collective-permute-start.5 = (bf16[3,4,128,128]{3,2,1,0:T(8,128)(2,1)S(1)}, bf16[3,4,128,128]{3,2,1,0:T(8,128)(2,1)S(1)}, u32[]{:S(2)}, u32[]{:S(2)}) collective-permute-start(bf16[3,4,128,128]{3,2,1,0:T(8,128)(2,1)S(1)} %collective-permute-done.2.rows_ref.refs_2_), channel_id=1, source_target_pairs={{0,1},{1,0},{2,3},{3,2},{4,5},{5,4},{6,7},{7,6},{8,9},{9,8},{10,11... | collective-permute-start | bytes 1179656 | tf_op jit(solution)/shard_map/ppermute | solution.py:302
  13.4 6.1 %collective-permute-start.4 = (bf16[3,4,128,128]{3,2,1,0:T(8,128)(2,1)S(1)}, bf16[3,4,128,128]{3,2,1,0:T(8,128)(2,1)S(1)}, u32[]{:S(2)}, u32[]{:S(2)}) collective-permute-start(bf16[3,4,128,128]{3,2,1,0:T(8,128)(2,1)S(1)} %mask.1.rows_ref.refs_0_), channel_id=1, source_target_pairs={{0,1},{1,0},{2,3},{3,2},{4,5},{5,4},{6,7},{7,6},{8,9},{9,8},{10,11... | collective-permute-start | bytes 1179656 | tf_op jit(solution)/shard_map/ppermute | solution.py:302
  13.9 7.1 %copy-start.2 = (s32[1,12]{1,0:T(1,128)S(1)}, s32[1,12]{1,0:T(1,128)}, u32[]{:S(2)}) copy-start(s32[1,12]{1,0:T(1,128)} %offset_ref.1) | copy-start | bytes 148
  17.6 1.9 %collective-permute-start.6 = (bf16[2,4,128,128]{3,2,1,0:T(8,128)(2,1)S(1)}, bf16[2,4,128,128]{3,2,1,0:T(8,128)(2,1)S(1)}, u32[]{:S(2)}, u32[]{:S(2)}) collective-permute-start(bf16[2,4,128,128]{3,2,1,0:T(8,128)(2,1)S(1)} %collective-permute-done.3.refs_4_), channel_id=1, source_target_pairs={{0,1},{1,0},{2,3},{3,2},{4,5},{5,4},{6,7},{7,6},{8,9},{9,8},{10,11... | collective-permute-start | bytes 786440 | tf_op jit(solution)/shard_map/ppermute | solution.py:302
  19.5 1.5 %collective-permute-start.8 = (bf16[2,4,128,128]{3,2,1,0:T(8,128)(2,1)S(1)}, bf16[2,4,128,128]{3,2,1,0:T(8,128)(2,1)S(1)}, u32[]{:S(2)}, u32[]{:S(2)}) collective-permute-start(bf16[2,4,128,128]{3,2,1,0:T(8,128)(2,1)S(1)} %collective-permute-done.7.refs_6_), channel_id=1, source_target_pairs={{0,1},{1,0},{2,3},{3,2},{4,5},{5,4},{6,7},{7,6},{8,9},{9,8},{10,11... | collective-permute-start | bytes 786440 | tf_op jit(solution)/shard_map/ppermute | solution.py:302
  24.2 1.2 %collective-permute-start.9 = (f32[32,128]{1,0:T(8,128)S(1)}, f32[32,128]{1,0:T(8,128)S(1)}, u32[]{:S(2)}, u32[]{:S(2)}) collective-permute-start(f32[32,128]{1,0:T(8,128)S(1)} %get-tuple-element.44), channel_id=1, source_target_pairs={{0,1},{1,0},{2,3},{3,2},{4,5},{5,4},{6,7},{7,6},{8,9},{9,8},{10,11... | collective-permute-start | bytes 49160 | tf_op jit(solution)/shard_map/ppermute | solution.py:302
  25.5 5.6 %collective-permute-start.12 = (f32[2,32,128]{2,1,0:T(8,128)S(1)}, f32[2,32,128]{2,1,0:T(8,128)S(1)}, u32[]{:S(2)}, u32[]{:S(2)}) collective-permute-start(f32[2,32,128]{2,1,0:T(8,128)S(1)} %pad_maximum_fusion.after_hbm.refs_0_), channel_id=1, source_target_pairs={{0,6},{1,7},{2,4},{3,5},{4,2},{5,3},{6,0},{7,1},{8,14},{9,15},{10,... | collective-permute-start | bytes 98312 | tf_op jit(solution)/shard_map/ppermute | solution.py:302
  26.9 4.2 %collective-permute-start.11 = (f32[2,32,128]{2,1,0:T(8,128)S(1)}, f32[2,32,128]{2,1,0:T(8,128)S(1)}, u32[]{:S(2)}, u32[]{:S(2)}) collective-permute-start(f32[2,32,128]{2,1,0:T(8,128)S(1)} %pad_maximum_fusion.after_hbm.refs_0_), channel_id=1, source_target_pairs={{0,4},{1,5},{2,6},{3,7},{4,0},{5,1},{6,2},{7,3},{8,12},{9,13},{10,... | collective-permute-start | bytes 98312 | tf_op jit(solution)/shard_map/ppermute | solution.py:302
  28.4 3.9 %collective-permute-start.10 = (f32[2,32,128]{2,1,0:T(8,128)S(1)}, f32[2,32,128]{2,1,0:T(8,128)S(1)}, u32[]{:S(2)}, u32[]{:S(2)}) collective-permute-start(f32[2,32,128]{2,1,0:T(8,128)S(1)} %pad_maximum_fusion.after_hbm.refs_0_), channel_id=1, source_target_pairs={{0,2},{1,3},{2,0},{3,1},{4,6},{5,7},{6,4},{7,5},{8,10},{9,11},{10,... | collective-permute-start | bytes 98312 | tf_op jit(solution)/shard_map/ppermute | solution.py:302
  32.7 6.3 %collective-permute-start.13 = (f32[32,256]{1,0:T(8,128)S(1)}, f32[32,256]{1,0:T(8,128)S(1)}, u32[]{:S(2)}, u32[]{:S(2)}) collective-permute-start(f32[32,256]{1,0:T(8,128)S(1)} %get-tuple-element.50), channel_id=1, source_target_pairs={{0,16},{8,24},{16,0},{24,8},{1,17},{9,25},{17,1},{25,9},{2,18},{10... | collective-permute-start | bytes 98312 | tf_op jit(solution)/shard_map/ppermute | solution.py:302
  35.4 5.7 %collective-permute-start.14 = (f32[32,256]{1,0:T(8,128)S(1)}, f32[32,256]{1,0:T(8,128)S(1)}, u32[]{:S(2)}, u32[]{:S(2)}) collective-permute-start(f32[32,256]{1,0:T(8,128)S(1)} %get-tuple-element.51), channel_id=1, source_target_pairs={{0,24},{8,16},{16,8},{24,0},{1,25},{9,17},{17,9},{25,1},{2,26},{10... | collective-permute-start | bytes 98312 | tf_op jit(solution)/shard_map/ppermute | solution.py:302
  36.7 4.4 %collective-permute-start.15 = (f32[32,256]{1,0:T(8,128)S(1)}, f32[32,256]{1,0:T(8,128)S(1)}, u32[]{:S(2)}, u32[]{:S(2)}) collective-permute-start(f32[32,256]{1,0:T(8,128)S(1)} %get-tuple-element.52), channel_id=1, source_target_pairs={{0,8},{8,0},{16,24},{24,16},{1,9},{9,1},{17,25},{25,17},{2,10},{10... | collective-permute-start | bytes 98312 | tf_op jit(solution)/shard_map/ppermute | solution.py:302
